TPU v7x, 32 devices: a whole 2x2x4 slice. The times are simulated.
32 devices in a mesh: dp: 16 (over z, x, core), ctx: 2 (over y).
Axes of the slice: x: 2, y: 2, z: 4, core: 2. Of those that a mesh axis runs over, the one named last changes fastest.
Arguments:
- tokens: bfloat16 [2, 32, 1024, 768], P(None, 'dp', 'ctx'), may hold values from -6 to 6
- cotangent: bfloat16 [2, 32, 1024, 768], P(None, 'dp', 'ctx'), may hold values from -6 to 6
- placing: int32 [2, 32], replicated, may hold values from 0 to 31, as said below
- starts: int32 [2, 32], replicated, may hold values from 0 to 1, as said below
- memory_tokens: float32 [16, 768], replicated, may hold values from -6 to 6
- norm_one_gain: float32 [768], replicated, may hold values from 0.5 to 1.5
- norm_one_bias: float32 [768], replicated, may hold values from -1.8 to 1.8
- qkv_weight: bfloat16 [768, 2304], P('dp'), may hold values from -0.21875 to 0.21875
- qv_bias: float32 [2, 768], replicated, may hold values from -1.8 to 1.8
- out_weight: bfloat16 [768, 768], P('dp'), may hold values from -1.75 to 1.75
- out_bias: float32 [768], replicated, may hold values from -1.8 to 1.8
- norm_two_gain: float32 [768], replicated, may hold values from 0.5 to 1.5
- norm_two_bias: float32 [768], replicated, may hold values from -1.8 to 1.8
- expand_weight: bfloat16 [768, 3072], P('dp'), may hold values from -0.21875 to 0.21875
- expand_bias: float32 [3072], replicated, may hold values from -1.8 to 1.8
- contract_weight: bfloat16 [768, 3072], P('dp'), may hold values from -0.109375 to 0.109375
- contract_bias: float32 [768], replicated, may hold values from -1.8 to 1.8
- read_weight: bfloat16 [768, 384], P('dp'), may hold values from -0.21875 to 0.21875
- key_weight: bfloat16 [768, 384], P('dp'), may hold values from -0.21875 to 0.21875
- value_weight: bfloat16 [768, 768], P('dp'), may hold values from -0.21875 to 0.21875
Outputs:
- block_out: bfloat16 [2, 32, 1024, 768], P(None, 'dp', 'ctx')
- token_grad: bfloat16 [2, 32, 1024, 768], P(None, 'dp', 'ctx')
- memory_tokens_grad: float32 [16, 768], replicated
- norm_one_gain_grad: float32 [768], replicated
- norm_one_bias_grad: float32 [768], replicated
- qkv_weight_grad: float32 [768, 2304], P('dp')
- qv_bias_grad: float32 [2, 768], replicated
- out_weight_grad: float32 [768, 768], P('dp')
- out_bias_grad: float32 [768], replicated
- norm_two_gain_grad: float32 [768], replicated
- norm_two_bias_grad: float32 [768], replicated
- expand_weight_grad: float32 [768, 3072], P('dp')
- expand_bias_grad: float32 [3072], replicated
- contract_weight_grad: float32 [768, 3072], P('dp')
- contract_bias_grad: float32 [768], replicated
- read_weight_grad: float32 [768, 384], P('dp')
- key_weight_grad: float32 [768, 384], P('dp')
- value_weight_grad: float32 [768, 768], P('dp')
Inputs may be any that keep to these rules, and one draw needn't show every extreme that they name: In each micro-batch placing is a permutation; slot p belongs to index p // 2 of dp. A sequence is a run of given positions from one with starts = 1 to the next; its segments lie on consecutive slots of one index, in their order, so every slot p with p % 2 == 0 begins a sequence. `starts`: given position 0 of each micro-batch is 1. A sequence has 1 to 2 segments, and in every micro-batch one has exactly 2.
All inputs are finite; a program needn't handle non-finite values.
Results may differ from a plain program's by a relative error of at most 0.024.
Values may be sent and summed in bfloat16 or wider, within the bound.
A program may use at most 640 MiB of HBM per device.

v0:
```python
import jax
import jax.numpy as jnp
from jax import lax
from jax.sharding import PartitionSpec as P

H = 12
HD = 64


norm_eps = 1e-05


def layer_norm(rows_in, gain_vec, bias_vec):
    centred = rows_in - jnp.mean(rows_in, axis=-1, keepdims=True)
    spread = jnp.mean(centred * centred, axis=-1, keepdims=True)
    return centred * lax.rsqrt(spread + norm_eps) * gain_vec + bias_vec


def feature_map(rows_in):
    halves = jnp.concatenate([jax.nn.softplus(rows_in), jax.nn.softplus(-rows_in)], axis=-1)
    return jnp.concatenate(
        [halves * jnp.roll(halves, amount, axis=-1) for amount in (1, 2, 3)], axis=-1
    )


def gelu_tanh(rows_in):
    return jax.nn.gelu(rows_in, approximate=True)


def divide_rows(read_numer, read_denom):
    return read_numer / read_denom[:, None]


def exact_dot(left_side, right_side):
    return jnp.dot(left_side, right_side, precision=lax.Precision.HIGHEST)


def exact_inner(left_side, right_side):
    return lax.dot_general(
        left_side, right_side, (((0,), (0,)), ((), ())), precision=lax.Precision.HIGHEST
    )


def exact_against(left_side, right_side):
    return lax.dot_general(
        left_side, right_side, (((1,), (1,)), ((), ())), precision=lax.Precision.HIGHEST
    )


def low_inner(left_side, right_side):
    return lax.dot_general(
        left_side, right_side, (((0,), (0,)), ((), ())), preferred_element_type=jnp.float32
    )


def low_against(left_side, right_side):
    return lax.dot_general(
        left_side, right_side, (((1,), (1,)), ((), ())), preferred_element_type=jnp.float32
    )


def positions(row_index, mem_rows, tok_rows, rank_count):
    stride = mem_rows + tok_rows
    source = row_index // stride
    offset = row_index - source * stride
    return jnp.where(
        offset < mem_rows,
        source * mem_rows + offset,
        mem_rows * rank_count + source * tok_rows + offset - mem_rows,
    )


def split_heads(rows_in):
    return rows_in.reshape(rows_in.shape[0], H, HD)


def attend(queries, gathered, causal, model_width):
    query_heads = split_heads(queries)
    key_heads = split_heads(gathered[:, :model_width])
    value_heads = split_heads(gathered[:, model_width:])
    scores = jnp.einsum(
        "qhd,khd->hqk", query_heads, key_heads, preferred_element_type=jnp.float32
    ) * HD ** (-0.5)
    raw_weights = jnp.where(causal[None], jnp.exp(scores), 0.0)
    totals = jnp.sum(raw_weights, axis=-1)
    normed_weights = (raw_weights / totals[:, :, None]).astype(jnp.bfloat16)
    mixed_heads = jnp.einsum(
        "hqk,khd->qhd", normed_weights, value_heads, preferred_element_type=jnp.float32
    )
    return (mixed_heads.reshape(queries.shape[0], model_width), jnp.log(totals))


def attend_back(queries, gathered, causal, log_total, grad_out, model_width):
    query_heads = split_heads(queries)
    key_heads = split_heads(gathered[:, :model_width])
    value_heads = split_heads(gathered[:, model_width:])
    grad_heads = split_heads(grad_out)
    scale_factor = HD ** (-0.5)
    scores = (
        jnp.einsum("qhd,khd->hqk", query_heads, key_heads, preferred_element_type=jnp.float32)
        * scale_factor
    )
    normed = jnp.where(causal[None], jnp.exp(scores - log_total[:, :, None]), 0.0)
    grad_normed = jnp.einsum(
        "qhd,khd->hqk", grad_heads, value_heads, preferred_element_type=jnp.float32
    )
    inner_sum = jnp.sum(normed * grad_normed, axis=-1, keepdims=True)
    grad_scores = (normed * (grad_normed - inner_sum) * scale_factor).astype(jnp.bfloat16)
    grad_query = jnp.einsum(
        "hqk,khd->qhd", grad_scores, key_heads, preferred_element_type=jnp.float32
    )
    grad_key = jnp.einsum(
        "hqk,qhd->khd", grad_scores, query_heads, preferred_element_type=jnp.float32
    )
    grad_value = jnp.einsum(
        "hqk,qhd->khd", normed.astype(jnp.bfloat16), grad_heads, preferred_element_type=jnp.float32
    )
    key_rows = gathered.shape[0]
    grad_kv_term = jnp.concatenate(
        [grad_key.reshape(key_rows, model_width), grad_value.reshape(key_rows, model_width)], axis=1
    )
    return (grad_query.reshape(queries.shape[0], model_width), grad_kv_term)


def local(
    tokens,
    cotangent,
    placing,
    starts,
    memory_tokens,
    norm_one_gain,
    norm_one_bias,
    qkv_weight,
    qv_bias,
    out_weight,
    out_bias,
    norm_two_gain,
    norm_two_bias,
    expand_weight,
    expand_bias,
    contract_weight,
    contract_bias,
    read_weight,
    key_weight,
    value_weight,
):
    groups = lax.axis_size("dp")
    rank_count = lax.axis_size("ctx")
    group_index = lax.axis_index("dp")
    rank_index = lax.axis_index("ctx")
    micro_count = tokens.shape[0]
    slot_count = tokens.shape[1]
    tok_rows = tokens.shape[2]
    model_width = tokens.shape[3]
    pieces = tok_rows // groups
    memory_total = memory_tokens.shape[0]
    mem_rows = memory_total // rank_count
    all_rows = mem_rows + tok_rows
    key_count = all_rows * rank_count
    shard_rows = qkv_weight.shape[0]
    mem_local = lax.dynamic_slice_in_dim(memory_tokens, rank_index * mem_rows, mem_rows, 0)
    qkv_shift = jnp.concatenate([qv_bias[0], jnp.zeros((model_width,), jnp.float32), qv_bias[1]])
    query_pos = positions(
        rank_index * all_rows + jnp.arange(all_rows, dtype=jnp.int32),
        mem_rows,
        tok_rows,
        rank_count,
    )
    key_pos = positions(jnp.arange(key_count, dtype=jnp.int32), mem_rows, tok_rows, rank_count)
    causal = key_pos[None, :] <= query_pos[:, None]
    col_widths = (
        3 * model_width,
        model_width,
        expand_weight.shape[1],
        contract_weight.shape[1],
        read_weight.shape[1],
        key_weight.shape[1],
        value_weight.shape[1],
    )
    weight_total = jnp.zeros((shard_rows, sum_widths(col_widths)), jnp.float32)
    small_total = (
        jnp.zeros((mem_rows, model_width), jnp.float32),
        jnp.zeros((model_width,), jnp.float32),
        jnp.zeros((model_width,), jnp.float32),
        jnp.zeros((2, model_width), jnp.float32),
        jnp.zeros((model_width,), jnp.float32),
        jnp.zeros((model_width,), jnp.float32),
        jnp.zeros((model_width,), jnp.float32),
        jnp.zeros((expand_weight.shape[1],), jnp.float32),
        jnp.zeros((model_width,), jnp.float32),
    )
    block_list = []
    grad_list = []
    for micro_index in range(micro_count):
        whole_weights = (
            lax.all_gather(qkv_weight, "dp", axis=0, tiled=True),
            lax.all_gather(out_weight, "dp", axis=0, tiled=True),
            lax.all_gather(expand_weight, "dp", axis=0, tiled=True),
            lax.all_gather(contract_weight, "dp", axis=0, tiled=True),
            lax.all_gather(read_weight, "dp", axis=0, tiled=True),
            lax.all_gather(key_weight, "dp", axis=0, tiled=True),
            lax.all_gather(value_weight, "dp", axis=0, tiled=True),
        )
        qkv_full, out_full, expand_full, contract_full, read_full, key_full, value_full = (
            whole_weights
        )
        read_exact = read_full.astype(jnp.float32)
        key_exact = key_full.astype(jnp.float32)
        value_exact = value_full.astype(jnp.float32)
        route_map = placing[micro_index]
        inverse = jnp.argsort(route_map)
        slot_ids = group_index * slot_count + jnp.arange(slot_count, dtype=jnp.int32)
        seq_flags = jnp.take(starts[micro_index], jnp.take(route_map, slot_ids))
        spread_tok, spread_cot = (
            lax.all_to_all(
                tokens[micro_index].reshape(slot_count, groups, pieces, model_width),
                "dp",
                split_axis=1,
                concat_axis=0,
                tiled=True,
            ),
            lax.all_to_all(
                cotangent[micro_index].reshape(slot_count, groups, pieces, model_width),
                "dp",
                split_axis=1,
                concat_axis=0,
                tiled=True,
            ),
        )
        routed_tok = jnp.take(spread_tok, route_map, axis=0).reshape(
            groups, slot_count, pieces, model_width
        )
        routed_cot = jnp.take(spread_cot, route_map, axis=0).reshape(
            groups, slot_count, pieces, model_width
        )
        seg_tokens, seg_cotangent = (
            lax.all_to_all(routed_tok, "dp", split_axis=0, concat_axis=2, tiled=True),
            lax.all_to_all(routed_cot, "dp", split_axis=0, concat_axis=2, tiled=True),
        )
        seg_tokens = seg_tokens.reshape(slot_count, tok_rows, model_width)
        seg_cotangent = seg_cotangent.reshape(slot_count, tok_rows, model_width)
        feat_every = feature_map(exact_dot(memory_tokens, read_exact))
        query_pre = exact_dot(mem_local, read_exact)
        query_feat, feat_pull = jax.vjp(feature_map, query_pre)
        feat_dim = query_feat.shape[1]

        def forward_step(carried, inputs):
            memory_state, normal = carried
            seg_rows, start_flag = inputs
            keep_factor = (start_flag == 0).astype(jnp.float32)
            memory_state = memory_state * keep_factor
            normal = normal * keep_factor
            read_numer = exact_dot(query_feat, memory_state)
            read_denom = 1.0 + exact_dot(query_feat, normal[:, None])[:, 0]
            hidden = jnp.concatenate(
                [mem_local + divide_rows(read_numer, read_denom), seg_rows.astype(jnp.float32)],
                axis=0,
            )
            normed_a = layer_norm(hidden, norm_one_gain, norm_one_bias).astype(jnp.bfloat16)
            qkv_low = (
                jnp.dot(normed_a, qkv_full, preferred_element_type=jnp.float32) + qkv_shift
            ).astype(jnp.bfloat16)
            gathered = lax.all_gather(qkv_low[:, model_width:], "ctx", axis=0, tiled=True)
            attended, log_total = attend(qkv_low[:, :model_width], gathered, causal, model_width)
            attn_low = attended.astype(jnp.bfloat16)
            after_attn = (
                hidden + jnp.dot(attn_low, out_full, preferred_element_type=jnp.float32) + out_bias
            )
            normed_b = layer_norm(after_attn, norm_two_gain, norm_two_bias).astype(jnp.bfloat16)
            expanded = (
                jnp.dot(normed_b, expand_full, preferred_element_type=jnp.float32) + expand_bias
            )
            activ_low = gelu_tanh(expanded).astype(jnp.bfloat16)
            result = after_attn + low_against(activ_low, contract_full) + contract_bias
            mem_out = result[:mem_rows]
            key_pre = exact_dot(mem_out, key_exact)
            key_feat = feature_map(key_pre)
            value_new = exact_dot(mem_out, value_exact)
            key_all, value_all = (
                lax.all_gather(key_feat, "ctx", axis=0, tiled=True),
                lax.all_gather(value_new, "ctx", axis=0, tiled=True),
            )
            new_state = memory_state + exact_inner(key_all, value_all)
            new_normal = normal + jnp.sum(key_all, axis=0)
            kept_values = (
                hidden,
                normed_a,
                qkv_low,
                attn_low,
                log_total,
                after_attn,
                normed_b,
                expanded,
                activ_low,
                mem_out,
                key_pre,
                key_feat,
                value_new,
                memory_state,
                normal,
                read_numer,
                read_denom,
            )
            return ((new_state, new_normal), (kept_values, result[mem_rows:]))

        initial = (
            jnp.zeros((feat_dim, model_width), jnp.float32),
            jnp.zeros((feat_dim,), jnp.float32),
        )
        final_state, (kept_all, results) = lax.scan(forward_step, initial, (seg_tokens, seq_flags))

        def backward_step(carried, inputs):
            grad_state, grad_normal = carried
            kept_values, seg_grad, start_flag = inputs
            (
                hidden,
                normed_a,
                qkv_low,
                attn_low,
                log_total,
                after_attn,
                normed_b,
                expanded,
                activ_low,
                mem_out,
                key_pre,
                key_feat,
                value_new,
                memory_state,
                normal,
                read_numer,
                read_denom,
            ) = kept_values[:17]
            keep_factor = (start_flag == 0).astype(jnp.float32)
            grad_key_feat = exact_against(value_new, grad_state) + grad_normal[None, :]
            grad_value_new = exact_dot(key_feat, grad_state)
            key_value, key_pull = jax.vjp(feature_map, key_pre)
            grad_key_pre = key_pull(grad_key_feat)[0]
            grad_mem_out = exact_against(grad_key_pre, key_exact) + exact_against(
                grad_value_new, value_exact
            )
            grad_result = jnp.concatenate([grad_mem_out, seg_grad.astype(jnp.float32)], axis=0)
            grad_contract = grad_result.astype(jnp.bfloat16)
            grad_activ = jnp.dot(grad_contract, contract_full, preferred_element_type=jnp.float32)
            gelu_value, gelu_pull = jax.vjp(gelu_tanh, expanded)
            grad_expanded = gelu_pull(grad_activ)[0].astype(jnp.bfloat16)
            grad_normed_b = low_against(grad_expanded, expand_full)
            two_value, two_pull = jax.vjp(layer_norm, after_attn, norm_two_gain, norm_two_bias)
            grad_after, grad_two_gain, grad_two_bias = two_pull(grad_normed_b)
            grad_after = grad_after + grad_result
            grad_attn_out = grad_after.astype(jnp.bfloat16)
            grad_attended = low_against(grad_attn_out, out_full).astype(jnp.bfloat16)
            gathered = lax.all_gather(qkv_low[:, model_width:], "ctx", axis=0, tiled=True)
            grad_query, grad_kv_term = attend_back(
                qkv_low[:, :model_width], gathered, causal, log_total, grad_attended, model_width
            )
            grad_kv = lax.psum_scatter(
                grad_kv_term.astype(jnp.bfloat16), "ctx", scatter_dimension=0, tiled=True
            ).astype(jnp.float32)
            grad_qkv = jnp.concatenate([grad_query, grad_kv], axis=1).astype(jnp.bfloat16)
            grad_normed_a = low_against(grad_qkv, qkv_full)
            one_value, one_pull = jax.vjp(layer_norm, hidden, norm_one_gain, norm_one_bias)
            grad_hidden, grad_one_gain, grad_one_bias = one_pull(grad_normed_a)
            grad_hidden = grad_hidden + grad_after
            grad_read = grad_hidden[:mem_rows]
            divide_value, divide_pull = jax.vjp(divide_rows, read_numer, read_denom)
            grad_numer, grad_denom = divide_pull(grad_read)
            numer_all, denom_all = (
                lax.all_gather(grad_numer, "ctx", axis=0, tiled=True),
                lax.all_gather(grad_denom, "ctx", axis=0, tiled=True),
            )
            grad_state_in = (grad_state + exact_inner(feat_every, numer_all)) * keep_factor
            grad_normal_in = (
                grad_normal + exact_inner(feat_every, denom_all[:, None])[:, 0]
            ) * keep_factor
            grad_feat = (
                exact_against(grad_numer, memory_state) + grad_denom[:, None] * normal[None, :]
            )
            grad_query_pre = feat_pull(grad_feat)[0]
            grad_mem_local = grad_read + exact_against(grad_query_pre, read_exact)
            outputs = (
                grad_hidden[mem_rows:],
                grad_qkv,
                grad_attn_out,
                grad_expanded,
                grad_contract,
                grad_key_pre,
                grad_value_new,
                grad_query_pre,
                grad_mem_local,
                grad_one_gain,
                grad_one_bias,
                grad_two_gain,
                grad_two_bias,
            )
            return ((grad_state_in, grad_normal_in), outputs)

        final_grad, back_all = lax.scan(
            backward_step, initial, (kept_all, seg_cotangent, seq_flags), reverse=True
        )
        (
            token_part,
            grad_qkv_all,
            grad_attn_all,
            grad_expand_all,
            grad_contract_all,
            grad_key_all,
            grad_value_all,
            grad_query_all,
            grad_mem_all,
            grad_one_gain_all,
            grad_one_bias_all,
            grad_two_gain_all,
            grad_two_bias_all,
        ) = back_all
        normed_a_rows = kept_all[1].reshape(-1, model_width)
        attn_rows = kept_all[3].reshape(-1, model_width)
        normed_b_rows = kept_all[6].reshape(-1, model_width)
        activ_rows = kept_all[8].reshape(-1, activ_low_width(kept_all))
        mem_out_rows = kept_all[9].reshape(-1, model_width)
        grad_qkv_rows = grad_qkv_all.reshape(-1, 3 * model_width)
        grad_attn_rows = grad_attn_all.reshape(-1, model_width)
        grad_expand_rows = grad_expand_all.reshape(-1, grad_expand_all.shape[2])
        grad_contract_rows = grad_contract_all.reshape(-1, model_width)
        grad_key_rows = grad_key_all.reshape(-1, grad_key_all.shape[2])
        grad_value_rows = grad_value_all.reshape(-1, model_width)
        grad_query_sum = jnp.sum(grad_query_all, axis=0)
        shard_grad = lax.psum_scatter(
            jnp.concatenate(
                [
                    low_inner(normed_a_rows, grad_qkv_rows),
                    low_inner(attn_rows, grad_attn_rows),
                    low_inner(normed_b_rows, grad_expand_rows),
                    low_inner(grad_contract_rows, activ_rows),
                    exact_inner(mem_local, grad_query_sum),
                    exact_inner(mem_out_rows, grad_key_rows),
                    exact_inner(mem_out_rows, grad_value_rows),
                ],
                axis=1,
            ).astype(jnp.bfloat16),
            "dp",
            scatter_dimension=0,
            tiled=True,
        )
        weight_total = weight_total + lax.psum(shard_grad, "ctx").astype(jnp.float32)
        qkv_sums = jnp.sum(grad_qkv_rows.astype(jnp.float32), axis=0)
        small_total = (
            small_total[0] + jnp.sum(grad_mem_all, axis=0),
            small_total[1] + jnp.sum(grad_one_gain_all, axis=0),
            small_total[2] + jnp.sum(grad_one_bias_all, axis=0),
            small_total[3] + jnp.stack([qkv_sums[:model_width], qkv_sums[2 * model_width :]]),
            small_total[4] + jnp.sum(grad_attn_rows.astype(jnp.float32), axis=0),
            small_total[5] + jnp.sum(grad_two_gain_all, axis=0),
            small_total[6] + jnp.sum(grad_two_bias_all, axis=0),
            small_total[7] + jnp.sum(grad_expand_rows.astype(jnp.float32), axis=0),
            small_total[8] + jnp.sum(grad_contract_rows.astype(jnp.float32), axis=0),
        )
        out_low = results.astype(jnp.bfloat16).reshape(slot_count, groups, pieces, model_width)
        grad_low = token_part.astype(jnp.bfloat16).reshape(slot_count, groups, pieces, model_width)
        spread_out, spread_grad = (
            lax.all_to_all(out_low, "dp", split_axis=1, concat_axis=0, tiled=True),
            lax.all_to_all(grad_low, "dp", split_axis=1, concat_axis=0, tiled=True),
        )
        back_out = jnp.take(spread_out, inverse, axis=0).reshape(
            groups, slot_count, pieces, model_width
        )
        back_grad = jnp.take(spread_grad, inverse, axis=0).reshape(
            groups, slot_count, pieces, model_width
        )
        home_out, home_grad = (
            lax.all_to_all(back_out, "dp", split_axis=0, concat_axis=2, tiled=True),
            lax.all_to_all(back_grad, "dp", split_axis=0, concat_axis=2, tiled=True),
        )
        block_list.append(home_out.reshape(slot_count, tok_rows, model_width))
        grad_list.append(home_grad.reshape(slot_count, tok_rows, model_width))
    mem_full = lax.dynamic_update_slice_in_dim(
        jnp.zeros((memory_total, model_width), jnp.float32),
        small_total[0],
        rank_index * mem_rows,
        0,
    )
    summed = lax.psum(
        (
            mem_full,
            small_total[1],
            small_total[2],
            small_total[3],
            small_total[4],
            small_total[5],
            small_total[6],
            small_total[7],
            small_total[8],
        ),
        ("dp", "ctx"),
    )
    bounds = [0]
    for col_width in col_widths:
        bounds.append(bounds[-1] + col_width)
    parts_out = [weight_total[:, bounds[position] : bounds[position + 1]] for position in range(7)]
    return (
        jnp.stack(block_list, axis=0),
        jnp.stack(grad_list, axis=0),
        summed[0],
        summed[1],
        summed[2],
        parts_out[0],
        summed[3],
        parts_out[1],
        summed[4],
        summed[5],
        summed[6],
        parts_out[2],
        summed[7],
        parts_out[3],
        summed[8],
        parts_out[4],
        parts_out[5],
        parts_out[6],
    )


def sum_widths(col_widths):
    running = 0
    for col_width in col_widths:
        running = running + col_width
    return running


def activ_low_width(kept_all):
    return kept_all[8].shape[2]


def solution(mesh):
    return jax.shard_map(
        local,
        mesh=mesh,
        in_specs=(
            P(None, "dp", "ctx", None),
            P(None, "dp", "ctx", None),
            P(),
            P(),
            P(),
            P(),
            P(),
            P("dp", None),
            P(),
            P("dp", None),
            P(),
            P(),
            P(),
            P("dp", None),
            P(),
            P("dp", None),
            P(),
            P("dp", None),
            P("dp", None),
            P("dp", None),
        ),
        out_specs=(
            P(None, "dp", "ctx", None),
            P(None, "dp", "ctx", None),
            P(),
            P(),
            P(),
            P("dp", None),
            P(),
            P("dp", None),
            P(),
            P(),
            P(),
            P("dp", None),
            P(),
            P("dp", None),
            P(),
            P("dp", None),
            P("dp", None),
            P("dp", None),
        ),
        check_vma=False,
    )
```

profile of v0, /device:TPU:0, one launch (start us, length us, event | category | flops | bytes accessed | tf_op | source)
XLA Modules:
  0.0 3043.2 jit_solution(2133708851281912446)
XLA Ops:
  21.4 35.5 %all-to-all-done = bf16[2,16,32,768]{3,2,0,1:T(8,128)(2,1)S(1)} async-done(((bf16[2,16,32,768]{3,2,0,1:T(8,128)(2,1)}), bf16[2,16,32,768]{3,2,0,1:T(8,128)(2,1)S(1)}, u32[]{:S(2)}, u32[]{:S(2)}) %all-to-all-start) | async-done | bytes 1572896 | tf_op jit(solution)/shard_map/all_to_all | solution.py:215
  56.9 10.7 all-to-all-start.4
  72.1 29.8 all-to-all-done.4
  101.9 11.1 all-to-all-start.8
  116.3 35.9 %all-to-all-done.8 = bf16[2,16,32,768]{3,2,0,1:T(8,128)(2,1)} async-done(((bf16[2,16,32,768]{3,2,0,1:T(8,128)(2,1)}), bf16[2,16,32,768]{3,2,0,1:T(8,128)(2,1)}, u32[]{:S(2)}, u32[]{:S(2)}) %all-to-all-start.8) | async-done | bytes 1572896 | tf_op jit(solution)/shard_map/all_to_all | solution.py:222
  167.3 33.9 %all-to-all-done.12 = bf16[2,16,32,768]{3,2,0,1:T(8,128)(2,1)} async-done(((bf16[2,16,32,768]{3,2,0,1:T(8,128)(2,1)}), bf16[2,16,32,768]{3,2,0,1:T(8,128)(2,1)}, u32[]{:S(2)}, u32[]{:S(2)}) %all-to-all-start.12) | async-done | bytes 1572896 | tf_op jit(solution)/shard_map/all_to_all | solution.py:222
  208.7 67.5 %all_to_all.276 = bf16[16,2,32,768]{3,2,1,0:T(8,128)(2,1)} all-to-all(bf16[16,2,32,768]{3,2,1,0:T(8,128)(2,1)S(1)} %bitcast.1127), channel_id=1, replica_groups=mesh['dp'=16,'ctx'=2] {'dp'}, dimensions={0} | all-to-all | bytes 3145728 | tf_op jit(solution)/shard_map/all_to_all | solution.py:237
  281.4 40.8 %all-to-all-done.9 = bf16[16,2,32,768]{3,2,1,0:T(8,128)(2,1)S(1)} async-done(((bf16[16,2,32,768]{3,2,1,0:T(8,128)(2,1)}), bf16[16,2,32,768]{3,2,1,0:T(8,128)(2,1)S(1)}, u32[]{:S(2)}, u32[]{:S(2)}) %all-to-all-start.9) | async-done | bytes 1572896 | tf_op jit(solution)/shard_map/all_to_all | solution.py:238
  332.1 57.1 %all_gather.100 = bf16[768,384]{1,0:T(8,128)(2,1)S(1)} all-gather(bf16[48,384]{1,0:T(8,128)(2,1)S(1)} %copy-done.203), channel_id=1, replica_groups=mesh['dp'=16,'ctx'=2] {'dp'}, dimensions={0}, use_global_device_ids=true | all-gather | bytes 626688 | tf_op jit(solution)/shard_map/all_gather | solution.py:200
  390.5 24.0 all_gather.105
  434.1 16.9 all-to-all-done.13
  484.4 344.2 %while.184 = (s32[]{:T(128)}, f32[2304,768]{1,0:T(8,128)}, f32[2304]{0:T(1024)S(1)}, f32[2,520,768]{2,1,0:T(8,128)}, bf16[2,520,768]{2,1,0:T(8,128)(2,1)}, /*ind...) while((s32[]{:T(128)}, f32[2304,768]{1,0:T(8,128)}, ...), condition=%wide.region_7.11_spmd.clone, body=%wide.region_0.10_spmd.clone.sunk | while | flops 9714619392 | bytes 473438752 | solution.py:310
  533.0 41.1 %all-gather.20.cloned.1.call-done = bf16[1040,1536]{1,0:T(8,128)(2,1)} async-done(((bf16[520,1536]{1,0:T(8,128)(2,1)}), bf16[1040,1536]{1,0:T(8,128)(2,1)}) %all-gather.20.cloned.1.call-update) | async-done | bytes 3194896 | tf_op jit(solution)/shard_map/while/body/eval_jaxpr/all_gather | solution.py:263
  585.5 18.7 fusion.659
  604.2 13.3 fusion.660
  700.0 33.0 %all-gather.20.cloned.1.call-done = bf16[1040,1536]{1,0:T(8,128)(2,1)} async-done(((bf16[520,1536]{1,0:T(8,128)(2,1)}), bf16[1040,1536]{1,0:T(8,128)(2,1)}) %all-gather.20.cloned.1.call-update) | async-done | bytes 3194896 | tf_op jit(solution)/shard_map/while/body/eval_jaxpr/all_gather | solution.py:263
  744.4 18.7 fusion.659
  763.1 13.3 fusion.660
  809.8 10.1 convolution_add_fusion.12
  843.8 507.7 %while.186 = (s32[]{:T(128)}, f32[2304,768]{0,1:T(8,128)}, f32[2304]{0:T(1024)S(1)}, bf16[2,512,768]{2,1,0:T(8,128)(2,1)}, bf16[2,520,2304]{1,2,0:T(8,128)(2,1)}...) while((s32[]{:T(128)}, f32[2304,768]{0,1:T(8,128)}, ...), condition=%wide.region_34.38_spmd.clone, body=%wide.region_18.37_spmd.clone.sunk | while | flops 12649980928 | bytes 601820160 | solution.py:398
  912.7 11.7 fusion.738
  924.4 13.1 exponential_select_fusion.6
  937.4 12.1 fusion.737
  949.5 42.9 %fusion.739 = bf16[12,64,1040]{2,1,0:T(8,128)(2,1)} fusion(bf16[520,12,64]{0,2,1:T(8,128)(2,1)} %bitcast.1096, f32[12,520,1040]{2,1,0:T(8,128)} %exponential_select_fusion.6, f32[12,520,1040]{2,1,0:T(8,128)} %fusion.738), kind=kOutput, calls=%fused_computation.231.clone.1 | convolution fusion | flops 863922816 | bytes 54312960 | tf_op jit(solution)/shard_map/while/body/eval_jaxpr/hqk,qhd->khd/dot_general | solution.py:112
  1011.2 42.5 %fusion.740 = bf16[12,64,520]{2,1,0:T(8,128)(2,1)} fusion(bf16[1040,12,64]{0,2,1:T(8,128)(2,1)} %bitcast.1082, f32[12,520,1040]{2,1,0:T(8,128)} %exponential_select_fusion.6, f32[12,520,1040]{2,1,0:T(8,128)} %fusion.738), kind=kOutput, calls=%fused_computation.259.clone.1 | convolution fusion | flops 863523456 | bytes 54312960 | tf_op jit(solution)/shard_map/while/body/eval_jaxpr/hqk,khd->qhd/dot_general | solution.py:109
  1157.8 11.7 fusion.738
  1169.5 12.8 exponential_select_fusion.6
  1182.3 12.1 fusion.737
  1194.4 42.9 %fusion.739 = bf16[12,64,1040]{2,1,0:T(8,128)(2,1)} fusion(bf16[520,12,64]{0,2,1:T(8,128)(2,1)} %bitcast.1096, f32[12,520,1040]{2,1,0:T(8,128)} %exponential_select_fusion.6, f32[12,520,1040]{2,1,0:T(8,128)} %fusion.738), kind=kOutput, calls=%fused_computation.231.clone.1 | convolution fusion | flops 863922816 | bytes 54312960 | tf_op jit(solution)/shard_map/while/body/eval_jaxpr/hqk,qhd->khd/dot_general | solution.py:112
  1256.0 42.5 %fusion.740 = bf16[12,64,520]{2,1,0:T(8,128)(2,1)} fusion(bf16[1040,12,64]{0,2,1:T(8,128)(2,1)} %bitcast.1082, f32[12,520,1040]{2,1,0:T(8,128)} %exponential_select_fusion.6, f32[12,520,1040]{2,1,0:T(8,128)} %fusion.738), kind=kOutput, calls=%fused_computation.259.clone.1 | convolution fusion | flops 863523456 | bytes 54312960 | tf_op jit(solution)/shard_map/while/body/eval_jaxpr/hqk,khd->qhd/dot_general | solution.py:109
  1370.0 10.5 fusion.308
  1380.5 11.1 fusion.309
  1430.7 338.6 %while.185 = (s32[]{:T(128)}, f32[2304,768]{1,0:T(8,128)}, f32[2304]{0:T(1024)S(1)}, f32[2,520,768]{2,1,0:T(8,128)}, bf16[2,520,768]{2,1,0:T(8,128)(2,1)}, /*ind...) while((s32[]{:T(128)}, f32[2304,768]{1,0:T(8,128)}, ...), condition=%wide.region_16.20_spmd.clone, body=%wide.region_9.19_spmd.clone.sunk | while | flops 9714619392 | bytes 474576960 | solution.py:310
  1476.2 39.2 %all-gather.22.cloned.1.call-done = bf16[1040,1536]{1,0:T(8,128)(2,1)} async-done(((bf16[520,1536]{1,0:T(8,128)(2,1)}), bf16[1040,1536]{1,0:T(8,128)(2,1)}) %all-gather.22.cloned.1.call-update) | async-done | bytes 3194896 | tf_op jit(solution)/shard_map/while/body/eval_jaxpr/all_gather | solution.py:263
  1526.7 18.7 fusion.688
  1545.4 13.3 fusion.689
  1637.9 35.9 %all-gather.22.cloned.1.call-done = bf16[1040,1536]{1,0:T(8,128)(2,1)} async-done(((bf16[520,1536]{1,0:T(8,128)(2,1)}), bf16[1040,1536]{1,0:T(8,128)(2,1)}) %all-gather.22.cloned.1.call-update) | async-done | bytes 3194896 | tf_op jit(solution)/shard_map/while/body/eval_jaxpr/all_gather | solution.py:263
  1685.1 18.7 fusion.688
  1703.8 13.3 fusion.689
  1750.5 10.1 convolution_add_fusion.13
  1784.6 504.4 %while.187 = (s32[]{:T(128)}, f32[2304,768]{0,1:T(8,128)}, f32[2304]{0:T(1024)S(1)}, bf16[2,512,768]{2,1,0:T(8,128)(2,1)}, bf16[2,520,2304]{1,2,0:T(8,128)(2,1)}...) while((s32[]{:T(128)}, f32[2304,768]{0,1:T(8,128)}, ...), condition=%wide.region_51.55_spmd.clone, body=%wide.region_35.54_spmd.clone.sunk | while | flops 12649980928 | bytes 601820224 | solution.py:398
  1853.6 11.7 fusion.789
  1865.3 13.1 exponential_select_fusion.7
  1878.3 12.1 fusion.788
  1890.4 42.9 %fusion.790 = bf16[12,64,1040]{2,1,0:T(8,128)(2,1)} fusion(bf16[520,12,64]{0,2,1:T(8,128)(2,1)} %bitcast.1098, f32[12,520,1040]{2,1,0:T(8,128)} %exponential_select_fusion.7, f32[12,520,1040]{2,1,0:T(8,128)} %fusion.789), kind=kOutput, calls=%fused_computation.406.clone.1 | convolution fusion | flops 863922816 | bytes 54312960 | tf_op jit(solution)/shard_map/while/body/eval_jaxpr/hqk,qhd->khd/dot_general | solution.py:112
  1951.9 42.5 %fusion.791 = bf16[12,64,520]{2,1,0:T(8,128)(2,1)} fusion(bf16[1040,12,64]{0,2,1:T(8,128)(2,1)} %bitcast.1084, f32[12,520,1040]{2,1,0:T(8,128)} %exponential_select_fusion.7, f32[12,520,1040]{2,1,0:T(8,128)} %fusion.789), kind=kOutput, calls=%fused_computation.434.clone.1 | convolution fusion | flops 863523456 | bytes 54312960 | tf_op jit(solution)/shard_map/while/body/eval_jaxpr/hqk,khd->qhd/dot_general | solution.py:109
  2098.7 11.7 fusion.789
  2110.5 12.8 exponential_select_fusion.7
  2123.3 12.1 fusion.788
  2135.3 42.9 %fusion.790 = bf16[12,64,1040]{2,1,0:T(8,128)(2,1)} fusion(bf16[520,12,64]{0,2,1:T(8,128)(2,1)} %bitcast.1098, f32[12,520,1040]{2,1,0:T(8,128)} %exponential_select_fusion.7, f32[12,520,1040]{2,1,0:T(8,128)} %fusion.789), kind=kOutput, calls=%fused_computation.406.clone.1 | convolution fusion | flops 863922816 | bytes 54312960 | tf_op jit(solution)/shard_map/while/body/eval_jaxpr/hqk,qhd->khd/dot_general | solution.py:112
  2196.9 42.5 %fusion.791 = bf16[12,64,520]{2,1,0:T(8,128)(2,1)} fusion(bf16[1040,12,64]{0,2,1:T(8,128)(2,1)} %bitcast.1084, f32[12,520,1040]{2,1,0:T(8,128)} %exponential_select_fusion.7, f32[12,520,1040]{2,1,0:T(8,128)} %fusion.789), kind=kOutput, calls=%fused_computation.434.clone.1 | convolution fusion | flops 863523456 | bytes 54312960 | tf_op jit(solution)/shard_map/while/body/eval_jaxpr/hqk,khd->qhd/dot_general | solution.py:109
  2289.8 10.1 fusion.307
  2338.7 54.0 %all-to-all-done.10 = bf16[2,16,32,768]{3,2,0,1:T(8,128)(2,1)S(1)} async-done(((bf16[2,16,32,768]{3,2,0,1:T(8,128)(2,1)}), bf16[2,16,32,768]{3,2,0,1:T(8,128)(2,1)S(1)}, u32[]{:S(2)}, u32[]{:S(2)}) %all-to-all-start.10) | async-done | bytes 1572896 | tf_op jit(solution)/shard_map/all_to_all | solution.py:462
  2392.8 21.2 all-to-all-start.2
  2416.7 45.1 %all-to-all-done.2 = bf16[2,16,32,768]{3,2,0,1:T(8,128)(2,1)S(1)} async-done(((bf16[2,16,32,768]{3,2,0,1:T(8,128)(2,1)}), bf16[2,16,32,768]{3,2,0,1:T(8,128)(2,1)S(1)}, u32[]{:S(2)}, u32[]{:S(2)}) %all-to-all-start.2) | async-done | bytes 1572896 | tf_op jit(solution)/shard_map/all_to_all | solution.py:461
  2474.7 29.3 all-to-all-done.14
  2504.0 13.5 all-to-all-start.6
  2527.7 43.2 %all-to-all-done.6 = bf16[2,16,32,768]{3,2,0,1:T(8,128)(2,1)} async-done(((bf16[2,16,32,768]{3,2,0,1:T(8,128)(2,1)}), bf16[2,16,32,768]{3,2,0,1:T(8,128)(2,1)}, u32[]{:S(2)}, u32[]{:S(2)}) %all-to-all-start.6) | async-done | bytes 1572896 | tf_op jit(solution)/shard_map/all_to_all | solution.py:461
  2591.5 21.0 all-to-all-done.11
  2612.5 85.4 %all_to_all.277 = bf16[16,2,32,768]{3,2,1,0:T(8,128)(2,1)} all-to-all(bf16[16,2,32,768]{3,2,1,0:T(8,128)(2,1)} %bitcast.1140), channel_id=1, replica_groups=mesh['dp'=16,'ctx'=2] {'dp'}, dimensions={0} | all-to-all | bytes 3145728 | tf_op jit(solution)/shard_map/all_to_all | solution.py:472
  2698.0 53.4 %all_to_all.278 = bf16[16,2,32,768]{3,2,1,0:T(8,128)(2,1)} all-to-all(bf16[16,2,32,768]{3,2,1,0:T(8,128)(2,1)S(1)} %bitcast.1132), channel_id=1, replica_groups=mesh['dp'=16,'ctx'=2] {'dp'}, dimensions={0} | all-to-all | bytes 3145728 | tf_op jit(solution)/shard_map/all_to_all | solution.py:471
  2764.3 64.6 %reduce-scatter.15.cloned.1.call-done = bf16[48,10752]{1,0:T(8,128)(2,1)} async-done(((bf16[768,10752]{1,0:T(8,128)(2,1)}), bf16[48,10752]{1,0:T(8,128)(2,1)}) %reduce-scatter.15.cloned.1.call-update) | async-done | bytes 1032208 | tf_op jit(solution)/shard_map/reduce_scatter | solution.py:428
  2853.3 38.7 %all-reduce.39.cloned.1.call-done = (bf16[48,10752]{1,0:T(8,128)(2,1)}, bf16[48,10752]{1,0:T(8,128)(2,1)}) async-done(((bf16[48,10752]{1,0:T(8,128)(2,1)}, bf16[48,10752]{1,0:T(8,128)(2,1)}), (bf16[48,10752]{1,0:T(8,128)(2,1)}, bf16[48,10752]{1,0:T(8,128)(2,1)})) %all-reduce.39.cloned.1.call-update) | async-done | bytes 2064400 | tf_op jit(solution)/shard_map/psum | solution.py:445
  2897.1 127.4 %all-reduce.37.cloned.1.call-done = (f32[16,768]{1,0:T(8,128)}, f32[768]{0:T(1024)}, f32[768]{0:T(1024)}, f32[2,768]{1,0:T(2,128)}, f32[768]{0:T(1024)}, /*index...) async-done(((f32[16,768]{1,0:T(8,128)}, f32[768]{0:T(1024)}, f32[768]{0:T(1024)}, f32[2,768]{1,0:T(2,128)}, f32[768]{0:T(1024)}, /*index=5*/f32[768]{0:T(1024)}, ...) | async-done | bytes 86032 | tf_op jit(solution)/shard_map/psum | solution.py:482
  (1781 shorter events, 1163.9 us)
Async XLA Ops:
  7.2 324.9 %copy-start = (f32[16,768]{1,0:T(8,128)S(1)}, f32[16,768]{1,0:T(8,128)}, u32[]{:S(2)}) copy-start(f32[16,768]{1,0:T(8,128)} %param.37) | copy-start | bytes 147460
  7.2 419.3 %all-gather.18.cloned.1.call-start = ((), (), s32[]{:S(2)}) async-start(), calls=%async_computation.24 | async-start | bytes 1253376 | tf_op jit(solution)/shard_map/all_gather | solution.py:202
  7.9 445.7 %all-gather.12.cloned.1.call-start = ((), (), s32[]{:S(2)}) async-start(), calls=%async_computation.21 | async-start | bytes 1253376 | tf_op jit(solution)/shard_map/all_gather | solution.py:197
  12.1 44.8 %all-to-all-start = ((bf16[2,16,32,768]{3,2,0,1:T(8,128)(2,1)}), bf16[2,16,32,768]{3,2,0,1:T(8,128)(2,1)S(1)}, u32[]{:S(2)}, u32[]{:S(2)}) async-start(bf16[2,16,32,768]{3,2,0,1:T(8,128)(2,1)} %copy.148), calls=%async_computation.2 | async-start | bytes 3145728 | tf_op jit(solution)/shard_map/all_to_all | solution.py:215
  19.4 434.3 %all-gather.10.cloned.1.call-start = ((), (), s32[]{:S(2)}) async-start(), calls=%async_computation.20 | async-start | bytes 3760128 | tf_op jit(solution)/shard_map/all_gather | solution.py:196
  56.9 45.0 %all-to-all-start.4 = ((bf16[2,16,32,768]{3,2,0,1:T(8,128)(2,1)}), bf16[2,16,32,768]{3,2,0,1:T(8,128)(2,1)S(1)}, u32[]{:S(2)}, u32[]{:S(2)}) async-start(bf16[2,16,32,768]{3,2,0,1:T(8,128)(2,1)} %copy.154), calls=%async_computation.6 | async-start | bytes 3145728 | tf_op jit(solution)/shard_map/all_to_all | solution.py:215
  101.9 14.4 copy-start.89
  101.9 50.2 %all-to-all-start.8 = ((bf16[2,16,32,768]{3,2,0,1:T(8,128)(2,1)}), bf16[2,16,32,768]{3,2,0,1:T(8,128)(2,1)}, u32[]{:S(2)}, u32[]{:S(2)}) async-start(bf16[2,16,32,768]{3,2,0,1:T(8,128)(2,1)} %copy.160), calls=%async_computation.10 | async-start | bytes 3145728 | tf_op jit(solution)/shard_map/all_to_all | solution.py:222
  113.0 340.7 %all-gather.14.cloned.1.call-start = ((), (), s32[]{:S(2)}) async-start(), calls=%async_computation.22 | async-start | bytes 5013504 | tf_op jit(solution)/shard_map/all_gather | solution.py:198
  116.3 45.0 %copy-start.223 = (s32[2,32]{1,0:T(2,128)S(1)}, s32[2,32]{1,0:T(2,128)}, u32[]{:S(2)}) copy-start(s32[2,32]{1,0:T(2,128)} %param.35) | copy-start | bytes 772
  152.1 49.1 %all-to-all-start.12 = ((bf16[2,16,32,768]{3,2,0,1:T(8,128)(2,1)}), bf16[2,16,32,768]{3,2,0,1:T(8,128)(2,1)}, u32[]{:S(2)}, u32[]{:S(2)}) async-start(bf16[2,16,32,768]{3,2,0,1:T(8,128)(2,1)} %copy.164), calls=%async_computation.14 | async-start | bytes 3145728 | tf_op jit(solution)/shard_map/all_to_all | solution.py:222
  276.3 45.9 %all-to-all-start.9 = ((bf16[16,2,32,768]{3,2,1,0:T(8,128)(2,1)}), bf16[16,2,32,768]{3,2,1,0:T(8,128)(2,1)S(1)}, u32[]{:S(2)}, u32[]{:S(2)}) async-start(bf16[16,2,32,768]{3,2,1,0:T(8,128)(2,1)} %bitcast.50), calls=%async_computation.11 | async-start | bytes 3145728 | tf_op jit(solution)/shard_map/all_to_all | solution.py:238
  280.8 51.3 %copy-start.203 = (bf16[48,384]{1,0:T(8,128)(2,1)S(1)}, bf16[48,384]{1,0:T(8,128)(2,1)}, u32[]{:S(2)}) copy-start(bf16[48,384]{1,0:T(8,128)(2,1)} %param.50) | copy-start | bytes 110596
  280.8 172.9 %all-gather.16.cloned.1.call-start = ((), (), s32[]{:S(2)}) async-start(), calls=%async_computation.23 | async-start | bytes 5013504 | tf_op jit(solution)/shard_map/all_gather | solution.py:199
  322.1 92.4 %all-to-all-start.5 = ((bf16[16,2,32,768]{3,2,1,0:T(8,128)(2,1)}), bf16[16,2,32,768]{3,2,1,0:T(8,128)(2,1)S(1)}, u32[]{:S(2)}, u32[]{:S(2)}) async-start(bf16[16,2,32,768]{3,2,1,0:T(8,128)(2,1)} %bitcast.1126), calls=%async_computation.7 | async-start | bytes 3145728 | tf_op jit(solution)/shard_map/all_to_all | solution.py:237
  331.3 59.2 %copy-start.204 = (bf16[48,384]{1,0:T(8,128)(2,1)S(1)}, bf16[48,384]{1,0:T(8,128)(2,1)}, u32[]{:S(2)}) copy-start(bf16[48,384]{1,0:T(8,128)(2,1)} %param.51) | copy-start | bytes 110596
  331.4 83.2 %copy-start.14 = (s32[32]{0:T(128)}, s32[32]{0:T(128)S(1)}, u32[]{:S(2)}) copy-start(s32[32]{0:T(128)S(1)} %get-tuple-element.4099) | copy-start | bytes 388
  331.4 89.1 %copy-start.12 = (s32[32]{0:T(128)}, s32[32]{0:T(128)S(1)}, u32[]{:S(2)}) copy-start(s32[32]{0:T(128)S(1)} %get-tuple-element.4100) | copy-start | bytes 388
  414.6 36.4 %all-to-all-start.13 = ((bf16[16,2,32,768]{3,2,1,0:T(8,128)(2,1)}), bf16[16,2,32,768]{3,2,1,0:T(8,128)(2,1)}, u32[]{:S(2)}, u32[]{:S(2)}) async-start(bf16[16,2,32,768]{3,2,1,0:T(8,128)(2,1)} %bitcast.70), calls=%async_computation.15 | async-start | bytes 3145728 | tf_op jit(solution)/shard_map/all_to_all | solution.py:238
  506.7 67.4 %all-gather.20.cloned.1.call-start = ((), (), s32[]{:S(2)}) async-start(), calls=%async_computation.29 | async-start | bytes 4792320 | tf_op jit(solution)/shard_map/while/body/eval_jaxpr/all_gather | solution.py:263
  604.2 13.3 copy-start.7
  604.2 13.3 copy-start.231
  628.7 16.1 slice-start.22
  628.8 16.1 slice-start.23
  633.0 17.0 copy-start.68
  667.7 65.3 %all-gather.20.cloned.1.call-start = ((), (), s32[]{:S(2)}) async-start(), calls=%async_computation.29 | async-start | bytes 4792320 | tf_op jit(solution)/shard_map/while/body/eval_jaxpr/all_gather | solution.py:263
  763.1 13.3 copy-start.7
  763.1 13.3 copy-start.231
  787.5 16.1 slice-start.22
  787.6 16.1 slice-start.23
  791.8 17.0 copy-start.68
  851.3 51.1 %all-gather.24.cloned.1.call-start = ((), (), s32[]{:S(2)}) async-start(), calls=%async_computation.31 | async-start | bytes 4792320 | tf_op jit(solution)/shard_map/while/body/eval_jaxpr/all_gather | solution.py:353
  856.7 197.0 %reduce-scatter.17.cloned.1.call-start = ((), (), s32[]{:S(2)}) async-start(), calls=%async_computation.32 | async-start | bytes 4792320 | tf_op jit(solution)/shard_map/while
  1096.4 51.1 %all-gather.24.cloned.1.call-start = ((), (), s32[]{:S(2)}) async-start(), calls=%async_computation.31 | async-start | bytes 4792320 | tf_op jit(solution)/shard_map/while/body/eval_jaxpr/all_gather | solution.py:353
  1101.9 196.7 %reduce-scatter.17.cloned.1.call-start = ((), (), s32[]{:S(2)}) async-start(), calls=%async_computation.32 | async-start | bytes 4792320 | tf_op jit(solution)/shard_map/while
  1452.8 62.6 %all-gather.22.cloned.1.call-start = ((), (), s32[]{:S(2)}) async-start(), calls=%async_computation.30 | async-start | bytes 4792320 | tf_op jit(solution)/shard_map/while/body/eval_jaxpr/all_gather | solution.py:263
  1569.9 16.1 slice-start.24
  1570.0 16.1 slice-start.25
  1574.2 17.0 copy-start.69
  1609.0 64.8 %all-gather.22.cloned.1.call-start = ((), (), s32[]{:S(2)}) async-start(), calls=%async_computation.30 | async-start | bytes 4792320 | tf_op jit(solution)/shard_map/while/body/eval_jaxpr/all_gather | solution.py:263
  1728.2 16.1 slice-start.24
  1728.2 16.1 slice-start.25
  1732.4 17.0 copy-start.69
  1792.1 51.2 %all-gather.26.cloned.1.call-start = ((), (), s32[]{:S(2)}) async-start(), calls=%async_computation.33 | async-start | bytes 4792320 | tf_op jit(solution)/shard_map/while/body/eval_jaxpr/all_gather | solution.py:353
  1797.6 196.9 %reduce-scatter.19.cloned.1.call-start = ((), (), s32[]{:S(2)}) async-start(), calls=%async_computation.34 | async-start | bytes 4792320 | tf_op jit(solution)/shard_map/while
  2037.3 51.1 %all-gather.26.cloned.1.call-start = ((), (), s32[]{:S(2)}) async-start(), calls=%async_computation.33 | async-start | bytes 4792320 | tf_op jit(solution)/shard_map/while/body/eval_jaxpr/all_gather | solution.py:353
  2042.8 196.6 %reduce-scatter.19.cloned.1.call-start = ((), (), s32[]{:S(2)}) async-start(), calls=%async_computation.34 | async-start | bytes 4792320 | tf_op jit(solution)/shard_map/while
  2289.0 475.2 %reduce-scatter.13.cloned.1.call-start = ((), (), s32[]{:S(2)}) async-start(), calls=%async_computation.25 | async-start | bytes 17547264 | tf_op jit(solution)/shard_map/reduce_scatter | solution.py:428
  2289.1 13.6 slice-start.18
  2289.6 539.3 %reduce-scatter.15.cloned.1.call-start = ((), (), s32[]{:S(2)}) async-start(), calls=%async_computation.26 | async-start | bytes 17547264 | tf_op jit(solution)/shard_map/reduce_scatter | solution.py:428
  2330.4 62.4 %all-to-all-start.10 = ((bf16[2,16,32,768]{3,2,0,1:T(8,128)(2,1)}), bf16[2,16,32,768]{3,2,0,1:T(8,128)(2,1)S(1)}, u32[]{:S(2)}, u32[]{:S(2)}) async-start(bf16[2,16,32,768]{3,2,0,1:T(8,128)(2,1)} %copy.162), calls=%async_computation.12 | async-start | bytes 3145728 | tf_op jit(solution)/shard_map/all_to_all | solution.py:462
  2392.8 69.0 %all-to-all-start.2 = ((bf16[2,16,32,768]{3,2,0,1:T(8,128)(2,1)}), bf16[2,16,32,768]{3,2,0,1:T(8,128)(2,1)S(1)}, u32[]{:S(2)}, u32[]{:S(2)}) async-start(bf16[2,16,32,768]{3,2,0,1:T(8,128)(2,1)} %copy.152), calls=%async_computation.4 | async-start | bytes 3145728 | tf_op jit(solution)/shard_map/all_to_all | solution.py:461
  2462.9 41.1 %all-to-all-start.14 = ((bf16[2,16,32,768]{3,2,0,1:T(8,128)(2,1)}), bf16[2,16,32,768]{3,2,0,1:T(8,128)(2,1)S(1)}, u32[]{:S(2)}, u32[]{:S(2)}) async-start(bf16[2,16,32,768]{3,2,0,1:T(8,128)(2,1)} %copy.166), calls=%async_computation.16 | async-start | bytes 3145728 | tf_op jit(solution)/shard_map/all_to_all | solution.py:462
  2474.7 42.8 %copy-start.15 = (s32[32]{0:T(128)S(1)}, s32[32]{0:T(128)}, u32[]{:S(2)}) copy-start(s32[32]{0:T(128)} %copy-done.14) | copy-start | bytes 388
  2504.0 66.9 %all-to-all-start.6 = ((bf16[2,16,32,768]{3,2,0,1:T(8,128)(2,1)}), bf16[2,16,32,768]{3,2,0,1:T(8,128)(2,1)}, u32[]{:S(2)}, u32[]{:S(2)}) async-start(bf16[2,16,32,768]{3,2,0,1:T(8,128)(2,1)} %copy.158), calls=%async_computation.8 | async-start | bytes 3145728 | tf_op jit(solution)/shard_map/all_to_all | solution.py:461
  2527.7 52.9 %copy-start.13 = (s32[32]{0:T(128)S(1)}, s32[32]{0:T(128)}, u32[]{:S(2)}) copy-start(s32[32]{0:T(128)} %copy-done.12) | copy-start | bytes 388
  2570.9 41.6 %all-to-all-start.11 = ((bf16[16,2,32,768]{3,2,1,0:T(8,128)(2,1)}), bf16[16,2,32,768]{3,2,1,0:T(8,128)(2,1)S(1)}, u32[]{:S(2)}, u32[]{:S(2)}) async-start(bf16[16,2,32,768]{3,2,1,0:T(8,128)(2,1)} %bitcast.1134), calls=%async_computation.13 | async-start | bytes 3145728 | tf_op jit(solution)/shard_map/all_to_all | solution.py:472
  2591.5 106.5 %copy-start.90 = (bf16[32,1,32,768]{3,2,0,1:T(8,128)(2,1)S(1)}, bf16[32,1,32,768]{3,2,0,1:T(8,128)(2,1)}, u32[]{:S(2)}) copy-start(bf16[32,1,32,768]{3,2,0,1:T(8,128)(2,1)} %get-tuple-element.4104) | copy-start | bytes 4718596
  2612.5 138.8 %copy-start.85 = (bf16[16,2,32,768]{3,2,1,0:T(8,128)(2,1)}, bf16[16,2,32,768]{3,2,1,0:T(8,128)(2,1)S(1)}, u32[]{:S(2)}) copy-start(bf16[16,2,32,768]{3,2,1,0:T(8,128)(2,1)S(1)} %all-to-all-done.11) | copy-start | bytes 4718596
  2751.3 96.2 %all-to-all-start.7 = ((bf16[16,2,32,768]{3,2,1,0:T(8,128)(2,1)}), bf16[16,2,32,768]{3,2,1,0:T(8,128)(2,1)}, u32[]{:S(2)}, u32[]{:S(2)}) async-start(bf16[16,2,32,768]{3,2,1,0:T(8,128)(2,1)} %bitcast.40), calls=%async_computation.9 | async-start | bytes 3145728 | tf_op jit(solution)/shard_map/all_to_all | solution.py:471
  2756.5 135.5 %all-reduce.39.cloned.1.call-start = ((), (), s32[]{:S(2)}) async-start(), calls=%async_computation.28 | async-start | bytes 4128768 | tf_op jit(solution)/shard_map/psum | solution.py:445
  2760.4 75.1 %slice-start.20 = ((s8[6389760]{0:T(1024)(128)(4,1)}), s8[2195456]{0:T(1024)(128)(4,1)S(1)}, s32[]{:S(2)}) async-start(s8[6389760]{0:T(1024)(128)(4,1)} %bitcast.1092), calls=%async_computation.55 | async-start | bytes 4390912
  2828.9 195.6 %all-reduce.37.cloned.1.call-start = ((), (), s32[]{:S(2)}) async-start(), calls=%async_computation.27 | async-start | bytes 184320 | tf_op jit(solution)/shard_map/psum | solution.py:482
  2892.0 144.1 %copy-start.1 = (f32[16,768]{1,0:T(8,128)S(1)}, f32[16,768]{1,0:T(8,128)}, u32[]{:S(2)}) copy-start(f32[16,768]{1,0:T(8,128)} %param.37) | copy-start | bytes 147460
  (422 other events, 2391.1 us)
Sparse Core Ops, SparseCore 0:
  10.3 51.8 all-gather.17
  64.5 52.6 all-gather.11
  119.5 67.3 all-gather.9
  189.1 82.1 all-gather.13
  283.6 88.1 all-gather.15
  524.2 49.8 all-gather.19
  687.5 45.4 all-gather.19
  856.8 45.5 all-gather.23
  1001.8 43.8 reduce-scatter.16
  1102.0 45.5 all-gather.23
  1246.7 43.9 reduce-scatter.16
  1469.8 45.5 all-gather.21
  1628.2 45.4 all-gather.21
  1797.7 45.5 all-gather.25
  1942.7 43.8 reduce-scatter.18
  2042.9 45.4 all-gather.25
  2187.6 43.8 reduce-scatter.18
  2293.8 278.1 reduce-scatter.12
  2576.8 251.9 reduce-scatter.14
  2831.1 60.8 all-reduce.38
  2899.6 124.8 all-reduce.36
where the time goes:
time: 3060 us; the launch traced here: 3040 us
  matrix products  1050 us (34%)
  waiting for transfers between devices  784 us (26%)
  local copies, waits for them, and re-layouts  460 us (15%)
  blocking collectives  363 us (12%)
  other arithmetic  162 us (5%)
  starting transfers between devices  122 us (4%)
  loops' own time  86.1 us (3%)
    dot_general x4, matrix products, attend_back(): jnp.einsum('hqk,qhd->khd', grad_scores, query_heads, preferred_element_ty...  172 us
    dot_general x4, matrix products, attend_back(): jnp.einsum('hqk,khd->qhd', grad_scores, key_heads, preferred_element_type...  170 us
    all_gather x4, waiting for transfers between devices, forward_step(): lax.all_gather(qkv_low[:, model_width:], 'ctx', axis=0, tiled=True)  149 us
    psum x1, waiting for transfers between devices, local(): lax.psum((mem_full, small_total[1], small_total[2], small_total[3], small...  127 us
    while x712, local copies, waits for them, and re-layouts  114 us
    another operation x63, local copies, waits for them, and re-layouts  93.3 us
    dot_general x18, matrix products, exact_inner(): lax.dot_general(left_side, right_side, (((0,), (0,)), ((), ())), precisio...  90.1 us
    all_to_all x2, waiting for transfers between devices, local(): lax.all_to_all(out_low, 'dp', split_axis=1, concat_axis=0, tiled=True)  88.3 us
  transfers between devices with their start and end apart: 34, of which 22 were waited for; matrix products, arithmetic and copies ran while one was open for 18% of the time, Pallas kernels for 0%

commit v1 on v0

v1 whole, which is shorter than its diff:
```python
import functools

import jax
import jax.numpy as jnp
from jax import lax
from jax.experimental import pallas as pl
from jax.experimental.pallas import tpu as pltpu
from jax.sharding import PartitionSpec as P

H = 12
HD = 64
EPS = 1e-05
CHUNK = 256
F32 = jnp.float32
BF16 = jnp.bfloat16


def norm_parts(rows):
    centred = rows - jnp.mean(rows, axis=-1, keepdims=True)
    spread = jnp.mean(centred * centred, axis=-1, keepdims=True)
    rstd = lax.rsqrt(spread + EPS)
    return centred * rstd, rstd


def norm_back(grad, unit, rstd, gain):
    scaled = grad * gain
    first = jnp.mean(scaled, axis=-1, keepdims=True)
    second = jnp.mean(scaled * unit, axis=-1, keepdims=True)
    grad_rows = rstd * (scaled - first - unit * second)
    return grad_rows, jnp.sum(grad * unit, axis=0), jnp.sum(grad, axis=0)


def feature_map(rows):
    halves = jnp.concatenate([jax.nn.softplus(rows), jax.nn.softplus(-rows)], axis=-1)
    return jnp.concatenate([halves * jnp.roll(halves, j, axis=-1) for j in (1, 2, 3)], axis=-1)


def gelu_tanh(rows):
    return jax.nn.gelu(rows, approximate=True)


def dot_dims(a, b, ca, cb, precision=None):
    return lax.dot_general(
        a, b, (((ca,), (cb,)), ((), ())), precision=precision, preferred_element_type=F32
    )


exact = functools.partial(dot_dims, precision=lax.Precision.HIGHEST)


def head_rows(scale):
    lane = lax.broadcasted_iota(jnp.int32, (1, 2 * HD), 1)
    low = jnp.where(lane < HD, scale, 0.0).astype(BF16)
    high = jnp.where(lane < HD, 0.0, scale).astype(BF16)
    return low, high


def causal_tail(scores, first):
    key = lax.broadcasted_iota(jnp.int32, scores.shape, 0)
    query = lax.broadcasted_iota(jnp.int32, scores.shape, 1)
    return jnp.where(key - first <= query, scores, 0.0)


def attn_fwd_kernel(q_ref, k_ref, v_ref, km_ref, vm_ref, o_ref, lse_ref, keys, vals_t, vmem_t):
    mem = km_ref.shape[1]
    rows = q_ref.shape[0]
    keys[0:mem, :] = km_ref[0]
    keys[mem:, :] = k_ref[...]
    vals_t[...] = v_ref[...].T
    vmem_t[...] = vm_ref[0].T
    picks = head_rows(HD**-0.5)
    for part in range(rows // CHUNK):
        lo, hi = part * CHUNK, (part + 1) * CHUNK
        query = q_ref[lo:hi, :]
        outs = []
        for head in range(2):
            band = slice(head * HD, (head + 1) * HD)
            scores = dot_dims(keys[0 : mem + hi, :], query * picks[head], 1, 1)
            raw = jnp.exp(scores)
            tail = causal_tail(raw[mem + lo :], 0)
            if lo:
                raw = jnp.concatenate([raw[: mem + lo], tail], axis=0)
            else:
                raw = jnp.concatenate([raw[:mem], tail], axis=0)
            total = jnp.sum(raw, axis=0, keepdims=True)
            lse_ref[0, 0, head : head + 1, lo:hi] = jnp.log(total)
            weights = (raw * (1.0 / total)).astype(BF16)
            outs.append(
                dot_dims(vals_t[band, 0:hi], weights[mem:], 1, 0)
                + dot_dims(vmem_t[band, :], weights[:mem], 1, 0)
            )
        o_ref[lo:hi, :] = jnp.concatenate(outs, axis=0).T.astype(BF16)


def attn_fwd(qkv, kv_mem, segs):
    rows, width = qkv.shape[0] // segs, qkv.shape[1] // 3
    mem = kv_mem.shape[1]
    pairs = H // 2
    wide = 2 * HD
    spec = lambda off: pl.BlockSpec((rows, wide), lambda s, p, off=off: (s, off * pairs + p))
    mspec = lambda off: pl.BlockSpec((1, mem, wide), lambda s, p, off=off: (s, 0, off * pairs + p))
    return pl.pallas_call(
        attn_fwd_kernel,
        grid=(segs, pairs),
        in_specs=[spec(0), spec(1), spec(2), mspec(0), mspec(1)],
        out_specs=[
            pl.BlockSpec((rows, wide), lambda s, p: (s, p)),
            pl.BlockSpec((1, 1, 2, rows), lambda s, p: (s, p, 0, 0)),
        ],
        out_shape=[
            jax.ShapeDtypeStruct((segs * rows, width), BF16),
            jax.ShapeDtypeStruct((segs, pairs, 2, rows), F32),
        ],
        scratch_shapes=[
            pltpu.VMEM((mem + rows, wide), BF16),
            pltpu.VMEM((wide, rows), BF16),
            pltpu.VMEM((wide, mem), BF16),
        ],
        compiler_params=pltpu.CompilerParams(vmem_limit_bytes=40 * 2**20),
        cost_estimate=pl.CostEstimate(
            flops=segs * H * rows * rows * 512,
            bytes_accessed=segs * rows * width * 8,
            transcendentals=segs * H * rows * rows // 2,
        ),
        name="attn_fwd",
    )(qkv, qkv, qkv, kv_mem, kv_mem)


def attn_bwd_kernel(
    q_ref, k_ref, v_ref, km_ref, vm_ref, o_ref, g_ref, lse_ref,
    out_ref, dkm_ref, dvm_ref,
    keys, vals, keys_t, kmem_t, dq, dk, dv,
):
    phase = pl.program_id(2)
    mem = km_ref.shape[1]
    rows = q_ref.shape[0]

    @pl.when(phase == 0)
    def _():
        keys[0:mem, :] = km_ref[0]
        keys[mem:, :] = k_ref[...]
        vals[0:mem, :] = vm_ref[0]
        vals[mem:, :] = v_ref[...]
        keys_t[...] = k_ref[...].T
        kmem_t[...] = km_ref[0].T
        dk[...] = jnp.zeros_like(dk)
        dv[...] = jnp.zeros_like(dv)
        scaled_picks = head_rows(HD**-0.5)
        picks = head_rows(1.0)
        for part in range(rows // CHUNK):
            lo, hi = part * CHUNK, (part + 1) * CHUNK
            end = mem + hi
            query = q_ref[lo:hi, :]
            grad = g_ref[lo:hi, :]
            inner = (grad.astype(F32) * o_ref[lo:hi, :].astype(F32)).T
            dqs = []
            for head in range(2):
                band = slice(head * HD, (head + 1) * HD)
                query_h = query * scaled_picks[head]
                grad_h = grad * picks[head]
                log_total = lse_ref[0, 0, head : head + 1, lo:hi]
                centre = jnp.sum(inner[band], axis=0, keepdims=True)
                prob = jnp.exp(dot_dims(keys[0:end, :], query_h, 1, 1) - log_total)
                prob = jnp.concatenate(
                    [prob[: mem + lo], causal_tail(prob[mem + lo :], 0)], axis=0
                )
                grad_p = dot_dims(vals[0:end, :], grad_h, 1, 1)
                grad_s = (prob * (grad_p - centre)).astype(BF16)
                dv[0:end, :] += dot_dims(prob.astype(BF16), grad_h, 1, 0)
                dk[0:end, :] += dot_dims(grad_s, query_h, 1, 0)
                dqs.append(
                    dot_dims(keys_t[band, 0:hi], grad_s[mem:], 1, 0)
                    + dot_dims(kmem_t[band, :], grad_s[:mem], 1, 0)
                )
            dq[lo:hi, :] = (jnp.concatenate(dqs, axis=0) * HD**-0.5).T.astype(BF16)
        out_ref[...] = dq[...]
        dkm_ref[0] = dk[0:mem, :]
        dvm_ref[0] = dv[0:mem, :]

    @pl.when(phase == 1)
    def _():
        out_ref[...] = dk[mem:, :].astype(BF16)

    @pl.when(phase == 2)
    def _():
        out_ref[...] = dv[mem:, :].astype(BF16)


def attn_bwd(qkv, kv_mem, attended, grad, lse, segs):
    rows, width = qkv.shape[0] // segs, qkv.shape[1] // 3
    mem = kv_mem.shape[1]
    pairs = H // 2
    wide = 2 * HD
    spec = lambda off: pl.BlockSpec((rows, wide), lambda s, p, f, off=off: (s, off * pairs + p))
    mspec = lambda off: pl.BlockSpec(
        (1, mem, wide), lambda s, p, f, off=off: (s, 0, off * pairs + p)
    )
    return pl.pallas_call(
        attn_bwd_kernel,
        grid=(segs, pairs, 3),
        in_specs=[
            spec(0), spec(1), spec(2), mspec(0), mspec(1), spec(0), spec(0),
            pl.BlockSpec((1, 1, 2, rows), lambda s, p, f: (s, p, 0, 0)),
        ],
        out_specs=[
            pl.BlockSpec((rows, wide), lambda s, p, f: (s, f * pairs + p)),
            mspec(0),
            mspec(0),
        ],
        out_shape=[
            jax.ShapeDtypeStruct(qkv.shape, BF16),
            jax.ShapeDtypeStruct((segs, mem, width), F32),
            jax.ShapeDtypeStruct((segs, mem, width), F32),
        ],
        scratch_shapes=[
            pltpu.VMEM((mem + rows, wide), BF16),
            pltpu.VMEM((mem + rows, wide), BF16),
            pltpu.VMEM((wide, rows), BF16),
            pltpu.VMEM((wide, mem), BF16),
            pltpu.VMEM((rows, wide), BF16),
            pltpu.VMEM((mem + rows, wide), F32),
            pltpu.VMEM((mem + rows, wide), F32),
        ],
        compiler_params=pltpu.CompilerParams(vmem_limit_bytes=48 * 2**20),
        cost_estimate=pl.CostEstimate(
            flops=segs * H * rows * rows * 1280,
            bytes_accessed=segs * rows * width * 18,
            transcendentals=segs * H * rows * rows // 2,
        ),
        name="attn_bwd",
    )(qkv, qkv, qkv, kv_mem, kv_mem, attended, grad, lse)


def assemble_kernel(widths, *refs):
    piece_refs = refs[:4]
    out_refs = refs[4 : 4 + len(widths)]
    sem = refs[-1]
    index = lax.axis_index("dp")
    deep, _, _ = index // 4, (index // 2) % 2, index % 2
    cross = (index // 2) % 2
    core = index % 2
    shard = piece_refs[0].shape[1]
    copies = []
    for which in range(4):
        flip_x, flip_c = which % 2, which // 2
        for dz in range(4):
            slot = ((deep ^ dz) * 2 + (cross ^ flip_x)) * 2 + (core ^ flip_c)
            start = 0
            for k, width in enumerate(widths):
                copies.append(
                    pltpu.make_async_copy(
                        piece_refs[which].at[dz, :, pl.ds(start, width)],
                        out_refs[k].at[pl.ds(pl.multiple_of(slot * shard, 16), shard), :],
                        sem.at[len(copies)],
                    )
                )
                start += width
    for copy in copies:
        copy.start()
    for copy in copies:
        copy.wait()


def dp_pairs(flip):
    return [(i, i ^ flip) for i in range(16)]


def gather_group(shards):
    widths = tuple(s.shape[1] for s in shards)
    mine = shards[0] if len(shards) == 1 else jnp.concatenate(shards, axis=1)
    deep = jnp.stack([mine] + [lax.ppermute(mine, "dp", dp_pairs(4 * k)) for k in (1, 2, 3)])
    cross = lax.ppermute(deep, "dp", dp_pairs(2))
    pieces = [deep, cross, lax.ppermute(deep, "dp", dp_pairs(1)), lax.ppermute(cross, "dp", dp_pairs(1))]
    rows = mine.shape[0] * 16
    return pl.pallas_call(
        functools.partial(assemble_kernel, widths),
        in_specs=[pl.BlockSpec(memory_space=pl.ANY)] * 4,
        out_specs=[pl.BlockSpec(memory_space=pl.ANY)] * len(widths),
        out_shape=[jax.ShapeDtypeStruct((rows, w), BF16) for w in widths],
        scratch_shapes=[pltpu.SemaphoreType.DMA((16 * len(widths),))],
        compiler_params=pltpu.CompilerParams(vmem_limit_bytes=4 * 2**20),
        cost_estimate=pl.CostEstimate(
            flops=0, bytes_accessed=4 * rows * sum(widths), transcendentals=0
        ),
        name="assemble",
    )(*pieces)


def pick(parts, at, axis):
    return lax.dynamic_index_in_dim(parts, at, axis, keepdims=False)


def add_low(a, b):
    return (a.astype(F32) + b.astype(F32)).astype(BF16)


def scatter_group(grad):
    index = lax.axis_index("dp")
    deep, cross, core = index // 4, (index // 2) % 2, index % 2
    shard = grad.shape[0] // 16
    parts = grad.reshape(4, 2, 2, shard, grad.shape[1])
    got = lax.ppermute(pick(parts, 1 - core, 2), "dp", dp_pairs(1))
    parts = add_low(pick(parts, core, 2), got)
    got = lax.ppermute(pick(parts, 1 - cross, 1), "dp", dp_pairs(2))
    parts = add_low(pick(parts, cross, 1), got)
    total = pick(parts, deep, 0).astype(F32)
    for k in (1, 2, 3):
        total = total + lax.ppermute(pick(parts, deep ^ k, 0), "dp", dp_pairs(4 * k)).astype(F32)
    low = total.astype(BF16)
    return low.astype(F32) + lax.ppermute(low, "ctx", [(0, 1), (1, 0)]).astype(F32)


def sum_everywhere(flat):
    flat = flat + lax.ppermute(flat, "dp", dp_pairs(1))
    flat = flat + lax.ppermute(flat, "dp", dp_pairs(2))
    far = [lax.ppermute(flat, "dp", dp_pairs(4 * k)) for k in (1, 2, 3)]
    flat = (flat + far[0]) + (far[1] + far[2])
    return flat + lax.ppermute(flat, "ctx", [(0, 1), (1, 0)])


def split_heads(rows):
    return rows.reshape(rows.shape[0], rows.shape[1], H, HD)


def plain_scores(query, key, allowed):
    scores = jnp.einsum("sqhd,skhd->shqk", query, key, preferred_element_type=F32) * HD**-0.5
    return scores, allowed[None, None]


def plain_fwd(qkv, kv_all, allowed):
    width = qkv.shape[2] // 3
    query = split_heads(qkv[:, :, :width])
    key, value = split_heads(kv_all[:, :, :width]), split_heads(kv_all[:, :, width:])
    scores, allowed = plain_scores(query, key, allowed)
    raw = jnp.where(allowed, jnp.exp(scores), 0.0)
    total = jnp.sum(raw, axis=-1)
    weights = (raw / total[..., None]).astype(BF16)
    mixed = jnp.einsum("shqk,skhd->sqhd", weights, value, preferred_element_type=F32)
    return mixed.reshape(qkv.shape[0], -1, width).astype(BF16), jnp.log(total)


def plain_bwd(qkv, kv_all, allowed, log_total, grad):
    segs, width = qkv.shape[0], qkv.shape[2] // 3
    query = split_heads(qkv[:, :, :width])
    key, value = split_heads(kv_all[:, :, :width]), split_heads(kv_all[:, :, width:])
    grad = split_heads(grad)
    scores, allowed = plain_scores(query, key, allowed)
    prob = jnp.where(allowed, jnp.exp(scores - log_total[..., None]), 0.0)
    grad_p = jnp.einsum("sqhd,skhd->shqk", grad, value, preferred_element_type=F32)
    inner = jnp.sum(prob * grad_p, axis=-1, keepdims=True)
    grad_s = (prob * (grad_p - inner) * HD**-0.5).astype(BF16)
    dq = jnp.einsum("shqk,skhd->sqhd", grad_s, key, preferred_element_type=F32)
    dk = jnp.einsum("shqk,sqhd->skhd", grad_s, query, preferred_element_type=F32)
    dv = jnp.einsum("shqk,sqhd->skhd", prob.astype(BF16), grad, preferred_element_type=F32)
    flat = lambda a: a.reshape(segs, -1, width)
    return flat(dq), jnp.concatenate([flat(dk), flat(dv)], axis=2)


def memory_forward(mt, p):
    mem = mt.shape[0]
    keep = {}
    width = mt.shape[1]
    unit, rstd = norm_parts(mt)
    normed = (unit * p["one_gain"] + p["one_bias"]).astype(BF16)
    qkv = (dot_dims(normed, p["qkv"], 1, 0) + p["shift"]).astype(BF16)
    at = jnp.arange(mem, dtype=jnp.int32)
    allowed = at[None, :] <= at[:, None]
    attended, log_total = plain_fwd(qkv[None], qkv[None, :, width:], allowed)
    attended = attended[0]
    after = mt + dot_dims(attended, p["out"], 1, 0) + p["out_bias"]
    unit_b, rstd_b = norm_parts(after)
    normed_b = (unit_b * p["two_gain"] + p["two_bias"]).astype(BF16)
    expanded = dot_dims(normed_b, p["expand"], 1, 0) + p["expand_bias"]
    activ = gelu_tanh(expanded).astype(BF16)
    result = after + dot_dims(activ, p["contract"], 1, 1) + p["contract_bias"]
    key_pre = exact(result, p["key"].astype(F32), 1, 0)
    value_new = exact(result, p["value"].astype(F32), 1, 0)
    read_pre = exact(mt, p["read"].astype(F32), 1, 0)
    key_feat, key_pull = jax.vjp(feature_map, key_pre)
    read_feat, read_pull = jax.vjp(feature_map, read_pre)
    mix = exact(read_feat, key_feat, 1, 1)
    numer = exact(mix, value_new, 1, 0)
    denom = 1.0 + jnp.sum(mix, axis=1, keepdims=True)
    follow = mt + numer / denom
    unit_f, rstd_f = norm_parts(follow)
    normed_f = (unit_f * p["one_gain"] + p["one_bias"]).astype(BF16)
    kv_follow = (dot_dims(normed_f, p["qkv"][:, width:], 1, 0) + p["shift"][width:]).astype(BF16)
    keep = dict(
        unit=unit, rstd=rstd, normed=normed, qkv=qkv, allowed=allowed, attended=attended,
        log_total=log_total, unit_b=unit_b, rstd_b=rstd_b, normed_b=normed_b, expanded=expanded,
        activ=activ, result=result, key_feat=key_feat, read_feat=read_feat, key_pull=key_pull,
        read_pull=read_pull, value_new=value_new, mix=mix, numer=numer, denom=denom, unit_f=unit_f,
        rstd_f=rstd_f, normed_f=normed_f,
    )
    return qkv[:, width:], kv_follow, keep


def memory_backward(mt, p, m, grad_kv_first, grad_kv_follow, mine):
    width = mt.shape[1]
    low = lambda a: a.astype(BF16)
    grad_f = low(grad_kv_follow)
    grad_follow, gain_f, bias_f = norm_back(
        dot_dims(grad_f, p["qkv"][:, width:], 1, 1), m["unit_f"], m["rstd_f"], p["one_gain"]
    )
    grad_mt = grad_follow
    grad_numer = grad_follow / m["denom"]
    grad_denom = -jnp.sum(grad_follow * m["numer"], axis=1, keepdims=True) / (m["denom"] * m["denom"])
    grad_mix = exact(grad_numer, m["value_new"], 1, 1) + grad_denom
    grad_value = exact(m["mix"], grad_numer, 0, 0)
    [grad_read_pre] = m["read_pull"](exact(grad_mix, m["key_feat"], 1, 0))
    [grad_key_pre] = m["key_pull"](exact(grad_mix, m["read_feat"], 0, 0))
    grad_mt = grad_mt + exact(grad_read_pre, p["read"].astype(F32), 1, 1)
    grad_result = exact(grad_key_pre, p["key"].astype(F32), 1, 1) + exact(
        grad_value, p["value"].astype(F32), 1, 1
    )
    grad_contract = low(grad_result)
    _, gelu_pull = jax.vjp(gelu_tanh, m["expanded"])
    grad_expanded = low(gelu_pull(dot_dims(grad_contract, p["contract"], 1, 0))[0])
    grad_after, two_gain, two_bias = norm_back(
        dot_dims(grad_expanded, p["expand"], 1, 1), m["unit_b"], m["rstd_b"], p["two_gain"]
    )
    grad_after = grad_after + grad_result
    grad_attn_out = low(grad_after)
    grad_attended = low(dot_dims(grad_attn_out, p["out"], 1, 1))
    dq, dkv = plain_bwd(
        m["qkv"][None], m["qkv"][None, :, width:], m["allowed"], m["log_total"], grad_attended[None]
    )
    grad_qkv = low(jnp.concatenate([dq[0], dkv[0] + grad_kv_first], axis=1))
    grad_first, gain_a, bias_a = norm_back(
        dot_dims(grad_qkv, p["qkv"], 1, 1), m["unit"], m["rstd"], p["one_gain"]
    )
    grad_mt = grad_mt + grad_first + grad_after
    wide = grad_qkv.astype(F32)
    kv_rows = grad_f.astype(F32)
    sums = jnp.sum(wide, axis=0)
    follow_sums = jnp.sum(kv_rows, axis=0)
    matrices = (
        dot_dims(mine(m["normed"]), grad_qkv, 0, 0)
        + jnp.concatenate(
            [
                jnp.zeros((mine(mt).shape[1], width), F32),
                dot_dims(mine(m["normed_f"]), grad_f, 0, 0),
            ],
            axis=1,
        ),
        dot_dims(mine(m["attended"]), grad_attn_out, 0, 0),
        dot_dims(mine(m["normed_b"]), grad_expanded, 0, 0),
        dot_dims(mine(grad_contract), m["activ"], 0, 0),
        exact(mine(mt), grad_read_pre, 0, 0),
        exact(mine(m["result"]), grad_key_pre, 0, 0),
        exact(mine(m["result"]), grad_value, 0, 0),
    )
    column_sum = lambda a: jnp.sum(a.astype(F32), axis=0)
    vectors = (
        gain_f + gain_a,
        bias_f + bias_a,
        jnp.stack([sums[:width], sums[2 * width :] + follow_sums[width:]]),
        column_sum(grad_attn_out),
        two_gain,
        two_bias,
        column_sum(grad_expanded),
        column_sum(grad_contract),
    )
    return grad_mt, matrices, vectors


def local(
    tokens,
    cotangent,
    placing,
    starts,
    memory_tokens,
    norm_one_gain,
    norm_one_bias,
    qkv_weight,
    qv_bias,
    out_weight,
    out_bias,
    norm_two_gain,
    norm_two_bias,
    expand_weight,
    expand_bias,
    contract_weight,
    contract_bias,
    read_weight,
    key_weight,
    value_weight,
):
    del placing
    groups, ranks = lax.axis_size("dp"), lax.axis_size("ctx")
    group, rank = lax.axis_index("dp"), lax.axis_index("ctx")
    micros, segs_local, tok_rows, width = tokens.shape
    mem = memory_tokens.shape[0]
    shard = qkv_weight.shape[0]
    quick = groups == 16 and ranks == 2 and micros == 2 and (tok_rows * ranks) % CHUNK == 0
    names = ("qkv", "out", "expand", "contract", "read", "key", "value")
    shards = (qkv_weight, out_weight, expand_weight, contract_weight, read_weight, key_weight, value_weight)
    if quick:
        whole = (
            *gather_group(shards[:1]),
            *gather_group(shards[1:3]),
            *gather_group(shards[3:]),
        )
    else:
        whole = tuple(lax.all_gather(s, "dp", axis=0, tiled=True) for s in shards)
    p = dict(zip(names, whole))
    p.update(
        one_gain=norm_one_gain, one_bias=norm_one_bias, out_bias=out_bias, two_gain=norm_two_gain,
        two_bias=norm_two_bias, expand_bias=expand_bias, contract_bias=contract_bias,
        shift=jnp.concatenate([qv_bias[0], jnp.zeros((width,), F32), qv_bias[1]]),
    )
    flags = lax.dynamic_slice_in_dim(starts, group * segs_local, segs_local, 1)

    swap = [(0, 1), (1, 0)]

    def to_segments(held):
        keep, give = pick(held, rank, 0), pick(held, 1 - rank, 0)
        got = lax.ppermute(give, "ctx", swap)
        first = jnp.where(rank == 0, keep, got)
        last = jnp.where(rank == 0, got, keep)
        return jnp.concatenate([first, last], axis=1).reshape(-1, width)

    def from_segments(rows):
        rows = rows.reshape(segs_local, ranks, tok_rows, width)
        keep, give = pick(rows, rank, 1), pick(rows, 1 - rank, 1)
        got = lax.ppermute(give, "ctx", swap)
        return jnp.stack([jnp.where(rank == 0, keep, got), jnp.where(rank == 0, got, keep)])

    if quick:
        rows_in, rows_grad = to_segments(tokens), to_segments(cotangent)
        flags = pick(flags, rank, 0)
        segs = segs_local
    else:
        rows_in, rows_grad = tokens.reshape(-1, width), cotangent.reshape(-1, width)
        flags = flags.reshape(-1)
        segs = micros * segs_local
    seg_rows = rows_in.shape[0] // segs

    kv_first, kv_follow, m = memory_forward(memory_tokens, p)
    kv_mem = jnp.where((flags == 0)[:, None, None], kv_follow[None], kv_first[None])
    hidden = rows_in.astype(F32)
    unit_a, rstd_a = norm_parts(hidden)
    normed_a = (unit_a * norm_one_gain + norm_one_bias).astype(BF16)
    qkv = (dot_dims(normed_a, p["qkv"], 1, 0) + p["shift"]).astype(BF16)
    if quick:
        attended, lse = attn_fwd(qkv, kv_mem, segs)
    else:
        seg_qkv = qkv.reshape(segs, seg_rows, 3 * width)
        kv_all = lax.all_gather(seg_qkv[:, :, width:], "ctx", axis=1, tiled=True)
        kv_all = jnp.concatenate([kv_mem, kv_all], axis=1)
        query_at = mem + rank * seg_rows + jnp.arange(seg_rows, dtype=jnp.int32)
        key_at = jnp.arange(mem + ranks * seg_rows, dtype=jnp.int32)
        allowed = key_at[None, :] <= query_at[:, None]
        attended, lse = plain_fwd(seg_qkv, kv_all, allowed)
        attended = attended.reshape(-1, width)
    after = hidden + dot_dims(attended, p["out"], 1, 0) + out_bias
    unit_b, rstd_b = norm_parts(after)
    normed_b = (unit_b * norm_two_gain + norm_two_bias).astype(BF16)
    expanded = (dot_dims(normed_b, p["expand"], 1, 0) + expand_bias).astype(BF16)
    activ = gelu_tanh(expanded.astype(F32)).astype(BF16)
    result = (after + dot_dims(activ, p["contract"], 1, 1) + contract_bias).astype(BF16)

    grad_activ = dot_dims(rows_grad, p["contract"], 1, 0)
    _, gelu_pull = jax.vjp(gelu_tanh, expanded.astype(F32))
    grad_expanded = gelu_pull(grad_activ)[0].astype(BF16)
    unit_b, rstd_b = norm_parts(after)
    grad_after, two_gain, two_bias = norm_back(
        dot_dims(grad_expanded, p["expand"], 1, 1), unit_b, rstd_b, norm_two_gain
    )
    grad_after = grad_after + rows_grad.astype(F32)
    grad_attn_out = grad_after.astype(BF16)
    grad_attended = dot_dims(grad_attn_out, p["out"], 1, 1).astype(BF16)
    if quick:
        grad_qkv, dk_mem, dv_mem = attn_bwd(qkv, kv_mem, attended, grad_attended, lse, segs)
        dkv_mem = jnp.concatenate([dk_mem, dv_mem], axis=2)
    else:
        dq, dkv = plain_bwd(
            seg_qkv, kv_all, allowed, lse, grad_attended.reshape(segs, seg_rows, width)
        )
        dkv_mem = dkv[:, :mem]
        dkv = lax.psum_scatter(
            dkv[:, mem:].astype(BF16), "ctx", scatter_dimension=1, tiled=True
        )
        grad_qkv = jnp.concatenate([dq.astype(BF16), dkv], axis=2).reshape(-1, 3 * width)
    follows = (flags == 0).astype(F32)[:, None, None]
    pooled = jnp.stack([jnp.sum(dkv_mem * (1.0 - follows), axis=0), jnp.sum(dkv_mem * follows, axis=0)])
    unit_a, rstd_a = norm_parts(hidden)
    grad_hidden, one_gain, one_bias = norm_back(
        dot_dims(grad_qkv, p["qkv"], 1, 1), unit_a, rstd_a, norm_one_gain
    )
    grad_rows = (grad_hidden + grad_after).astype(BF16)

    terms = (
        dot_dims(normed_a, grad_qkv, 0, 0).astype(BF16),
        dot_dims(attended, grad_attn_out, 0, 0).astype(BF16),
        dot_dims(normed_b, grad_expanded, 0, 0).astype(BF16),
        dot_dims(rows_grad, activ, 0, 0).astype(BF16),
    )
    column_sum = lambda a: jnp.sum(a.astype(F32), axis=0)
    qkv_sums = column_sum(grad_qkv)
    vectors = (
        one_gain,
        one_bias,
        jnp.stack([qkv_sums[:width], qkv_sums[2 * width :]]),
        column_sum(grad_attn_out),
        two_gain,
        two_bias,
        column_sum(grad_expanded),
        column_sum(rows_grad),
    )
    if quick:
        summed = tuple(scatter_group(t) for t in terms)
        pooled = sum_everywhere(pooled)
        lengths = [v.size for v in vectors]
        flat = sum_everywhere(jnp.concatenate([v.reshape(-1) for v in vectors]).reshape(-1, 128))
        flat = flat.reshape(-1)
        split, at = [], 0
        for v in vectors:
            split.append(flat[at : at + v.size].reshape(v.shape))
            at += v.size
        vectors = tuple(split)
        del lengths
    else:
        summed = tuple(
            lax.psum(
                lax.psum_scatter(t, "dp", scatter_dimension=0, tiled=True).astype(F32), "ctx"
            )
            for t in terms
        )
        pooled, vectors = lax.psum((pooled, vectors), ("dp", "ctx"))

    mine = lambda a: lax.dynamic_slice_in_dim(a, group * shard, shard, 1)
    grad_mt, mem_matrices, mem_vectors = memory_backward(
        memory_tokens, p, m, pooled[0], pooled[1], mine
    )
    matrices = tuple(a + b for a, b in zip(summed, mem_matrices)) + mem_matrices[4:]
    vectors = tuple(a + b for a, b in zip(vectors, mem_vectors))
    if quick:
        block_out, token_grad = from_segments(result), from_segments(grad_rows)
    else:
        block_out, token_grad = result.reshape(tokens.shape), grad_rows.reshape(tokens.shape)
    return (
        block_out,
        token_grad,
        grad_mt,
        vectors[0],
        vectors[1],
        matrices[0],
        vectors[2],
        matrices[1],
        vectors[3],
        vectors[4],
        vectors[5],
        matrices[2],
        vectors[6],
        matrices[3],
        vectors[7],
        matrices[4],
        matrices[5],
        matrices[6],
    )


def solution(mesh):
    rows = P(None, "dp", "ctx", None)
    matrix = P("dp", None)
    full = P()
    return jax.shard_map(
        local,
        mesh=mesh,
        in_specs=(
            rows, rows, full, full, full, full, full, matrix, full, matrix, full, full, full,
            matrix, full, matrix, full, matrix, matrix, matrix,
        ),
        out_specs=(
            rows, rows, full, full, full, matrix, full, matrix, full, full, full, matrix, full,
            matrix, full, matrix, matrix, matrix,
        ),
        check_vma=False,
    )
```

time: 3060 us -> 831 us (0.27)
  matrix products: 1050 us -> 210 us
  waiting for transfers between devices: 784 us -> 251 us
  local copies, waits for them, and re-layouts: 460 us -> 72.9 us
  blocking collectives: 363 us -> 0 us
  Pallas kernels: 0 us -> 130 us
  other arithmetic: 162 us -> 63.7 us
  loops' own time: 86.1 us -> 0 us
    dot_general x128 -> x48, matrix products: 1050 us -> 210 us  [the longest x42 201 us: dot_dims(): lax.dot_general(a, b, (((ca,), (cb,)), ((), ())), precision=precision, pr...]
    all_to_all x13 -> x0, waiting for transfers between devices: 385 us -> none  [the longest x2 88.3 us: local(): lax.all_to_all(out_low, 'dp', split_axis=1, concat_axis=0, tiled=True)]
    ppermute x0 -> x58, waiting for transfers between devices: none -> 251 us  [the longest x2 58.6 us: sum_everywhere(): return flat + lax.ppermute(flat, 'ctx', [(0, 1), (1, 0)])]
    all_to_all x3 -> x0, blocking collectives: 206 us -> none  [the longest x1 85.4 us: local(): lax.all_to_all(back_grad, 'dp', split_axis=0, concat_axis=2, tiled=True)]
    psum x2 -> x0, waiting for transfers between devices: 166 us -> none  [the longest x1 127 us: local(): lax.psum((mem_full, small_total[1], small_total[2], small_total[3], small...]
    all_gather x13 -> x0, waiting for transfers between devices: 164 us -> none  [the longest x4 149 us: forward_step(): lax.all_gather(qkv_low[:, model_width:], 'ctx', axis=0, tiled=True)]
    all_gather x14 -> x0, blocking collectives: 137 us -> none  [the longest x1 57.1 us: local(): lax.all_gather(read_weight, 'dp', axis=0, tiled=True)]
    pallas_call x0 -> x5, Pallas kernels: none -> 130 us  [the longest x1 72.3 us: attn_bwd(): pl.pallas_call(attn_bwd_kernel, grid=(segs, pairs, 3), in_specs=[spec(0),...]
  transfers between devices with their start and end apart: 34 -> 58, of which waited for: 22 -> 24; matrix products, arithmetic and copies ran while one was open for 18% -> 18% of each run, Pallas kernels for 0% -> 1%
where the time goes in v1:
time: 831 us; the launch traced here: 825 us
  waiting for transfers between devices  251 us (30%)
  matrix products  210 us (25%)
  Pallas kernels  130 us (16%)
  starting transfers between devices  93.3 us (11%)
  local copies, waits for them, and re-layouts  72.9 us (9%)
  other arithmetic  63.7 us (8%)
    dot_general x42, matrix products, dot_dims(): lax.dot_general(a, b, (((ca,), (cb,)), ((), ())), precision=precision, pr...  201 us
    pallas_call x1, Pallas kernels, attn_bwd(): pl.pallas_call(attn_bwd_kernel, grid=(segs, pairs, 3), in_specs=[spec(0),...  72.3 us
    ppermute x2, waiting for transfers between devices, sum_everywhere(): return flat + lax.ppermute(flat, 'ctx', [(0, 1), (1, 0)])  58.6 us
    ppermute x3, waiting for transfers between devices, gather_group(): cross = lax.ppermute(deep, 'dp', dp_pairs(2))  56.6 us
    ppermute x12, waiting for transfers between devices, scatter_group(): lax.ppermute(pick(parts, deep ^ k, 0), 'dp', dp_pairs(4 * k)).astype(F32)  51.8 us
    pallas_call x1, Pallas kernels, attn_fwd(): pl.pallas_call(attn_fwd_kernel, grid=(segs, pairs), in_specs=[spec(0), sp...  45.2 us
    ppermute x9, starting transfers between devices, gather_group(): lax.ppermute(mine, 'dp', dp_pairs(4 * k))  44.7 us
    ppermute x4, waiting for transfers between devices, scatter_group(): got = lax.ppermute(pick(parts, 1 - cross, 1), 'dp', dp_pairs(2))  34.7 us
  transfers between devices with their start and end apart: 58, of which 24 were waited for; matrix products, arithmetic and copies ran while one was open for 18% of the time, Pallas kernels for 1%

profile of v1, /device:TPU:0, one launch (start us, length us, event | category | flops | bytes accessed | tf_op | source)
XLA Modules:
  0.0 825.1 jit_solution(13708853626411008114)
XLA Ops:
  0.7 3.1 collective-permute-start.1
  3.8 2.5 collective-permute-start.3
  9.6 2.9 collective-permute-start.15
  12.5 2.7 dynamic-slice_bitcast_fusion.3
  21.4 17.5 %collective-permute-start.13 = (bf16[48,3840]{1,0:T(8,128)(2,1)}, bf16[48,3840]{1,0:T(8,128)(2,1)}, u32[]{:S(2)}, u32[]{:S(2)}) collective-permute-start(bf16[48,3840]{1,0:T(8,128)(2,1)} %constant_dynamic-update-slice_fusion.4), channel_id=1, source_target_pairs={{0,8},{2,10},{4,12},{6,14},{8,0},{10,2},{12,4},{14,6},{16,24},{18,... | collective-permute-start | bytes 1105928 | tf_op jit(solution)/shard_map/ppermute | solution.py:271
  39.5 3.6 collective-permute-done.2
  43.1 2.9 collective-permute-start.9
  47.3 15.2 %collective-permute-start.8 = (bf16[48,4608]{1,0:T(8,128)(2,1)}, bf16[48,4608]{1,0:T(8,128)(2,1)S(1)}, u32[]{:S(2)}, u32[]{:S(2)}) collective-permute-start(bf16[48,4608]{1,0:T(8,128)(2,1)} %copy-done.59), channel_id=1, source_target_pairs={{0,16},{2,18},{4,20},{6,22},{8,24},{10,26},{12,28},{14,30},{16,0},... | collective-permute-start | bytes 1327112 | tf_op jit(solution)/shard_map/ppermute | solution.py:271
  62.5 15.3 %collective-permute-done.14 = bf16[48,3840]{1,0:T(8,128)(2,1)} collective-permute-done((bf16[48,3840]{1,0:T(8,128)(2,1)}, bf16[48,3840]{1,0:T(8,128)(2,1)}, u32[]{:S(2)}, u32[]{:S(2)}) %collective-permute-start.14) | collective-permute-done | bytes 368672 | tf_op jit(solution)/shard_map/ppermute | solution.py:271
  79.5 2.7 pad_maximum_fusion.5.refs_0_
  82.2 13.4 %collective-permute-done.8 = bf16[48,4608]{1,0:T(8,128)(2,1)S(1)} collective-permute-done((bf16[48,4608]{1,0:T(8,128)(2,1)}, bf16[48,4608]{1,0:T(8,128)(2,1)S(1)}, u32[]{:S(2)}, u32[]{:S(2)}) %collective-permute-start.8) | collective-permute-done | bytes 442400 | tf_op jit(solution)/shard_map/ppermute | solution.py:271
  102.5 2.2 pad_maximum_fusion
  104.7 13.6 %collective-permute-done.4.refs_1_ = bf16[4,48,2304]{2,1,0:T(8,128)(2,1)S(1)} collective-permute-done((bf16[4,48,2304]{2,1,0:T(8,128)(2,1)S(1)}, bf16[4,48,2304]{2,1,0:T(8,128)(2,1)S(1)}, u32[]{:S(2)}, u32[]{:S(2)}) %collective-permute-start.4) | collective-permute-done | bytes 884768 | tf_op jit(solution)/shard_map/ppermute | solution.py:272
  126.4 23.6 %collective-permute-done.16.refs_1_ = bf16[4,48,3840]{2,1,0:T(8,128)(2,1)} collective-permute-done((bf16[4,48,3840]{2,1,0:T(8,128)(2,1)}, bf16[4,48,3840]{2,1,0:T(8,128)(2,1)}, u32[]{:S(2)}, u32[]{:S(2)}) %collective-permute-start.16) | collective-permute-done | bytes 1474592 | tf_op jit(solution)/shard_map/ppermute | solution.py:272
  150.0 5.3 assemble.3
  155.3 9.8 %add_convert_fusion.1.q_ref.k_ref.v_ref = bf16[2048,2304]{1,0:T(8,128)(2,1)} fusion(bf16[2048,768]{1,0:T(8,128)(2,1)S(1)} %fusion.19, bf16[768,2304]{1,0:T(8,128)(2,1)S(1)} %assemble.3, f32[2304]{0:T(1024)S(1)} %pad_maximum_fusion.27), kind=kOutput, calls=%fused_computation.19 | convolution fusion | flops 7257194496 | bytes 16131072 | tf_op jit(solution)/shard_map/dot_general | solution.py:43
  166.3 19.5 %collective-permute-done.10.refs_1_ = bf16[4,48,4608]{2,1,0:T(8,128)(2,1)} collective-permute-done((bf16[4,48,4608]{2,1,0:T(8,128)(2,1)}, bf16[4,48,4608]{2,1,0:T(8,128)(2,1)}, u32[]{:S(2)}, u32[]{:S(2)}) %collective-permute-start.10) | collective-permute-done | bytes 1769504 | tf_op jit(solution)/shard_map/ppermute | solution.py:272
  198.0 3.0 assemble.5
  203.5 4.3 assemble.4
  217.1 45.2 %attn_fwd.1 = (bf16[2048,768]{1,0:T(8,128)(2,1)S(1)}, f32[2,6,2,1024]{3,2,1,0:T(2,128)S(1)}) custom-call(bf16[2048,2304]{1,0:T(8,128)(2,1)S(1)} %bitcast.310, bf16[2048,2304]{1,0:T(8,128)(2,1)S(1)} %bitcast.310, bf16[2048,2304]{1,0:T(8,128)(2,1)S(1)} %bitcast.310, bf16[2,16,1536]{2,1,0:T(8,128)(2,1)S(1)} %broadcast_select_fusion.km_ref.vm_ref, ...), custom_call_target="tpu_custom_call" | custom-call | flops 12884901888 | bytes 12582912 | tf_op jit(solution)/shard_map/attn_fwd/pallas_call | solution.py:102
  264.1 6.1 fusion.180
  270.2 2.7 copy-done.27
  273.8 16.7 %add_convert_fusion = bf16[2048,3072]{1,0:T(8,128)(2,1)} fusion(f32[3072]{0:T(1024)S(1)} %copy-done.166, bf16[768,3072]{1,0:T(8,128)(2,1)S(1)} %bitcast.308, f32[2048,768]{1,0:T(8,128)} %copy-done.27, f32[768]{0:T(1024)S(1)} %copy-done.191, f32[768]{0:T(1024)S(1)} %copy-done.143, f32[2048]{0:T(1024)S(1)} %add_rsqrt_fusion, ...), kind=kOutput, calls=%fused_computation.17 | convolution fusion | flops 9684123648 | bytes 23627776 | tf_op jit(solution)/shard_map/dot_general | solution.py:43
  290.5 21.2 %add_convert_fusion.2 = bf16[2048,768]{1,0:T(8,128)(2,1)} fusion(f32[2048,768]{1,0:T(8,128)} %copy-done.27, bf16[768,3072]{1,0:T(8,128)(2,1)S(1)} %get-tuple-element.42, f32[768]{0:T(1024)S(1)} %copy-done.193, bf16[2048,3072]{1,0:T(8,128)(2,1)} %add_convert_fusion), kind=kOutput, calls=%fused_computation.45 | convolution fusion | flops 9731309568 | bytes 26741760 | tf_op jit(solution)/shard_map/dot_general | solution.py:43
  311.7 18.2 %convolution_convert_fusion = bf16[768,3072]{1,0:T(8,128)(2,1)} fusion(bf16[2048,768]{1,0:T(8,128)(2,1)} %bitcast.315, bf16[2048,3072]{1,0:T(8,128)(2,1)} %add_convert_fusion), kind=kOutput, calls=%fused_computation.51 | convolution fusion | flops 9728950272 | bytes 20447232 | tf_op jit(solution)/shard_map/dot_general | solution.py:43
  329.9 30.7 %convert_reduce_fusion = (f32[3072]{0:T(1024)}, bf16[2048,3072]{1,0:T(8,128)(2,1)}) fusion(bf16[2048,3072]{1,0:T(8,128)(2,1)} %add_convert_fusion, bf16[2048,768]{1,0:T(8,128)(2,1)S(1)} %bitcast.316, bf16[768,3072]{1,0:T(8,128)(2,1)S(1)} %get-tuple-element.42), kind=kOutput, calls=%fused_computation.16 | convolution fusion | flops 9808376832 | bytes 33042432 | tf_op jit(solution)/shard_map/dot_general | solution.py:43
  360.6 16.5 %convolution_convert_fusion.1 = bf16[768,3072]{1,0:T(8,128)(2,1)} fusion(bf16[2048,3072]{1,0:T(8,128)(2,1)} %get-tuple-element.172, f32[2048,768]{1,0:T(8,128)S(1)} %bitcast.312, f32[768]{0:T(1024)S(1)} %copy-done.191, f32[768]{0:T(1024)S(1)} %copy-done.143, f32[2048]{0:T(1024)S(1)} %add_rsqrt_fusion, f32[2048]{0:T(1024)S(1)} %broadcast_multiply_fusion.4), kind=kOutput, calls=%fused_computation.52 | convolution fusion | flops 9673900032 | bytes 23615488 | tf_op jit(solution)/shard_map/dot_general | solution.py:43
  377.1 17.6 %multiply_reduce_fusion = (f32[768]{0:T(1024)}, f32[2048]{0:T(1024)S(1)}, f32[2048]{0:T(1024)S(1)}, f32[768]{0:T(1024)}, f32[2048,768]{1,0:T(8,128)}) fusion(f32[2048,768]{1,0:T(8,128)} %copy-done.27, f32[2048]{0:T(1024)S(1)} %add_rsqrt_fusion, f32[2048]{0:T(1024)S(1)} %broadcast_multiply_fusion.4, f32[768]{0:T(1024)S(1)} %copy-done.143, ...), kind=kOutput, calls=%fused_computation.41 | convolution fusion | flops 9677826048 | bytes 29926400 | tf_op jit(solution)/shard_map/dot_general | solution.py:43
  394.7 6.7 convert_reduce_fusion.4
  401.4 2.7 convolution_convert_fusion.4
  404.2 4.1 convolution_convert_fusion.3.g_ref
  408.3 72.3 %attn_bwd.1 = (bf16[2048,2304]{1,0:T(8,128)(2,1)}, f32[2,16,768]{2,1,0:T(8,128)S(1)}, f32[2,16,768]{2,1,0:T(8,128)S(1)}) custom-call(bf16[2048,2304]{1,0:T(8,128)(2,1)} %add_convert_fusion.1.q_ref.k_ref.v_ref, bf16[2048,2304]{1,0:T(8,128)(2,1)} %add_convert_fusion.1.q_ref.k_ref.v_ref, bf16[2048,2304]{1,0:T(8,128)(2,1)} %add_convert_fusion.1.q_ref.k_ref.v_ref, ...), custom_call_target="tpu_custom_call" | custom-call | flops 32212254720 | bytes 28311552 | tf_op jit(solution)/shard_map/attn_bwd/pallas_call | solution.py:198
  480.6 5.2 convert_reduce_fusion.1
  487.0 9.9 %convolution_convert_fusion.2 = bf16[768,2304]{1,0:T(8,128)(2,1)} fusion(bf16[2048,768]{1,0:T(8,128)(2,1)S(1)} %copy-done.44, bf16[2048,2304]{1,0:T(8,128)(2,1)S(1)} %copy-done.36), kind=kOutput, calls=%fused_computation.53 | convolution fusion | flops 7249526784 | bytes 16121856 | tf_op jit(solution)/shard_map/dot_general | solution.py:43
  497.0 11.4 %fusion.25 = (f32[768]{0:T(1024)}, f32[2048]{0:T(1024)}, f32[2048]{0:T(1024)}, f32[768]{0:T(1024)}, f32[2048,768]{1,0:T(8,128)}) fusion(f32[2048]{0:T(1024)S(1)} %copy-done.126, f32[2048]{0:T(1024)S(1)} %copy-done.128, bf16[2,512,768]{2,1,0:T(8,128)(2,1)S(1)} %copy-done.25, bf16[2,512,768]{2,1,0:T(8,128)(2,1)S(1)} %copy-done.22, f32[768]{0:T(1024)S(1)} %copy-done.91, ...), kind=kOutput, calls=%fused_computation.38 | convolution fusion | flops 7268198400 | bytes 22455296 | tf_op jit(solution)/shard_map/dot_general | solution.py:43
  509.6 5.1 constant_dynamic-slice_fusion.4
  514.6 4.9 constant_dynamic-slice_fusion.7
  524.8 3.6 constant_dynamic-slice_fusion.14
  528.9 6.0 fusion.24
  539.5 2.4 collective-permute-start.32
  541.9 2.1 collective-permute-start.30
  544.7 2.3 collective-permute-start.26
  560.2 3.0 collective-permute-done.25
  570.3 58.6 %collective-permute-done.27 = f32[2,16,1536]{2,1,0:T(8,128)S(1)} collective-permute-done((f32[2,16,1536]{2,1,0:T(8,128)S(1)}, f32[2,16,1536]{2,1,0:T(8,128)S(1)}, u32[]{:S(2)}, u32[]{:S(2)}) %collective-permute-start.27) | collective-permute-done | bytes 196640 | tf_op jit(solution)/shard_map/ppermute | solution.py:318
  644.4 4.4 multiply_reduce_fusion.8
  661.7 2.1 fusion.138
  663.8 2.1 fusion.137
  676.7 2.1 multiply_reduce_fusion.9
  686.0 2.4 collective-permute-start.44
  692.3 3.1 collective-permute-done.43
  696.7 3.2 collective-permute-done.45
  711.1 2.4 collective-permute-start.35
  714.9 19.1 %collective-permute-done.35 = bf16[4,48,2304]{2,1,0:T(8,128)(2,1)S(1)} collective-permute-done((bf16[4,48,2304]{2,1,0:T(8,128)(2,1)S(1)}, bf16[4,48,2304]{2,1,0:T(8,128)(2,1)S(1)}, u32[]{:S(2)}, u32[]{:S(2)}) %collective-permute-start.35) | collective-permute-done | bytes 884768 | tf_op jit(solution)/shard_map/ppermute | solution.py:304
  734.3 2.4 collective-permute-start.38
  738.7 3.8 collective-permute-done.36
  742.5 5.2 collective-permute-done.38
  747.7 9.1 %collective-permute-done.37 = bf16[48,2304]{1,0:T(8,128)(2,1)S(1)} collective-permute-done((bf16[48,2304]{1,0:T(8,128)(2,1)S(1)}, bf16[48,2304]{1,0:T(8,128)(2,1)S(1)}, u32[]{:S(2)}, u32[]{:S(2)}) %collective-permute-start.37) | collective-permute-done | bytes 221216 | tf_op jit(solution)/shard_map/ppermute | solution.py:308
  759.2 3.7 collective-permute-done.39
  765.2 2.4 collective-permute-start.56
  768.7 15.6 %collective-permute-done.47 = bf16[4,48,3072]{2,1,0:T(8,128)(2,1)S(1)} collective-permute-done((bf16[4,48,3072]{2,1,0:T(8,128)(2,1)S(1)}, bf16[4,48,3072]{2,1,0:T(8,128)(2,1)S(1)}, u32[]{:S(2)}, u32[]{:S(2)}) %collective-permute-start.47) | collective-permute-done | bytes 1179680 | tf_op jit(solution)/shard_map/ppermute | solution.py:304
  784.9 2.4 collective-permute-start.50
  788.4 19.1 %collective-permute-done.55 = bf16[48,3072]{1,0:T(8,128)(2,1)S(1)} collective-permute-done((bf16[48,3072]{1,0:T(8,128)(2,1)S(1)}, bf16[48,3072]{1,0:T(8,128)(2,1)S(1)}, u32[]{:S(2)}, u32[]{:S(2)}) %collective-permute-start.55) | collective-permute-done | bytes 294944 | tf_op jit(solution)/shard_map/ppermute | solution.py:308
  808.2 8.7 %collective-permute-done.49 = bf16[48,3072]{1,0:T(8,128)(2,1)S(1)} collective-permute-done((bf16[48,3072]{1,0:T(8,128)(2,1)S(1)}, bf16[48,3072]{1,0:T(8,128)(2,1)S(1)}, u32[]{:S(2)}, u32[]{:S(2)}) %collective-permute-start.49) | collective-permute-done | bytes 294944 | tf_op jit(solution)/shard_map/ppermute | solution.py:308
  818.6 5.3 collective-permute-done.51
  (722 shorter events, 164.8 us)
Async XLA Ops:
  0.7 20.4 %collective-permute-start.1 = (bf16[48,2304]{1,0:T(8,128)(2,1)}, bf16[48,2304]{1,0:T(8,128)(2,1)}, u32[]{:S(2)}, u32[]{:S(2)}) collective-permute-start(bf16[48,2304]{1,0:T(8,128)(2,1)} %param.27), channel_id=1, source_target_pairs={{0,8},{2,10},{4,12},{6,14},{8,0},{10,2},{12,4},{14,6},{16,24},{18,... | collective-permute-start | bytes 663560 | tf_op jit(solution)/shard_map/ppermute | solution.py:271
  3.8 17.6 %collective-permute-start.3 = (bf16[48,2304]{1,0:T(8,128)(2,1)}, bf16[48,2304]{1,0:T(8,128)(2,1)}, u32[]{:S(2)}, u32[]{:S(2)}) collective-permute-start(bf16[48,2304]{1,0:T(8,128)(2,1)} %param.27), channel_id=1, source_target_pairs={{0,24},{2,26},{4,28},{6,30},{8,16},{10,18},{12,20},{14,22},{16,8},... | collective-permute-start | bytes 663560 | tf_op jit(solution)/shard_map/ppermute | solution.py:271
  6.3 36.8 %collective-permute-start.2 = (bf16[48,2304]{1,0:T(8,128)(2,1)}, bf16[48,2304]{1,0:T(8,128)(2,1)}, u32[]{:S(2)}, u32[]{:S(2)}) collective-permute-start(bf16[48,2304]{1,0:T(8,128)(2,1)} %param.27), channel_id=1, source_target_pairs={{0,16},{2,18},{4,20},{6,22},{8,24},{10,26},{12,28},{14,30},{16,0},... | collective-permute-start | bytes 663560 | tf_op jit(solution)/shard_map/ppermute | solution.py:271
  9.6 37.7 %collective-permute-start.15 = (bf16[48,3840]{1,0:T(8,128)(2,1)}, bf16[48,3840]{1,0:T(8,128)(2,1)}, u32[]{:S(2)}, u32[]{:S(2)}) collective-permute-start(bf16[48,3840]{1,0:T(8,128)(2,1)} %constant_dynamic-update-slice_fusion.4), channel_id=1, source_target_pairs={{0,24},{2,26},{4,28},{6,30},{8,16},{10,18},{12,20},{14,22},{16,8},... | collective-permute-start | bytes 1105928 | tf_op jit(solution)/shard_map/ppermute | solution.py:271
  15.2 83.7 %collective-permute-start = (bf16[2,512,768]{2,1,0:T(8,128)(2,1)}, bf16[2,512,768]{2,1,0:T(8,128)(2,1)}, u32[]{:S(2)}, u32[]{:S(2)}) collective-permute-start(bf16[2,512,768]{2,1,0:T(8,128)(2,1)} %dynamic-slice_bitcast_fusion.3), channel_id=1, source_target_pairs={{0,1},{1,0},{2,3},{3,2},{4,5},{5,4},{6,7},{7,6},{8,9},{9,8},{10,11... | collective-permute-start | bytes 4718600 | tf_op jit(solution)/shard_map/ppermute | solution.py:518
  21.1 56.8 %collective-permute-start.14 = (bf16[48,3840]{1,0:T(8,128)(2,1)}, bf16[48,3840]{1,0:T(8,128)(2,1)}, u32[]{:S(2)}, u32[]{:S(2)}) collective-permute-start(bf16[48,3840]{1,0:T(8,128)(2,1)} %constant_dynamic-update-slice_fusion.4), channel_id=1, source_target_pairs={{0,16},{2,18},{4,20},{6,22},{8,24},{10,26},{12,28},{14,30},{16,0},... | collective-permute-start | bytes 1105928 | tf_op jit(solution)/shard_map/ppermute | solution.py:271
  21.4 56.5 %collective-permute-start.13 = (bf16[48,3840]{1,0:T(8,128)(2,1)}, bf16[48,3840]{1,0:T(8,128)(2,1)}, u32[]{:S(2)}, u32[]{:S(2)}) collective-permute-start(bf16[48,3840]{1,0:T(8,128)(2,1)} %constant_dynamic-update-slice_fusion.4), channel_id=1, source_target_pairs={{0,8},{2,10},{4,12},{6,14},{8,0},{10,2},{12,4},{14,6},{16,24},{18,... | collective-permute-start | bytes 1105928 | tf_op jit(solution)/shard_map/ppermute | solution.py:271
  43.1 39.1 %collective-permute-start.9 = (bf16[48,4608]{1,0:T(8,128)(2,1)}, bf16[48,4608]{1,0:T(8,128)(2,1)S(1)}, u32[]{:S(2)}, u32[]{:S(2)}) collective-permute-start(bf16[48,4608]{1,0:T(8,128)(2,1)} %copy-done.59), channel_id=1, source_target_pairs={{0,24},{2,26},{4,28},{6,30},{8,16},{10,18},{12,20},{14,22},{16,8},... | collective-permute-start | bytes 1327112 | tf_op jit(solution)/shard_map/ppermute | solution.py:271
  47.3 48.4 %collective-permute-start.8 = (bf16[48,4608]{1,0:T(8,128)(2,1)}, bf16[48,4608]{1,0:T(8,128)(2,1)S(1)}, u32[]{:S(2)}, u32[]{:S(2)}) collective-permute-start(bf16[48,4608]{1,0:T(8,128)(2,1)} %copy-done.59), channel_id=1, source_target_pairs={{0,16},{2,18},{4,20},{6,22},{8,24},{10,26},{12,28},{14,30},{16,0},... | collective-permute-start | bytes 1327112 | tf_op jit(solution)/shard_map/ppermute | solution.py:271
  77.8 19.6 %collective-permute-start.7 = (bf16[48,4608]{1,0:T(8,128)(2,1)}, bf16[48,4608]{1,0:T(8,128)(2,1)S(1)}, u32[]{:S(2)}, u32[]{:S(2)}) collective-permute-start(bf16[48,4608]{1,0:T(8,128)(2,1)} %copy-done.59), channel_id=1, source_target_pairs={{0,8},{2,10},{4,12},{6,14},{8,0},{10,2},{12,4},{14,6},{16,24},{18,... | collective-permute-start | bytes 1327112 | tf_op jit(solution)/shard_map/ppermute | solution.py:271
  78.0 40.3 %collective-permute-start.20 = (bf16[2,512,768]{2,1,0:T(8,128)(2,1)}, bf16[2,512,768]{2,1,0:T(8,128)(2,1)S(1)}, u32[]{:S(2)}, u32[]{:S(2)}) collective-permute-start(bf16[2,512,768]{2,1,0:T(8,128)(2,1)} %dynamic-slice_bitcast_fusion.1), channel_id=1, source_target_pairs={{0,1},{1,0},{2,3},{3,2},{4,5},{5,4},{6,7},{7,6},{8,9},{9,8},{10,11... | collective-permute-start | bytes 4718600 | tf_op jit(solution)/shard_map/ppermute | solution.py:518
  82.2 42.6 %collective-permute-start.5 = (bf16[4,48,2304]{2,1,0:T(8,128)(2,1)S(1)}, bf16[4,48,2304]{2,1,0:T(8,128)(2,1)S(1)}, u32[]{:S(2)}, u32[]{:S(2)}) collective-permute-start(bf16[4,48,2304]{2,1,0:T(8,128)(2,1)S(1)} %pad_maximum_fusion.6.refs_0_), channel_id=1, source_target_pairs={{0,2},{2,0},{4,6},{6,4},{8,10},{10,8},{12,14},{14,12},{16,18},{18,... | collective-permute-start | bytes 2654216 | tf_op jit(solution)/shard_map/ppermute | solution.py:273
  95.7 22.6 %collective-permute-start.4 = (bf16[4,48,2304]{2,1,0:T(8,128)(2,1)S(1)}, bf16[4,48,2304]{2,1,0:T(8,128)(2,1)S(1)}, u32[]{:S(2)}, u32[]{:S(2)}) collective-permute-start(bf16[4,48,2304]{2,1,0:T(8,128)(2,1)S(1)} %pad_maximum_fusion.6.refs_0_), channel_id=1, source_target_pairs={{0,4},{2,6},{4,0},{6,2},{8,12},{10,14},{12,8},{14,10},{16,20},{18,... | collective-permute-start | bytes 2654216 | tf_op jit(solution)/shard_map/ppermute | solution.py:272
  97.4 100.5 %collective-permute-start.17 = (bf16[4,48,3840]{2,1,0:T(8,128)(2,1)}, bf16[4,48,3840]{2,1,0:T(8,128)(2,1)}, u32[]{:S(2)}, u32[]{:S(2)}) collective-permute-start(bf16[4,48,3840]{2,1,0:T(8,128)(2,1)} %pad_maximum_fusion.5.refs_0_), channel_id=1, source_target_pairs={{0,2},{2,0},{4,6},{6,4},{8,10},{10,8},{12,14},{14,12},{16,18},{18,... | collective-permute-start | bytes 4423688 | tf_op jit(solution)/shard_map/ppermute | solution.py:273
  98.9 51.1 %collective-permute-start.16 = (bf16[4,48,3840]{2,1,0:T(8,128)(2,1)}, bf16[4,48,3840]{2,1,0:T(8,128)(2,1)}, u32[]{:S(2)}, u32[]{:S(2)}) collective-permute-start(bf16[4,48,3840]{2,1,0:T(8,128)(2,1)} %pad_maximum_fusion.5.refs_0_), channel_id=1, source_target_pairs={{0,4},{2,6},{4,0},{6,2},{8,12},{10,14},{12,8},{14,10},{16,20},{18,... | collective-permute-start | bytes 4423688 | tf_op jit(solution)/shard_map/ppermute | solution.py:272
  118.2 85.3 %collective-permute-start.11 = (bf16[4,48,4608]{2,1,0:T(8,128)(2,1)}, bf16[4,48,4608]{2,1,0:T(8,128)(2,1)}, u32[]{:S(2)}, u32[]{:S(2)}) collective-permute-start(bf16[4,48,4608]{2,1,0:T(8,128)(2,1)} %pad_maximum_fusion.4.refs_0_), channel_id=1, source_target_pairs={{0,2},{2,0},{4,6},{6,4},{8,10},{10,8},{12,14},{14,12},{16,18},{18,... | collective-permute-start | bytes 5308424 | tf_op jit(solution)/shard_map/ppermute | solution.py:273
  118.3 31.7 %collective-permute-start.6 = (bf16[4,48,2304]{2,1,0:T(8,128)(2,1)S(1)}, bf16[4,48,2304]{2,1,0:T(8,128)(2,1)S(1)}, u32[]{:S(2)}, u32[]{:S(2)}) collective-permute-start(bf16[4,48,2304]{2,1,0:T(8,128)(2,1)S(1)} %collective-permute-done.4.refs_1_), channel_id=1, source_target_pairs={{0,2},{2,0},{4,6},{6,4},{8,10},{10,8},{12,14},{14,12},{16,18},{18,... | collective-permute-start | bytes 2654216 | tf_op jit(solution)/shard_map/ppermute | solution.py:273
  124.8 60.9 %collective-permute-start.10 = (bf16[4,48,4608]{2,1,0:T(8,128)(2,1)}, bf16[4,48,4608]{2,1,0:T(8,128)(2,1)}, u32[]{:S(2)}, u32[]{:S(2)}) collective-permute-start(bf16[4,48,4608]{2,1,0:T(8,128)(2,1)} %pad_maximum_fusion.4.refs_0_), channel_id=1, source_target_pairs={{0,4},{2,6},{4,0},{6,2},{8,12},{10,14},{12,8},{14,10},{16,20},{18,... | collective-permute-start | bytes 5308424 | tf_op jit(solution)/shard_map/ppermute | solution.py:272
  150.0 48.0 %collective-permute-start.18 = (bf16[4,48,3840]{2,1,0:T(8,128)(2,1)}, bf16[4,48,3840]{2,1,0:T(8,128)(2,1)}, u32[]{:S(2)}, u32[]{:S(2)}) collective-permute-start(bf16[4,48,3840]{2,1,0:T(8,128)(2,1)} %collective-permute-done.16.refs_1_), channel_id=1, source_target_pairs={{0,2},{2,0},{4,6},{6,4},{8,10},{10,8},{12,14},{14,12},{16,18},{18,... | collective-permute-start | bytes 4423688 | tf_op jit(solution)/shard_map/ppermute | solution.py:273
  185.7 17.8 %collective-permute-start.12 = (bf16[4,48,4608]{2,1,0:T(8,128)(2,1)}, bf16[4,48,4608]{2,1,0:T(8,128)(2,1)}, u32[]{:S(2)}, u32[]{:S(2)}) collective-permute-start(bf16[4,48,4608]{2,1,0:T(8,128)(2,1)} %collective-permute-done.10.refs_1_), channel_id=1, source_target_pairs={{0,2},{2,0},{4,6},{6,4},{8,10},{10,8},{12,14},{14,12},{16,18},{18,... | collective-permute-start | bytes 5308424 | tf_op jit(solution)/shard_map/ppermute | solution.py:273
  207.9 121.9 %copy-start.2 = (bf16[768,3072]{1,0:T(8,128)(2,1)}, bf16[768,3072]{1,0:T(8,128)(2,1)S(1)}, u32[]{:S(2)}) copy-start(bf16[768,3072]{1,0:T(8,128)(2,1)S(1)} %get-tuple-element.42) | copy-start | bytes 14155780
  408.3 77.5 %copy-start.44 = (bf16[2048,768]{1,0:T(8,128)(2,1)S(1)}, bf16[2048,768]{1,0:T(8,128)(2,1)}, u32[]{:S(2)}) copy-start(bf16[2048,768]{1,0:T(8,128)(2,1)} %copy-done.43) | copy-start | bytes 9437188
  521.3 45.0 %collective-permute-start.40 = (bf16[4,2,48,768]{3,2,0,1:T(8,128)(2,1)}, bf16[4,2,48,768]{3,2,0,1:T(8,128)(2,1)}, u32[]{:S(2)}, u32[]{:S(2)}) collective-permute-start(bf16[4,2,48,768]{3,2,0,1:T(8,128)(2,1)} %bitcast.304), channel_id=1, source_target_pairs={{0,2},{2,0},{4,6},{6,4},{8,10},{10,8},{12,14},{14,12},{16,18},{18,... | collective-permute-start | bytes 1769480 | tf_op jit(solution)/shard_map/ppermute | solution.py:302
  528.7 6.8 collective-permute-start.28
  534.9 2.1 collective-permute-start.22
  535.5 4.0 collective-permute-start.29
  537.1 6.9 collective-permute-start.23
  539.5 7.5 collective-permute-start.32
  541.9 5.3 collective-permute-start.31
  541.9 7.2 collective-permute-start.30
  544.7 13.9 %collective-permute-start.26 = (f32[2,16,1536]{2,1,0:T(8,128)}, f32[2,16,1536]{2,1,0:T(8,128)}, u32[]{:S(2)}, u32[]{:S(2)}) collective-permute-start(f32[2,16,1536]{2,1,0:T(8,128)} %fusion.234), channel_id=1, source_target_pairs={{0,24},{2,26},{4,28},{6,30},{8,16},{10,18},{12,20},{14,22},{16,8},... | collective-permute-start | bytes 589832 | tf_op jit(solution)/shard_map/ppermute | solution.py:316
  547.0 16.2 %collective-permute-start.25 = (f32[2,16,1536]{2,1,0:T(8,128)}, f32[2,16,1536]{2,1,0:T(8,128)}, u32[]{:S(2)}, u32[]{:S(2)}) collective-permute-start(f32[2,16,1536]{2,1,0:T(8,128)} %fusion.234), channel_id=1, source_target_pairs={{0,16},{2,18},{4,20},{6,22},{8,24},{10,26},{12,28},{14,30},{16,0},... | collective-permute-start | bytes 589832 | tf_op jit(solution)/shard_map/ppermute | solution.py:316
  547.1 16.2 %collective-permute-start.24 = (f32[2,16,1536]{2,1,0:T(8,128)}, f32[2,16,1536]{2,1,0:T(8,128)}, u32[]{:S(2)}, u32[]{:S(2)}) collective-permute-start(f32[2,16,1536]{2,1,0:T(8,128)} %fusion.234), channel_id=1, source_target_pairs={{0,8},{2,10},{4,12},{6,14},{8,0},{10,2},{12,4},{14,6},{16,24},{18,... | collective-permute-start | bytes 589832 | tf_op jit(solution)/shard_map/ppermute | solution.py:316
  549.1 7.7 collective-permute-start.33
  556.8 143.8 %collective-permute-start.19 = (bf16[2,512,768]{2,1,0:T(8,128)(2,1)}, bf16[2,512,768]{2,1,0:T(8,128)(2,1)}, u32[]{:S(2)}, u32[]{:S(2)}) collective-permute-start(bf16[2,512,768]{2,1,0:T(8,128)(2,1)} %dynamic-slice_bitcast_fusion.2), channel_id=1, source_target_pairs={{0,1},{1,0},{2,3},{3,2},{4,5},{5,4},{6,7},{7,6},{8,9},{9,8},{10,11... | collective-permute-start | bytes 4718600 | tf_op jit(solution)/shard_map/ppermute | solution.py:526
  558.6 72.3 %copy-start.101 = (f32[16,768]{1,0:T(8,128)S(1)}, f32[16,768]{1,0:T(8,128)}, u32[]{:S(2)}) copy-start(f32[16,768]{1,0:T(8,128)} %copy-done.100) | copy-start | bytes 147460
  558.6 72.3 %copy-start.103 = (f32[16,768]{1,0:T(8,128)S(1)}, f32[16,768]{1,0:T(8,128)}, u32[]{:S(2)}) copy-start(f32[16,768]{1,0:T(8,128)} %copy-done.102) | copy-start | bytes 147460
  558.6 72.3 %copy-start.105 = (f32[16,768]{1,0:T(8,128)S(1)}, f32[16,768]{1,0:T(8,128)}, u32[]{:S(2)}) copy-start(f32[16,768]{1,0:T(8,128)} %copy-done.104) | copy-start | bytes 147460
  558.6 145.6 %collective-permute-start.21 = (bf16[2,512,768]{2,1,0:T(8,128)(2,1)}, bf16[2,512,768]{2,1,0:T(8,128)(2,1)}, u32[]{:S(2)}, u32[]{:S(2)}) collective-permute-start(bf16[2,512,768]{2,1,0:T(8,128)(2,1)} %dynamic-slice_bitcast_fusion), channel_id=1, source_target_pairs={{0,1},{1,0},{2,3},{3,2},{4,5},{5,4},{6,7},{7,6},{8,9},{9,8},{10,11... | collective-permute-start | bytes 4718600 | tf_op jit(solution)/shard_map/ppermute | solution.py:526
  563.2 145.7 %collective-permute-start.34 = (bf16[4,2,48,2304]{3,2,0,1:T(8,128)(2,1)}, bf16[4,2,48,2304]{3,2,0,1:T(8,128)(2,1)}, u32[]{:S(2)}, u32[]{:S(2)}) collective-permute-start(bf16[4,2,48,2304]{3,2,0,1:T(8,128)(2,1)} %bitcast.326), channel_id=1, source_target_pairs={{0,2},{2,0},{4,6},{6,4},{8,10},{10,8},{12,14},{14,12},{16,18},{18,... | collective-permute-start | bytes 5308424 | tf_op jit(solution)/shard_map/ppermute | solution.py:302
  563.3 79.7 %slice-start = ((s8[4718592]{0:T(1024)(128)(4,1)}), s8[4194304]{0:T(1024)(128)(4,1)S(1)}, s32[]{:S(2)}) async-start(s8[4718592]{0:T(1024)(128)(4,1)} %bitcast.305), calls=%async_computation | async-start | bytes 8388608
  564.7 64.2 %collective-permute-start.27 = (f32[2,16,1536]{2,1,0:T(8,128)S(1)}, f32[2,16,1536]{2,1,0:T(8,128)S(1)}, u32[]{:S(2)}, u32[]{:S(2)}) collective-permute-start(f32[2,16,1536]{2,1,0:T(8,128)S(1)} %add_add_fusion.3), channel_id=1, source_target_pairs={{0,1},{1,0},{2,3},{3,2},{4,5},{5,4},{6,7},{7,6},{8,9},{9,8},{10,11... | collective-permute-start | bytes 589832 | tf_op jit(solution)/shard_map/ppermute | solution.py:318
  568.5 115.1 %collective-permute-start.41 = (bf16[4,48,768]{2,1,0:T(8,128)(2,1)}, bf16[4,48,768]{2,1,0:T(8,128)(2,1)}, u32[]{:S(2)}, u32[]{:S(2)}) collective-permute-start(bf16[4,48,768]{2,1,0:T(8,128)(2,1)} %dynamic-slice_bitcast_fusion.13), channel_id=1, source_target_pairs={{0,4},{2,6},{4,0},{6,2},{8,12},{10,14},{12,8},{14,10},{16,20},{18,... | collective-permute-start | bytes 884744 | tf_op jit(solution)/shard_map/ppermute | solution.py:304
  684.7 4.7 collective-permute-start.42
  686.0 6.3 collective-permute-start.44
  689.5 6.0 collective-permute-start.43
  692.3 21.1 %collective-permute-start.52 = (bf16[4,2,48,3072]{3,2,0,1:T(8,128)(2,1)}, bf16[4,2,48,3072]{3,2,0,1:T(8,128)(2,1)S(1)}, u32[]{:S(2)}, u32[]{:S(2)}) collective-permute-start(bf16[4,2,48,3072]{3,2,0,1:T(8,128)(2,1)} %bitcast.325), channel_id=1, source_target_pairs={{0,2},{2,0},{4,6},{6,4},{8,10},{10,8},{12,14},{14,12},{16,18},{18,... | collective-permute-start | bytes 7077896 | tf_op jit(solution)/shard_map/ppermute | solution.py:302
  695.5 4.4 collective-permute-start.45
  699.9 37.8 %collective-permute-start.46 = (bf16[4,2,48,3072]{3,2,0,1:T(8,128)(2,1)S(1)}, bf16[4,2,48,3072]{3,2,0,1:T(8,128)(2,1)S(1)}, u32[]{:S(2)}, u32[]{:S(2)}) collective-permute-start(bf16[4,2,48,3072]{3,2,0,1:T(8,128)(2,1)S(1)} %bitcast.324), channel_id=1, source_target_pairs={{0,2},{2,0},{4,6},{6,4},{8,10},{10,8},{12,14},{14,12},{16,18},{18,... | collective-permute-start | bytes 7077896 | tf_op jit(solution)/shard_map/ppermute | solution.py:302
  711.1 22.9 %collective-permute-start.35 = (bf16[4,48,2304]{2,1,0:T(8,128)(2,1)S(1)}, bf16[4,48,2304]{2,1,0:T(8,128)(2,1)S(1)}, u32[]{:S(2)}, u32[]{:S(2)}) collective-permute-start(bf16[4,48,2304]{2,1,0:T(8,128)(2,1)S(1)} %dynamic-slice_bitcast_fusion.6), channel_id=1, source_target_pairs={{0,4},{2,6},{4,0},{6,2},{8,12},{10,14},{12,8},{14,10},{16,20},{18,... | collective-permute-start | bytes 2654216 | tf_op jit(solution)/shard_map/ppermute | solution.py:304
  714.8 49.9 %collective-permute-start.53 = (bf16[4,48,3072]{2,1,0:T(8,128)(2,1)S(1)}, bf16[4,48,3072]{2,1,0:T(8,128)(2,1)S(1)}, u32[]{:S(2)}, u32[]{:S(2)}) collective-permute-start(bf16[4,48,3072]{2,1,0:T(8,128)(2,1)S(1)} %dynamic-slice_bitcast_fusion.4), channel_id=1, source_target_pairs={{0,4},{2,6},{4,0},{6,2},{8,12},{10,14},{12,8},{14,10},{16,20},{18,... | collective-permute-start | bytes 3538952 | tf_op jit(solution)/shard_map/ppermute | solution.py:304
  734.2 8.3 %collective-permute-start.36 = (bf16[48,2304]{1,0:T(8,128)(2,1)S(1)}, bf16[48,2304]{1,0:T(8,128)(2,1)S(1)}, u32[]{:S(2)}, u32[]{:S(2)}) collective-permute-start(bf16[48,2304]{1,0:T(8,128)(2,1)S(1)} %get-tuple-element.116), channel_id=1, source_target_pairs={{0,8},{2,10},{4,12},{6,14},{8,0},{10,2},{12,4},{14,6},{16,24},{18,... | collective-permute-start | bytes 663560 | tf_op jit(solution)/shard_map/ppermute | solution.py:308
  734.3 13.4 %collective-permute-start.38 = (bf16[48,2304]{1,0:T(8,128)(2,1)S(1)}, bf16[48,2304]{1,0:T(8,128)(2,1)S(1)}, u32[]{:S(2)}, u32[]{:S(2)}) collective-permute-start(bf16[48,2304]{1,0:T(8,128)(2,1)S(1)} %get-tuple-element.117), channel_id=1, source_target_pairs={{0,24},{2,26},{4,28},{6,30},{8,16},{10,18},{12,20},{14,22},{16,8},... | collective-permute-start | bytes 663560 | tf_op jit(solution)/shard_map/ppermute | solution.py:308
  736.7 20.1 %collective-permute-start.37 = (bf16[48,2304]{1,0:T(8,128)(2,1)S(1)}, bf16[48,2304]{1,0:T(8,128)(2,1)S(1)}, u32[]{:S(2)}, u32[]{:S(2)}) collective-permute-start(bf16[48,2304]{1,0:T(8,128)(2,1)S(1)} %get-tuple-element.118), channel_id=1, source_target_pairs={{0,16},{2,18},{4,20},{6,22},{8,24},{10,26},{12,28},{14,30},{16,0},... | collective-permute-start | bytes 663560 | tf_op jit(solution)/shard_map/ppermute | solution.py:308
  756.9 6.0 collective-permute-start.39
  757.6 26.8 %collective-permute-start.47 = (bf16[4,48,3072]{2,1,0:T(8,128)(2,1)S(1)}, bf16[4,48,3072]{2,1,0:T(8,128)(2,1)S(1)}, u32[]{:S(2)}, u32[]{:S(2)}) collective-permute-start(bf16[4,48,3072]{2,1,0:T(8,128)(2,1)S(1)} %dynamic-slice_bitcast_fusion.5), channel_id=1, source_target_pairs={{0,4},{2,6},{4,0},{6,2},{8,12},{10,14},{12,8},{14,10},{16,20},{18,... | collective-permute-start | bytes 3538952 | tf_op jit(solution)/shard_map/ppermute | solution.py:304
  765.2 22.1 %collective-permute-start.54 = (bf16[48,3072]{1,0:T(8,128)(2,1)S(1)}, bf16[48,3072]{1,0:T(8,128)(2,1)S(1)}, u32[]{:S(2)}, u32[]{:S(2)}) collective-permute-start(bf16[48,3072]{1,0:T(8,128)(2,1)S(1)} %get-tuple-element.108), channel_id=1, source_target_pairs={{0,8},{2,10},{4,12},{6,14},{8,0},{10,2},{12,4},{14,6},{16,24},{18,... | collective-permute-start | bytes 884744 | tf_op jit(solution)/shard_map/ppermute | solution.py:308
  765.2 23.1 %collective-permute-start.56 = (bf16[48,3072]{1,0:T(8,128)(2,1)S(1)}, bf16[48,3072]{1,0:T(8,128)(2,1)S(1)}, u32[]{:S(2)}, u32[]{:S(2)}) collective-permute-start(bf16[48,3072]{1,0:T(8,128)(2,1)S(1)} %get-tuple-element.109), channel_id=1, source_target_pairs={{0,24},{2,26},{4,28},{6,30},{8,16},{10,18},{12,20},{14,22},{16,8},... | collective-permute-start | bytes 884744 | tf_op jit(solution)/shard_map/ppermute | solution.py:308
  767.6 39.9 %collective-permute-start.55 = (bf16[48,3072]{1,0:T(8,128)(2,1)S(1)}, bf16[48,3072]{1,0:T(8,128)(2,1)S(1)}, u32[]{:S(2)}, u32[]{:S(2)}) collective-permute-start(bf16[48,3072]{1,0:T(8,128)(2,1)S(1)} %get-tuple-element.110), channel_id=1, source_target_pairs={{0,16},{2,18},{4,20},{6,22},{8,24},{10,26},{12,28},{14,30},{16,0},... | collective-permute-start | bytes 884744 | tf_op jit(solution)/shard_map/ppermute | solution.py:308
  784.8 23.4 %collective-permute-start.48 = (bf16[48,3072]{1,0:T(8,128)(2,1)S(1)}, bf16[48,3072]{1,0:T(8,128)(2,1)S(1)}, u32[]{:S(2)}, u32[]{:S(2)}) collective-permute-start(bf16[48,3072]{1,0:T(8,128)(2,1)S(1)} %get-tuple-element.111), channel_id=1, source_target_pairs={{0,8},{2,10},{4,12},{6,14},{8,0},{10,2},{12,4},{14,6},{16,24},{18,... | collective-permute-start | bytes 884744 | tf_op jit(solution)/shard_map/ppermute | solution.py:308
  784.9 23.3 %collective-permute-start.50 = (bf16[48,3072]{1,0:T(8,128)(2,1)S(1)}, bf16[48,3072]{1,0:T(8,128)(2,1)S(1)}, u32[]{:S(2)}, u32[]{:S(2)}) collective-permute-start(bf16[48,3072]{1,0:T(8,128)(2,1)S(1)} %get-tuple-element.112), channel_id=1, source_target_pairs={{0,24},{2,26},{4,28},{6,30},{8,16},{10,18},{12,20},{14,22},{16,8},... | collective-permute-start | bytes 884744 | tf_op jit(solution)/shard_map/ppermute | solution.py:308
  787.3 29.7 %collective-permute-start.49 = (bf16[48,3072]{1,0:T(8,128)(2,1)S(1)}, bf16[48,3072]{1,0:T(8,128)(2,1)S(1)}, u32[]{:S(2)}, u32[]{:S(2)}) collective-permute-start(bf16[48,3072]{1,0:T(8,128)(2,1)S(1)} %get-tuple-element.113), channel_id=1, source_target_pairs={{0,16},{2,18},{4,20},{6,22},{8,24},{10,26},{12,28},{14,30},{16,0},... | collective-permute-start | bytes 884744 | tf_op jit(solution)/shard_map/ppermute | solution.py:308
  807.6 10.1 %collective-permute-start.57 = (bf16[48,3072]{1,0:T(8,128)(2,1)S(1)}, bf16[48,3072]{1,0:T(8,128)(2,1)S(1)}, u32[]{:S(2)}, u32[]{:S(2)}) collective-permute-start(bf16[48,3072]{1,0:T(8,128)(2,1)S(1)} %fusion.55), channel_id=1, source_target_pairs={{0,1},{1,0},{2,3},{3,2},{4,5},{5,4},{6,7},{7,6},{8,9},{9,8},{10,11... | collective-permute-start | bytes 884744 | tf_op jit(solution)/shard_map/ppermute | solution.py:310
  817.1 6.8 collective-permute-start.51
  (208 other events, 3644.4 us)

commit v2 on v1

v2 whole, which is shorter than its diff:
```python
import functools

import jax
import jax.numpy as jnp
from jax import lax
from jax.experimental import pallas as pl
from jax.experimental.pallas import tpu as pltpu
from jax.sharding import PartitionSpec as P

H = 12
HD = 64
EPS = 1e-05
CHUNK = 256
F32 = jnp.float32
BF16 = jnp.bfloat16


def norm_parts(rows):
    centred = rows - jnp.mean(rows, axis=-1, keepdims=True)
    spread = jnp.mean(centred * centred, axis=-1, keepdims=True)
    rstd = lax.rsqrt(spread + EPS)
    return centred * rstd, rstd


def norm_back(grad, unit, rstd, gain):
    scaled = grad * gain
    first = jnp.mean(scaled, axis=-1, keepdims=True)
    second = jnp.mean(scaled * unit, axis=-1, keepdims=True)
    grad_rows = rstd * (scaled - first - unit * second)
    return grad_rows, jnp.sum(grad * unit, axis=0), jnp.sum(grad, axis=0)


def feature_map(rows):
    halves = jnp.concatenate([jax.nn.softplus(rows), jax.nn.softplus(-rows)], axis=-1)
    return jnp.concatenate([halves * jnp.roll(halves, j, axis=-1) for j in (1, 2, 3)], axis=-1)


def gelu_tanh(rows):
    return jax.nn.gelu(rows, approximate=True)


def dot_dims(a, b, ca, cb, precision=None):
    return lax.dot_general(
        a, b, (((ca,), (cb,)), ((), ())), precision=precision, preferred_element_type=F32
    )


exact = functools.partial(dot_dims, precision=lax.Precision.HIGHEST)


def head_rows(scale):
    lane = lax.broadcasted_iota(jnp.int32, (1, 2 * HD), 1)
    low = jnp.where(lane < HD, scale, 0.0).astype(BF16)
    high = jnp.where(lane < HD, 0.0, scale).astype(BF16)
    return low, high


def causal_tail(scores, first):
    key = lax.broadcasted_iota(jnp.int32, scores.shape, 0)
    query = lax.broadcasted_iota(jnp.int32, scores.shape, 1)
    return jnp.where(key - first <= query, scores, 0.0)


def attn_fwd_kernel(q_ref, k_ref, v_ref, km_ref, vm_ref, o_ref, lse_ref, keys, vals_t, vmem_t):
    mem = km_ref.shape[0]
    rows = q_ref.shape[0]
    keys[0:mem, :] = km_ref[...]
    keys[mem:, :] = k_ref[...]
    vals_t[...] = v_ref[...].T
    vmem_t[...] = vm_ref[...].T
    picks = head_rows(HD**-0.5)
    for part in range(rows // CHUNK):
        lo, hi = part * CHUNK, (part + 1) * CHUNK
        query = q_ref[lo:hi, :]
        outs = []
        for head in range(2):
            band = slice(head * HD, (head + 1) * HD)
            scores = dot_dims(keys[0 : mem + hi, :], query * picks[head], 1, 1)
            raw = jnp.exp(scores)
            tail = causal_tail(raw[mem + lo :], 0)
            if lo:
                raw = jnp.concatenate([raw[: mem + lo], tail], axis=0)
            else:
                raw = jnp.concatenate([raw[:mem], tail], axis=0)
            total = jnp.sum(raw, axis=0, keepdims=True)
            lse_ref[0, head : head + 1, lo:hi] = jnp.log(total)
            weights = (raw * (1.0 / total)).astype(BF16)
            outs.append(
                dot_dims(vals_t[band, 0:hi], weights[mem:], 1, 0)
                + dot_dims(vmem_t[band, :], weights[:mem], 1, 0)
            )
        o_ref[lo:hi, :] = jnp.concatenate(outs, axis=0).T.astype(BF16)


def attn_fwd_after_kernel(q_ref, k_ref, v_ref, km_ref, vm_ref, held_ref, *rest):
    del held_ref
    attn_fwd_kernel(q_ref, k_ref, v_ref, km_ref, vm_ref, *rest)


def attn_fwd(qkv, kv_mem, seg, rows, held):
    width = qkv.shape[1] // 3
    mem = kv_mem.shape[0]
    pairs = H // 2
    wide = 2 * HD
    spec = lambda off: pl.BlockSpec((rows, wide), lambda p, off=off: (seg, off * pairs + p))
    mspec = lambda off: pl.BlockSpec((mem, wide), lambda p, off=off: (0, off * pairs + p))
    more = [] if held is None else [held]
    return pl.pallas_call(
        attn_fwd_kernel if held is None else attn_fwd_after_kernel,
        grid=(pairs,),
        in_specs=[spec(0), spec(1), spec(2), mspec(0), mspec(1)]
        + [pl.BlockSpec(memory_space=pl.ANY)] * len(more),
        out_specs=[
            pl.BlockSpec((rows, wide), lambda p: (seg, p)),
            pl.BlockSpec((1, 2, rows), lambda p: (p, 0, 0)),
        ],
        out_shape=[
            jax.ShapeDtypeStruct((qkv.shape[0], width), BF16),
            jax.ShapeDtypeStruct((pairs, 2, rows), F32),
        ],
        scratch_shapes=[
            pltpu.VMEM((mem + rows, wide), BF16),
            pltpu.VMEM((wide, rows), BF16),
            pltpu.VMEM((wide, mem), BF16),
        ],
        input_output_aliases={5: 0} if more else {},
        compiler_params=pltpu.CompilerParams(vmem_limit_bytes=40 * 2**20),
        cost_estimate=pl.CostEstimate(
            flops=pairs * rows * rows * 4000,
            bytes_accessed=rows * width * 8,
            transcendentals=0,
        ),
        name="attn_fwd",
    )(qkv, qkv, qkv, kv_mem, kv_mem, *more)


def attn_mem_kernel(q_ref, km_ref, vm_ref, o_ref, g_ref, lse_ref, dkm_ref, dvm_ref, mid_ref):
    scaled_picks, picks = head_rows(HD**-0.5), head_rows(1.0)
    grad, query = g_ref[...], q_ref[...]
    inner = (grad.astype(F32) * o_ref[...].astype(F32)).T
    dk, dv = 0.0, 0.0
    for head in range(2):
        band = slice(head * HD, (head + 1) * HD)
        query_h, grad_h = query * scaled_picks[head], grad * picks[head]
        centre = jnp.sum(inner[band], axis=0, keepdims=True)
        mid_ref[0, head : head + 1, :] = centre
        prob = jnp.exp(dot_dims(km_ref[0], query_h, 1, 1) - lse_ref[0, head : head + 1, :])
        grad_s = (prob * (dot_dims(vm_ref[0], grad_h, 1, 1) - centre)).astype(BF16)
        dv = dv + dot_dims(prob.astype(BF16), grad_h, 1, 0)
        dk = dk + dot_dims(grad_s, query_h, 1, 0)
    dkm_ref[0] = dk
    dvm_ref[0] = dv


def attn_mem(qkv, kv_mem, attended, grad, lse):
    segs, pairs, mem, wide = kv_mem.shape[0], H // 2, kv_mem.shape[1], 2 * HD
    rows, width = lse.shape[2], qkv.shape[1] // 3
    spec = pl.BlockSpec((rows, wide), lambda s, p: (s, p))
    mspec = lambda off: pl.BlockSpec((1, mem, wide), lambda s, p, off=off: (s, 0, off * pairs + p))
    lspec = pl.BlockSpec((1, 2, rows), lambda s, p: (s * pairs + p, 0, 0))
    return pl.pallas_call(
        attn_mem_kernel,
        grid=(segs, pairs),
        in_specs=[spec, mspec(0), mspec(1), spec, spec, lspec],
        out_specs=[mspec(0), mspec(0), lspec],
        out_shape=[
            jax.ShapeDtypeStruct((segs, mem, width), F32),
            jax.ShapeDtypeStruct((segs, mem, width), F32),
            jax.ShapeDtypeStruct((segs * pairs, 2, rows), F32),
        ],
        compiler_params=pltpu.CompilerParams(vmem_limit_bytes=40 * 2**20),
        cost_estimate=pl.CostEstimate(
            flops=segs * rows * width * 4000, bytes_accessed=segs * rows * width * 6, transcendentals=0
        ),
        name="attn_mem",
    )(qkv, kv_mem, kv_mem, attended, grad, lse)


def attn_bwd_kernel(
    q_ref, k_ref, v_ref, km_ref, vm_ref, g_ref, lse_ref, mid_ref,
    out_ref,
    keys, vals, keys_t, kmem_t, dq, dk, dv,
):
    phase = pl.program_id(1)
    mem = km_ref.shape[0]
    rows = q_ref.shape[0]

    @pl.when(phase == 0)
    def _():
        keys[0:mem, :] = km_ref[...]
        keys[mem:, :] = k_ref[...]
        vals[0:mem, :] = vm_ref[...]
        vals[mem:, :] = v_ref[...]
        keys_t[...] = k_ref[...].T
        kmem_t[...] = km_ref[...].T
        dk[...] = jnp.zeros_like(dk)
        dv[...] = jnp.zeros_like(dv)
        scaled_picks = head_rows(HD**-0.5)
        picks = head_rows(1.0)
        for part in range(rows // CHUNK):
            lo, hi = part * CHUNK, (part + 1) * CHUNK
            end = mem + hi
            query = q_ref[lo:hi, :]
            grad = g_ref[lo:hi, :]
            dqs = []
            for head in range(2):
                band = slice(head * HD, (head + 1) * HD)
                query_h = query * scaled_picks[head]
                grad_h = grad * picks[head]
                log_total = lse_ref[0, head : head + 1, lo:hi]
                centre = mid_ref[0, head : head + 1, lo:hi]
                prob = jnp.exp(dot_dims(keys[0:end, :], query_h, 1, 1) - log_total)
                prob = jnp.concatenate(
                    [prob[: mem + lo], causal_tail(prob[mem + lo :], 0)], axis=0
                )
                grad_p = dot_dims(vals[0:end, :], grad_h, 1, 1)
                grad_s = (prob * (grad_p - centre)).astype(BF16)
                dv[0:end, :] += dot_dims(prob.astype(BF16), grad_h, 1, 0)
                dk[0:end, :] += dot_dims(grad_s, query_h, 1, 0)
                dqs.append(
                    dot_dims(keys_t[band, 0:hi], grad_s[mem:], 1, 0)
                    + dot_dims(kmem_t[band, :], grad_s[:mem], 1, 0)
                )
            dq[lo:hi, :] = (jnp.concatenate(dqs, axis=0) * HD**-0.5).T.astype(BF16)
        out_ref[...] = dq[...]

    @pl.when(phase == 1)
    def _():
        out_ref[...] = dk[mem:, :].astype(BF16)

    @pl.when(phase == 2)
    def _():
        out_ref[...] = dv[mem:, :].astype(BF16)


def attn_bwd(qkv, kv_mem, grad, lse, middle, seg, first, count):
    pairs = H // 2
    rows, width = lse.shape[2], qkv.shape[1] // 3
    mem = kv_mem.shape[0]
    wide = 2 * HD
    spec = lambda off: pl.BlockSpec((rows, wide), lambda p, f, off=off: (seg, off * pairs + first + p))
    mspec = lambda off: pl.BlockSpec((mem, wide), lambda p, f, off=off: (0, off * pairs + first + p))
    lspec = pl.BlockSpec((1, 2, rows), lambda p, f: (seg * pairs + first + p, 0, 0))
    return pl.pallas_call(
        attn_bwd_kernel,
        grid=(count, 3),
        in_specs=[
            spec(0), spec(1), spec(2), mspec(0), mspec(1), spec(0), lspec, lspec,
        ],
        out_specs=pl.BlockSpec((rows, wide), lambda p, f: (0, f * count + p)),
        out_shape=jax.ShapeDtypeStruct((rows, 3 * count * wide), BF16),
        scratch_shapes=[
            pltpu.VMEM((mem + rows, wide), BF16),
            pltpu.VMEM((mem + rows, wide), BF16),
            pltpu.VMEM((wide, rows), BF16),
            pltpu.VMEM((wide, mem), BF16),
            pltpu.VMEM((rows, wide), BF16),
            pltpu.VMEM((mem + rows, wide), F32),
            pltpu.VMEM((mem + rows, wide), F32),
        ],
        compiler_params=pltpu.CompilerParams(vmem_limit_bytes=48 * 2**20),
        cost_estimate=pl.CostEstimate(
            flops=count * rows * rows * 6500,
            bytes_accessed=rows * count * wide * 18,
            transcendentals=0,
        ),
        name="attn_bwd",
    )(qkv, qkv, qkv, kv_mem, kv_mem, grad, lse, middle)


def choose(told, kept, got, out):
    own = pl.program_id(0) % 2 == told[1]

    @pl.when(own)
    def _():
        out[...] = kept[0]

    @pl.when(jnp.logical_not(own))
    def _():
        out[...] = got[0]


def half_specs(rows, width):
    return [pl.BlockSpec((1, rows, width), lambda i, told: ((i // 2) ^ told[0], 0, 0))] * 2


def enter_kernel(told, kept, got, gain, bias, weight, shift, rows_ref, normed_ref, qkv_ref):
    choose(told, kept, got, rows_ref)
    unit, _ = norm_parts(rows_ref[...].astype(F32))
    normed = (unit * gain[...] + bias[...]).astype(BF16)
    normed_ref[...] = normed
    wide = weight.shape[1] // 3
    for k in range(3):
        at = slice(k * wide, (k + 1) * wide)
        qkv_ref[:, at] = (dot_dims(normed, weight[:, at], 1, 0) + shift[:, at]).astype(BF16)


def enter(told, kept, got, gain, bias, weight, shift):
    segs, rows, width = kept.shape
    whole = lambda r, c: pl.BlockSpec((r, c), lambda i, told: (0, 0), pipeline_mode=pl.Buffered(1))
    block = lambda c: pl.BlockSpec((rows, c), lambda i, told: (i, 0))
    sizes = (width, width, 3 * width)
    return pl.pallas_call(
        enter_kernel,
        grid_spec=pltpu.PrefetchScalarGridSpec(
            num_scalar_prefetch=1,
            grid=(2 * segs,),
            in_specs=[*half_specs(rows, width), whole(1, width), whole(1, width), whole(width, 3 * width), whole(1, 3 * width)],
            out_specs=[block(c) for c in sizes],
        ),
        out_shape=[jax.ShapeDtypeStruct((2 * segs * rows, c), BF16) for c in sizes],
        compiler_params=pltpu.CompilerParams(vmem_limit_bytes=48 * 2**20),
        cost_estimate=pl.CostEstimate(
            flops=8 * segs * rows * width * width * 3, bytes_accessed=segs * rows * width * 28, transcendentals=0
        ),
        name="enter",
    )(told, kept, got, gain[None], bias[None], weight, shift[None])


def middle_kernel(
    told, kept, got, rows_ref, attended, out_w, expand_w, contract_w, out_b, gain, bias, expand_b, contract_b,
    result_ref, cot_ref, normed_ref, activ_ref, grad_exp_ref, grad_out_ref, grad_att_ref,
    sums_ref, exp_sums_ref,
):
    choose(told, kept, got, cot_ref)
    cot = cot_ref[...]
    after = rows_ref[...].astype(F32) + dot_dims(attended[...], out_w[...], 1, 0) + out_b[...]
    unit, rstd = norm_parts(after)
    normed = (unit * gain[...] + bias[...]).astype(BF16)
    normed_ref[...] = normed
    total = after + contract_b[...]
    back = 0.0

    @pl.when(pl.program_id(0) == 0)
    def _():
        sums_ref[...] = jnp.zeros_like(sums_ref)
        exp_sums_ref[...] = jnp.zeros_like(exp_sums_ref)

    parts = 6
    wide = expand_w.shape[1] // parts
    bend, cube = 0.7978845608028654, 0.044715
    for part in range(parts):
        at = slice(part * wide, (part + 1) * wide)
        value = dot_dims(normed, expand_w[:, at], 1, 0) + expand_b[:, at]
        square = value * value
        curve = jnp.tanh(bend * value * (1.0 + cube * square))
        half = 0.5 * (1.0 + curve)
        activ = (value * half).astype(BF16)
        activ_ref[:, at] = activ
        slope = half + 0.5 * bend * value * (1.0 - curve * curve) * (1.0 + 3.0 * cube * square)
        grad = (dot_dims(cot, contract_w[:, at], 1, 0) * slope).astype(BF16)
        grad_exp_ref[:, at] = grad
        exp_sums_ref[:, at] += jnp.sum(grad.astype(F32), axis=0, keepdims=True)
        total = total + dot_dims(activ, contract_w[:, at], 1, 1)
        back = back + dot_dims(grad, expand_w[:, at], 1, 1)
    result_ref[...] = total.astype(BF16)
    wide_cot = cot.astype(F32)
    grad_rows, gain_sum, bias_sum = norm_back(back, unit, rstd, gain[...])
    grad_out = (grad_rows + wide_cot).astype(BF16)
    grad_out_ref[...] = grad_out
    grad_att_ref[...] = dot_dims(grad_out, out_w[...], 1, 1).astype(BF16)
    sums = (
        jnp.sum(grad_out.astype(F32), axis=0, keepdims=True),
        gain_sum[None],
        bias_sum[None],
        jnp.sum(wide_cot, axis=0, keepdims=True),
    )
    for k, value in enumerate(sums):
        sums_ref[k : k + 1, :] += value


def middle(told, kept, got, rows_in, attended, out_w, expand_w, contract_w, out_b, gain, bias, expand_b, contract_b):
    segs, rows, width = kept.shape
    wide = expand_w.shape[1]
    whole = lambda r, c: pl.BlockSpec((r, c), lambda i, told: (0, 0), pipeline_mode=pl.Buffered(1))
    block = lambda c: pl.BlockSpec((rows, c), lambda i, told: (i, 0))
    sizes = (width, width, width, wide, wide, width, width)
    count = 2 * segs * rows
    fixed = lambda r, c: pl.BlockSpec((r, c), lambda i, told: (0, 0))
    return pl.pallas_call(
        middle_kernel,
        grid_spec=pltpu.PrefetchScalarGridSpec(
            num_scalar_prefetch=1,
            grid=(2 * segs,),
            in_specs=[
                *half_specs(rows, width), block(width), block(width), whole(width, width), whole(width, wide),
                whole(width, wide), whole(1, width), whole(1, width), whole(1, width), whole(1, wide), whole(1, width),
            ],
            out_specs=[*[block(c) for c in sizes], fixed(8, width), fixed(1, wide)],
        ),
        out_shape=[
            *[jax.ShapeDtypeStruct((count, c), BF16) for c in sizes],
            jax.ShapeDtypeStruct((8, width), F32),
            jax.ShapeDtypeStruct((1, wide), F32),
        ],
        compiler_params=pltpu.CompilerParams(vmem_limit_bytes=60 * 2**20),
        cost_estimate=pl.CostEstimate(
            flops=count * width * (8 * wide + 4 * width) * 2, bytes_accessed=count * (14 * width + 4 * wide), transcendentals=0
        ),
        name="middle",
    )(
        told, kept, got, rows_in, attended, out_w, expand_w, contract_w, out_b[None], gain[None], bias[None],
        expand_b[None], contract_b[None],
    )


def gather_kernel(halved, count, kinds, *refs):
    shards, outs = refs[:count], refs[count : 2 * count]
    send_sem, recv_sem, local_sem = refs[2 * count :]
    index, plane = lax.axis_index("dp"), lax.axis_index("ctx")
    deep, cross, core = index // 4, (index // 2) % 2, index % 2
    place = lambda z, x, c: (z * 2 + x) * 2 + c
    up, down = {"dp": place(deep + 1, cross, core)}, {"dp": place(deep - 1, cross, core)}
    beside, sibling = {"dp": place(deep, 1 - cross, core)}, {"dp": place(deep, cross, 1 - core)}
    other = {"ctx": 1 - plane}
    rows = shards[0].shape[0]
    numbers, sends = {}, []

    def valid(kind):
        way, far = kind
        return deep >= 0 if way == "own" else deep >= far if way == "below" else deep + far <= 3

    def level(kind):
        way, far = kind
        return deep if way == "own" else deep - far if way == "below" else deep + far

    def view(k, z, x, c, part):
        at = pl.ds(pl.multiple_of(place(z, x, c) * rows, 16), rows)
        return outs[k].at[at, :] if part is None else outs[k].at[at, half(k, part)]

    def half(k, part):
        wide = outs[k].shape[1] // 2
        return pl.ds(pl.multiple_of(part * wide, 128), wide)

    def copy(key, source, landing, device):
        number = numbers.setdefault(key, len(numbers))
        return pltpu.make_async_remote_copy(
            source, landing, send_sem.at[number], recv_sem.at[number],
            device_id=device, device_id_type=pl.DeviceIdType.MESH,
        )

    def send(when, key, source, landing, device):
        def begin():
            copy(key, source, landing, device).start()

        def end():
            copy(key, source, landing, device).wait_send()

        sends.append((when, end))
        if when is None:
            begin()
        else:
            pl.when(when)(begin)

    def arrived(key, landing):
        copy(key, landing, landing, sibling).wait_recv()

    barrier = pltpu.get_barrier_semaphore()
    for device in (beside, sibling, other):
        pl.semaphore_signal(barrier, inc=1, device_id=device, device_id_type=pl.DeviceIdType.MESH)
    for when, device in ((deep < 3, up), (deep > 0, down)):

        @pl.when(when)
        def _(device=device):
            pl.semaphore_signal(barrier, inc=1, device_id=device, device_id_type=pl.DeviceIdType.MESH)

    inner = (deep > 0) & (deep < 3)
    for when, peers in ((inner, 5), (jnp.logical_not(inner), 4)):

        @pl.when(when)
        def _(peers=peers):
            pl.semaphore_wait(barrier, peers)

    own = ("own", 0)
    locals_ = []
    for k in range(count):
        part = plane if k in halved else None
        mine = view(k, deep, cross, core, None)
        locals_.append(pltpu.make_async_copy(shards[k], mine, local_sem.at[k]))
        locals_[-1].start()
        source = shards[k] if part is None else shards[k].at[:, half(k, part)]
        landing = view(k, deep, cross, core, part)
        send(deep < 3, ("z", ("below", 1), k), source, landing, up)
        send(deep > 0, ("z", ("above", 1), k), source, landing, down)
        send(None, ("x", own, k), source, landing, beside)
        send(None, ("core", "z", own, k), shards[k], mine, sibling)

    def onward(k, flow, kind, x):
        part = plane if k in halved else None
        block = view(k, level(kind), x, core, part)
        ok = valid(kind)
        if flow == "z":
            way, far = kind
            if far < 3:
                if way == "below":
                    send(ok & (deep < 3), ("z", (way, far + 1), k), block, block, up)
                else:
                    send(ok & (deep > 0), ("z", (way, far + 1), k), block, block, down)
            send(ok, ("x", kind, k), block, block, beside)
        send(ok, ("core", flow, kind, k), block, block, sibling)
        if k in halved:
            send(ok, ("y", flow, kind, k), block, block, other)

    def take(flow, kind):
        x = cross if flow == "z" else 1 - cross
        for k in range(count):
            part = plane if k in halved else None

            @pl.when(valid(kind))
            def _():
                arrived((flow, kind, k), view(k, level(kind), x, core, part))

            onward(k, flow, kind, x)

    for far in range(1, 4):
        take("z", ("below", far))
        take("z", ("above", far))
        for kind in kinds:
            if kind[1] == far - 1:
                take("x", kind)
    for kind in kinds:
        if kind[1] == 3:
            take("x", kind)
    crossing = [(flow, kind, k) for flow in ("z", "x") for kind in kinds for k in halved]
    crossing = [c for c in crossing if c[:2] != ("z", own)]
    for flow, kind, k in crossing:
        x = cross if flow == "z" else 1 - cross
        block = lambda c: view(k, level(kind), x, c, 1 - plane)

        @pl.when(valid(kind))
        def _():
            arrived(("y", flow, kind, k), block(core))

        send(valid(kind), ("core", "y", flow, kind, k), block(core), block(core), sibling)
    for flow in ("z", "x"):
        x = cross if flow == "z" else 1 - cross
        for kind in kinds:
            for k in range(count):
                part = plane if k in halved and (flow, kind) != ("z", own) else None

                @pl.when(valid(kind))
                def _():
                    arrived(("core", flow, kind, k), view(k, level(kind), x, 1 - core, part))

    for flow, kind, k in crossing:
        x = cross if flow == "z" else 1 - cross

        @pl.when(valid(kind))
        def _():
            arrived(("core", "y", flow, kind, k), view(k, level(kind), x, 1 - core, 1 - plane))

    for when, end in sends:
        if when is None:
            end()
        else:
            pl.when(when)(end)
    for held in locals_:
        held.wait()


def gather_weights(shards, halved):
    kinds = [("own", 0)] + [(way, far) for far in (1, 2, 3) for way in ("below", "above")]
    count = len(shards)
    rows = shards[0].shape[0] * 16
    copies = 6 * count + 7 * count + 13 * len(halved) + 14 * count + 13 * len(halved)
    any_space = pl.BlockSpec(memory_space=pl.ANY)
    return pl.pallas_call(
        functools.partial(gather_kernel, halved, count, kinds),
        in_specs=[any_space] * count,
        out_specs=[any_space] * count,
        out_shape=[jax.ShapeDtypeStruct((rows, s.shape[1]), BF16) for s in shards],
        scratch_shapes=[
            pltpu.SemaphoreType.DMA((copies,)),
            pltpu.SemaphoreType.DMA((copies,)),
            pltpu.SemaphoreType.DMA((count,)),
        ],
        compiler_params=pltpu.CompilerParams(
            collective_id=0, has_side_effects=True, vmem_limit_bytes=4 * 2**20
        ),
        cost_estimate=pl.CostEstimate(
            flops=8 * 10**10, bytes_accessed=4 * rows * sum(s.shape[1] for s in shards), transcendentals=0
        ),
        name="gather_weights",
    )(*shards)


def dp_pairs(flip):
    return [(i, i ^ flip) for i in range(16)]


def behind(value, *earlier):
    return lax.optimization_barrier((value, earlier))[0]


def pick(parts, at, axis):
    return lax.dynamic_index_in_dim(parts, at, axis, keepdims=False)


def add_low(a, b):
    return (a.astype(F32) + b.astype(F32)).astype(BF16)


class Scatter:
    def __init__(self, grad):
        index = lax.axis_index("dp")
        self.deep, self.cross, self.core = index // 4, (index // 2) % 2, index % 2
        parts = grad.reshape(4, 2, 2, grad.shape[0] // 16, grad.shape[1])
        self.keep, self.give = pick(parts, self.core, 2), pick(parts, 1 - self.core, 2)

    def over_core(self, *beside):
        got = behind(lax.ppermute(self.give, "dp", dp_pairs(1)), *beside)
        parts = add_low(self.keep, got)
        self.keep, self.give = pick(parts, self.cross, 1), pick(parts, 1 - self.cross, 1)
        return self

    def over_x(self, *beside):
        got = behind(lax.ppermute(self.give, "dp", dp_pairs(2)), *beside)
        parts = add_low(self.keep, got)
        self.keep = pick(parts, self.deep, 0)
        self.give = tuple(pick(parts, self.deep ^ k, 0) for k in (1, 2, 3))
        return self

    def over_z(self, *beside):
        far = [lax.ppermute(self.give[k - 1], "dp", dp_pairs(4 * k)) for k in (1, 2, 3)]
        total = self.keep.astype(F32)
        for part in behind(far, *beside):
            total = total + part.astype(F32)
        self.keep = self.give = total.astype(BF16)
        return self

    def over_y(self, *beside):
        got = behind(lax.ppermute(self.give, "ctx", [(0, 1), (1, 0)]), *beside)
        return self.keep.astype(F32) + got.astype(F32)


def sum_over(flat, step, *beside):
    if step == 0:
        return flat + behind(lax.ppermute(flat, "ctx", [(0, 1), (1, 0)]), *beside)
    if step < 3:
        return flat + behind(lax.ppermute(flat, "dp", dp_pairs(step)), *beside)
    far = behind([lax.ppermute(flat, "dp", dp_pairs(4 * k)) for k in (1, 2, 3)], *beside)
    return (flat + far[0]) + (far[1] + far[2])


def split_heads(rows):
    return rows.reshape(rows.shape[0], rows.shape[1], H, HD)


def plain_scores(query, key, allowed):
    scores = jnp.einsum("sqhd,skhd->shqk", query, key, preferred_element_type=F32) * HD**-0.5
    return scores, allowed[None, None]


def plain_fwd(qkv, kv_all, allowed):
    width = qkv.shape[2] // 3
    query = split_heads(qkv[:, :, :width])
    key, value = split_heads(kv_all[:, :, :width]), split_heads(kv_all[:, :, width:])
    scores, allowed = plain_scores(query, key, allowed)
    raw = jnp.where(allowed, jnp.exp(scores), 0.0)
    total = jnp.sum(raw, axis=-1)
    weights = (raw / total[..., None]).astype(BF16)
    mixed = jnp.einsum("shqk,skhd->sqhd", weights, value, preferred_element_type=F32)
    return mixed.reshape(qkv.shape[0], -1, width).astype(BF16), jnp.log(total)


def plain_bwd(qkv, kv_all, allowed, log_total, grad):
    segs, width = qkv.shape[0], qkv.shape[2] // 3
    query = split_heads(qkv[:, :, :width])
    key, value = split_heads(kv_all[:, :, :width]), split_heads(kv_all[:, :, width:])
    grad = split_heads(grad)
    scores, allowed = plain_scores(query, key, allowed)
    prob = jnp.where(allowed, jnp.exp(scores - log_total[..., None]), 0.0)
    grad_p = jnp.einsum("sqhd,skhd->shqk", grad, value, preferred_element_type=F32)
    inner = jnp.sum(prob * grad_p, axis=-1, keepdims=True)
    grad_s = (prob * (grad_p - inner) * HD**-0.5).astype(BF16)
    dq = jnp.einsum("shqk,skhd->sqhd", grad_s, key, preferred_element_type=F32)
    dk = jnp.einsum("shqk,sqhd->skhd", grad_s, query, preferred_element_type=F32)
    dv = jnp.einsum("shqk,sqhd->skhd", prob.astype(BF16), grad, preferred_element_type=F32)
    flat = lambda a: a.reshape(segs, -1, width)
    return flat(dq), jnp.concatenate([flat(dk), flat(dv)], axis=2)


def memory_forward(mt, p):
    mem = mt.shape[0]
    keep = {}
    width = mt.shape[1]
    unit, rstd = norm_parts(mt)
    normed = (unit * p["one_gain"] + p["one_bias"]).astype(BF16)
    qkv = (dot_dims(normed, p["qkv"], 1, 0) + p["shift"]).astype(BF16)
    at = jnp.arange(mem, dtype=jnp.int32)
    allowed = at[None, :] <= at[:, None]
    attended, log_total = plain_fwd(qkv[None], qkv[None, :, width:], allowed)
    attended = attended[0]
    after = mt + dot_dims(attended, p["out"], 1, 0) + p["out_bias"]
    unit_b, rstd_b = norm_parts(after)
    normed_b = (unit_b * p["two_gain"] + p["two_bias"]).astype(BF16)
    expanded = dot_dims(normed_b, p["expand"], 1, 0) + p["expand_bias"]
    activ = gelu_tanh(expanded).astype(BF16)
    result = after + dot_dims(activ, p["contract"], 1, 1) + p["contract_bias"]
    key_pre = exact(result, p["key"].astype(F32), 1, 0)
    value_new = exact(result, p["value"].astype(F32), 1, 0)
    read_pre = exact(mt, p["read"].astype(F32), 1, 0)
    key_feat, key_pull = jax.vjp(feature_map, key_pre)
    read_feat, read_pull = jax.vjp(feature_map, read_pre)
    mix = exact(read_feat, key_feat, 1, 1)
    numer = exact(mix, value_new, 1, 0)
    denom = 1.0 + jnp.sum(mix, axis=1, keepdims=True)
    follow = mt + numer / denom
    unit_f, rstd_f = norm_parts(follow)
    normed_f = (unit_f * p["one_gain"] + p["one_bias"]).astype(BF16)
    kv_follow = (dot_dims(normed_f, p["qkv"][:, width:], 1, 0) + p["shift"][width:]).astype(BF16)
    keep = dict(
        unit=unit, rstd=rstd, normed=normed, qkv=qkv, allowed=allowed, attended=attended,
        log_total=log_total, unit_b=unit_b, rstd_b=rstd_b, normed_b=normed_b, expanded=expanded,
        activ=activ, result=result, key_feat=key_feat, read_feat=read_feat, key_pull=key_pull,
        read_pull=read_pull, value_new=value_new, mix=mix, numer=numer, denom=denom, unit_f=unit_f,
        rstd_f=rstd_f, normed_f=normed_f,
    )
    return qkv[:, width:], kv_follow, keep


def memory_backward(mt, p, m, grad_kv_first, grad_kv_follow, mine, turn):
    width = mt.shape[1]
    low = lambda a: a.astype(BF16)
    grad_f = low(turn(0, grad_kv_follow))
    grad_follow, gain_f, bias_f = norm_back(
        dot_dims(grad_f, p["qkv"][:, width:], 1, 1), m["unit_f"], m["rstd_f"], p["one_gain"]
    )
    grad_mt = grad_follow
    grad_numer = grad_follow / m["denom"]
    grad_denom = -jnp.sum(grad_follow * m["numer"], axis=1, keepdims=True) / (m["denom"] * m["denom"])
    grad_mix = exact(grad_numer, m["value_new"], 1, 1) + grad_denom
    grad_value = exact(m["mix"], grad_numer, 0, 0)
    [grad_read_pre] = m["read_pull"](exact(grad_mix, m["key_feat"], 1, 0))
    [grad_key_pre] = m["key_pull"](exact(grad_mix, m["read_feat"], 0, 0))
    grad_mt = grad_mt + exact(grad_read_pre, p["read"].astype(F32), 1, 1)
    grad_result = exact(grad_key_pre, p["key"].astype(F32), 1, 1) + exact(
        grad_value, p["value"].astype(F32), 1, 1
    )
    grad_result = turn(1, grad_result)
    grad_contract = low(grad_result)
    _, gelu_pull = jax.vjp(gelu_tanh, m["expanded"])
    grad_expanded = low(gelu_pull(dot_dims(grad_contract, p["contract"], 1, 0))[0])
    grad_after, two_gain, two_bias = norm_back(
        dot_dims(grad_expanded, p["expand"], 1, 1), m["unit_b"], m["rstd_b"], p["two_gain"]
    )
    grad_after = grad_after + grad_result
    grad_attn_out = low(grad_after)
    grad_attended = low(dot_dims(grad_attn_out, p["out"], 1, 1))
    dq, dkv = plain_bwd(
        m["qkv"][None], m["qkv"][None, :, width:], m["allowed"], m["log_total"], grad_attended[None]
    )
    grad_qkv = low(turn(2, jnp.concatenate([dq[0], dkv[0] + grad_kv_first], axis=1)))
    grad_first, gain_a, bias_a = norm_back(
        dot_dims(grad_qkv, p["qkv"], 1, 1), m["unit"], m["rstd"], p["one_gain"]
    )
    grad_mt = grad_mt + grad_first + grad_after
    wide = grad_qkv.astype(F32)
    kv_rows = grad_f.astype(F32)
    sums = jnp.sum(wide, axis=0)
    follow_sums = jnp.sum(kv_rows, axis=0)
    matrices = (
        dot_dims(mine(m["normed"]), grad_qkv, 0, 0)
        + jnp.concatenate(
            [
                jnp.zeros((mine(mt).shape[1], width), F32),
                dot_dims(mine(m["normed_f"]), grad_f, 0, 0),
            ],
            axis=1,
        ),
        dot_dims(mine(m["attended"]), grad_attn_out, 0, 0),
        dot_dims(mine(m["normed_b"]), grad_expanded, 0, 0),
        dot_dims(mine(grad_contract), m["activ"], 0, 0),
        exact(mine(mt), grad_read_pre, 0, 0),
        exact(mine(m["result"]), grad_key_pre, 0, 0),
        exact(mine(m["result"]), grad_value, 0, 0),
    )
    column_sum = lambda a: jnp.sum(a.astype(F32), axis=0)
    vectors = (
        gain_f + gain_a,
        bias_f + bias_a,
        jnp.stack([sums[:width], sums[2 * width :] + follow_sums[width:]]),
        column_sum(grad_attn_out),
        two_gain,
        two_bias,
        column_sum(grad_expanded),
        column_sum(grad_contract),
    )
    return grad_mt, matrices, vectors


def local(
    tokens,
    cotangent,
    placing,
    starts,
    memory_tokens,
    norm_one_gain,
    norm_one_bias,
    qkv_weight,
    qv_bias,
    out_weight,
    out_bias,
    norm_two_gain,
    norm_two_bias,
    expand_weight,
    expand_bias,
    contract_weight,
    contract_bias,
    read_weight,
    key_weight,
    value_weight,
):
    del placing
    groups, ranks = lax.axis_size("dp"), lax.axis_size("ctx")
    group, rank = lax.axis_index("dp"), lax.axis_index("ctx")
    micros, segs_local, tok_rows, width = tokens.shape
    mem = memory_tokens.shape[0]
    shard = qkv_weight.shape[0]
    quick = groups == 16 and ranks == 2 and micros == 2 and segs_local == 2 and (tok_rows * ranks) % CHUNK == 0
    names = ("qkv", "out", "expand", "contract", "read", "key", "value")
    shards = (qkv_weight, out_weight, expand_weight, contract_weight, read_weight, key_weight, value_weight)
    if quick:
        give = pick(tokens, 1 - rank, 0)
        joined = (
            jnp.concatenate([qkv_weight, read_weight, key_weight], axis=1),
            expand_weight,
            contract_weight,
            jnp.concatenate([out_weight, value_weight], axis=1),
        )
        qkv_read_key, expand_full, contract_full, out_value = gather_weights(
            behind(joined, give), (2, 3)
        )
        feat = read_weight.shape[1]
        whole = (
            qkv_read_key[:, : 3 * width],
            out_value[:, :width],
            expand_full,
            contract_full,
            qkv_read_key[:, 3 * width : 3 * width + feat],
            qkv_read_key[:, 3 * width + feat :],
            out_value[:, width:],
        )
    else:
        whole = tuple(lax.all_gather(s, "dp", axis=0, tiled=True) for s in shards)
    p = dict(zip(names, whole))
    p.update(
        one_gain=norm_one_gain, one_bias=norm_one_bias, out_bias=out_bias, two_gain=norm_two_gain,
        two_bias=norm_two_bias, expand_bias=expand_bias, contract_bias=contract_bias,
        shift=jnp.concatenate([qv_bias[0], jnp.zeros((width,), F32), qv_bias[1]]),
    )
    flags = lax.dynamic_slice_in_dim(starts, group * segs_local, segs_local, 1)

    swap = [(0, 1), (1, 0)]

    def own_and_other(rows):
        halves = rows.reshape(ranks, tok_rows, width)
        return pick(halves, rank, 0), pick(halves, 1 - rank, 0)

    def swapped(given):
        return lax.ppermute(given, "ctx", swap)

    def settle(halves, flips):
        micro_rows = []
        for micro in range(2):
            pair = [jnp.where(rank == micro, kept, got) for kept, got in halves]
            flip = flips[micro]
            micro_rows.append(
                jnp.stack([jnp.where(flip, pair[1], pair[0]), jnp.where(flip, pair[0], pair[1])])
            )
        return jnp.stack(micro_rows)

    if quick:
        flips = flags[:, 1] == 1
        flip = pick(flips, rank, 0)
        told = jnp.stack([flip.astype(jnp.int32), rank.astype(jnp.int32)])
        got = swapped(give)
        give_grad = behind(pick(cotangent, 1 - rank, 0), got, expand_full)
        flags = pick(flags, rank, 0)
        flags = jnp.where(flip, flags[::-1], flags)
        segs = segs_local
        seg_rows = ranks * tok_rows
    else:
        rows_in, rows_grad = tokens.reshape(-1, width), cotangent.reshape(-1, width)
        flags = flags.reshape(-1)
        segs = micros * segs_local
        seg_rows = tok_rows

    kv_first, kv_follow, m = memory_forward(memory_tokens, p)
    kv_mem = jnp.where((flags == 0)[:, None, None], kv_follow[None], kv_first[None])
    if quick:
        rows_in, normed_a, qkv = enter(
            told, pick(tokens, rank, 0), got, norm_one_gain, norm_one_bias, qkv_read_key, p["shift"]
        )
        attended, lse_first = attn_fwd(behind(qkv, give_grad), kv_first, 0, seg_rows, None)
        got_grad = swapped(give_grad)
        attended, lse_second = attn_fwd(qkv, kv_mem[1], 1, seg_rows, attended)
        attended, got_grad = lax.optimization_barrier((attended, got_grad))
        (
            result, rows_grad, normed_b, activ, grad_expanded, grad_attn_out, grad_attended, mid_sums, expand_sums,
        ) = middle(
            told, pick(cotangent, rank, 0), got_grad, rows_in, attended, p["out"], p["expand"], p["contract"], out_bias,
            norm_two_gain, norm_two_bias, expand_bias, contract_bias,
        )
        grad_after = grad_attn_out
    else:
        hidden = rows_in.astype(F32)
        unit_a, rstd_a = norm_parts(hidden)
        normed_a = (unit_a * norm_one_gain + norm_one_bias).astype(BF16)
        qkv = (dot_dims(normed_a, p["qkv"], 1, 0) + p["shift"]).astype(BF16)
        seg_qkv = qkv.reshape(segs, seg_rows, 3 * width)
        kv_all = lax.all_gather(seg_qkv[:, :, width:], "ctx", axis=1, tiled=True)
        kv_all = jnp.concatenate([kv_mem, kv_all], axis=1)
        query_at = mem + rank * seg_rows + jnp.arange(seg_rows, dtype=jnp.int32)
        key_at = jnp.arange(mem + ranks * seg_rows, dtype=jnp.int32)
        allowed = key_at[None, :] <= query_at[:, None]
        attended, lse = plain_fwd(seg_qkv, kv_all, allowed)
        attended = attended.reshape(-1, width)
        after = hidden + dot_dims(attended, p["out"], 1, 0) + out_bias
        unit_b, rstd_b = norm_parts(after)
        normed_b = (unit_b * norm_two_gain + norm_two_bias).astype(BF16)
        expanded = dot_dims(normed_b, p["expand"], 1, 0) + expand_bias
        activ = gelu_tanh(expanded).astype(BF16)
        result = (after + dot_dims(activ, p["contract"], 1, 1) + contract_bias).astype(BF16)

    def input_back(at, grads, weights):
        grad = dot_dims(grads[0], weights[0], 1, 1)
        for g, w in zip(grads[1:], weights[1:]):
            grad = grad + dot_dims(g, w, 1, 1)
        unit, rstd = norm_parts(rows_in[at].astype(F32))
        grad_hidden, gain, bias = norm_back(grad, unit, rstd, norm_one_gain)
        return (grad_hidden + grad_after[at].astype(F32)).astype(BF16), gain, bias

    def pool(dkv_mem):
        follows = (flags == 0).astype(F32)[:, None, None]
        kinds = [jnp.sum(dkv_mem * (1.0 - follows), axis=0), jnp.sum(dkv_mem * follows, axis=0)]
        return jnp.stack(kinds)

    if quick:
        pairs, most = H // 2, H // 3
        cut = most * 2 * HD
        columns = lambda a, lo, hi: jnp.concatenate(
            [a[..., k * width + lo : k * width + hi] for k in range(3)], axis=-1
        )
        weights = [columns(p["qkv"], 0, cut), columns(p["qkv"], cut, width)]
        lse = jnp.concatenate([lse_first, lse_second], axis=0)
        mems = (kv_first, kv_mem[1])
        spans = [slice(0, seg_rows), slice(seg_rows, 2 * seg_rows)]

        block_halves = [own_and_other(result[a]) for a in spans]
        on_contract = Scatter(dot_dims(rows_grad, activ, 0, 0).astype(BF16))
        grad_expanded = behind(grad_expanded, on_contract.give)
        term_expand = dot_dims(normed_b, grad_expanded, 0, 0).astype(BF16)
        on_expand = Scatter(term_expand)
        on_contract.over_core(term_expand)
        grad_attn_out = behind(grad_attn_out, on_contract.give, on_expand.give)
        on_out = Scatter(dot_dims(attended, grad_attn_out, 0, 0).astype(BF16))
        dk_mem, dv_mem, middle_sums = attn_mem(
            qkv, kv_mem, attended, behind(grad_attended, on_out.give), lse
        )
        on_expand.over_core(middle_sums)
        pooled = pool(jnp.concatenate([dk_mem, dv_mem], axis=2))
        others = behind([other for _, other in block_halves], middle_sums)

        def back(seg, first, count, *earlier):
            grad = behind(grad_attended, *earlier)
            return attn_bwd(qkv, mems[seg], grad, lse, middle_sums, seg, first, count)

        normed = [normed_a[a] for a in spans]
        term = lambda grads: sum(dot_dims(normed[k], grads[k], 0, 0) for k in range(2)).astype(BF16)
        turn_a = back(0, 0, most, pooled, others, on_expand.give)
        pooled = sum_over(pooled, 0, turn_a)
        on_out.over_core(turn_a)
        on_contract.over_x(turn_a)
        turn_b = back(1, 0, most, turn_a, pooled, on_contract.give, on_out.give)
        pooled = sum_over(pooled, 1, turn_b)
        others = behind([swapped(other) for other in others], turn_b)
        block_halves = [(own, other) for (own, _), other in zip(block_halves, others)]
        on_expand.over_x(turn_b)
        on_contract.over_z(turn_b)
        most_grads = [turn_a, turn_b]
        on_most = Scatter(term(most_grads))
        turn_c = back(
            0, most, pairs - most, on_most.give, on_expand.give, on_contract.give, pooled
        )
        pooled = sum_over(pooled, 2, turn_c)
        on_most.over_core(turn_c)
        on_out.over_x(turn_c)
        got_contract = on_contract.over_y(turn_c)
        first_end = input_back(
            spans[0],
            [behind(most_grads[0], on_most.give, on_out.give, pooled), turn_c],
            weights,
        )
        kept_first, given_first = own_and_other(first_end[0])
        turn_d = back(1, most, pairs - most, given_first, got_contract)
        pooled = sum_over(pooled, 3, turn_d)
        on_expand.over_z(turn_d)
        on_most.over_x(turn_d)
        got_first = behind(swapped(given_first), turn_d)
        rest_grads = [turn_c, behind(turn_d, on_expand.give, on_most.give)]
        second_end = input_back(spans[1], [most_grads[1], rest_grads[1]], weights)
        kept_second, given_second = own_and_other(second_end[0])
        on_rest = Scatter(term(rest_grads))
        one_gain, one_bias = first_end[1] + second_end[1], first_end[2] + second_end[2]
        qkv_sums = [
            sum(jnp.sum(g[k].astype(F32), axis=0) for k in range(2)).reshape(3, -1)
            for g in (most_grads, rest_grads)
        ]
        qkv_sums = jnp.concatenate(qkv_sums, axis=1)
    else:
        _, gelu_pull = jax.vjp(gelu_tanh, expanded)
        grad_expanded = gelu_pull(dot_dims(rows_grad, p["contract"], 1, 0))[0].astype(BF16)
        grad_after, two_gain, two_bias = norm_back(
            dot_dims(grad_expanded, p["expand"], 1, 1), unit_b, rstd_b, norm_two_gain
        )
        grad_after = grad_after + rows_grad.astype(F32)
        grad_attn_out = grad_after.astype(BF16)
        grad_attended = dot_dims(grad_attn_out, p["out"], 1, 1).astype(BF16)
        dq, dkv = plain_bwd(
            seg_qkv, kv_all, allowed, lse, grad_attended.reshape(segs, seg_rows, width)
        )
        pooled = pool(dkv[:, :mem])
        dkv = lax.psum_scatter(
            dkv[:, mem:].astype(BF16), "ctx", scatter_dimension=1, tiled=True
        )
        grad_qkv = jnp.concatenate([dq.astype(BF16), dkv], axis=2).reshape(-1, 3 * width)
        grad_rows, one_gain, one_bias = input_back(slice(None), [grad_qkv], [p["qkv"]])
        terms = (
            dot_dims(normed_a, grad_qkv, 0, 0).astype(BF16),
            dot_dims(attended, grad_attn_out, 0, 0).astype(BF16),
            dot_dims(normed_b, grad_expanded, 0, 0).astype(BF16),
            dot_dims(rows_grad, activ, 0, 0).astype(BF16),
        )
        qkv_sums = jnp.sum(grad_qkv.astype(F32), axis=0).reshape(3, width)
    column_sum = lambda a: jnp.sum(a.astype(F32), axis=0)
    if quick:
        mid = (mid_sums[0], mid_sums[1], mid_sums[2], expand_sums[0], mid_sums[3])
    else:
        mid = (
            column_sum(grad_attn_out), two_gain, two_bias, column_sum(grad_expanded), column_sum(rows_grad),
        )
    vectors = (one_gain, one_bias, jnp.stack([qkv_sums[0], qkv_sums[2]]), *mid)
    flat = jnp.concatenate([v.reshape(-1) for v in vectors]).reshape(-1, 128)
    got = {}

    def turn(step, value):
        if not quick:
            return value
        if step == 0:
            return behind(value, flat, on_rest.give, on_most.give, given_second)
        if step == 1:
            got["second"] = behind(swapped(given_second), value)
            on_rest.over_core(value)
            on_most.over_z(value)
            on_out.over_z(value)
            got["flat"] = sum_over(flat, 0, value)
            return behind(value, on_rest.give, on_most.give, on_out.give, got["flat"])
        if step == 2:
            on_rest.over_x(value)
            got["most"], got["out"], got["expand"] = (
                on_most.over_y(value), on_out.over_y(value), on_expand.over_y(value)
            )
            got["flat"] = sum_over(sum_over(got["flat"], 1), 2, value)
            return behind(value, on_rest.give, got["flat"], got["most"], got["out"], got["expand"])
        return value

    if not quick:
        summed = tuple(
            lax.psum(
                lax.psum_scatter(t, "dp", scatter_dimension=0, tiled=True).astype(F32), "ctx"
            )
            for t in terms
        )
        pooled, vectors = lax.psum((pooled, vectors), ("dp", "ctx"))

    mine = lambda a: lax.dynamic_slice_in_dim(a, group * shard, shard, 1)
    grad_mt, mem_matrices, mem_vectors = memory_backward(
        memory_tokens, p, m, pooled[0], pooled[1], mine, turn
    )
    if quick:
        most_part = got["most"].reshape(shard, 3, cut)
        rest_part = on_rest.over_z().over_y().reshape(shard, 3, width - cut)
        summed = (
            jnp.concatenate([most_part, rest_part], axis=2).reshape(shard, 3 * width),
            got["out"],
            got["expand"],
            got_contract,
        )
        flat = sum_over(got["flat"], 3).reshape(-1)
        split, place = [], 0
        for v in vectors:
            split.append(flat[place : place + v.size].reshape(v.shape))
            place += v.size
        vectors = tuple(split)
    matrices = tuple(a + b for a, b in zip(summed, mem_matrices)) + mem_matrices[4:]
    vectors = tuple(a + b for a, b in zip(vectors, mem_vectors))
    if quick:
        block_out = settle(block_halves, flips)
        token_grad = settle([(kept_first, got_first), (kept_second, got["second"])], flips)
    else:
        block_out, token_grad = result.reshape(tokens.shape), grad_rows.reshape(tokens.shape)
    return (
        block_out,
        token_grad,
        grad_mt,
        vectors[0],
        vectors[1],
        matrices[0],
        vectors[2],
        matrices[1],
        vectors[3],
        vectors[4],
        vectors[5],
        matrices[2],
        vectors[6],
        matrices[3],
        vectors[7],
        matrices[4],
        matrices[5],
        matrices[6],
    )


def solution(mesh):
    rows = P(None, "dp", "ctx", None)
    matrix = P("dp", None)
    full = P()
    return jax.shard_map(
        local,
        mesh=mesh,
        in_specs=(
            rows, rows, full, full, full, full, full, matrix, full, matrix, full, full, full,
            matrix, full, matrix, full, matrix, matrix, matrix,
        ),
        out_specs=(
            rows, rows, full, full, full, matrix, full, matrix, full, full, full, matrix, full,
            matrix, full, matrix, matrix, matrix,
        ),
        check_vma=False,
    )
```

time: 831 us -> 597 us (0.72)
  waiting for transfers between devices: 251 us -> 31.7 us
  Pallas kernels: 130 us -> 284 us
  matrix products: 210 us -> 102 us
  starting transfers between devices: 93.3 us -> 59.7 us
  other arithmetic: 63.7 us -> 45.2 us
  local copies, waits for them, and re-layouts: 72.9 us -> 60.5 us
    ppermute x58 -> x48, waiting for transfers between devices: 251 us -> 31.7 us  [the longest x5 14.5 us: over_y(): got = behind(lax.ppermute(self.give, 'ctx', [(0, 1), (1, 0)]), *beside)]
    pallas_call x5 -> x10, Pallas kernels: 130 us -> 284 us  [the longest x1 80.3 us: gather_weights(): pl.pallas_call(functools.partial(gather_kernel, halved, count, kinds), in...]
    dot_general x42 -> x41, matrix products: 201 us -> 96.1 us  [dot_dims(): lax.dot_general(a, b, (((ca,), (cb,)), ((), ())), precision=precision, pr...]
    ppermute x58 -> x48, starting transfers between devices: 93.3 us -> 59.7 us  [the longest x15 27.2 us: over_z(): lax.ppermute(self.give[k - 1], 'dp', dp_pairs(4 * k))]
    dynamic_slice x8 -> x10, local copies, waits for them, and re-layouts: 20.1 us -> 4.22 us  [pick(): return lax.dynamic_index_in_dim(parts, at, axis, keepdims=False)]
    reduce_sum x4 -> x5, other arithmetic: 13.1 us -> 1.65 us  [the longest x4 1.55 us: local(): jnp.sum(g[k].astype(F32), axis=0)]
    squeeze x12 -> x16, local copies, waits for them, and re-layouts: 7.69 us -> 18.3 us  [pick(): return lax.dynamic_index_in_dim(parts, at, axis, keepdims=False)]
    unnamed x440 -> x401, local copies, waits for them, and re-layouts: 14.7 us -> 21.3 us
  transfers between devices with their start and end apart: 58 -> 48, of which waited for: 24 -> 8; matrix products, arithmetic and copies ran while one was open for 18% -> 28% of each run, Pallas kernels for 1% -> 36%
where the time goes in v2:
time: 597 us; the launch traced here: 588 us
  Pallas kernels  284 us (48%)
  matrix products  102 us (17%)
  local copies, waits for them, and re-layouts  60.5 us (10%)
  starting transfers between devices  59.7 us (10%)
  other arithmetic  45.2 us (8%)
  waiting for transfers between devices  31.7 us (5%)
    dot_general x41, matrix products, dot_dims(): lax.dot_general(a, b, (((ca,), (cb,)), ((), ())), precision=precision, pr...  96.1 us
    pallas_call x1, Pallas kernels, gather_weights(): pl.pallas_call(functools.partial(gather_kernel, halved, count, kinds), in...  80.3 us
    pallas_call x1, Pallas kernels, middle(): pl.pallas_call(middle_kernel, grid_spec=pltpu.PrefetchScalarGridSpec(num_...  69.3 us
    pallas_call x4, Pallas kernels, attn_bwd(): pl.pallas_call(attn_bwd_kernel, grid=(count, 3), in_specs=[spec(0), spec(...  65.2 us
    pallas_call x2, Pallas kernels, attn_fwd(): pl.pallas_call(attn_fwd_kernel if held is None else attn_fwd_after_kernel...  45 us
    ppermute x15, starting transfers between devices, over_z(): lax.ppermute(self.give[k - 1], 'dp', dp_pairs(4 * k))  27.2 us
    unnamed x401, local copies, waits for them, and re-layouts  21.3 us
    squeeze x16, local copies, waits for them, and re-layouts, pick(): return lax.dynamic_index_in_dim(parts, at, axis, keepdims=False)  18.3 us
  transfers between devices with their start and end apart: 48, of which 8 were waited for; matrix products, arithmetic and copies ran while one was open for 28% of the time, Pallas kernels for 36%

profile of v2, /device:TPU:0, one launch (start us, length us, event | category | flops | bytes accessed | tf_op | source)
XLA Modules:
  0.0 588.3 jit_solution(17321891033618521754)
XLA Ops:
  0.7 3.9 dynamic-slice_bitcast_fusion.1
  4.6 3.0 collective-permute-start
  7.7 80.3 %gather_weights.1 = (bf16[768,3072]{1,0:T(8,128)(2,1)S(1)}, bf16[768,3072]{1,0:T(8,128)(2,1)S(1)}, bf16[768,3072]{1,0:T(8,128)(2,1)S(1)}, bf16[768,1536]{1,0:T(8,128)(2,1)S(1)}) custom-call(bf16[48,3072]{1,0:T(8,128)(2,1)S(1)} %pad_maximum_fusion.9.refs_0_, bf16[48,3072]{1,0:T(8,128)(2,1)S(1)} %copy-done.14, bf16[48,3072]{1,0:T(8,128)(2,1)S(1)} %copy-done.15, ...), custom_call_target="tpu_custom_call" | custom-call | flops 80000000000 | bytes 33030144 | tf_op jit(solution)/shard_map/gather_weights/pallas_call | solution.py:567
  88.1 2.1 copy-done.1
  90.2 2.1 copy-done.3
  92.3 2.1 copy-done
  96.2 2.6 fusion.14
  101.2 3.2 convolution_add_fusion.4
  106.9 2.0 compare_select_fusion.2
  112.8 2.3 fusion.191
  117.8 3.8 dynamic-slice_bitcast_fusion
  126.5 2.1 fusion.35
  128.6 3.2 fusion.192
  134.1 14.3 %enter.1 = (bf16[2048,768]{1,0:T(8,128)(2,1)}, bf16[2048,768]{1,0:T(8,128)(2,1)}, bf16[2048,2304]{1,0:T(8,128)(2,1)}) custom-call(s32[2]{0:T(128)S(1)} %pad_add_fusion.told, bf16[2,512,768]{2,1,0:T(8,128)(2,1)S(1)} %copy-done.7, bf16[2,512,768]{2,1,0:T(8,128)(2,1)} %collective-permute-done.got, f32[1,768]{1,0:T(1,128)S(1)} %broadcast_in_dim.64.gain, ...), custom_call_target="tpu_custom_call" | custom-call | flops 14495514624 | bytes 22020096 | tf_op jit(solution)/shard_map/enter/pallas_call | solution.py:303
  148.4 3.7 copy-done.19
  152.1 22.5 %attn_fwd.2 = (bf16[2048,768]{1,0:T(8,128)(2,1)S(1)}, f32[6,2,1024]{2,1,0:T(2,128)S(1)}) custom-call(bf16[2048,2304]{1,0:T(8,128)(2,1)S(1)} %copy-done.19, bf16[2048,2304]{1,0:T(8,128)(2,1)S(1)} %copy-done.19, bf16[2048,2304]{1,0:T(8,128)(2,1)S(1)} %copy-done.19, bf16[16,1536]{1,0:T(8,128)(2,1)S(1)} %get-tuple-element.307.km_ref.vm_ref, ...), custom_call_target="tpu_custom_call" | custom-call | flops 25165824000 | bytes 6291456 | tf_op jit(solution)/shard_map/attn_fwd/pallas_call | solution.py:108
  174.6 22.5 %attn_fwd.3 = (bf16[2048,768]{1,0:T(8,128)(2,1)S(1)}, f32[6,2,1024]{2,1,0:T(2,128)S(1)}) custom-call(bf16[2048,2304]{1,0:T(8,128)(2,1)S(1)} %copy-done.19, bf16[2048,2304]{1,0:T(8,128)(2,1)S(1)} %copy-done.19, bf16[2048,2304]{1,0:T(8,128)(2,1)S(1)} %copy-done.19, ...), custom_call_target="tpu_custom_call", output_to_operand_aliasing={{0}: (5, {})} | custom-call | flops 25165824000 | bytes 6291456 | tf_op jit(solution)/shard_map/attn_fwd/pallas_call | solution.py:108
  199.4 69.3 %middle.1 = (bf16[2048,768]{1,0:T(8,128)(2,1)}, bf16[2048,768]{1,0:T(8,128)(2,1)}, bf16[2048,768]{1,0:T(8,128)(2,1)}, bf16[2048,3072]{1,0:T(8,128)(2,1)}, bf16[2...) custom-call(s32[2]{0:T(128)} %copy-done.16, ...), custom_call_target="tpu_custom_call" | custom-call | flops 86973087744 | bytes 47185920 | tf_op jit(solution)/shard_map/middle/pallas_call | solution.py:380
  268.6 13.9 %convolution_convert_fusion.1 = bf16[768,3072]{1,0:T(8,128)(2,1)S(1)} fusion(bf16[2048,768]{1,0:T(8,128)(2,1)} %get-tuple-element.138, bf16[2048,3072]{1,0:T(8,128)(2,1)} %get-tuple-element.139), kind=kOutput, calls=%fused_computation.4 | convolution fusion | flops 9666035712 | bytes 20447232 | tf_op jit(solution)/shard_map/dot_general | solution.py:43
  284.9 13.2 %convolution_convert_fusion = bf16[768,3072]{1,0:T(8,128)(2,1)S(1)} fusion(bf16[2048,768]{1,0:T(8,128)(2,1)S(1)} %copy-done.187, bf16[2048,3072]{1,0:T(8,128)(2,1)} %get-tuple-element.142), kind=kOutput, calls=%fused_computation.3 | convolution fusion | flops 9666035712 | bytes 20447232 | tf_op jit(solution)/shard_map/dot_general | solution.py:43
  305.7 2.7 convolution_convert_fusion.2
  310.3 9.9 %attn_mem.1 = (f32[2,16,768]{2,1,0:T(8,128)S(1)}, f32[2,16,768]{2,1,0:T(8,128)S(1)}, f32[12,2,1024]{2,1,0:T(2,128)S(1)}) custom-call(bf16[2048,2304]{1,0:T(8,128)(2,1)} %get-tuple-element.129.q_ref.k_ref.v_ref, bf16[2,16,1536]{2,1,0:T(8,128)(2,1)S(1)} %copy-done.9, bf16[2,16,1536]{2,1,0:T(8,128)(2,1)S(1)} %copy-done.9, bf16[2048,768]{1,0:T(8,128)(2,1)S(1)} %copy-done.18, ...), custom_call_target="tpu_custom_call" | custom-call | flops 6291456000 | bytes 9437184 | tf_op jit(solution)/shard_map/attn_mem/pallas_call | solution.py:161
  325.2 21.4 %attn_bwd.4 = bf16[1024,1536]{1,0:T(8,128)(2,1)S(1)} custom-call(bf16[2048,2304]{1,0:T(8,128)(2,1)} %get-tuple-element.129.q_ref.k_ref.v_ref, bf16[2048,2304]{1,0:T(8,128)(2,1)} %get-tuple-element.129.q_ref.k_ref.v_ref, bf16[2048,2304]{1,0:T(8,128)(2,1)} %get-tuple-element.129.q_ref.k_ref.v_ref, bf16[16,1536]{1,0:T(8,128)(2,1)S(1)} %copy-done.11, ...), custom_call_target="tpu_custom_call" | custom-call | flops 27262976000 | bytes 9437184 | tf_op jit(solution)/shard_map/attn_bwd/pallas_call | solution.py:244
  353.3 22.1 %attn_bwd.5 = bf16[1024,1536]{1,0:T(8,128)(2,1)S(1)} custom-call(bf16[2048,2304]{1,0:T(8,128)(2,1)} %get-tuple-element.129.q_ref.k_ref.v_ref, bf16[2048,2304]{1,0:T(8,128)(2,1)} %get-tuple-element.129.q_ref.k_ref.v_ref, bf16[2048,2304]{1,0:T(8,128)(2,1)} %get-tuple-element.129.q_ref.k_ref.v_ref, bf16[16,1536]{1,0:T(8,128)(2,1)S(1)} %copy-done.13, ...), custom_call_target="tpu_custom_call" | custom-call | flops 27262976000 | bytes 9437184 | tf_op jit(solution)/shard_map/attn_bwd/pallas_call | solution.py:244
  375.4 2.6 fusion.41
  378.1 3.9 add_convert_fusion
  384.1 1.9 constant_dynamic-slice_fusion.10
  386.1 2.6 collective-permute-start.12
  388.8 1.8 fusion.32
  392.6 2.9 select_bitcast_fusion.7
  395.9 1.9 pad_maximum_fusion
  398.8 10.8 %collective-permute-done.12 = bf16[48,3072]{1,0:T(8,128)(2,1)S(1)} collective-permute-done((bf16[48,3072]{1,0:T(8,128)(2,1)S(1)}, bf16[48,3072]{1,0:T(8,128)(2,1)S(1)}, u32[]{:S(2)}, u32[]{:S(2)}) %collective-permute-start.12) | collective-permute-done | bytes 294944 | tf_op jit(solution)/shard_map/ppermute | solution.py:624
  409.6 6.9 %collective-permute-start.19 = (bf16[48,3072]{1,0:T(8,128)(2,1)}, bf16[48,3072]{1,0:T(8,128)(2,1)}, u32[]{:S(2)}, u32[]{:S(2)}) collective-permute-start(bf16[48,3072]{1,0:T(8,128)(2,1)} %get-tuple-element.284), channel_id=1, source_target_pairs={{0,16},{2,18},{4,20},{6,22},{8,24},{10,26},{12,28},{14,30},{16,0},... | collective-permute-start | bytes 884744 | tf_op jit(solution)/shard_map/ppermute | solution.py:624
  417.7 10.9 %attn_bwd.6 = bf16[1024,768]{1,0:T(8,128)(2,1)S(1)} custom-call(bf16[2048,2304]{1,0:T(8,128)(2,1)} %get-tuple-element.129.q_ref.k_ref.v_ref, bf16[2048,2304]{1,0:T(8,128)(2,1)} %get-tuple-element.129.q_ref.k_ref.v_ref, bf16[2048,2304]{1,0:T(8,128)(2,1)} %get-tuple-element.129.q_ref.k_ref.v_ref, bf16[16,1536]{1,0:T(8,128)(2,1)S(1)} %copy-done.11, ...), custom_call_target="tpu_custom_call" | custom-call | flops 13631488000 | bytes 4718592 | tf_op jit(solution)/shard_map/attn_bwd/pallas_call | solution.py:244
  434.5 3.9 collective-permute-done.17
  438.4 3.0 collective-permute-start.24
  443.3 2.6 fusion.60
  446.0 2.5 fusion.20
  450.9 10.8 %attn_bwd.7 = bf16[1024,768]{1,0:T(8,128)(2,1)S(1)} custom-call(bf16[2048,2304]{1,0:T(8,128)(2,1)} %get-tuple-element.129.q_ref.k_ref.v_ref, bf16[2048,2304]{1,0:T(8,128)(2,1)} %get-tuple-element.129.q_ref.k_ref.v_ref, bf16[2048,2304]{1,0:T(8,128)(2,1)} %get-tuple-element.129.q_ref.k_ref.v_ref, bf16[16,1536]{1,0:T(8,128)(2,1)S(1)} %copy-done.13, ...), custom_call_target="tpu_custom_call" | custom-call | flops 13631488000 | bytes 4718592 | tf_op jit(solution)/shard_map/attn_bwd/pallas_call | solution.py:244
  463.2 3.0 collective-permute-start.32
  468.2 2.4 collective-permute-done.25
  474.0 2.3 fusion.64
  476.3 2.7 collective-permute-done.21
  481.7 3.1 fusion.75
  487.4 7.5 %fusion.27 = (f32[768]{0:T(1024)S(1)}, f32[1024]{0:T(1024)S(1)}, f32[1024]{0:T(1024)S(1)}, f32[768]{0:T(1024)S(1)}, f32[1024,768]{1,0:T(8,128)S(1)}) fusion(f32[1024]{0:T(1024)S(1)} %add_rsqrt_fusion.1, f32[1024]{0:T(1024)S(1)} %copy-done.152, bf16[2048,768]{1,0:T(8,128)(2,1)} %get-tuple-element.133.rows_ref, f32[768]{0:T(1024)S(1)} %copy-done.115, ...), kind=kOutput, calls=%fused_computation.43 | convolution fusion | flops 2431644160 | bytes 13394944 | tf_op jit(solution)/shard_map/dot_general | solution.py:43
  499.0 2.2 multiply_reduce_fusion.7
  510.3 1.7 fusion.149
  512.1 1.8 fusion.147
  516.3 2.0 collective-permute-start.29
  522.3 1.7 fusion.145
  532.7 1.9 multiply_reduce_fusion.5
  538.1 1.9 convolution_bitcast_fusion.1
  544.9 2.8 collective-permute-start.42
  547.6 2.1 convolution_add_fusion.1
  549.7 7.5 %collective-permute-done.38 = bf16[48,1536]{1,0:T(8,128)(2,1)} collective-permute-done((bf16[48,1536]{1,0:T(8,128)(2,1)S(1)}, bf16[48,1536]{1,0:T(8,128)(2,1)}, u32[]{:S(2)}, u32[]{:S(2)}) %collective-permute-start.38) | collective-permute-done | bytes 147488 | tf_op jit(solution)/shard_map/ppermute | solution.py:632
  557.3 2.5 collective-permute-start.43
  560.7 2.2 convolution_add_fusion.2
  563.4 1.9 convolution_add_fusion.8
  566.1 3.2 select_bitcast_fusion.3
  569.7 1.9 pad_maximum_fusion.1
  573.1 2.0 collective-permute-start.45
  575.0 2.4 collective-permute-start.46
  582.7 3.1 collective-permute-done.47
  586.1 1.8 fusion.13
  (699 shorter events, 118.4 us)
Async XLA Ops:
  4.6 128.0 %collective-permute-start = (bf16[2,512,768]{2,1,0:T(8,128)(2,1)}, bf16[2,512,768]{2,1,0:T(8,128)(2,1)}, u32[]{:S(2)}, u32[]{:S(2)}) collective-permute-start(bf16[2,512,768]{2,1,0:T(8,128)(2,1)} %get-tuple-element.277), channel_id=1, source_target_pairs={{0,1},{1,0},{2,3},{3,2},{4,5},{5,4},{6,7},{7,6},{8,9},{9,8},{10,11... | collective-permute-start | bytes 4718600 | tf_op jit(solution)/shard_map/ppermute | solution.py:861
  7.6 91.9 %copy-start.165 = (pred[16,16]{0,1:T(8,128)(4,1)}, pred[16,16]{0,1:T(8,128)(4,1)S(1)}, u32[]{:S(2)}) copy-start(pred[16,16]{0,1:T(8,128)(4,1)S(1)} %iota_compare_fusion) | copy-start | bytes 772
  7.7 86.7 %copy-start.41 = (f32[16,768]{1,0:T(8,128)S(1)}, f32[16,768]{1,0:T(8,128)}, u32[]{:S(2)}) copy-start(f32[16,768]{1,0:T(8,128)} %param.24) | copy-start | bytes 147460
  7.7 87.9 %copy-start.171 = (f32[2,768]{1,0:T(2,128)S(1)}, f32[2,768]{1,0:T(2,128)}, u32[]{:S(2)}) copy-start(f32[2,768]{1,0:T(2,128)} %param.28) | copy-start | bytes 18436
  7.7 88.1 %copy-start.114 = (f32[768]{0:T(1024)S(1)}, f32[768]{0:T(1024)}, u32[]{:S(2)}) copy-start(f32[768]{0:T(1024)} %param.25) | copy-start | bytes 9220
  7.7 88.1 %copy-start.147 = (f32[768]{0:T(1024)S(1)}, f32[768]{0:T(1024)}, u32[]{:S(2)}) copy-start(f32[768]{0:T(1024)} %param.26) | copy-start | bytes 9220
  95.3 26.2 %copy-start.55 = (f32[16,384]{1,0:T(8,128)}, f32[16,384]{1,0:T(8,128)S(1)}, u32[]{:S(2)}) copy-start(f32[16,384]{1,0:T(8,128)S(1)} %get-tuple-element.323) | copy-start | bytes 73732
  98.9 49.6 %copy-start.10 = (bf16[16,1536]{1,0:T(8,128)(2,1)}, bf16[16,1536]{1,0:T(8,128)(2,1)S(1)}, u32[]{:S(2)}) copy-start(bf16[16,1536]{1,0:T(8,128)(2,1)S(1)} %get-tuple-element.307.km_ref.vm_ref) | copy-start | bytes 147460
  132.6 42.0 %copy-start.12 = (bf16[16,1536]{1,0:T(8,128)(2,1)}, bf16[16,1536]{1,0:T(8,128)(2,1)S(1)}, u32[]{:S(2)}) copy-start(bf16[16,1536]{1,0:T(8,128)(2,1)S(1)} %slice_bitcast_fusion.1.km_ref.vm_ref) | copy-start | bytes 147460
  132.6 66.8 %collective-permute-start.1 = (bf16[2,512,768]{2,1,0:T(8,128)(2,1)}, bf16[2,512,768]{2,1,0:T(8,128)(2,1)}, u32[]{:S(2)}, u32[]{:S(2)}) collective-permute-start(bf16[2,512,768]{2,1,0:T(8,128)(2,1)} %get-tuple-element.128), channel_id=1, source_target_pairs={{0,1},{1,0},{2,3},{3,2},{4,5},{5,4},{6,7},{7,6},{8,9},{9,8},{10,11... | collective-permute-start | bytes 4718600 | tf_op jit(solution)/shard_map/ppermute | solution.py:861
  283.2 19.0 %collective-permute-start.2 = (bf16[4,2,48,3072]{3,2,0,1:T(8,128)(2,1)S(1)}, bf16[4,2,48,3072]{3,2,0,1:T(8,128)(2,1)S(1)}, u32[]{:S(2)}, u32[]{:S(2)}) collective-permute-start(bf16[4,2,48,3072]{3,2,0,1:T(8,128)(2,1)S(1)} %bitcast.340), channel_id=1, source_target_pairs={{0,2},{2,0},{4,6},{6,4},{8,10},{10,8},{12,14},{14,12},{16,18},{18,... | collective-permute-start | bytes 7077896 | tf_op jit(solution)/shard_map/ppermute | solution.py:611
  298.8 21.4 %collective-permute-start.5 = (bf16[4,2,48,3072]{3,2,0,1:T(8,128)(2,1)S(1)}, bf16[4,2,48,3072]{3,2,0,1:T(8,128)(2,1)S(1)}, u32[]{:S(2)}, u32[]{:S(2)}) collective-permute-start(bf16[4,2,48,3072]{3,2,0,1:T(8,128)(2,1)S(1)} %bitcast.339), channel_id=1, source_target_pairs={{0,2},{2,0},{4,6},{6,4},{8,10},{10,8},{12,14},{14,12},{16,18},{18,... | collective-permute-start | bytes 7077896 | tf_op jit(solution)/shard_map/ppermute | solution.py:611
  303.9 44.9 %collective-permute-start.7 = (bf16[4,48,3072]{2,1,0:T(8,128)(2,1)S(1)}, bf16[4,48,3072]{2,1,0:T(8,128)(2,1)}, u32[]{:S(2)}, u32[]{:S(2)}) collective-permute-start(bf16[4,48,3072]{2,1,0:T(8,128)(2,1)S(1)} %dynamic-slice_bitcast_fusion.5), channel_id=1, source_target_pairs={{0,4},{2,6},{4,0},{6,2},{8,12},{10,14},{12,8},{14,10},{16,20},{18,... | collective-permute-start | bytes 3538952 | tf_op jit(solution)/shard_map/ppermute | solution.py:617
  308.5 39.2 %collective-permute-start.8 = (bf16[4,2,48,768]{3,2,0,1:T(8,128)(2,1)S(1)}, bf16[4,2,48,768]{3,2,0,1:T(8,128)(2,1)S(1)}, u32[]{:S(2)}, u32[]{:S(2)}) collective-permute-start(bf16[4,2,48,768]{3,2,0,1:T(8,128)(2,1)S(1)} %bitcast.353), channel_id=1, source_target_pairs={{0,2},{2,0},{4,6},{6,4},{8,10},{10,8},{12,14},{14,12},{16,18},{18,... | collective-permute-start | bytes 1769480 | tf_op jit(solution)/shard_map/ppermute | solution.py:611
  322.6 24.6 %collective-permute-start.6 = (f32[2,16,1536]{2,1,0:T(8,128)S(1)}, f32[2,16,1536]{2,1,0:T(8,128)S(1)}, u32[]{:S(2)}, u32[]{:S(2)}) collective-permute-start(f32[2,16,1536]{2,1,0:T(8,128)S(1)} %pad_maximum_fusion.10), channel_id=1, source_target_pairs={{0,1},{1,0},{2,3},{3,2},{4,5},{5,4},{6,7},{7,6},{8,9},{9,8},{10,11... | collective-permute-start | bytes 589832 | tf_op jit(solution)/shard_map/ppermute | solution.py:638
  323.1 63.0 %collective-permute-start.10 = (bf16[4,48,3072]{2,1,0:T(8,128)(2,1)}, bf16[4,48,3072]{2,1,0:T(8,128)(2,1)}, u32[]{:S(2)}, u32[]{:S(2)}) collective-permute-start(bf16[4,48,3072]{2,1,0:T(8,128)(2,1)} %dynamic-slice_bitcast_fusion.4), channel_id=1, source_target_pairs={{0,4},{2,6},{4,0},{6,2},{8,12},{10,14},{12,8},{14,10},{16,20},{18,... | collective-permute-start | bytes 3538952 | tf_op jit(solution)/shard_map/ppermute | solution.py:617
  323.6 67.0 %collective-permute-start.3 = (bf16[512,768]{1,0:T(8,128)(2,1)}, bf16[512,768]{1,0:T(8,128)(2,1)}, u32[]{:S(2)}, u32[]{:S(2)}) collective-permute-start(bf16[512,768]{1,0:T(8,128)(2,1)} %get-tuple-element.149), channel_id=1, source_target_pairs={{0,1},{1,0},{2,3},{3,2},{4,5},{5,4},{6,7},{7,6},{8,9},{9,8},{10,11... | collective-permute-start | bytes 2359304 | tf_op jit(solution)/shard_map/ppermute | solution.py:861
  347.2 44.9 %collective-permute-start.4 = (bf16[512,768]{1,0:T(8,128)(2,1)}, bf16[512,768]{1,0:T(8,128)(2,1)}, u32[]{:S(2)}, u32[]{:S(2)}) collective-permute-start(bf16[512,768]{1,0:T(8,128)(2,1)} %get-tuple-element.150), channel_id=1, source_target_pairs={{0,1},{1,0},{2,3},{3,2},{4,5},{5,4},{6,7},{7,6},{8,9},{9,8},{10,11... | collective-permute-start | bytes 2359304 | tf_op jit(solution)/shard_map/ppermute | solution.py:861
  347.7 34.2 %collective-permute-start.14 = (f32[2,16,1536]{2,1,0:T(8,128)S(1)}, f32[2,16,1536]{2,1,0:T(8,128)S(1)}, u32[]{:S(2)}, u32[]{:S(2)}) collective-permute-start(f32[2,16,1536]{2,1,0:T(8,128)S(1)} %fusion.180), channel_id=1, source_target_pairs={{0,2},{2,0},{4,6},{6,4},{8,10},{10,8},{12,14},{14,12},{16,18},{18,... | collective-permute-start | bytes 589832 | tf_op jit(solution)/shard_map/ppermute | solution.py:640
  348.9 81.9 %collective-permute-start.15 = (bf16[4,48,768]{2,1,0:T(8,128)(2,1)}, bf16[4,48,768]{2,1,0:T(8,128)(2,1)}, u32[]{:S(2)}, u32[]{:S(2)}) collective-permute-start(bf16[4,48,768]{2,1,0:T(8,128)(2,1)} %dynamic-slice_bitcast_fusion.15), channel_id=1, source_target_pairs={{0,4},{2,6},{4,0},{6,2},{8,12},{10,14},{12,8},{14,10},{16,20},{18,... | collective-permute-start | bytes 884744 | tf_op jit(solution)/shard_map/ppermute | solution.py:617
  382.0 16.8 %collective-permute-start.11 = (bf16[48,3072]{1,0:T(8,128)(2,1)}, bf16[48,3072]{1,0:T(8,128)(2,1)}, u32[]{:S(2)}, u32[]{:S(2)}) collective-permute-start(bf16[48,3072]{1,0:T(8,128)(2,1)} %get-tuple-element.290), channel_id=1, source_target_pairs={{0,8},{2,10},{4,12},{6,14},{8,0},{10,2},{12,4},{14,6},{16,24},{18,... | collective-permute-start | bytes 884744 | tf_op jit(solution)/shard_map/ppermute | solution.py:624
  386.1 23.5 %collective-permute-start.12 = (bf16[48,3072]{1,0:T(8,128)(2,1)S(1)}, bf16[48,3072]{1,0:T(8,128)(2,1)S(1)}, u32[]{:S(2)}, u32[]{:S(2)}) collective-permute-start(bf16[48,3072]{1,0:T(8,128)(2,1)S(1)} %copy-done.93), channel_id=1, source_target_pairs={{0,16},{2,18},{4,20},{6,22},{8,24},{10,26},{12,28},{14,30},{16,0},... | collective-permute-start | bytes 884744 | tf_op jit(solution)/shard_map/ppermute | solution.py:624
  390.7 18.9 %collective-permute-start.13 = (bf16[48,3072]{1,0:T(8,128)(2,1)S(1)}, bf16[48,3072]{1,0:T(8,128)(2,1)S(1)}, u32[]{:S(2)}, u32[]{:S(2)}) collective-permute-start(bf16[48,3072]{1,0:T(8,128)(2,1)S(1)} %copy-done.92), channel_id=1, source_target_pairs={{0,24},{2,26},{4,28},{6,30},{8,16},{10,18},{12,20},{14,22},{16,8},... | collective-permute-start | bytes 884744 | tf_op jit(solution)/shard_map/ppermute | solution.py:624
  392.1 36.6 %collective-permute-start.16 = (f32[2,16,1536]{2,1,0:T(8,128)S(1)}, f32[2,16,1536]{2,1,0:T(8,128)S(1)}, u32[]{:S(2)}, u32[]{:S(2)}) collective-permute-start(f32[2,16,1536]{2,1,0:T(8,128)S(1)} %fusion.241), channel_id=1, source_target_pairs={{0,4},{2,6},{4,0},{6,2},{8,12},{10,14},{12,8},{14,10},{16,20},{18,... | collective-permute-start | bytes 589832 | tf_op jit(solution)/shard_map/ppermute | solution.py:640
  398.8 39.6 %collective-permute-start.9 = (bf16[4,2,48,1536]{3,2,0,1:T(8,128)(2,1)S(1)}, bf16[4,2,48,1536]{3,2,0,1:T(8,128)(2,1)S(1)}, u32[]{:S(2)}, u32[]{:S(2)}) collective-permute-start(bf16[4,2,48,1536]{3,2,0,1:T(8,128)(2,1)S(1)} %bitcast.349), channel_id=1, source_target_pairs={{0,2},{2,0},{4,6},{6,4},{8,10},{10,8},{12,14},{14,12},{16,18},{18,... | collective-permute-start | bytes 3538952 | tf_op jit(solution)/shard_map/ppermute | solution.py:611
  409.6 52.2 %collective-permute-start.18 = (bf16[48,3072]{1,0:T(8,128)(2,1)}, bf16[48,3072]{1,0:T(8,128)(2,1)}, u32[]{:S(2)}, u32[]{:S(2)}) collective-permute-start(bf16[48,3072]{1,0:T(8,128)(2,1)} %get-tuple-element.285), channel_id=1, source_target_pairs={{0,8},{2,10},{4,12},{6,14},{8,0},{10,2},{12,4},{14,6},{16,24},{18,... | collective-permute-start | bytes 884744 | tf_op jit(solution)/shard_map/ppermute | solution.py:624
  409.6 53.6 %collective-permute-start.19 = (bf16[48,3072]{1,0:T(8,128)(2,1)}, bf16[48,3072]{1,0:T(8,128)(2,1)}, u32[]{:S(2)}, u32[]{:S(2)}) collective-permute-start(bf16[48,3072]{1,0:T(8,128)(2,1)} %get-tuple-element.284), channel_id=1, source_target_pairs={{0,16},{2,18},{4,20},{6,22},{8,24},{10,26},{12,28},{14,30},{16,0},... | collective-permute-start | bytes 884744 | tf_op jit(solution)/shard_map/ppermute | solution.py:624
  428.7 34.6 %collective-permute-start.20 = (bf16[48,3072]{1,0:T(8,128)(2,1)}, bf16[48,3072]{1,0:T(8,128)(2,1)}, u32[]{:S(2)}, u32[]{:S(2)}) collective-permute-start(bf16[48,3072]{1,0:T(8,128)(2,1)} %get-tuple-element.283), channel_id=1, source_target_pairs={{0,24},{2,26},{4,28},{6,30},{8,16},{10,18},{12,20},{14,22},{16,8},... | collective-permute-start | bytes 884744 | tf_op jit(solution)/shard_map/ppermute | solution.py:624
  430.8 7.6 %collective-permute-start.17 = (bf16[48,3072]{1,0:T(8,128)(2,1)S(1)}, bf16[48,3072]{1,0:T(8,128)(2,1)S(1)}, u32[]{:S(2)}, u32[]{:S(2)}) collective-permute-start(bf16[48,3072]{1,0:T(8,128)(2,1)S(1)} %fusion.68), channel_id=1, source_target_pairs={{0,1},{1,0},{2,3},{3,2},{4,5},{5,4},{6,7},{7,6},{8,9},{9,8},{10,11... | collective-permute-start | bytes 884744 | tf_op jit(solution)/shard_map/ppermute | solution.py:632
  438.4 27.9 %collective-permute-start.23 = (f32[2,16,1536]{2,1,0:T(8,128)}, f32[2,16,1536]{2,1,0:T(8,128)}, u32[]{:S(2)}, u32[]{:S(2)}) collective-permute-start(f32[2,16,1536]{2,1,0:T(8,128)} %add.577), channel_id=1, source_target_pairs={{0,8},{2,10},{4,12},{6,14},{8,0},{10,2},{12,4},{14,6},{16,24},{18,... | collective-permute-start | bytes 589832 | tf_op jit(solution)/shard_map/ppermute | solution.py:641
  438.4 29.2 %collective-permute-start.24 = (f32[2,16,1536]{2,1,0:T(8,128)}, f32[2,16,1536]{2,1,0:T(8,128)}, u32[]{:S(2)}, u32[]{:S(2)}) collective-permute-start(f32[2,16,1536]{2,1,0:T(8,128)} %add.577), channel_id=1, source_target_pairs={{0,16},{2,18},{4,20},{6,22},{8,24},{10,26},{12,28},{14,30},{16,0},... | collective-permute-start | bytes 589832 | tf_op jit(solution)/shard_map/ppermute | solution.py:641
  461.8 8.8 %collective-permute-start.25 = (f32[2,16,1536]{2,1,0:T(8,128)}, f32[2,16,1536]{2,1,0:T(8,128)S(1)}, u32[]{:S(2)}, u32[]{:S(2)}) collective-permute-start(f32[2,16,1536]{2,1,0:T(8,128)} %add.577), channel_id=1, source_target_pairs={{0,24},{2,26},{4,28},{6,30},{8,16},{10,18},{12,20},{14,22},{16,8},... | collective-permute-start | bytes 589832 | tf_op jit(solution)/shard_map/ppermute | solution.py:641
  463.2 52.0 %collective-permute-start.31 = (bf16[48,768]{1,0:T(8,128)(2,1)}, bf16[48,768]{1,0:T(8,128)(2,1)}, u32[]{:S(2)}, u32[]{:S(2)}) collective-permute-start(bf16[48,768]{1,0:T(8,128)(2,1)} %get-tuple-element.299), channel_id=1, source_target_pairs={{0,8},{2,10},{4,12},{6,14},{8,0},{10,2},{12,4},{14,6},{16,24},{18,... | collective-permute-start | bytes 221192 | tf_op jit(solution)/shard_map/ppermute | solution.py:624
  463.2 53.1 %collective-permute-start.32 = (bf16[48,768]{1,0:T(8,128)(2,1)}, bf16[48,768]{1,0:T(8,128)(2,1)}, u32[]{:S(2)}, u32[]{:S(2)}) collective-permute-start(bf16[48,768]{1,0:T(8,128)(2,1)} %get-tuple-element.298), channel_id=1, source_target_pairs={{0,16},{2,18},{4,20},{6,22},{8,24},{10,26},{12,28},{14,30},{16,0},... | collective-permute-start | bytes 221192 | tf_op jit(solution)/shard_map/ppermute | solution.py:624
  466.3 52.1 %collective-permute-start.33 = (bf16[48,768]{1,0:T(8,128)(2,1)}, bf16[48,768]{1,0:T(8,128)(2,1)}, u32[]{:S(2)}, u32[]{:S(2)}) collective-permute-start(bf16[48,768]{1,0:T(8,128)(2,1)} %get-tuple-element.297), channel_id=1, source_target_pairs={{0,24},{2,26},{4,28},{6,30},{8,16},{10,18},{12,20},{14,22},{16,8},... | collective-permute-start | bytes 221192 | tf_op jit(solution)/shard_map/ppermute | solution.py:624
  467.6 11.4 %collective-permute-start.21 = (bf16[4,48,1536]{2,1,0:T(8,128)(2,1)S(1)}, bf16[4,48,1536]{2,1,0:T(8,128)(2,1)S(1)}, u32[]{:S(2)}, u32[]{:S(2)}) collective-permute-start(bf16[4,48,1536]{2,1,0:T(8,128)(2,1)S(1)} %copy-done.69), channel_id=1, source_target_pairs={{0,4},{2,6},{4,0},{6,2},{8,12},{10,14},{12,8},{14,10},{16,20},{18,... | collective-permute-start | bytes 1769480 | tf_op jit(solution)/shard_map/ppermute | solution.py:617
  470.6 58.3 %collective-permute-start.26 = (bf16[512,768]{1,0:T(8,128)(2,1)}, bf16[512,768]{1,0:T(8,128)(2,1)}, u32[]{:S(2)}, u32[]{:S(2)}) collective-permute-start(bf16[512,768]{1,0:T(8,128)(2,1)} %dynamic-slice_bitcast_fusion.7), channel_id=1, source_target_pairs={{0,1},{1,0},{2,3},{3,2},{4,5},{5,4},{6,7},{7,6},{8,9},{9,8},{10,11... | collective-permute-start | bytes 2359304 | tf_op jit(solution)/shard_map/ppermute | solution.py:861
  494.9 26.4 %copy-start.74 = (f32[16,765]{1,0:T(8,128)S(1)}, f32[16,765]{1,0:T(8,128)}, u32[]{:S(2)}) copy-start(f32[16,765]{1,0:T(8,128)} %copy-done.73) | copy-start | bytes 146884
  495.0 26.4 %copy-start.76 = (f32[16,766]{1,0:T(8,128)S(1)}, f32[16,766]{1,0:T(8,128)}, u32[]{:S(2)}) copy-start(f32[16,766]{1,0:T(8,128)} %copy-done.75) | copy-start | bytes 147076
  495.0 26.4 %copy-start.78 = (f32[16,767]{1,0:T(8,128)S(1)}, f32[16,767]{1,0:T(8,128)}, u32[]{:S(2)}) copy-start(f32[16,767]{1,0:T(8,128)} %copy-done.77) | copy-start | bytes 147268
  495.0 36.8 %slice-start.4 = ((s8[4718592]{0:T(1024)(128)(4,1)}), s8[524288]{0:T(1024)(128)(4,1)S(1)}, s32[]{:S(2)}) async-start(s8[4718592]{0:T(1024)(128)(4,1)} %bitcast.324), calls=%async_computation.4 | async-start | bytes 1048576
  496.8 28.5 %copy-start.68 = (bf16[4,2,1,48,768]{4,3,0,1,2:T(8,128)(2,1)S(1)}, bf16[4,2,1,48,768]{4,3,0,1,2:T(8,128)(2,1)}, u32[]{:S(2)}) copy-start(bf16[4,2,1,48,768]{4,3,0,1,2:T(8,128)(2,1)} %copy.130) | copy-start | bytes 1769476
  499.0 32.8 %slice-start.5 = ((s8[4718592]{0:T(1024)(128)(4,1)}), s8[4194304]{0:T(1024)(128)(4,1)S(1)}, s32[]{:S(2)}) async-start(s8[4718592]{0:T(1024)(128)(4,1)} %bitcast.324), calls=%async_computation.5 | async-start | bytes 8388608
  499.0 33.6 %slice-start.6 = ((s8[4718592]{0:T(1024)(128)(4,1)}), s8[4194304]{0:T(1024)(128)(4,1)S(1)}, s32[]{:S(2)}) async-start(s8[4718592]{0:T(1024)(128)(4,1)} %bitcast.326), calls=%async_computation.6 | async-start | bytes 8388608
  506.2 17.8 %collective-permute-start.34 = (f32[72,128]{1,0:T(8,128)S(1)}, f32[72,128]{1,0:T(8,128)S(1)}, u32[]{:S(2)}, u32[]{:S(2)}) collective-permute-start(f32[72,128]{1,0:T(8,128)S(1)} %bitcast.355), channel_id=1, source_target_pairs={{0,1},{1,0},{2,3},{3,2},{4,5},{5,4},{6,7},{7,6},{8,9},{9,8},{10,11... | collective-permute-start | bytes 110600 | tf_op jit(solution)/shard_map/ppermute | solution.py:638
  515.2 10.9 %collective-permute-start.28 = (bf16[48,1536]{1,0:T(8,128)(2,1)S(1)}, bf16[48,1536]{1,0:T(8,128)(2,1)S(1)}, u32[]{:S(2)}, u32[]{:S(2)}) collective-permute-start(bf16[48,1536]{1,0:T(8,128)(2,1)S(1)} %copy-done.119), channel_id=1, source_target_pairs={{0,8},{2,10},{4,12},{6,14},{8,0},{10,2},{12,4},{14,6},{16,24},{18,... | collective-permute-start | bytes 442376 | tf_op jit(solution)/shard_map/ppermute | solution.py:624
  516.3 10.5 %collective-permute-start.29 = (bf16[48,1536]{1,0:T(8,128)(2,1)S(1)}, bf16[48,1536]{1,0:T(8,128)(2,1)S(1)}, u32[]{:S(2)}, u32[]{:S(2)}) collective-permute-start(bf16[48,1536]{1,0:T(8,128)(2,1)S(1)} %copy-done.118), channel_id=1, source_target_pairs={{0,16},{2,18},{4,20},{6,22},{8,24},{10,26},{12,28},{14,30},{16,0},... | collective-permute-start | bytes 442376 | tf_op jit(solution)/shard_map/ppermute | solution.py:624
  518.3 9.8 %collective-permute-start.30 = (bf16[48,1536]{1,0:T(8,128)(2,1)S(1)}, bf16[48,1536]{1,0:T(8,128)(2,1)S(1)}, u32[]{:S(2)}, u32[]{:S(2)}) collective-permute-start(bf16[48,1536]{1,0:T(8,128)(2,1)S(1)} %copy-done.117), channel_id=1, source_target_pairs={{0,24},{2,26},{4,28},{6,30},{8,16},{10,18},{12,20},{14,22},{16,8},... | collective-permute-start | bytes 442376 | tf_op jit(solution)/shard_map/ppermute | solution.py:624
  524.0 1.3 collective-permute-start.36
  525.3 4.2 collective-permute-start.27
  526.1 18.8 %collective-permute-start.40 = (bf16[48,3072]{1,0:T(8,128)(2,1)}, bf16[48,3072]{1,0:T(8,128)(2,1)}, u32[]{:S(2)}, u32[]{:S(2)}) collective-permute-start(bf16[48,3072]{1,0:T(8,128)(2,1)} %fusion.64), channel_id=1, source_target_pairs={{0,1},{1,0},{2,3},{3,2},{4,5},{5,4},{6,7},{7,6},{8,9},{9,8},{10,11... | collective-permute-start | bytes 884744 | tf_op jit(solution)/shard_map/ppermute | solution.py:632
  526.8 39.3 %collective-permute-start.22 = (bf16[512,768]{1,0:T(8,128)(2,1)}, bf16[512,768]{1,0:T(8,128)(2,1)}, u32[]{:S(2)}, u32[]{:S(2)}) collective-permute-start(bf16[512,768]{1,0:T(8,128)(2,1)} %dynamic-slice_bitcast_fusion.6), channel_id=1, source_target_pairs={{0,1},{1,0},{2,3},{3,2},{4,5},{5,4},{6,7},{7,6},{8,9},{9,8},{10,11... | collective-permute-start | bytes 2359304 | tf_op jit(solution)/shard_map/ppermute | solution.py:861
  528.1 34.8 %collective-permute-start.39 = (bf16[48,768]{1,0:T(8,128)(2,1)}, bf16[48,768]{1,0:T(8,128)(2,1)}, u32[]{:S(2)}, u32[]{:S(2)}) collective-permute-start(bf16[48,768]{1,0:T(8,128)(2,1)} %fusion.95), channel_id=1, source_target_pairs={{0,1},{1,0},{2,3},{3,2},{4,5},{5,4},{6,7},{7,6},{8,9},{9,8},{10,11... | collective-permute-start | bytes 221192 | tf_op jit(solution)/shard_map/ppermute | solution.py:632
  528.9 14.9 %collective-permute-start.37 = (f32[72,128]{1,0:T(8,128)}, f32[72,128]{1,0:T(8,128)}, u32[]{:S(2)}, u32[]{:S(2)}) collective-permute-start(f32[72,128]{1,0:T(8,128)} %fusion.240), channel_id=1, source_target_pairs={{0,4},{2,6},{4,0},{6,2},{8,12},{10,14},{12,8},{14,10},{16,20},{18,... | collective-permute-start | bytes 110600 | tf_op jit(solution)/shard_map/ppermute | solution.py:640
  529.5 27.8 %collective-permute-start.38 = (bf16[48,1536]{1,0:T(8,128)(2,1)S(1)}, bf16[48,1536]{1,0:T(8,128)(2,1)}, u32[]{:S(2)}, u32[]{:S(2)}) collective-permute-start(bf16[48,1536]{1,0:T(8,128)(2,1)S(1)} %fusion.78), channel_id=1, source_target_pairs={{0,1},{1,0},{2,3},{3,2},{4,5},{5,4},{6,7},{7,6},{8,9},{9,8},{10,11... | collective-permute-start | bytes 442376 | tf_op jit(solution)/shard_map/ppermute | solution.py:632
  535.4 28.0 %copy-start.71 = (f32[16,768]{1,0:T(8,128)}, f32[16,768]{1,0:T(8,128)S(1)}, u32[]{:S(2)}) copy-start(f32[16,768]{1,0:T(8,128)S(1)} %get-tuple-element.248) | copy-start | bytes 147460
  544.6 20.8 %collective-permute-start.41 = (f32[72,128]{1,0:T(8,128)S(1)}, f32[72,128]{1,0:T(8,128)S(1)}, u32[]{:S(2)}, u32[]{:S(2)}) collective-permute-start(f32[72,128]{1,0:T(8,128)S(1)} %add.614), channel_id=1, source_target_pairs={{0,8},{2,10},{4,12},{6,14},{8,0},{10,2},{12,4},{14,6},{16,24},{18,... | collective-permute-start | bytes 110600 | tf_op jit(solution)/shard_map/ppermute | solution.py:641
  544.9 20.6 %collective-permute-start.42 = (f32[72,128]{1,0:T(8,128)S(1)}, f32[72,128]{1,0:T(8,128)S(1)}, u32[]{:S(2)}, u32[]{:S(2)}) collective-permute-start(f32[72,128]{1,0:T(8,128)S(1)} %add.614), channel_id=1, source_target_pairs={{0,16},{2,18},{4,20},{6,22},{8,24},{10,26},{12,28},{14,30},{16,0},... | collective-permute-start | bytes 110600 | tf_op jit(solution)/shard_map/ppermute | solution.py:641
  557.3 8.2 %collective-permute-start.43 = (f32[72,128]{1,0:T(8,128)S(1)}, f32[72,128]{1,0:T(8,128)S(1)}, u32[]{:S(2)}, u32[]{:S(2)}) collective-permute-start(f32[72,128]{1,0:T(8,128)S(1)} %add.614), channel_id=1, source_target_pairs={{0,24},{2,26},{4,28},{6,30},{8,16},{10,18},{12,20},{14,22},{16,8},... | collective-permute-start | bytes 110600 | tf_op jit(solution)/shard_map/ppermute | solution.py:641
  562.9 8.7 %collective-permute-start.35 = (bf16[4,48,768]{2,1,0:T(8,128)(2,1)}, bf16[4,48,768]{2,1,0:T(8,128)(2,1)}, u32[]{:S(2)}, u32[]{:S(2)}) collective-permute-start(bf16[4,48,768]{2,1,0:T(8,128)(2,1)} %dynamic-slice_bitcast_fusion.11), channel_id=1, source_target_pairs={{0,4},{2,6},{4,0},{6,2},{8,12},{10,14},{12,8},{14,10},{16,20},{18,... | collective-permute-start | bytes 884744 | tf_op jit(solution)/shard_map/ppermute | solution.py:617
  573.0 7.8 %collective-permute-start.44 = (bf16[48,768]{1,0:T(8,128)(2,1)S(1)}, bf16[48,768]{1,0:T(8,128)(2,1)S(1)}, u32[]{:S(2)}, u32[]{:S(2)}) collective-permute-start(bf16[48,768]{1,0:T(8,128)(2,1)S(1)} %get-tuple-element.296), channel_id=1, source_target_pairs={{0,8},{2,10},{4,12},{6,14},{8,0},{10,2},{12,4},{14,6},{16,24},{18,... | collective-permute-start | bytes 221192 | tf_op jit(solution)/shard_map/ppermute | solution.py:624
  573.1 7.7 %collective-permute-start.45 = (bf16[48,768]{1,0:T(8,128)(2,1)S(1)}, bf16[48,768]{1,0:T(8,128)(2,1)S(1)}, u32[]{:S(2)}, u32[]{:S(2)}) collective-permute-start(bf16[48,768]{1,0:T(8,128)(2,1)S(1)} %get-tuple-element.295), channel_id=1, source_target_pairs={{0,16},{2,18},{4,20},{6,22},{8,24},{10,26},{12,28},{14,30},{16,0},... | collective-permute-start | bytes 221192 | tf_op jit(solution)/shard_map/ppermute | solution.py:624
  575.0 6.3 %collective-permute-start.46 = (bf16[48,768]{1,0:T(8,128)(2,1)S(1)}, bf16[48,768]{1,0:T(8,128)(2,1)S(1)}, u32[]{:S(2)}, u32[]{:S(2)}) collective-permute-start(bf16[48,768]{1,0:T(8,128)(2,1)S(1)} %get-tuple-element.294), channel_id=1, source_target_pairs={{0,24},{2,26},{4,28},{6,30},{8,16},{10,18},{12,20},{14,22},{16,8},... | collective-permute-start | bytes 221192 | tf_op jit(solution)/shard_map/ppermute | solution.py:624
  581.3 4.4 collective-permute-start.47
  (180 other events, 1300.3 us)

commit v3 on v2

--- a/solution.py
+++ b/solution.py
@@ -404,6 +404,277 @@
     )
 
 
+def thirds(rows):
+    parts = []
+    for _ in range(3):
+        parts.append(rows.astype(BF16))
+        rows = rows - parts[-1].astype(F32)
+    return jnp.concatenate(parts, axis=0)
+
+
+def exact_low(rows, weight, side):
+    count = rows.shape[0]
+    out = dot_dims(thirds(rows), weight, 1, side)
+    return out[:count] + out[count : 2 * count] + out[2 * count :]
+
+
+def softplus(rows):
+    return jnp.maximum(rows, 0.0) + jnp.log1p(jnp.exp(-jnp.abs(rows)))
+
+
+def feature_parts(rows):
+    halves = jnp.concatenate([softplus(rows), softplus(-rows)], axis=1)
+    turned = [pltpu.roll(halves, j, 1) for j in (1, 2, 3)]
+    return halves, turned, jnp.concatenate([halves * t for t in turned], axis=1)
+
+
+def feature_back(rows, grad):
+    halves, turned, _ = feature_parts(rows)
+    wide = halves.shape[1]
+    total = 0.0
+    for j in (1, 2, 3):
+        part = grad[:, (j - 1) * wide : j * wide]
+        total = total + part * turned[j - 1] + pltpu.roll(part * halves, wide - j, 1)
+    first, last = total[:, : wide // 2], total[:, wide // 2 :]
+    return first * jax.nn.sigmoid(rows) - last * jax.nn.sigmoid(-rows)
+
+
+def per_head(rows):
+    tall = jnp.concatenate([rows] * H, axis=0)
+    return tall * head_mask(tall.shape, rows.shape[0]).astype(rows.dtype)
+
+
+def head_mask(shape, count):
+    head = lax.broadcasted_iota(jnp.int32, shape, 0) // count
+    return (lax.broadcasted_iota(jnp.int32, shape, 1) // HD == head).astype(F32)
+
+
+def from_heads(tall, count):
+    tall = tall * head_mask(tall.shape, count)
+    total = tall[:count]
+    for head in range(1, H):
+        total = total + tall[head * count : (head + 1) * count]
+    return total
+
+
+def mem_weights(query, key):
+    count = key.shape[0]
+    tall = per_head(query)
+    scores = dot_dims(tall, key, 1, 1) * HD**-0.5
+    at = lax.rem(lax.broadcasted_iota(jnp.int32, scores.shape, 0), count)
+    raw = jnp.where(lax.broadcasted_iota(jnp.int32, scores.shape, 1) <= at, jnp.exp(scores), 0.0)
+    return tall, raw / jnp.sum(raw, axis=1, keepdims=True)
+
+
+def read_parts(read_feat, key_feat, value_new):
+    mix = exact(read_feat, key_feat, 1, 1)
+    return mix, exact(mix, value_new, 1, 0), 1.0 + jnp.sum(mix, axis=1, keepdims=True)
+
+
+def bring(sources, targets, sem):
+    copies = [pltpu.make_async_copy(a, b, sem.at[k]) for k, (a, b) in enumerate(zip(sources, targets))]
+    for copy in copies:
+        copy.start()
+    return copies
+
+
+def mem_fwd_kernel(
+    mt_ref, one_gain, one_bias, two_gain, two_bias, shift, out_b, expand_b, contract_b,
+    qrk_hbm, ov_hbm, expand_hbm, contract_hbm,
+    qkv_ref, attended_ref, after_ref, expanded_ref, result_ref, pre_ref, value_ref, follow_ref, kv_ref,
+    qrk, ov, expand_w, contract_w, sem,
+):
+    copies = bring((qrk_hbm, ov_hbm, expand_hbm, contract_hbm), (qrk, ov, expand_w, contract_w), sem)
+    mt = mt_ref[...]
+    width = mt.shape[1]
+    feat = pre_ref.shape[1] // 2
+    unit, _ = norm_parts(mt)
+    normed = (unit * one_gain[...] + one_bias[...]).astype(BF16)
+    copies[0].wait()
+    qkv = (dot_dims(normed, qrk[:, : 3 * width], 1, 0) + shift[...]).astype(BF16)
+    qkv_ref[...] = qkv
+    read_pre = exact_low(mt, qrk[:, 3 * width : 3 * width + feat], 0)
+    _, weights = mem_weights(qkv[:, :width], qkv[:, width : 2 * width])
+    mixed = dot_dims(weights.astype(BF16), qkv[:, 2 * width :], 1, 0)
+    attended = from_heads(mixed, mt.shape[0]).astype(BF16)
+    attended_ref[...] = attended
+    copies[1].wait()
+    after = mt + dot_dims(attended, ov[:, :width], 1, 0) + out_b[...]
+    after_ref[...] = after
+    unit, _ = norm_parts(after)
+    normed = (unit * two_gain[...] + two_bias[...]).astype(BF16)
+    copies[2].wait()
+    expanded = dot_dims(normed, expand_w[...], 1, 0) + expand_b[...]
+    expanded_ref[...] = expanded
+    activ = gelu_tanh(expanded).astype(BF16)
+    copies[3].wait()
+    result = after + dot_dims(activ, contract_w[...], 1, 1) + contract_b[...]
+    result_ref[...] = result
+    key_pre = exact_low(result, qrk[:, 3 * width + feat :], 0)
+    value_new = exact_low(result, ov[:, width:], 0)
+    value_ref[...] = value_new
+    pre_ref[:, :feat] = read_pre
+    pre_ref[:, feat:] = key_pre
+    _, numer, denom = read_parts(feature_parts(read_pre)[2], feature_parts(key_pre)[2], value_new)
+    follow = mt + numer / denom
+    follow_ref[...] = follow
+    unit, _ = norm_parts(follow)
+    normed = (unit * one_gain[...] + one_bias[...]).astype(BF16)
+    kv_ref[...] = (dot_dims(normed, qrk[:, width : 3 * width], 1, 0) + shift[:, width:]).astype(BF16)
+
+
+def mem_call(kernel, name, given, weights, outs, cycles):
+    vmem = pl.BlockSpec(memory_space=pltpu.VMEM)
+    return pl.pallas_call(
+        kernel,
+        in_specs=[vmem] * len(given) + [pl.BlockSpec(memory_space=pl.ANY)] * len(weights),
+        out_specs=[vmem] * len(outs),
+        out_shape=outs,
+        scratch_shapes=[
+            *[pltpu.VMEM(w.shape, w.dtype) for w in weights],
+            pltpu.SemaphoreType.DMA((len(weights),)),
+        ],
+        compiler_params=pltpu.CompilerParams(vmem_limit_bytes=48 * 2**20),
+        cost_estimate=pl.CostEstimate(flops=cycles * 10**9, bytes_accessed=17 * 10**6, transcendentals=0),
+        name=name,
+    )(*given, *weights)
+
+
+def mem_forward(mt, given, weights):
+    mem, width = mt.shape
+    wide, feat = weights[2].shape[1], (weights[0].shape[1] - 3 * width) // 2
+    shape = jax.ShapeDtypeStruct
+    outs = [
+        shape((mem, 3 * width), BF16), shape((mem, width), BF16), shape((mem, width), F32), shape((mem, wide), F32),
+        shape((mem, width), F32), shape((mem, 2 * feat), F32), shape((mem, width), F32), shape((mem, width), F32),
+        shape((mem, 2 * width), BF16),
+    ]
+    return mem_call(mem_fwd_kernel, "mem_fwd", (mt, *given), weights, outs, 15)
+
+
+def mem_bwd_kernel(
+    mt_ref, one_gain, one_bias, two_gain, two_bias, pooled, chosen,
+    qkv_ref, attended_ref, after_ref, expanded_ref, result_ref, pre_ref, value_ref, follow_ref,
+    qrk_hbm, ov_hbm, expand_hbm, contract_hbm,
+    grad_mt_ref, qkv_grad, out_grad, expand_grad, contract_grad, read_grad, key_grad, value_grad, sums_ref, exp_sums_ref,
+    qrk, ov, expand_w, contract_w, sem,
+):
+    copies = bring((qrk_hbm, ov_hbm, expand_hbm, contract_hbm), (qrk, ov, expand_w, contract_w), sem)
+    mt = mt_ref[...]
+    mem, width = mt.shape
+    feat = pre_ref.shape[1] // 2
+    sums_ref[...] = jnp.zeros_like(sums_ref)
+
+    def add_row(k, value):
+        sums_ref[k : k + 1, :] += value[None]
+
+    def column(value):
+        return jnp.sum(value.astype(F32), axis=0)
+
+    unit_f, rstd_f = norm_parts(follow_ref[...])
+    normed_f = (unit_f * one_gain[...] + one_bias[...]).astype(BF16)
+    grad_f = pooled[1].astype(BF16)
+    copies[0].wait()
+    grad_follow, gain, bias = norm_back(
+        dot_dims(grad_f, qrk[:, width : 3 * width], 1, 1), unit_f, rstd_f, one_gain[...]
+    )
+    add_row(0, gain)
+    add_row(1, bias)
+    add_row(3, column(grad_f[:, width:]))
+    read_pre, key_pre, value_new = pre_ref[:, :feat], pre_ref[:, feat:], value_ref[...]
+    read_feat, key_feat = feature_parts(read_pre)[2], feature_parts(key_pre)[2]
+    mix, numer, denom = read_parts(read_feat, key_feat, value_new)
+    grad_numer = grad_follow / denom
+    grad_denom = -jnp.sum(grad_follow * numer, axis=1, keepdims=True) / (denom * denom)
+    grad_mix = exact(grad_numer, value_new, 1, 1) + grad_denom
+    grad_value = exact(mix, grad_numer, 0, 0)
+    grad_read_pre = feature_back(read_pre, exact(grad_mix, key_feat, 1, 0))
+    grad_key_pre = feature_back(key_pre, exact(grad_mix, read_feat, 0, 0))
+    grad_mt = grad_follow + exact_low(grad_read_pre, qrk[:, 3 * width : 3 * width + feat], 1)
+    copies[1].wait()
+    grad_result = exact_low(grad_key_pre, qrk[:, 3 * width + feat :], 1) + exact_low(
+        grad_value, ov[:, width:], 1
+    )
+    grad_contract = grad_result.astype(BF16)
+    add_row(7, column(grad_contract))
+    expanded = expanded_ref[...]
+    bend, cube = 0.7978845608028654, 0.044715
+    square = expanded * expanded
+    curve = jnp.tanh(bend * expanded * (1.0 + cube * square))
+    half = 0.5 * (1.0 + curve)
+    activ = (expanded * half).astype(BF16)
+    slope = half + 0.5 * bend * expanded * (1.0 - curve * curve) * (1.0 + 3.0 * cube * square)
+    copies[3].wait()
+    grad_expanded = (dot_dims(grad_contract, contract_w[...], 1, 0) * slope).astype(BF16)
+    exp_sums_ref[...] = column(grad_expanded)[None]
+    unit_b, rstd_b = norm_parts(after_ref[...])
+    normed_b = (unit_b * two_gain[...] + two_bias[...]).astype(BF16)
+    copies[2].wait()
+    grad_after, gain, bias = norm_back(
+        dot_dims(grad_expanded, expand_w[...], 1, 1), unit_b, rstd_b, two_gain[...]
+    )
+    add_row(5, gain)
+    add_row(6, bias)
+    grad_after = grad_after + grad_result
+    grad_attn_out = grad_after.astype(BF16)
+    add_row(4, column(grad_attn_out))
+    grad_attended = dot_dims(grad_attn_out, ov[:, :width], 1, 1).astype(BF16)
+    query, key, value = (qkv_ref[:, k * width : (k + 1) * width] for k in range(3))
+    tall, weights = mem_weights(query, key)
+    grad_tall = per_head(grad_attended)
+    grad_weights = dot_dims(grad_tall, value, 1, 1)
+    centre = jnp.sum(weights * grad_weights, axis=1, keepdims=True)
+    grad_s = (weights * (grad_weights - centre) * HD**-0.5).astype(BF16)
+    grad_qkv = jnp.concatenate(
+        [
+            from_heads(dot_dims(grad_s, key, 1, 0), mem),
+            dot_dims(grad_s, tall, 0, 0) + pooled[0, :, :width],
+            dot_dims(weights.astype(BF16), grad_tall, 0, 0) + pooled[0, :, width:],
+        ],
+        axis=1,
+    ).astype(BF16)
+    add_row(2, column(grad_qkv[:, :width]))
+    add_row(3, column(grad_qkv[:, 2 * width :]))
+    unit, rstd = norm_parts(mt)
+    normed = (unit * one_gain[...] + one_bias[...]).astype(BF16)
+    grad_first, gain, bias = norm_back(
+        dot_dims(grad_qkv, qrk[:, : 3 * width], 1, 1), unit, rstd, one_gain[...]
+    )
+    add_row(0, gain)
+    add_row(1, bias)
+    grad_mt_ref[...] = grad_mt + grad_first + grad_after
+
+    pick_low = lambda a: dot_dims(a, chosen[...], 1, 0).astype(BF16)
+    pick_exact = lambda a: exact_low(a, chosen[...], 0)
+    qkv_grad[...] = dot_dims(pick_low(normed), grad_qkv, 0, 0)
+    qkv_grad[:, width:] += dot_dims(pick_low(normed_f), grad_f, 0, 0)
+    out_grad[...] = dot_dims(pick_low(attended_ref[...]), grad_attn_out, 0, 0)
+    expand_grad[...] = dot_dims(pick_low(normed_b), grad_expanded, 0, 0)
+    contract_grad[...] = dot_dims(pick_low(grad_contract), activ, 0, 0)
+    my_result = pick_exact(result_ref[...])
+    read_grad[...] = exact(pick_exact(mt), grad_read_pre, 0, 0)
+    key_grad[...] = exact(my_result, grad_key_pre, 0, 0)
+    value_grad[...] = exact(my_result, grad_value, 0, 0)
+
+
+def mem_backward(mt, norms, pooled, shard, group, kept, weights):
+    mem, width = mt.shape
+    wide, feat = weights[2].shape[1], (weights[0].shape[1] - 3 * width) // 2
+    at = lax.broadcasted_iota(jnp.int32, (width, shard), 0) - group * shard
+    chosen = (at == lax.broadcasted_iota(jnp.int32, (width, shard), 1)).astype(BF16)
+    sizes = (3 * width, width, wide, wide, feat, feat, width)
+    shape = jax.ShapeDtypeStruct
+    outs = [
+        shape((mem, width), F32), *[shape((shard, c), F32) for c in sizes], shape((8, width), F32), shape((1, wide), F32),
+    ]
+    grad_mt, *rest = mem_call(
+        mem_bwd_kernel, "mem_bwd", (mt, *norms, pooled, chosen, *kept), weights, outs, 25
+    )
+    sums, expand_sums = rest[7:]
+    vectors = (sums[0], sums[1], sums[2:4], sums[4], sums[5], sums[6], expand_sums[0], sums[7])
+    return grad_mt, tuple(rest[:7]), vectors
+
+
 def gather_kernel(halved, count, kinds, *refs):
     shards, outs = refs[:count], refs[count : 2 * count]
     send_sem, recv_sem, local_sem = refs[2 * count :]
@@ -719,10 +990,10 @@
     return qkv[:, width:], kv_follow, keep
 
 
-def memory_backward(mt, p, m, grad_kv_first, grad_kv_follow, mine, turn):
+def memory_backward(mt, p, m, grad_kv_first, grad_kv_follow, mine):
     width = mt.shape[1]
     low = lambda a: a.astype(BF16)
-    grad_f = low(turn(0, grad_kv_follow))
+    grad_f = low(grad_kv_follow)
     grad_follow, gain_f, bias_f = norm_back(
         dot_dims(grad_f, p["qkv"][:, width:], 1, 1), m["unit_f"], m["rstd_f"], p["one_gain"]
     )
@@ -737,7 +1008,6 @@
     grad_result = exact(grad_key_pre, p["key"].astype(F32), 1, 1) + exact(
         grad_value, p["value"].astype(F32), 1, 1
     )
-    grad_result = turn(1, grad_result)
     grad_contract = low(grad_result)
     _, gelu_pull = jax.vjp(gelu_tanh, m["expanded"])
     grad_expanded = low(gelu_pull(dot_dims(grad_contract, p["contract"], 1, 0))[0])
@@ -750,7 +1020,7 @@
     dq, dkv = plain_bwd(
         m["qkv"][None], m["qkv"][None, :, width:], m["allowed"], m["log_total"], grad_attended[None]
     )
-    grad_qkv = low(turn(2, jnp.concatenate([dq[0], dkv[0] + grad_kv_first], axis=1)))
+    grad_qkv = low(jnp.concatenate([dq[0], dkv[0] + grad_kv_first], axis=1))
     grad_first, gain_a, bias_a = norm_back(
         dot_dims(grad_qkv, p["qkv"], 1, 1), m["unit"], m["rstd"], p["one_gain"]
     )
@@ -886,7 +1156,14 @@
         segs = micros * segs_local
         seg_rows = tok_rows
 
-    kv_first, kv_follow, m = memory_forward(memory_tokens, p)
+    if quick:
+        norms = tuple(v[None] for v in (norm_one_gain, norm_one_bias, norm_two_gain, norm_two_bias))
+        fixed = tuple(v[None] for v in (p["shift"], out_bias, expand_bias, contract_bias))
+        mem_weights_in = (qkv_read_key, out_value, expand_full, contract_full)
+        *kept, kv_follow = mem_forward(memory_tokens, (*norms, *fixed), mem_weights_in)
+        kv_first = kept[0][:, width:]
+    else:
+        kv_first, kv_follow, m = memory_forward(memory_tokens, p)
     kv_mem = jnp.where((flags == 0)[:, None, None], kv_follow[None], kv_first[None])
     if quick:
         rows_in, normed_a, qkv = enter(
@@ -954,9 +1231,9 @@
         on_expand = Scatter(term_expand)
         on_contract.over_core(term_expand)
         grad_attn_out = behind(grad_attn_out, on_contract.give, on_expand.give)
-        on_out = Scatter(dot_dims(attended, grad_attn_out, 0, 0).astype(BF16))
+        term_out = dot_dims(attended, grad_attn_out, 0, 0).astype(BF16)
         dk_mem, dv_mem, middle_sums = attn_mem(
-            qkv, kv_mem, attended, behind(grad_attended, on_out.give), lse
+            qkv, kv_mem, attended, behind(grad_attended, term_out), lse
         )
         on_expand.over_core(middle_sums)
         pooled = pool(jnp.concatenate([dk_mem, dv_mem], axis=2))
@@ -970,26 +1247,24 @@
         term = lambda grads: sum(dot_dims(normed[k], grads[k], 0, 0) for k in range(2)).astype(BF16)
         turn_a = back(0, 0, most, pooled, others, on_expand.give)
         pooled = sum_over(pooled, 0, turn_a)
-        on_out.over_core(turn_a)
         on_contract.over_x(turn_a)
-        turn_b = back(1, 0, most, turn_a, pooled, on_contract.give, on_out.give)
+        turn_b = back(1, 0, most, turn_a, pooled, on_contract.give)
         pooled = sum_over(pooled, 1, turn_b)
         others = behind([swapped(other) for other in others], turn_b)
         block_halves = [(own, other) for (own, _), other in zip(block_halves, others)]
         on_expand.over_x(turn_b)
         on_contract.over_z(turn_b)
         most_grads = [turn_a, turn_b]
-        on_most = Scatter(term(most_grads))
+        on_most = Scatter(jnp.concatenate([term(most_grads), term_out], axis=1))
         turn_c = back(
             0, most, pairs - most, on_most.give, on_expand.give, on_contract.give, pooled
         )
         pooled = sum_over(pooled, 2, turn_c)
         on_most.over_core(turn_c)
-        on_out.over_x(turn_c)
         got_contract = on_contract.over_y(turn_c)
         first_end = input_back(
             spans[0],
-            [behind(most_grads[0], on_most.give, on_out.give, pooled), turn_c],
+            [behind(most_grads[0], on_most.give, pooled), turn_c],
             weights,
         )
         kept_first, given_first = own_and_other(first_end[0])
@@ -998,10 +1273,12 @@
         on_expand.over_z(turn_d)
         on_most.over_x(turn_d)
         got_first = behind(swapped(given_first), turn_d)
-        rest_grads = [turn_c, behind(turn_d, on_expand.give, on_most.give)]
-        second_end = input_back(spans[1], [most_grads[1], rest_grads[1]], weights)
+        rest_grads = [turn_c, turn_d]
+        on_rest = Scatter(term(rest_grads))
+        last = behind(turn_d, on_expand.give, on_most.give, on_rest.give, pooled)
+        second_end = input_back(spans[1], [most_grads[1], last], weights)
+        on_rest.over_core(second_end[0])
         kept_second, given_second = own_and_other(second_end[0])
-        on_rest = Scatter(term(rest_grads))
         one_gain, one_bias = first_end[1] + second_end[1], first_end[2] + second_end[2]
         qkv_sums = [
             sum(jnp.sum(g[k].astype(F32), axis=0) for k in range(2)).reshape(3, -1)
@@ -1045,25 +1322,15 @@
     got = {}
 
     def turn(step, value):
-        if not quick:
-            return value
         if step == 0:
             return behind(value, flat, on_rest.give, on_most.give, given_second)
-        if step == 1:
-            got["second"] = behind(swapped(given_second), value)
-            on_rest.over_core(value)
-            on_most.over_z(value)
-            on_out.over_z(value)
-            got["flat"] = sum_over(flat, 0, value)
-            return behind(value, on_rest.give, on_most.give, on_out.give, got["flat"])
-        if step == 2:
-            on_rest.over_x(value)
-            got["most"], got["out"], got["expand"] = (
-                on_most.over_y(value), on_out.over_y(value), on_expand.over_y(value)
-            )
-            got["flat"] = sum_over(sum_over(got["flat"], 1), 2, value)
-            return behind(value, on_rest.give, got["flat"], got["most"], got["out"], got["expand"])
-        return value
+        got["second"] = behind(swapped(given_second), value)
+        on_rest.over_x(value)
+        on_most.over_z(value)
+        got["flat"] = sum_over(flat, 0, value)
+        got["expand"] = on_expand.over_y(value)
+        got["flat"] = sum_over(sum_over(got["flat"], 1), 2)
+        got["most"] = on_most.over_y()
 
     if not quick:
         summed = tuple(
@@ -1074,16 +1341,23 @@
         )
         pooled, vectors = lax.psum((pooled, vectors), ("dp", "ctx"))
 
-    mine = lambda a: lax.dynamic_slice_in_dim(a, group * shard, shard, 1)
-    grad_mt, mem_matrices, mem_vectors = memory_backward(
-        memory_tokens, p, m, pooled[0], pooled[1], mine, turn
-    )
     if quick:
-        most_part = got["most"].reshape(shard, 3, cut)
+        pooled = turn(0, pooled)
+        grad_mt, mem_matrices, mem_vectors = mem_backward(
+            memory_tokens, norms, pooled, shard, group, kept, mem_weights_in
+        )
+        turn(1, grad_mt)
+    else:
+        mine = lambda a: lax.dynamic_slice_in_dim(a, group * shard, shard, 1)
+        grad_mt, mem_matrices, mem_vectors = memory_backward(
+            memory_tokens, p, m, pooled[0], pooled[1], mine
+        )
+    if quick:
+        most_part = got["most"][:, : 3 * cut].reshape(shard, 3, cut)
         rest_part = on_rest.over_z().over_y().reshape(shard, 3, width - cut)
         summed = (
             jnp.concatenate([most_part, rest_part], axis=2).reshape(shard, 3 * width),
-            got["out"],
+            got["most"][:, 3 * cut :],
             got["expand"],
             got_contract,
         )

time: 597 us -> 556 us (0.931)
  matrix products: 102 us -> 48.1 us
  Pallas kernels: 284 us -> 305 us
  waiting for transfers between devices: 31.7 us -> 22.7 us
  starting transfers between devices: 59.7 us -> 50.9 us
  local copies, waits for them, and re-layouts: 60.5 us -> 67.5 us
    dot_general x41 -> x11, matrix products: 96.1 us -> 48.1 us  [dot_dims(): lax.dot_general(a, b, (((ca,), (cb,)), ((), ())), precision=precision, pr...]
    pallas_call x0 -> x2, Pallas kernels: none -> 21.5 us  [mem_call(): pl.pallas_call(kernel, in_specs=[vmem] * len(given) + [pl.BlockSpec(memor...]
    unnamed x401 -> x295, local copies, waits for them, and re-layouts: 21.3 us -> 31.9 us
    ppermute x5 -> x4, waiting for transfers between devices: 14.5 us -> 4.96 us  [over_y(): got = behind(lax.ppermute(self.give, 'ctx', [(0, 1), (1, 0)]), *beside)]
    ppermute x6, waiting for transfers between devices: 0.02 us -> 8.71 us  [swapped(): return lax.ppermute(given, 'ctx', swap)]
    ppermute x15 -> x12, starting transfers between devices: 27.2 us -> 19.4 us  [over_z(): lax.ppermute(self.give[k - 1], 'dp', dp_pairs(4 * k))]
    dot_general x6 -> x0, matrix products: 6.06 us -> none  [the longest x1 1.88 us: plain_bwd(): jnp.einsum('shqk,sqhd->skhd', grad_s, query, preferred_element_type=F32)]
    convert_element_type x10 -> x8, other arithmetic: 8.42 us -> 12.6 us  [add_low(): return (a.astype(F32) + b.astype(F32)).astype(BF16)]
  transfers between devices with their start and end apart: 48 -> 42, of which waited for: 8 -> 10; matrix products, arithmetic and copies ran while one was open for 28% -> 20% of each run, Pallas kernels for 36% -> 43%
where the time goes in v3:
time: 556 us; the launch traced here: 545 us
  Pallas kernels  305 us (55%)
  local copies, waits for them, and re-layouts  67.5 us (12%)
  starting transfers between devices  50.9 us (9%)
  matrix products  48.1 us (9%)
  other arithmetic  46.9 us (8%)
  waiting for transfers between devices  22.7 us (4%)
    pallas_call x1, Pallas kernels, gather_weights(): pl.pallas_call(functools.partial(gather_kernel, halved, count, kinds), in...  80.3 us
    pallas_call x1, Pallas kernels, middle(): pl.pallas_call(middle_kernel, grid_spec=pltpu.PrefetchScalarGridSpec(num_...  68.8 us
    pallas_call x4, Pallas kernels, attn_bwd(): pl.pallas_call(attn_bwd_kernel, grid=(count, 3), in_specs=[spec(0), spec(...  65.3 us
    dot_general x11, matrix products, dot_dims(): lax.dot_general(a, b, (((ca,), (cb,)), ((), ())), precision=precision, pr...  48.1 us
    pallas_call x2, Pallas kernels, attn_fwd(): pl.pallas_call(attn_fwd_kernel if held is None else attn_fwd_after_kernel...  45.3 us
    unnamed x295, local copies, waits for them, and re-layouts  31.9 us
    pallas_call x2, Pallas kernels, mem_call(): pl.pallas_call(kernel, in_specs=[vmem] * len(given) + [pl.BlockSpec(memor...  21.5 us
    ppermute x12, starting transfers between devices, over_z(): lax.ppermute(self.give[k - 1], 'dp', dp_pairs(4 * k))  19.4 us
  transfers between devices with their start and end apart: 42, of which 10 were waited for; matrix products, arithmetic and copies ran while one was open for 20% of the time, Pallas kernels for 43%

profile of v3, /device:TPU:0, one launch (start us, length us, event | category | flops | bytes accessed | tf_op | source)
XLA Modules:
  0.0 545.3 jit_solution(10072972364526653174)
XLA Ops:
  0.8 3.4 dynamic-slice_bitcast_fusion.1
  4.2 3.0 collective-permute-start
  8.8 3.8 dynamic-slice_bitcast_fusion
  12.8 80.3 %gather_weights.1 = (bf16[768,3072]{1,0:T(8,128)(2,1)S(1)}, bf16[768,3072]{1,0:T(8,128)(2,1)S(1)}, bf16[768,3072]{1,0:T(8,128)(2,1)S(1)}, bf16[768,1536]{1,0:T(8,128)(2,1)S(1)}) custom-call(bf16[48,3072]{1,0:T(8,128)(2,1)S(1)} %pad_maximum_fusion.10.refs_0_, bf16[48,3072]{1,0:T(8,128)(2,1)S(1)} %copy-done.25, bf16[48,3072]{1,0:T(8,128)(2,1)S(1)} %copy-done.26, ...), custom_call_target="tpu_custom_call" | custom-call | flops 80000000000 | bytes 33030144 | tf_op jit(solution)/shard_map/gather_weights/pallas_call | solution.py:838
  93.1 2.1 copy-done.2
  95.3 2.1 copy-done.37
  97.4 2.1 copy-done.38
  100.7 8.6 %mem_fwd.1 = (bf16[16,2304]{1,0:T(8,128)(2,1)S(1)}, bf16[16,768]{1,0:T(8,128)(2,1)S(1)}, f32[16,768]{1,0:T(8,128)S(1)}, f32[16,3072]{1,0:T(8,128)S(1)}, f32[16,7...) custom-call(f32[16,768]{1,0:T(8,128)S(1)} %copy-done.27, ...), custom_call_target="tpu_custom_call" | custom-call | flops 15000000512 | bytes 17000000 | tf_op jit(solution)/shard_map/mem_fwd/pallas_call | solution.py:528
  115.3 2.3 fusion.69
  117.6 3.2 fusion.70
  123.1 14.1 %enter.1 = (bf16[2048,768]{1,0:T(8,128)(2,1)}, bf16[2048,768]{1,0:T(8,128)(2,1)}, bf16[2048,2304]{1,0:T(8,128)(2,1)}) custom-call(s32[2]{0:T(128)S(1)} %pad_add_fusion.told, bf16[2,512,768]{2,1,0:T(8,128)(2,1)S(1)} %get-tuple-element.266.kept, bf16[2,512,768]{2,1,0:T(8,128)(2,1)} %collective-permute-done.got, f32[1,768]{1,0:T(1,128)S(1)} %broadcast_in_dim.42.gain.one_gain, ...), custom_call_target="tpu_custom_call" | custom-call | flops 14495514624 | bytes 22020096 | tf_op jit(solution)/shard_map/enter/pallas_call | solution.py:303
  137.2 3.7 copy-done.31
  140.9 22.5 %attn_fwd.2 = (bf16[2048,768]{1,0:T(8,128)(2,1)S(1)}, f32[6,2,1024]{2,1,0:T(2,128)S(1)}) custom-call(bf16[2048,2304]{1,0:T(8,128)(2,1)S(1)} %copy-done.31, bf16[2048,2304]{1,0:T(8,128)(2,1)S(1)} %copy-done.31, bf16[2048,2304]{1,0:T(8,128)(2,1)S(1)} %copy-done.31, bf16[16,1536]{1,0:T(8,128)(2,1)S(1)} %slice.173.km_ref.vm_ref, ...), custom_call_target="tpu_custom_call" | custom-call | flops 25165824000 | bytes 6291456 | tf_op jit(solution)/shard_map/attn_fwd/pallas_call | solution.py:108
  163.4 22.8 %attn_fwd.3 = (bf16[2048,768]{1,0:T(8,128)(2,1)S(1)}, f32[6,2,1024]{2,1,0:T(2,128)S(1)}) custom-call(bf16[2048,2304]{1,0:T(8,128)(2,1)S(1)} %copy-done.31, bf16[2048,2304]{1,0:T(8,128)(2,1)S(1)} %copy-done.31, bf16[2048,2304]{1,0:T(8,128)(2,1)S(1)} %copy-done.31, ...), custom_call_target="tpu_custom_call", output_to_operand_aliasing={{0}: (5, {})} | custom-call | flops 25165824000 | bytes 6291456 | tf_op jit(solution)/shard_map/attn_fwd/pallas_call | solution.py:108
  189.6 68.8 %middle.1 = (bf16[2048,768]{1,0:T(8,128)(2,1)}, bf16[2048,768]{1,0:T(8,128)(2,1)}, bf16[2048,768]{1,0:T(8,128)(2,1)}, bf16[2048,3072]{1,0:T(8,128)(2,1)}, bf16[2...) custom-call(s32[2]{0:T(128)} %copy-done.30, ...), custom_call_target="tpu_custom_call" | custom-call | flops 86973087744 | bytes 47185920 | tf_op jit(solution)/shard_map/middle/pallas_call | solution.py:380
  258.4 14.0 %convolution_convert_fusion.1 = bf16[768,3072]{1,0:T(8,128)(2,1)S(1)} fusion(bf16[2048,768]{1,0:T(8,128)(2,1)} %get-tuple-element.137, bf16[2048,3072]{1,0:T(8,128)(2,1)} %get-tuple-element.138), kind=kOutput, calls=%fused_computation.3 | convolution fusion | flops 9666035712 | bytes 20447232 | tf_op jit(solution)/shard_map/dot_general | solution.py:43
  273.4 3.6 copy-done.142
  277.0 12.5 %convolution_convert_fusion = bf16[768,3072]{1,0:T(8,128)(2,1)S(1)} fusion(bf16[2048,768]{1,0:T(8,128)(2,1)} %get-tuple-element.139, bf16[2048,3072]{1,0:T(8,128)(2,1)S(1)} %copy-done.142), kind=kOutput, calls=%fused_computation.2 | convolution fusion | flops 9666035712 | bytes 20447232 | tf_op jit(solution)/shard_map/dot_general | solution.py:43
  289.5 1.9 constant_dynamic-slice_fusion.4
  300.6 2.7 convolution_convert_fusion.2
  304.8 1.9 copy-done.32
  306.6 1.9 copy-done.36
  308.5 10.0 %attn_mem.1 = (f32[2,16,768]{2,1,0:T(8,128)S(1)}, f32[2,16,768]{2,1,0:T(8,128)S(1)}, f32[12,2,1024]{2,1,0:T(2,128)S(1)}) custom-call(bf16[2048,2304]{1,0:T(8,128)(2,1)} %get-tuple-element.128.q_ref.k_ref.v_ref, bf16[2,16,1536]{2,1,0:T(8,128)(2,1)S(1)} %copy-done.8, bf16[2,16,1536]{2,1,0:T(8,128)(2,1)S(1)} %copy-done.8, bf16[2048,768]{1,0:T(8,128)(2,1)S(1)} %copy-done.36, ...), custom_call_target="tpu_custom_call" | custom-call | flops 6291456000 | bytes 9437184 | tf_op jit(solution)/shard_map/attn_mem/pallas_call | solution.py:161
  318.6 2.6 fusion
  325.8 21.4 %attn_bwd.4 = bf16[1024,1536]{1,0:T(8,128)(2,1)S(1)} custom-call(bf16[2048,2304]{1,0:T(8,128)(2,1)} %get-tuple-element.128.q_ref.k_ref.v_ref, bf16[2048,2304]{1,0:T(8,128)(2,1)} %get-tuple-element.128.q_ref.k_ref.v_ref, bf16[2048,2304]{1,0:T(8,128)(2,1)} %get-tuple-element.128.q_ref.k_ref.v_ref, bf16[16,1536]{1,0:T(8,128)(2,1)S(1)} %slice.173.km_ref.vm_ref, ...), custom_call_target="tpu_custom_call" | custom-call | flops 27262976000 | bytes 9437184 | tf_op jit(solution)/shard_map/attn_bwd/pallas_call | solution.py:244
  348.5 1.7 copy-done.60
  350.2 1.7 fusion.28
  354.5 22.1 %attn_bwd.5 = bf16[1024,1536]{1,0:T(8,128)(2,1)S(1)} custom-call(bf16[2048,2304]{1,0:T(8,128)(2,1)} %get-tuple-element.128.q_ref.k_ref.v_ref, bf16[2048,2304]{1,0:T(8,128)(2,1)} %get-tuple-element.128.q_ref.k_ref.v_ref, bf16[2048,2304]{1,0:T(8,128)(2,1)} %get-tuple-element.128.q_ref.k_ref.v_ref, bf16[16,1536]{1,0:T(8,128)(2,1)S(1)} %copy-done.12, ...), custom_call_target="tpu_custom_call" | custom-call | flops 27262976000 | bytes 9437184 | tf_op jit(solution)/shard_map/attn_bwd/pallas_call | solution.py:244
  376.6 2.6 collective-permute-start.11
  379.2 2.6 fusion.32
  381.9 2.9 add_convert_fusion
  384.7 2.1 pad_maximum_fusion
  387.4 2.3 constant_dynamic-slice_fusion.3
  391.4 1.8 fusion.27
  394.8 2.9 select_bitcast_fusion.7
  398.1 1.9 pad_maximum_fusion.1
  401.5 3.0 collective-permute-start.17
  405.8 1.6 collective-permute-start.15
  407.4 10.8 %attn_bwd.6 = bf16[1024,768]{1,0:T(8,128)(2,1)S(1)} custom-call(bf16[2048,2304]{1,0:T(8,128)(2,1)} %get-tuple-element.128.q_ref.k_ref.v_ref, bf16[2048,2304]{1,0:T(8,128)(2,1)} %get-tuple-element.128.q_ref.k_ref.v_ref, bf16[2048,2304]{1,0:T(8,128)(2,1)} %get-tuple-element.128.q_ref.k_ref.v_ref, bf16[16,1536]{1,0:T(8,128)(2,1)S(1)} %copy-done.10, ...), custom_call_target="tpu_custom_call" | custom-call | flops 13631488000 | bytes 4718592 | tf_op jit(solution)/shard_map/attn_bwd/pallas_call | solution.py:244
  420.8 2.9 collective-permute-start.22
  423.8 2.0 fusion.12
  427.2 2.6 fusion.37
  429.9 3.1 fusion.18
  435.5 11.0 %attn_bwd.7 = bf16[1024,768]{1,0:T(8,128)(2,1)S(1)} custom-call(bf16[2048,2304]{1,0:T(8,128)(2,1)} %get-tuple-element.128.q_ref.k_ref.v_ref, bf16[2048,2304]{1,0:T(8,128)(2,1)} %get-tuple-element.128.q_ref.k_ref.v_ref, bf16[2048,2304]{1,0:T(8,128)(2,1)} %get-tuple-element.128.q_ref.k_ref.v_ref, bf16[16,1536]{1,0:T(8,128)(2,1)S(1)} %copy-done.12, ...), custom_call_target="tpu_custom_call" | custom-call | flops 13631488000 | bytes 4718592 | tf_op jit(solution)/shard_map/attn_bwd/pallas_call | solution.py:244
  454.6 3.1 collective-permute-done.18
  458.4 2.1 fusion.41
  462.5 8.7 %collective-permute-done.25 = bf16[512,768]{1,0:T(8,128)(2,1)} collective-permute-done((bf16[512,768]{1,0:T(8,128)(2,1)}, bf16[512,768]{1,0:T(8,128)(2,1)}, u32[]{:S(2)}, u32[]{:S(2)}) %collective-permute-start.25) | collective-permute-done | bytes 786464 | tf_op jit(solution)/shard_map/ppermute | solution.py:1131
  471.2 1.6 fusion.29
  473.8 2.4 collective-permute-start.33
  478.8 3.4 fusion.25
  482.3 1.7 fusion.24
  484.2 1.9 fusion.36
  488.0 12.9 %mem_bwd.1 = (f32[16,768]{1,0:T(8,128)}, f32[48,2304]{1,0:T(8,128)S(1)}, f32[48,768]{1,0:T(8,128)S(1)}, f32[48,3072]{1,0:T(8,128)S(1)}, f32[48,3072]{1,0:T(8,128...) custom-call(f32[16,768]{1,0:T(8,128)S(1)} %copy-done.28, ...), custom_call_target="tpu_custom_call" | custom-call | flops 24999999488 | bytes 17000000 | tf_op jit(solution)/shard_map/mem_bwd/pallas_call | solution.py:528
  503.7 1.9 add_add_fusion
  506.2 2.4 collective-permute-start.30
  508.6 2.0 collective-permute-start.31
  510.7 1.9 collective-permute-start.34
  519.6 3.4 collective-permute-start.37
  523.4 2.0 collective-permute-start.39
  528.2 2.4 collective-permute-done.38
  530.7 1.8 collective-permute-start.40
  532.6 4.5 collective-permute-done.35
  539.7 2.9 select_bitcast_fusion.3
  542.9 1.9 pad_maximum_fusion.2
  (466 shorter events, 79.6 us)
Async XLA Ops:
  4.2 117.4 %collective-permute-start = (bf16[2,512,768]{2,1,0:T(8,128)(2,1)}, bf16[2,512,768]{2,1,0:T(8,128)(2,1)}, u32[]{:S(2)}, u32[]{:S(2)}) collective-permute-start(bf16[2,512,768]{2,1,0:T(8,128)(2,1)} %get-tuple-element.265), channel_id=1, source_target_pairs={{0,1},{1,0},{2,3},{3,2},{4,5},{5,4},{6,7},{7,6},{8,9},{9,8},{10,11... | collective-permute-start | bytes 4718600 | tf_op jit(solution)/shard_map/ppermute | solution.py:1131
  8.7 114.4 %copy-start.15 = (f32[1,768]{1,0:T(1,128)}, f32[1,768]{1,0:T(1,128)S(1)}, u32[]{:S(2)}) copy-start(f32[1,768]{1,0:T(1,128)S(1)} %broadcast_in_dim.42.gain.one_gain) | copy-start | bytes 9220
  8.8 114.4 %copy-start.17 = (f32[1,768]{1,0:T(1,128)}, f32[1,768]{1,0:T(1,128)S(1)}, u32[]{:S(2)}) copy-start(f32[1,768]{1,0:T(1,128)S(1)} %broadcast_in_dim.43.bias.one_bias) | copy-start | bytes 9220
  12.7 88.0 %copy-start.19 = (f32[1,768]{1,0:T(1,128)}, f32[1,768]{1,0:T(1,128)S(1)}, u32[]{:S(2)}) copy-start(f32[1,768]{1,0:T(1,128)S(1)} %broadcast_in_dim.47.two_gain.gain) | copy-start | bytes 9220
  12.7 87.9 %copy-start.21 = (f32[1,768]{1,0:T(1,128)}, f32[1,768]{1,0:T(1,128)S(1)}, u32[]{:S(2)}) copy-start(f32[1,768]{1,0:T(1,128)S(1)} %broadcast_in_dim.48.two_bias.bias) | copy-start | bytes 9220
  12.8 87.9 %copy-start.23 = (f32[1,768]{1,0:T(1,128)}, f32[1,768]{1,0:T(1,128)S(1)}, u32[]{:S(2)}) copy-start(f32[1,768]{1,0:T(1,128)S(1)} %broadcast_in_dim.80.out_b) | copy-start | bytes 9220
  12.8 87.9 %copy-start.24 = (f32[1,768]{1,0:T(1,128)}, f32[1,768]{1,0:T(1,128)S(1)}, u32[]{:S(2)}) copy-start(f32[1,768]{1,0:T(1,128)S(1)} %broadcast_in_dim.82.contract_b) | copy-start | bytes 9220
  113.1 212.7 %copy-start.9 = (bf16[16,1536]{1,0:T(8,128)(2,1)}, bf16[16,1536]{1,0:T(8,128)(2,1)S(1)}, u32[]{:S(2)}) copy-start(bf16[16,1536]{1,0:T(8,128)(2,1)S(1)} %slice.173.km_ref.vm_ref) | copy-start | bytes 147460
  121.5 41.8 %copy-start.11 = (bf16[16,1536]{1,0:T(8,128)(2,1)}, bf16[16,1536]{1,0:T(8,128)(2,1)S(1)}, u32[]{:S(2)}) copy-start(bf16[16,1536]{1,0:T(8,128)(2,1)S(1)} %slice_bitcast_fusion.km_ref.vm_ref) | copy-start | bytes 147460
  121.5 67.0 %collective-permute-start.1 = (bf16[2,512,768]{2,1,0:T(8,128)(2,1)S(1)}, bf16[2,512,768]{2,1,0:T(8,128)(2,1)S(1)}, u32[]{:S(2)}, u32[]{:S(2)}) collective-permute-start(bf16[2,512,768]{2,1,0:T(8,128)(2,1)S(1)} %copy-done.83), channel_id=1, source_target_pairs={{0,1},{1,0},{2,3},{3,2},{4,5},{5,4},{6,7},{7,6},{8,9},{9,8},{10,11... | collective-permute-start | bytes 4718600 | tf_op jit(solution)/shard_map/ppermute | solution.py:1131
  163.4 22.9 %copy-start.53 = (bf16[2048,768]{1,0:T(8,128)(2,1)S(1)}, bf16[2048,768]{1,0:T(8,128)(2,1)}, u32[]{:S(2)}) copy-start(bf16[2048,768]{1,0:T(8,128)(2,1)} %get-tuple-element.132.rows_ref) | copy-start | bytes 9437188
  186.6 71.8 %copy-start.118 = (f32[1024]{0:T(1024)}, f32[1024]{0:T(1024)S(1)}, u32[]{:S(2)}) copy-start(f32[1024]{0:T(1024)S(1)} %broadcast_multiply_fusion.4) | copy-start | bytes 12292
  273.1 22.6 %collective-permute-start.2 = (bf16[4,2,48,3072]{3,2,0,1:T(8,128)(2,1)S(1)}, bf16[4,2,48,3072]{3,2,0,1:T(8,128)(2,1)S(1)}, u32[]{:S(2)}, u32[]{:S(2)}) collective-permute-start(bf16[4,2,48,3072]{3,2,0,1:T(8,128)(2,1)S(1)} %bitcast.258), channel_id=1, source_target_pairs={{0,2},{2,0},{4,6},{6,4},{8,10},{10,8},{12,14},{14,12},{16,18},{18,... | collective-permute-start | bytes 7077896 | tf_op jit(solution)/shard_map/ppermute | solution.py:882
  293.0 25.6 %collective-permute-start.5 = (bf16[4,2,48,3072]{3,2,0,1:T(8,128)(2,1)}, bf16[4,2,48,3072]{3,2,0,1:T(8,128)(2,1)}, u32[]{:S(2)}, u32[]{:S(2)}) collective-permute-start(bf16[4,2,48,3072]{3,2,0,1:T(8,128)(2,1)} %bitcast.240), channel_id=1, source_target_pairs={{0,2},{2,0},{4,6},{6,4},{8,10},{10,8},{12,14},{14,12},{16,18},{18,... | collective-permute-start | bytes 7077896 | tf_op jit(solution)/shard_map/ppermute | solution.py:882
  298.5 50.0 %collective-permute-start.7 = (bf16[4,48,3072]{2,1,0:T(8,128)(2,1)}, bf16[4,48,3072]{2,1,0:T(8,128)(2,1)}, u32[]{:S(2)}, u32[]{:S(2)}) collective-permute-start(bf16[4,48,3072]{2,1,0:T(8,128)(2,1)} %dynamic-slice_bitcast_fusion.5), channel_id=1, source_target_pairs={{0,4},{2,6},{4,0},{6,2},{8,12},{10,14},{12,8},{14,10},{16,20},{18,... | collective-permute-start | bytes 3538952 | tf_op jit(solution)/shard_map/ppermute | solution.py:888
  318.6 35.9 %copy-start.39 = (f32[12,2,1024]{2,1,0:T(2,128)}, f32[12,2,1024]{2,1,0:T(2,128)S(1)}, u32[]{:S(2)}) copy-start(f32[12,2,1024]{2,1,0:T(2,128)S(1)} %get-tuple-element.147.mid_ref) | copy-start | bytes 294916
  322.6 25.2 %copy-start.79 = (f32[16,1536]{1,0:T(8,128)}, f32[16,1536]{1,0:T(8,128)S(1)}, u32[]{:S(2)}) copy-start(f32[16,1536]{1,0:T(8,128)S(1)} %get-tuple-element.225) | copy-start | bytes 294916
  322.7 25.2 %copy-start.81 = (f32[16,1536]{1,0:T(8,128)}, f32[16,1536]{1,0:T(8,128)S(1)}, u32[]{:S(2)}) copy-start(f32[16,1536]{1,0:T(8,128)S(1)} %get-tuple-element.226) | copy-start | bytes 294916
  322.7 25.1 %collective-permute-start.6 = (f32[2,16,1536]{2,1,0:T(8,128)S(1)}, f32[2,16,1536]{2,1,0:T(8,128)S(1)}, u32[]{:S(2)}, u32[]{:S(2)}) collective-permute-start(f32[2,16,1536]{2,1,0:T(8,128)S(1)} %pad_maximum_fusion.11), channel_id=1, source_target_pairs={{0,1},{1,0},{2,3},{3,2},{4,5},{5,4},{6,7},{7,6},{8,9},{9,8},{10,11... | collective-permute-start | bytes 589832 | tf_op jit(solution)/shard_map/ppermute | solution.py:909
  323.3 67.1 %collective-permute-start.9 = (bf16[4,48,3072]{2,1,0:T(8,128)(2,1)}, bf16[4,48,3072]{2,1,0:T(8,128)(2,1)}, u32[]{:S(2)}, u32[]{:S(2)}) collective-permute-start(bf16[4,48,3072]{2,1,0:T(8,128)(2,1)} %dynamic-slice_bitcast_fusion.4), channel_id=1, source_target_pairs={{0,4},{2,6},{4,0},{6,2},{8,12},{10,14},{12,8},{14,10},{16,20},{18,... | collective-permute-start | bytes 3538952 | tf_op jit(solution)/shard_map/ppermute | solution.py:888
  323.8 69.5 %collective-permute-start.3 = (bf16[512,768]{1,0:T(8,128)(2,1)}, bf16[512,768]{1,0:T(8,128)(2,1)}, u32[]{:S(2)}, u32[]{:S(2)}) collective-permute-start(bf16[512,768]{1,0:T(8,128)(2,1)} %get-tuple-element.148), channel_id=1, source_target_pairs={{0,1},{1,0},{2,3},{3,2},{4,5},{5,4},{6,7},{7,6},{8,9},{9,8},{10,11... | collective-permute-start | bytes 2359304 | tf_op jit(solution)/shard_map/ppermute | solution.py:1131
  325.3 69.5 %collective-permute-start.4 = (bf16[512,768]{1,0:T(8,128)(2,1)}, bf16[512,768]{1,0:T(8,128)(2,1)}, u32[]{:S(2)}, u32[]{:S(2)}) collective-permute-start(bf16[512,768]{1,0:T(8,128)(2,1)} %get-tuple-element.149), channel_id=1, source_target_pairs={{0,1},{1,0},{2,3},{3,2},{4,5},{5,4},{6,7},{7,6},{8,9},{9,8},{10,11... | collective-permute-start | bytes 2359304 | tf_op jit(solution)/shard_map/ppermute | solution.py:1131
  347.3 34.5 %copy-start = (bf16[1024,1536]{1,0:T(8,128)(2,1)}, bf16[1024,1536]{1,0:T(8,128)(2,1)S(1)}, u32[]{:S(2)}) copy-start(bf16[1024,1536]{1,0:T(8,128)(2,1)S(1)} %attn_bwd.4) | copy-start | bytes 9437188
  347.9 28.7 %collective-permute-start.13 = (f32[2,16,1536]{2,1,0:T(8,128)S(1)}, f32[2,16,1536]{2,1,0:T(8,128)S(1)}, u32[]{:S(2)}, u32[]{:S(2)}) collective-permute-start(f32[2,16,1536]{2,1,0:T(8,128)S(1)} %fusion.65), channel_id=1, source_target_pairs={{0,2},{2,0},{4,6},{6,4},{8,10},{10,8},{12,14},{14,12},{16,18},{18,... | collective-permute-start | bytes 589832 | tf_op jit(solution)/shard_map/ppermute | solution.py:911
  351.9 24.7 %copy-start.72 = (bf16[4,48,3072]{2,1,0:T(8,128)(2,1)}, bf16[4,48,3072]{2,1,0:T(8,128)(2,1)S(1)}, u32[]{:S(2)}) copy-start(bf16[4,48,3072]{2,1,0:T(8,128)(2,1)S(1)} %fusion.28) | copy-start | bytes 3538948
  352.9 48.1 %collective-permute-start.10 = (bf16[48,3072]{1,0:T(8,128)(2,1)}, bf16[48,3072]{1,0:T(8,128)(2,1)}, u32[]{:S(2)}, u32[]{:S(2)}) collective-permute-start(bf16[48,3072]{1,0:T(8,128)(2,1)} %get-tuple-element.274), channel_id=1, source_target_pairs={{0,8},{2,10},{4,12},{6,14},{8,0},{10,2},{12,4},{14,6},{16,24},{18,... | collective-permute-start | bytes 884744 | tf_op jit(solution)/shard_map/ppermute | solution.py:895
  354.5 24.7 %copy-start.87 = (bf16[2048,768]{1,0:T(8,128)(2,1)S(1)}, bf16[2048,768]{1,0:T(8,128)(2,1)}, u32[]{:S(2)}) copy-start(bf16[2048,768]{1,0:T(8,128)(2,1)} %get-tuple-element.159) | copy-start | bytes 9437188
  376.6 24.9 %collective-permute-start.11 = (bf16[48,3072]{1,0:T(8,128)(2,1)}, bf16[48,3072]{1,0:T(8,128)(2,1)}, u32[]{:S(2)}, u32[]{:S(2)}) collective-permute-start(bf16[48,3072]{1,0:T(8,128)(2,1)} %get-tuple-element.273), channel_id=1, source_target_pairs={{0,16},{2,18},{4,20},{6,22},{8,24},{10,26},{12,28},{14,30},{16,0},... | collective-permute-start | bytes 884744 | tf_op jit(solution)/shard_map/ppermute | solution.py:895
  390.4 14.1 %collective-permute-start.12 = (bf16[48,3072]{1,0:T(8,128)(2,1)S(1)}, bf16[48,3072]{1,0:T(8,128)(2,1)S(1)}, u32[]{:S(2)}, u32[]{:S(2)}) collective-permute-start(bf16[48,3072]{1,0:T(8,128)(2,1)S(1)} %copy-done.107), channel_id=1, source_target_pairs={{0,24},{2,26},{4,28},{6,30},{8,16},{10,18},{12,20},{14,22},{16,8},... | collective-permute-start | bytes 884744 | tf_op jit(solution)/shard_map/ppermute | solution.py:895
  393.3 25.0 %collective-permute-start.14 = (f32[2,16,1536]{2,1,0:T(8,128)S(1)}, f32[2,16,1536]{2,1,0:T(8,128)S(1)}, u32[]{:S(2)}, u32[]{:S(2)}) collective-permute-start(f32[2,16,1536]{2,1,0:T(8,128)S(1)} %fusion.89), channel_id=1, source_target_pairs={{0,4},{2,6},{4,0},{6,2},{8,12},{10,14},{12,8},{14,10},{16,20},{18,... | collective-permute-start | bytes 589832 | tf_op jit(solution)/shard_map/ppermute | solution.py:911
  394.8 26.0 %collective-permute-start.8 = (bf16[4,2,48,2304]{3,2,0,1:T(8,128)(2,1)S(1)}, bf16[4,2,48,2304]{3,2,0,1:T(8,128)(2,1)}, u32[]{:S(2)}, u32[]{:S(2)}) collective-permute-start(bf16[4,2,48,2304]{3,2,0,1:T(8,128)(2,1)S(1)} %bitcast.260), channel_id=1, source_target_pairs={{0,2},{2,0},{4,6},{6,4},{8,10},{10,8},{12,14},{14,12},{16,18},{18,... | collective-permute-start | bytes 5308424 | tf_op jit(solution)/shard_map/ppermute | solution.py:882
  401.0 53.6 %collective-permute-start.16 = (bf16[48,3072]{1,0:T(8,128)(2,1)}, bf16[48,3072]{1,0:T(8,128)(2,1)}, u32[]{:S(2)}, u32[]{:S(2)}) collective-permute-start(bf16[48,3072]{1,0:T(8,128)(2,1)} %get-tuple-element.271), channel_id=1, source_target_pairs={{0,8},{2,10},{4,12},{6,14},{8,0},{10,2},{12,4},{14,6},{16,24},{18,... | collective-permute-start | bytes 884744 | tf_op jit(solution)/shard_map/ppermute | solution.py:895
  401.5 53.0 %collective-permute-start.17 = (bf16[48,3072]{1,0:T(8,128)(2,1)}, bf16[48,3072]{1,0:T(8,128)(2,1)}, u32[]{:S(2)}, u32[]{:S(2)}) collective-permute-start(bf16[48,3072]{1,0:T(8,128)(2,1)} %get-tuple-element.270), channel_id=1, source_target_pairs={{0,16},{2,18},{4,20},{6,22},{8,24},{10,26},{12,28},{14,30},{16,0},... | collective-permute-start | bytes 884744 | tf_op jit(solution)/shard_map/ppermute | solution.py:895
  405.8 13.8 %collective-permute-start.15 = (bf16[48,3072]{1,0:T(8,128)(2,1)S(1)}, bf16[48,3072]{1,0:T(8,128)(2,1)S(1)}, u32[]{:S(2)}, u32[]{:S(2)}) collective-permute-start(bf16[48,3072]{1,0:T(8,128)(2,1)S(1)} %fusion.44), channel_id=1, source_target_pairs={{0,1},{1,0},{2,3},{3,2},{4,5},{5,4},{6,7},{7,6},{8,9},{9,8},{10,11... | collective-permute-start | bytes 884744 | tf_op jit(solution)/shard_map/ppermute | solution.py:903
  419.0 29.0 %collective-permute-start.20 = (f32[2,16,1536]{2,1,0:T(8,128)}, f32[2,16,1536]{2,1,0:T(8,128)}, u32[]{:S(2)}, u32[]{:S(2)}) collective-permute-start(f32[2,16,1536]{2,1,0:T(8,128)} %add.326), channel_id=1, source_target_pairs={{0,8},{2,10},{4,12},{6,14},{8,0},{10,2},{12,4},{14,6},{16,24},{18,... | collective-permute-start | bytes 589832 | tf_op jit(solution)/shard_map/ppermute | solution.py:912
  419.6 29.3 %collective-permute-start.21 = (f32[2,16,1536]{2,1,0:T(8,128)}, f32[2,16,1536]{2,1,0:T(8,128)}, u32[]{:S(2)}, u32[]{:S(2)}) collective-permute-start(f32[2,16,1536]{2,1,0:T(8,128)} %add.326), channel_id=1, source_target_pairs={{0,16},{2,18},{4,20},{6,22},{8,24},{10,26},{12,28},{14,30},{16,0},... | collective-permute-start | bytes 589832 | tf_op jit(solution)/shard_map/ppermute | solution.py:912
  420.8 29.6 %collective-permute-start.22 = (f32[2,16,1536]{2,1,0:T(8,128)}, f32[2,16,1536]{2,1,0:T(8,128)}, u32[]{:S(2)}, u32[]{:S(2)}) collective-permute-start(f32[2,16,1536]{2,1,0:T(8,128)} %add.326), channel_id=1, source_target_pairs={{0,24},{2,26},{4,28},{6,30},{8,16},{10,18},{12,20},{14,22},{16,8},... | collective-permute-start | bytes 589832 | tf_op jit(solution)/shard_map/ppermute | solution.py:912
  448.0 9.7 %collective-permute-start.18 = (bf16[48,3072]{1,0:T(8,128)(2,1)S(1)}, bf16[48,3072]{1,0:T(8,128)(2,1)S(1)}, u32[]{:S(2)}, u32[]{:S(2)}) collective-permute-start(bf16[48,3072]{1,0:T(8,128)(2,1)S(1)} %copy-done.106), channel_id=1, source_target_pairs={{0,24},{2,26},{4,28},{6,30},{8,16},{10,18},{12,20},{14,22},{16,8},... | collective-permute-start | bytes 884744 | tf_op jit(solution)/shard_map/ppermute | solution.py:895
  449.0 22.3 %collective-permute-start.19 = (bf16[4,48,2304]{2,1,0:T(8,128)(2,1)}, bf16[4,48,2304]{2,1,0:T(8,128)(2,1)}, u32[]{:S(2)}, u32[]{:S(2)}) collective-permute-start(bf16[4,48,2304]{2,1,0:T(8,128)(2,1)} %dynamic-slice_bitcast_fusion.6), channel_id=1, source_target_pairs={{0,4},{2,6},{4,0},{6,2},{8,12},{10,14},{12,8},{14,10},{16,20},{18,... | collective-permute-start | bytes 2654216 | tf_op jit(solution)/shard_map/ppermute | solution.py:888
  450.5 20.8 %collective-permute-start.25 = (bf16[512,768]{1,0:T(8,128)(2,1)}, bf16[512,768]{1,0:T(8,128)(2,1)}, u32[]{:S(2)}, u32[]{:S(2)}) collective-permute-start(bf16[512,768]{1,0:T(8,128)(2,1)} %dynamic-slice_bitcast_fusion.8), channel_id=1, source_target_pairs={{0,1},{1,0},{2,3},{3,2},{4,5},{5,4},{6,7},{7,6},{8,9},{9,8},{10,11... | collective-permute-start | bytes 2359304 | tf_op jit(solution)/shard_map/ppermute | solution.py:1131
  458.4 25.8 %collective-permute-start.24 = (bf16[4,2,48,768]{3,2,0,1:T(8,128)(2,1)}, bf16[4,2,48,768]{3,2,0,1:T(8,128)(2,1)}, u32[]{:S(2)}, u32[]{:S(2)}) collective-permute-start(bf16[4,2,48,768]{3,2,0,1:T(8,128)(2,1)} %bitcast.243), channel_id=1, source_target_pairs={{0,2},{2,0},{4,6},{6,4},{8,10},{10,8},{12,14},{14,12},{16,18},{18,... | collective-permute-start | bytes 1769480 | tf_op jit(solution)/shard_map/ppermute | solution.py:882
  460.6 41.4 %collective-permute-start.41 = (bf16[48,3072]{1,0:T(8,128)(2,1)}, bf16[48,3072]{1,0:T(8,128)(2,1)}, u32[]{:S(2)}, u32[]{:S(2)}) collective-permute-start(bf16[48,3072]{1,0:T(8,128)(2,1)} %fusion.41), channel_id=1, source_target_pairs={{0,1},{1,0},{2,3},{3,2},{4,5},{5,4},{6,7},{7,6},{8,9},{9,8},{10,11... | collective-permute-start | bytes 884744 | tf_op jit(solution)/shard_map/ppermute | solution.py:903
  461.1 15.1 %copy-start.4 = (bf16[1024,768]{1,0:T(8,128)(2,1)S(1)}, bf16[1024,768]{1,0:T(8,128)(2,1)}, u32[]{:S(2)}) copy-start(bf16[1024,768]{1,0:T(8,128)(2,1)} %copy-done.3) | copy-start | bytes 4718596
  461.1 15.1 %copy-start.99 = (bf16[768,256]{1,0:T(8,128)(2,1)S(1)}, bf16[768,256]{1,0:T(8,128)(2,1)}, u32[]{:S(2)}) copy-start(bf16[768,256]{1,0:T(8,128)(2,1)} %get-tuple-element.245) | copy-start | bytes 1179652
  461.1 15.1 %copy-start.101 = (bf16[768,256]{1,0:T(8,128)(2,1)S(1)}, bf16[768,256]{1,0:T(8,128)(2,1)}, u32[]{:S(2)}) copy-start(bf16[768,256]{1,0:T(8,128)(2,1)} %get-tuple-element.246) | copy-start | bytes 1179652
  461.1 15.1 %copy-start.103 = (bf16[768,256]{1,0:T(8,128)(2,1)S(1)}, bf16[768,256]{1,0:T(8,128)(2,1)}, u32[]{:S(2)}) copy-start(bf16[768,256]{1,0:T(8,128)(2,1)} %get-tuple-element.247) | copy-start | bytes 1179652
  473.8 44.5 %collective-permute-start.32 = (bf16[48,2304]{1,0:T(8,128)(2,1)}, bf16[48,2304]{1,0:T(8,128)(2,1)}, u32[]{:S(2)}, u32[]{:S(2)}) collective-permute-start(bf16[48,2304]{1,0:T(8,128)(2,1)} %get-tuple-element.277), channel_id=1, source_target_pairs={{0,8},{2,10},{4,12},{6,14},{8,0},{10,2},{12,4},{14,6},{16,24},{18,... | collective-permute-start | bytes 663560 | tf_op jit(solution)/shard_map/ppermute | solution.py:895
  473.8 44.5 %collective-permute-start.33 = (bf16[48,2304]{1,0:T(8,128)(2,1)}, bf16[48,2304]{1,0:T(8,128)(2,1)}, u32[]{:S(2)}, u32[]{:S(2)}) collective-permute-start(bf16[48,2304]{1,0:T(8,128)(2,1)} %get-tuple-element.276), channel_id=1, source_target_pairs={{0,16},{2,18},{4,20},{6,22},{8,24},{10,26},{12,28},{14,30},{16,0},... | collective-permute-start | bytes 663560 | tf_op jit(solution)/shard_map/ppermute | solution.py:895
  487.2 13.7 %collective-permute-start.26 = (f32[72,128]{1,0:T(8,128)S(1)}, f32[72,128]{1,0:T(8,128)S(1)}, u32[]{:S(2)}, u32[]{:S(2)}) collective-permute-start(f32[72,128]{1,0:T(8,128)S(1)} %bitcast.269), channel_id=1, source_target_pairs={{0,1},{1,0},{2,3},{3,2},{4,5},{5,4},{6,7},{7,6},{8,9},{9,8},{10,11... | collective-permute-start | bytes 110600 | tf_op jit(solution)/shard_map/ppermute | solution.py:909
  488.0 13.0 %copy-start.85 = (bf16[48,3072]{1,0:T(8,128)(2,1)S(1)}, bf16[48,3072]{1,0:T(8,128)(2,1)}, u32[]{:S(2)}) copy-start(bf16[48,3072]{1,0:T(8,128)(2,1)} %copy-done.84) | copy-start | bytes 884740
  488.0 15.8 %copy-start.86 = (bf16[48,3072]{1,0:T(8,128)(2,1)S(1)}, bf16[48,3072]{1,0:T(8,128)(2,1)}, u32[]{:S(2)}) copy-start(bf16[48,3072]{1,0:T(8,128)(2,1)} %fusion.41) | copy-start | bytes 884740
  500.9 1.3 collective-permute-start.27
  502.2 4.0 collective-permute-start.28
  506.2 4.4 collective-permute-start.29
  506.2 6.4 %collective-permute-start.30 = (f32[72,128]{1,0:T(8,128)S(1)}, f32[72,128]{1,0:T(8,128)S(1)}, u32[]{:S(2)}, u32[]{:S(2)}) collective-permute-start(f32[72,128]{1,0:T(8,128)S(1)} %add.349), channel_id=1, source_target_pairs={{0,16},{2,18},{4,20},{6,22},{8,24},{10,26},{12,28},{14,30},{16,0},... | collective-permute-start | bytes 110600 | tf_op jit(solution)/shard_map/ppermute | solution.py:912
  508.6 6.3 %collective-permute-start.31 = (f32[72,128]{1,0:T(8,128)S(1)}, f32[72,128]{1,0:T(8,128)S(1)}, u32[]{:S(2)}, u32[]{:S(2)}) collective-permute-start(f32[72,128]{1,0:T(8,128)S(1)} %add.349), channel_id=1, source_target_pairs={{0,24},{2,26},{4,28},{6,30},{8,16},{10,18},{12,20},{14,22},{16,8},... | collective-permute-start | bytes 110600 | tf_op jit(solution)/shard_map/ppermute | solution.py:912
  510.7 8.2 %collective-permute-start.34 = (bf16[48,2304]{1,0:T(8,128)(2,1)S(1)}, bf16[48,2304]{1,0:T(8,128)(2,1)S(1)}, u32[]{:S(2)}, u32[]{:S(2)}) collective-permute-start(bf16[48,2304]{1,0:T(8,128)(2,1)S(1)} %copy-done.110), channel_id=1, source_target_pairs={{0,24},{2,26},{4,28},{6,30},{8,16},{10,18},{12,20},{14,22},{16,8},... | collective-permute-start | bytes 663560 | tf_op jit(solution)/shard_map/ppermute | solution.py:895
  512.6 6.8 %collective-permute-start.36 = (bf16[4,48,768]{2,1,0:T(8,128)(2,1)S(1)}, bf16[4,48,768]{2,1,0:T(8,128)(2,1)S(1)}, u32[]{:S(2)}, u32[]{:S(2)}) collective-permute-start(bf16[4,48,768]{2,1,0:T(8,128)(2,1)S(1)} %dynamic-slice_bitcast_fusion.11), channel_id=1, source_target_pairs={{0,4},{2,6},{4,0},{6,2},{8,12},{10,14},{12,8},{14,10},{16,20},{18,... | collective-permute-start | bytes 884744 | tf_op jit(solution)/shard_map/ppermute | solution.py:888
  514.9 24.8 %collective-permute-start.23 = (bf16[512,768]{1,0:T(8,128)(2,1)}, bf16[512,768]{1,0:T(8,128)(2,1)}, u32[]{:S(2)}, u32[]{:S(2)}) collective-permute-start(bf16[512,768]{1,0:T(8,128)(2,1)} %dynamic-slice_bitcast_fusion.7), channel_id=1, source_target_pairs={{0,1},{1,0},{2,3},{3,2},{4,5},{5,4},{6,7},{7,6},{8,9},{9,8},{10,11... | collective-permute-start | bytes 2359304 | tf_op jit(solution)/shard_map/ppermute | solution.py:1131
  519.6 8.7 %collective-permute-start.37 = (bf16[48,768]{1,0:T(8,128)(2,1)S(1)}, bf16[48,768]{1,0:T(8,128)(2,1)S(1)}, u32[]{:S(2)}, u32[]{:S(2)}) collective-permute-start(bf16[48,768]{1,0:T(8,128)(2,1)S(1)} %get-tuple-element.280), channel_id=1, source_target_pairs={{0,8},{2,10},{4,12},{6,14},{8,0},{10,2},{12,4},{14,6},{16,24},{18,... | collective-permute-start | bytes 221192 | tf_op jit(solution)/shard_map/ppermute | solution.py:895
  523.0 7.7 %collective-permute-start.38 = (bf16[48,768]{1,0:T(8,128)(2,1)S(1)}, bf16[48,768]{1,0:T(8,128)(2,1)S(1)}, u32[]{:S(2)}, u32[]{:S(2)}) collective-permute-start(bf16[48,768]{1,0:T(8,128)(2,1)S(1)} %get-tuple-element.279), channel_id=1, source_target_pairs={{0,16},{2,18},{4,20},{6,22},{8,24},{10,26},{12,28},{14,30},{16,0},... | collective-permute-start | bytes 221192 | tf_op jit(solution)/shard_map/ppermute | solution.py:895
  523.4 7.2 %collective-permute-start.39 = (bf16[48,768]{1,0:T(8,128)(2,1)S(1)}, bf16[48,768]{1,0:T(8,128)(2,1)S(1)}, u32[]{:S(2)}, u32[]{:S(2)}) collective-permute-start(bf16[48,768]{1,0:T(8,128)(2,1)S(1)} %get-tuple-element.278), channel_id=1, source_target_pairs={{0,24},{2,26},{4,28},{6,30},{8,16},{10,18},{12,20},{14,22},{16,8},... | collective-permute-start | bytes 221192 | tf_op jit(solution)/shard_map/ppermute | solution.py:895
  526.7 10.4 %collective-permute-start.35 = (bf16[48,2304]{1,0:T(8,128)(2,1)S(1)}, bf16[48,2304]{1,0:T(8,128)(2,1)S(1)}, u32[]{:S(2)}, u32[]{:S(2)}) collective-permute-start(bf16[48,2304]{1,0:T(8,128)(2,1)S(1)} %fusion.48), channel_id=1, source_target_pairs={{0,1},{1,0},{2,3},{3,2},{4,5},{5,4},{6,7},{7,6},{8,9},{9,8},{10,11... | collective-permute-start | bytes 663560 | tf_op jit(solution)/shard_map/ppermute | solution.py:903
  530.7 7.1 %collective-permute-start.40 = (bf16[48,768]{1,0:T(8,128)(2,1)S(1)}, bf16[48,768]{1,0:T(8,128)(2,1)S(1)}, u32[]{:S(2)}, u32[]{:S(2)}) collective-permute-start(bf16[48,768]{1,0:T(8,128)(2,1)S(1)} %fusion.52), channel_id=1, source_target_pairs={{0,1},{1,0},{2,3},{3,2},{4,5},{5,4},{6,7},{7,6},{8,9},{9,8},{10,11... | collective-permute-start | bytes 221192 | tf_op jit(solution)/shard_map/ppermute | solution.py:903
  (121 other events, 471.1 us)

commit v4 on v3

--- a/solution.py
+++ b/solution.py
@@ -11,6 +11,7 @@
 HD = 64
 EPS = 1e-05
 CHUNK = 256
+WIDE = 512
 F32 = jnp.float32
 BF16 = jnp.bfloat16
 
@@ -55,41 +56,43 @@
     return low, high
 
 
-def causal_tail(scores, first):
+def causal_tail(scores):
     key = lax.broadcasted_iota(jnp.int32, scores.shape, 0)
-    query = lax.broadcasted_iota(jnp.int32, scores.shape, 1)
-    return jnp.where(key - first <= query, scores, 0.0)
+    return jnp.where(key <= lax.broadcasted_iota(jnp.int32, scores.shape, 1), scores, 0.0)
 
 
 def attn_fwd_kernel(q_ref, k_ref, v_ref, km_ref, vm_ref, o_ref, lse_ref, keys, vals_t, vmem_t):
     mem = km_ref.shape[0]
-    rows = q_ref.shape[0]
     keys[0:mem, :] = km_ref[...]
     keys[mem:, :] = k_ref[...]
     vals_t[...] = v_ref[...].T
     vmem_t[...] = vm_ref[...].T
     picks = head_rows(HD**-0.5)
-    for part in range(rows // CHUNK):
-        lo, hi = part * CHUNK, (part + 1) * CHUNK
-        query = q_ref[lo:hi, :]
-        outs = []
-        for head in range(2):
-            band = slice(head * HD, (head + 1) * HD)
-            scores = dot_dims(keys[0 : mem + hi, :], query * picks[head], 1, 1)
-            raw = jnp.exp(scores)
-            tail = causal_tail(raw[mem + lo :], 0)
-            if lo:
-                raw = jnp.concatenate([raw[: mem + lo], tail], axis=0)
-            else:
-                raw = jnp.concatenate([raw[:mem], tail], axis=0)
-            total = jnp.sum(raw, axis=0, keepdims=True)
-            lse_ref[0, head : head + 1, lo:hi] = jnp.log(total)
-            weights = (raw * (1.0 / total)).astype(BF16)
-            outs.append(
-                dot_dims(vals_t[band, 0:hi], weights[mem:], 1, 0)
-                + dot_dims(vmem_t[band, :], weights[:mem], 1, 0)
-            )
-        o_ref[lo:hi, :] = jnp.concatenate(outs, axis=0).T.astype(BF16)
+    steps = [(part, head) for part in range(q_ref.shape[0] // WIDE) for head in range(2)]
+
+    def begin(part, head):
+        lo, hi = part * WIDE, (part + 1) * WIDE
+        return dot_dims(keys[0 : mem + hi, :], q_ref[lo:hi, :] * picks[head], 1, 1)
+
+    ahead = begin(*steps[0])
+    outs = []
+    for n, (part, head) in enumerate(steps):
+        lo, hi = part * WIDE, (part + 1) * WIDE
+        band = slice(head * HD, (head + 1) * HD)
+        raw = jnp.exp(ahead)
+        if n + 1 < len(steps):
+            ahead = begin(*steps[n + 1])
+        raw = jnp.concatenate([raw[: mem + lo], causal_tail(raw[mem + lo :])], axis=0)
+        total = jnp.sum(raw, axis=0, keepdims=True)
+        lse_ref[0, head : head + 1, lo:hi] = jnp.log(total)
+        weights = (raw * (1.0 / total)).astype(BF16)
+        outs.append(
+            dot_dims(vals_t[band, 0:hi], weights[mem:], 1, 0)
+            + dot_dims(vmem_t[band, :], weights[:mem], 1, 0)
+        )
+        if head == 1:
+            o_ref[lo:hi, :] = jnp.concatenate(outs, axis=0).T.astype(BF16)
+            outs = []
 
 
 def attn_fwd_after_kernel(q_ref, k_ref, v_ref, km_ref, vm_ref, held_ref, *rest):
@@ -124,7 +127,7 @@
             pltpu.VMEM((wide, mem), BF16),
         ],
         input_output_aliases={5: 0} if more else {},
-        compiler_params=pltpu.CompilerParams(vmem_limit_bytes=40 * 2**20),
+        compiler_params=pltpu.CompilerParams(vmem_limit_bytes=60 * 2**20),
         cost_estimate=pl.CostEstimate(
             flops=pairs * rows * rows * 4000,
             bytes_accessed=rows * width * 8,
@@ -168,7 +171,7 @@
             jax.ShapeDtypeStruct((segs, mem, width), F32),
             jax.ShapeDtypeStruct((segs * pairs, 2, rows), F32),
         ],
-        compiler_params=pltpu.CompilerParams(vmem_limit_bytes=40 * 2**20),
+        compiler_params=pltpu.CompilerParams(vmem_limit_bytes=60 * 2**20),
         cost_estimate=pl.CostEstimate(
             flops=segs * rows * width * 4000, bytes_accessed=segs * rows * width * 6, transcendentals=0
         ),
@@ -185,7 +188,7 @@
     mem = km_ref.shape[0]
     rows = q_ref.shape[0]
 
-    @pl.when(phase == 0)
+    @pl.when((phase == 2) & (pl.program_id(0) < pl.num_programs(0) - 1))
     def _():
         keys[0:mem, :] = km_ref[...]
         keys[mem:, :] = k_ref[...]
@@ -211,7 +214,7 @@
                 centre = mid_ref[0, head : head + 1, lo:hi]
                 prob = jnp.exp(dot_dims(keys[0:end, :], query_h, 1, 1) - log_total)
                 prob = jnp.concatenate(
-                    [prob[: mem + lo], causal_tail(prob[mem + lo :], 0)], axis=0
+                    [prob[: mem + lo], causal_tail(prob[mem + lo :])], axis=0
                 )
                 grad_p = dot_dims(vals[0:end, :], grad_h, 1, 1)
                 grad_s = (prob * (grad_p - centre)).astype(BF16)
@@ -224,11 +227,11 @@
             dq[lo:hi, :] = (jnp.concatenate(dqs, axis=0) * HD**-0.5).T.astype(BF16)
         out_ref[...] = dq[...]
 
-    @pl.when(phase == 1)
+    @pl.when((phase == 0) & (pl.program_id(0) > 0))
     def _():
         out_ref[...] = dk[mem:, :].astype(BF16)
 
-    @pl.when(phase == 2)
+    @pl.when((phase == 1) & (pl.program_id(0) > 0))
     def _():
         out_ref[...] = dv[mem:, :].astype(BF16)
 
@@ -238,16 +241,23 @@
     rows, width = lse.shape[2], qkv.shape[1] // 3
     mem = kv_mem.shape[0]
     wide = 2 * HD
-    spec = lambda off: pl.BlockSpec((rows, wide), lambda p, f, off=off: (seg, off * pairs + first + p))
-    mspec = lambda off: pl.BlockSpec((mem, wide), lambda p, f, off=off: (0, off * pairs + first + p))
-    lspec = pl.BlockSpec((1, 2, rows), lambda p, f: (seg * pairs + first + p, 0, 0))
+    at = lambda p: first + jnp.minimum(p, count - 1)
+    spec = lambda off: pl.BlockSpec((rows, wide), lambda p, f, off=off: (seg, off * pairs + at(p)))
+    mspec = lambda off: pl.BlockSpec((mem, wide), lambda p, f, off=off: (0, off * pairs + at(p)))
+    lspec = pl.BlockSpec((1, 2, rows), lambda p, f: (seg * pairs + at(p), 0, 0))
+
+    def place(p, f):
+        late = jnp.where(f == 0, count, 2 * count) + p - 1
+        now = jnp.where(p == count, 3 * count - 1, p)
+        return (0, jnp.where((f == 2) | (p == 0), now, late))
+
     return pl.pallas_call(
         attn_bwd_kernel,
-        grid=(count, 3),
+        grid=(count + 1, 3),
         in_specs=[
             spec(0), spec(1), spec(2), mspec(0), mspec(1), spec(0), lspec, lspec,
         ],
-        out_specs=pl.BlockSpec((rows, wide), lambda p, f: (0, f * count + p)),
+        out_specs=pl.BlockSpec((rows, wide), place),
         out_shape=jax.ShapeDtypeStruct((rows, 3 * count * wide), BF16),
         scratch_shapes=[
             pltpu.VMEM((mem + rows, wide), BF16),
@@ -258,7 +268,7 @@
             pltpu.VMEM((mem + rows, wide), F32),
             pltpu.VMEM((mem + rows, wide), F32),
         ],
-        compiler_params=pltpu.CompilerParams(vmem_limit_bytes=48 * 2**20),
+        compiler_params=pltpu.CompilerParams(vmem_limit_bytes=60 * 2**20),
         cost_estimate=pl.CostEstimate(
             flops=count * rows * rows * 6500,
             bytes_accessed=rows * count * wide * 18,
@@ -273,7 +283,7 @@
 
     @pl.when(own)
     def _():
-        out[...] = kept[0]
+        out[...] = kept[0, 0]
 
     @pl.when(jnp.logical_not(own))
     def _():
@@ -281,7 +291,10 @@
 
 
 def half_specs(rows, width):
-    return [pl.BlockSpec((1, rows, width), lambda i, told: ((i // 2) ^ told[0], 0, 0))] * 2
+    return [
+        pl.BlockSpec((1, 1, rows, width), lambda i, told: (told[1], (i // 2) ^ told[0], 0, 0)),
+        pl.BlockSpec((1, rows, width), lambda i, told: ((i // 2) ^ told[0], 0, 0)),
+    ]
 
 
 def enter_kernel(told, kept, got, gain, bias, weight, shift, rows_ref, normed_ref, qkv_ref):
@@ -296,7 +309,7 @@
 
 
 def enter(told, kept, got, gain, bias, weight, shift):
-    segs, rows, width = kept.shape
+    _, segs, rows, width = kept.shape
     whole = lambda r, c: pl.BlockSpec((r, c), lambda i, told: (0, 0), pipeline_mode=pl.Buffered(1))
     block = lambda c: pl.BlockSpec((rows, c), lambda i, told: (i, 0))
     sizes = (width, width, 3 * width)
@@ -309,7 +322,7 @@
             out_specs=[block(c) for c in sizes],
         ),
         out_shape=[jax.ShapeDtypeStruct((2 * segs * rows, c), BF16) for c in sizes],
-        compiler_params=pltpu.CompilerParams(vmem_limit_bytes=48 * 2**20),
+        compiler_params=pltpu.CompilerParams(vmem_limit_bytes=60 * 2**20),
         cost_estimate=pl.CostEstimate(
             flops=8 * segs * rows * width * width * 3, bytes_accessed=segs * rows * width * 28, transcendentals=0
         ),
@@ -336,18 +349,17 @@
         sums_ref[...] = jnp.zeros_like(sums_ref)
         exp_sums_ref[...] = jnp.zeros_like(exp_sums_ref)
 
-    parts = 6
+    parts = 4
     wide = expand_w.shape[1] // parts
     bend, cube = 0.7978845608028654, 0.044715
     for part in range(parts):
         at = slice(part * wide, (part + 1) * wide)
         value = dot_dims(normed, expand_w[:, at], 1, 0) + expand_b[:, at]
         square = value * value
-        curve = jnp.tanh(bend * value * (1.0 + cube * square))
-        half = 0.5 * (1.0 + curve)
+        half = 0.5 + 0.5 * jnp.tanh(value * (bend + bend * cube * square))
         activ = (value * half).astype(BF16)
         activ_ref[:, at] = activ
-        slope = half + 0.5 * bend * value * (1.0 - curve * curve) * (1.0 + 3.0 * cube * square)
+        slope = half + (half - half * half) * (value * (2.0 * bend + 6.0 * bend * cube * square))
         grad = (dot_dims(cot, contract_w[:, at], 1, 0) * slope).astype(BF16)
         grad_exp_ref[:, at] = grad
         exp_sums_ref[:, at] += jnp.sum(grad.astype(F32), axis=0, keepdims=True)
@@ -370,7 +382,7 @@
 
 
 def middle(told, kept, got, rows_in, attended, out_w, expand_w, contract_w, out_b, gain, bias, expand_b, contract_b):
-    segs, rows, width = kept.shape
+    _, segs, rows, width = kept.shape
     wide = expand_w.shape[1]
     whole = lambda r, c: pl.BlockSpec((r, c), lambda i, told: (0, 0), pipeline_mode=pl.Buffered(1))
     block = lambda c: pl.BlockSpec((rows, c), lambda i, told: (i, 0))
@@ -534,7 +546,7 @@
             *[pltpu.VMEM(w.shape, w.dtype) for w in weights],
             pltpu.SemaphoreType.DMA((len(weights),)),
         ],
-        compiler_params=pltpu.CompilerParams(vmem_limit_bytes=48 * 2**20),
+        compiler_params=pltpu.CompilerParams(vmem_limit_bytes=60 * 2**20),
         cost_estimate=pl.CostEstimate(flops=cycles * 10**9, bytes_accessed=17 * 10**6, transcendentals=0),
         name=name,
     )(*given, *weights)
@@ -871,46 +883,190 @@
     return (a.astype(F32) + b.astype(F32)).astype(BF16)
 
 
-class Scatter:
-    def __init__(self, grad):
-        index = lax.axis_index("dp")
-        self.deep, self.cross, self.core = index // 4, (index // 2) % 2, index % 2
-        parts = grad.reshape(4, 2, 2, grad.shape[0] // 16, grad.shape[1])
-        self.keep, self.give = pick(parts, self.core, 2), pick(parts, 1 - self.core, 2)
-
-    def over_core(self, *beside):
-        got = behind(lax.ppermute(self.give, "dp", dp_pairs(1)), *beside)
-        parts = add_low(self.keep, got)
-        self.keep, self.give = pick(parts, self.cross, 1), pick(parts, 1 - self.cross, 1)
-        return self
-
-    def over_x(self, *beside):
-        got = behind(lax.ppermute(self.give, "dp", dp_pairs(2)), *beside)
-        parts = add_low(self.keep, got)
-        self.keep = pick(parts, self.deep, 0)
-        self.give = tuple(pick(parts, self.deep ^ k, 0) for k in (1, 2, 3))
-        return self
-
-    def over_z(self, *beside):
-        far = [lax.ppermute(self.give[k - 1], "dp", dp_pairs(4 * k)) for k in (1, 2, 3)]
-        total = self.keep.astype(F32)
-        for part in behind(far, *beside):
-            total = total + part.astype(F32)
-        self.keep = self.give = total.astype(BF16)
-        return self
-
-    def over_y(self, *beside):
-        got = behind(lax.ppermute(self.give, "ctx", [(0, 1), (1, 0)]), *beside)
-        return self.keep.astype(F32) + got.astype(F32)
-
-
-def sum_over(flat, step, *beside):
-    if step == 0:
-        return flat + behind(lax.ppermute(flat, "ctx", [(0, 1), (1, 0)]), *beside)
-    if step < 3:
-        return flat + behind(lax.ppermute(flat, "dp", dp_pairs(step)), *beside)
-    far = behind([lax.ppermute(flat, "dp", dp_pairs(4 * k)) for k in (1, 2, 3)], *beside)
-    return (flat + far[0]) + (far[1] + far[2])
+def reduce_kernel(planes, cuts, swaps, *refs):
+    count = 1 + max(k for k, _, _ in cuts)
+    grads, gives = refs[:count], refs[count : count + swaps]
+    long_ref, short_ref = refs[count + swaps : count + swaps + 2]
+    outs = refs[count + swaps + 2 : 2 * count + swaps + 2]
+    gots = refs[2 * count + swaps + 2 : 2 * count + 2 * swaps + 2]
+    long_out, short_out = refs[2 * count + 2 * swaps + 2 : 2 * count + 2 * swaps + 4]
+    (
+        mine, got_core, got_x, line, got_z, low, got_y, parts, held, total,
+        load_sem, core_sem, x_sem, z_sem, y_sem, swap_sem, sum_sem,
+    ) = refs[2 * count + 2 * swaps + 4 :]
+    index, plane = lax.axis_index("dp"), lax.axis_index("ctx")
+    deep, cross, core = index // 4, (index // 2) % 2, index % 2
+    place = lambda z, x, c: (z * 2 + x) * 2 + c
+    deeps = (deep + 1 - 2 * lax.rem(deep, 2), lax.rem(deep + 2, 4), 3 - deep)
+    beside, sibling = {"dp": place(deep, 1 - cross, core)}, {"dp": place(deep, cross, 1 - core)}
+    other = {"ctx": 1 - plane}
+    chunks = len(cuts)
+    peers = long_ref.shape[0]
+    rows = long_ref.shape[1]
+    me = index * planes + plane
+
+    def remote(source, landing, sems, at, device):
+        return pltpu.make_async_remote_copy(
+            source, landing, sems.at[(0, *at)], sems.at[(1, *at)], device_id=device, device_id_type=pl.DeviceIdType.MESH
+        )
+
+    def device(j):
+        return (j // planes, lax.rem(j, planes))
+
+    def small(phase, j, sender):
+        source, landing = (parts.at[j], held.at[sender]) if phase == 0 else (total.at[sender], total.at[sender])
+        return pltpu.make_async_remote_copy(
+            source, landing, sum_sem.at[0, phase, j], sum_sem.at[1, phase, sender],
+            device_id=device(j), device_id_type=pl.DeviceIdType.MESH,
+        )
+
+    def every(work):
+        def body(step, carry):
+            work(lax.rem(me + step, peers))
+            return carry
+
+        lax.fori_loop(1, peers, body, 0)
+
+    def loop(first, last, work):
+        def body(c, carry):
+            work(c)
+            return carry
+
+        lax.fori_loop(first, last, body, 0)
+
+    def load(c, x):
+        k, start, wide = cuts[c]
+        return pltpu.make_async_copy(
+            grads[k].at[:, x, core, :, pl.ds(start, wide)], mine.at[c, x], load_sem.at[c, x]
+        )
+
+    def to_core(c, x):
+        k, start, wide = cuts[c]
+        return remote(
+            grads[k].at[:, x, 1 - core, :, pl.ds(start, wide)], got_core.at[c, x], core_sem, (c, x), sibling
+        )
+
+    def swap(k):
+        return remote(gives[k].at[1 - plane], gots[k], swap_sem, (k,), other)
+
+    def arrived(landing, sems, at):
+        remote(landing, landing, sems, at, sibling).wait_recv()
+
+    def to_x(c):
+        return remote(mine.at[c, 1 - cross], got_x.at[c], x_sem, (c,), beside)
+
+    def to_z(c, k):
+        return remote(line.at[c, deeps[k]], got_z.at[c, k], z_sem, (c, k), {"dp": place(deeps[k], cross, core)})
+
+    def to_y(c):
+        return remote(low.at[c], got_y.at[c], y_sem, (c,), other)
+
+    for c in range(chunks):
+        for x in range(2):
+            load(c, x).start()
+    parts[:, :rows, :] = long_ref[...]
+    parts[:, rows:, :] = short_ref[...]
+    barrier = pltpu.get_barrier_semaphore()
+    every(lambda j: pl.semaphore_signal(barrier, inc=1, device_id=device(j), device_id_type=pl.DeviceIdType.MESH))
+    pl.semaphore_wait(barrier, peers - 1)
+    for c in range(chunks):
+        for x in range(2):
+            to_core(c, x).start()
+    every(lambda j: small(0, j, me).start())
+    for k in range(swaps):
+        swap(k).start()
+    held[me] = parts[me]
+
+    def over_core(c):
+        for x in range(2):
+            pltpu.make_async_copy(mine.at[c, x], mine.at[c, x], load_sem.at[c, x]).wait()
+            arrived(got_core.at[c, x], core_sem, (c, x))
+            for z in range(4):
+                mine[c, x, z] = add_low(mine[c, x, z], got_core[c, x, z])
+        to_x(c).start()
+
+    loop(0, chunks, over_core)
+    every(lambda j: small(0, j, j).wait_recv())
+    total[me] = jnp.sum(held[...], axis=0)
+    every(lambda j: small(1, j, me).start())
+
+    def over_x(c):
+        arrived(got_x.at[c], x_sem, (c,))
+        for z in range(4):
+            line[c, z] = add_low(mine[c, cross, z], got_x[c, z])
+        for k in range(3):
+            to_z(c, k).start()
+
+    def over_z(c):
+        value = line[c, deep].astype(F32)
+        for k in range(3):
+            arrived(got_z.at[c, k], z_sem, (c, k))
+            value = value + got_z[c, k].astype(F32)
+        low[c] = value.astype(BF16)
+        to_y(c).start()
+
+    def both(c):
+        over_x(c)
+        over_z(c - 1)
+
+    over_x(0)
+    loop(1, chunks, both)
+    over_z(chunks - 1)
+    for c, (k, start, wide) in enumerate(cuts):
+        arrived(got_y.at[c], y_sem, (c,))
+        outs[k][:, start : start + wide] = low[c].astype(F32) + got_y[c].astype(F32)
+    every(lambda j: small(1, j, j).wait_recv())
+    long_out[...] = total[:, :rows, :]
+    short_out[...] = total[:, rows:, :]
+    for k in range(swaps):
+        swap(k).wait_recv()
+    every(lambda j: small(0, j, me).wait_send())
+    every(lambda j: small(1, j, me).wait_send())
+    for k in range(swaps):
+        swap(k).wait_send()
+    for c in range(chunks):
+        for x in range(2):
+            to_core(c, x).wait_send()
+
+    def finish(c):
+        to_x(c).wait_send()
+        for k in range(3):
+            to_z(c, k).wait_send()
+        to_y(c).wait_send()
+
+    loop(0, chunks, finish)
+
+
+def reduce_all(grads, gives, long, short, planes):
+    wide = 768
+    shard = grads[0].shape[0] // 16
+    cuts = [(k, at, wide) for k, g in enumerate(grads) for at in range(0, g.shape[1], wide)]
+    chunks, peers = len(cuts), long.shape[0]
+    small = (peers, long.shape[1] + short.shape[1], long.shape[2])
+    vmem, hbm = pl.BlockSpec(memory_space=pltpu.VMEM), pl.BlockSpec(memory_space=pl.ANY)
+    shape = jax.ShapeDtypeStruct
+    dma = pltpu.SemaphoreType.DMA
+    low = lambda *dims: pltpu.VMEM((chunks, *dims, shard, wide), BF16)
+    out = pl.pallas_call(
+        functools.partial(reduce_kernel, planes, cuts, len(gives)),
+        in_specs=[hbm] * (len(grads) + len(gives)) + [vmem] * 2,
+        out_specs=[vmem] * len(grads) + [hbm] * len(gives) + [vmem] * 2,
+        out_shape=[shape((shard, g.shape[1]), F32) for g in grads]
+        + [shape(g.shape[1:], BF16) for g in gives]
+        + [shape(v.shape, F32) for v in (long, short)],
+        scratch_shapes=[
+            low(2, 4), low(2, 4), low(4), low(4), low(3), low(), low(),
+            *[pltpu.VMEM(small, F32)] * 3,
+            dma((chunks, 2)), dma((2, chunks, 2)), dma((2, chunks)), dma((2, chunks, 3)), dma((2, chunks)),
+            dma((2, len(gives))), dma((2, 2, peers)),
+        ],
+        compiler_params=pltpu.CompilerParams(
+            collective_id=1, has_side_effects=True, vmem_limit_bytes=60 * 2**20
+        ),
+        cost_estimate=pl.CostEstimate(flops=8 * 10**10, bytes_accessed=50 * 10**6, transcendentals=0),
+        name="reduce_all",
+    )(*[g.reshape(4, 2, 2, shard, g.shape[1]) for g in grads], *gives, long, short)
+    return out[: len(grads)], out[len(grads) : len(grads) + len(gives)], out[-2], out[-1]
 
 
 def split_heads(rows):
@@ -1087,7 +1243,7 @@
     micros, segs_local, tok_rows, width = tokens.shape
     mem = memory_tokens.shape[0]
     shard = qkv_weight.shape[0]
-    quick = groups == 16 and ranks == 2 and micros == 2 and segs_local == 2 and (tok_rows * ranks) % CHUNK == 0
+    quick = groups == 16 and ranks == 2 and micros == 2 and segs_local == 2 and (tok_rows * ranks) % WIDE == 0
     names = ("qkv", "out", "expand", "contract", "read", "key", "value")
     shards = (qkv_weight, out_weight, expand_weight, contract_weight, read_weight, key_weight, value_weight)
     if quick:
@@ -1145,7 +1301,7 @@
         flip = pick(flips, rank, 0)
         told = jnp.stack([flip.astype(jnp.int32), rank.astype(jnp.int32)])
         got = swapped(give)
-        give_grad = behind(pick(cotangent, 1 - rank, 0), got, expand_full)
+        give_grad = pick(behind(cotangent, got, expand_full), 1 - rank, 0)
         flags = pick(flags, rank, 0)
         flags = jnp.where(flip, flags[::-1], flags)
         segs = segs_local
@@ -1167,7 +1323,7 @@
     kv_mem = jnp.where((flags == 0)[:, None, None], kv_follow[None], kv_first[None])
     if quick:
         rows_in, normed_a, qkv = enter(
-            told, pick(tokens, rank, 0), got, norm_one_gain, norm_one_bias, qkv_read_key, p["shift"]
+            told, tokens, got, norm_one_gain, norm_one_bias, qkv_read_key, p["shift"]
         )
         attended, lse_first = attn_fwd(behind(qkv, give_grad), kv_first, 0, seg_rows, None)
         got_grad = swapped(give_grad)
@@ -1176,7 +1332,7 @@
         (
             result, rows_grad, normed_b, activ, grad_expanded, grad_attn_out, grad_attended, mid_sums, expand_sums,
         ) = middle(
-            told, pick(cotangent, rank, 0), got_grad, rows_in, attended, p["out"], p["expand"], p["contract"], out_bias,
+            told, cotangent, got_grad, rows_in, attended, p["out"], p["expand"], p["contract"], out_bias,
             norm_two_gain, norm_two_bias, expand_bias, contract_bias,
         )
         grad_after = grad_attn_out
@@ -1214,77 +1370,23 @@
         return jnp.stack(kinds)
 
     if quick:
-        pairs, most = H // 2, H // 3
-        cut = most * 2 * HD
-        columns = lambda a, lo, hi: jnp.concatenate(
-            [a[..., k * width + lo : k * width + hi] for k in range(3)], axis=-1
-        )
-        weights = [columns(p["qkv"], 0, cut), columns(p["qkv"], cut, width)]
         lse = jnp.concatenate([lse_first, lse_second], axis=0)
         mems = (kv_first, kv_mem[1])
         spans = [slice(0, seg_rows), slice(seg_rows, 2 * seg_rows)]
-
-        block_halves = [own_and_other(result[a]) for a in spans]
-        on_contract = Scatter(dot_dims(rows_grad, activ, 0, 0).astype(BF16))
-        grad_expanded = behind(grad_expanded, on_contract.give)
-        term_expand = dot_dims(normed_b, grad_expanded, 0, 0).astype(BF16)
-        on_expand = Scatter(term_expand)
-        on_contract.over_core(term_expand)
-        grad_attn_out = behind(grad_attn_out, on_contract.give, on_expand.give)
-        term_out = dot_dims(attended, grad_attn_out, 0, 0).astype(BF16)
-        dk_mem, dv_mem, middle_sums = attn_mem(
-            qkv, kv_mem, attended, behind(grad_attended, term_out), lse
-        )
-        on_expand.over_core(middle_sums)
+        dk_mem, dv_mem, middle_sums = attn_mem(qkv, kv_mem, attended, grad_attended, lse)
         pooled = pool(jnp.concatenate([dk_mem, dv_mem], axis=2))
-        others = behind([other for _, other in block_halves], middle_sums)
-
-        def back(seg, first, count, *earlier):
-            grad = behind(grad_attended, *earlier)
-            return attn_bwd(qkv, mems[seg], grad, lse, middle_sums, seg, first, count)
-
-        normed = [normed_a[a] for a in spans]
-        term = lambda grads: sum(dot_dims(normed[k], grads[k], 0, 0) for k in range(2)).astype(BF16)
-        turn_a = back(0, 0, most, pooled, others, on_expand.give)
-        pooled = sum_over(pooled, 0, turn_a)
-        on_contract.over_x(turn_a)
-        turn_b = back(1, 0, most, turn_a, pooled, on_contract.give)
-        pooled = sum_over(pooled, 1, turn_b)
-        others = behind([swapped(other) for other in others], turn_b)
-        block_halves = [(own, other) for (own, _), other in zip(block_halves, others)]
-        on_expand.over_x(turn_b)
-        on_contract.over_z(turn_b)
-        most_grads = [turn_a, turn_b]
-        on_most = Scatter(jnp.concatenate([term(most_grads), term_out], axis=1))
-        turn_c = back(
-            0, most, pairs - most, on_most.give, on_expand.give, on_contract.give, pooled
-        )
-        pooled = sum_over(pooled, 2, turn_c)
-        on_most.over_core(turn_c)
-        got_contract = on_contract.over_y(turn_c)
-        first_end = input_back(
-            spans[0],
-            [behind(most_grads[0], on_most.give, pooled), turn_c],
-            weights,
-        )
-        kept_first, given_first = own_and_other(first_end[0])
-        turn_d = back(1, most, pairs - most, given_first, got_contract)
-        pooled = sum_over(pooled, 3, turn_d)
-        on_expand.over_z(turn_d)
-        on_most.over_x(turn_d)
-        got_first = behind(swapped(given_first), turn_d)
-        rest_grads = [turn_c, turn_d]
-        on_rest = Scatter(term(rest_grads))
-        last = behind(turn_d, on_expand.give, on_most.give, on_rest.give, pooled)
-        second_end = input_back(spans[1], [most_grads[1], last], weights)
-        on_rest.over_core(second_end[0])
-        kept_second, given_second = own_and_other(second_end[0])
-        one_gain, one_bias = first_end[1] + second_end[1], first_end[2] + second_end[2]
-        qkv_sums = [
-            sum(jnp.sum(g[k].astype(F32), axis=0) for k in range(2)).reshape(3, -1)
-            for g in (most_grads, rest_grads)
+        grads = [
+            attn_bwd(qkv, mems[seg], grad_attended, lse, middle_sums, seg, 0, H // 2) for seg in range(2)
         ]
-        qkv_sums = jnp.concatenate(qkv_sums, axis=1)
+        ends = [input_back(spans[k], [grads[k]], [p["qkv"]]) for k in range(2)]
+        one_gain, one_bias = ends[0][1] + ends[1][1], ends[0][2] + ends[1][2]
+        qkv_sums = sum(jnp.sum(g.astype(F32), axis=0) for g in grads).reshape(3, width)
+        terms = (
+            dot_dims(rows_grad, activ, 0, 0).astype(BF16),
+            dot_dims(normed_b, grad_expanded, 0, 0).astype(BF16),
+            sum(dot_dims(normed_a[spans[k]], grads[k], 0, 0) for k in range(2)).astype(BF16),
+            dot_dims(attended, grad_attn_out, 0, 0).astype(BF16),
+        )
     else:
         _, gelu_pull = jax.vjp(gelu_tanh, expanded)
         grad_expanded = gelu_pull(dot_dims(rows_grad, p["contract"], 1, 0))[0].astype(BF16)
@@ -1318,20 +1420,6 @@
             column_sum(grad_attn_out), two_gain, two_bias, column_sum(grad_expanded), column_sum(rows_grad),
         )
     vectors = (one_gain, one_bias, jnp.stack([qkv_sums[0], qkv_sums[2]]), *mid)
-    flat = jnp.concatenate([v.reshape(-1) for v in vectors]).reshape(-1, 128)
-    got = {}
-
-    def turn(step, value):
-        if step == 0:
-            return behind(value, flat, on_rest.give, on_most.give, given_second)
-        got["second"] = behind(swapped(given_second), value)
-        on_rest.over_x(value)
-        on_most.over_z(value)
-        got["flat"] = sum_over(flat, 0, value)
-        got["expand"] = on_expand.over_y(value)
-        got["flat"] = sum_over(sum_over(got["flat"], 1), 2)
-        got["most"] = on_most.over_y()
-
     if not quick:
         summed = tuple(
             lax.psum(
@@ -1342,26 +1430,26 @@
         pooled, vectors = lax.psum((pooled, vectors), ("dp", "ctx"))
 
     if quick:
-        pooled = turn(0, pooled)
+        peers = groups * ranks
+        flat = jnp.concatenate([v.reshape(-1) for v in vectors])
+        lines = pl.cdiv(flat.size, peers * 128)
+        flat = jnp.pad(flat, (0, peers * lines * 128 - flat.size)).reshape(peers, lines, 128)
+        halves = [r.reshape(ranks, tok_rows, width) for r in (result[spans[0]], result[spans[1]], ends[0][0], ends[1][0])]
+        summed, gots, pooled, flat = reduce_all(
+            terms, halves, pooled.reshape(peers, -1, 128), flat, ranks
+        )
+        summed = (summed[2], summed[3], summed[1], summed[0])
+        flat = flat.reshape(-1)
+        pooled = pooled.reshape(2, mem, 2 * width)
         grad_mt, mem_matrices, mem_vectors = mem_backward(
             memory_tokens, norms, pooled, shard, group, kept, mem_weights_in
         )
-        turn(1, grad_mt)
     else:
         mine = lambda a: lax.dynamic_slice_in_dim(a, group * shard, shard, 1)
         grad_mt, mem_matrices, mem_vectors = memory_backward(
             memory_tokens, p, m, pooled[0], pooled[1], mine
         )
     if quick:
-        most_part = got["most"][:, : 3 * cut].reshape(shard, 3, cut)
-        rest_part = on_rest.over_z().over_y().reshape(shard, 3, width - cut)
-        summed = (
-            jnp.concatenate([most_part, rest_part], axis=2).reshape(shard, 3 * width),
-            got["most"][:, 3 * cut :],
-            got["expand"],
-            got_contract,
-        )
-        flat = sum_over(got["flat"], 3).reshape(-1)
         split, place = [], 0
         for v in vectors:
             split.append(flat[place : place + v.size].reshape(v.shape))
@@ -1370,8 +1458,9 @@
     matrices = tuple(a + b for a, b in zip(summed, mem_matrices)) + mem_matrices[4:]
     vectors = tuple(a + b for a, b in zip(vectors, mem_vectors))
     if quick:
-        block_out = settle(block_halves, flips)
-        token_grad = settle([(kept_first, got_first), (kept_second, got["second"])], flips)
+        own = [pick(h, rank, 0) for h in halves]
+        block_out = settle(list(zip(own[:2], gots[:2])), flips)
+        token_grad = settle(list(zip(own[2:], gots[2:])), flips)
     else:
         block_out, token_grad = result.reshape(tokens.shape), grad_rows.reshape(tokens.shape)
     return (

time: 556 us -> 528 us (0.950)
  Pallas kernels: 305 us -> 393 us
  starting transfers between devices: 50.9 us -> 4.49 us
  local copies, waits for them, and re-layouts: 67.5 us -> 32.1 us
  waiting for transfers between devices: 22.7 us -> 0.01 us
  other arithmetic: 46.9 us -> 30 us
  matrix products: 48.1 us -> 59.5 us
    pallas_call x4 -> x3, Pallas kernels: 65.3 us -> 169 us  [the longest x1 108 us: reduce_all(): pl.pallas_call(functools.partial(reduce_kernel, planes, cuts, len(gives))...]
    ppermute x36 -> x0, starting transfers between devices: 42.2 us -> none  [the longest x12 19.4 us: over_z(): lax.ppermute(self.give[k - 1], 'dp', dp_pairs(4 * k))]
    unnamed x295 -> x131, local copies, waits for them, and re-layouts: 31.9 us -> 9.98 us
    pallas_call x2, Pallas kernels: 45.3 us -> 27.1 us  [attn_fwd(): pl.pallas_call(attn_fwd_kernel if held is None else attn_fwd_after_kernel...]
    convert_element_type x12 -> x0, other arithmetic: 17.3 us -> none  [the longest x8 12.6 us: add_low(): return (a.astype(F32) + b.astype(F32)).astype(BF16)]
    ppermute x36 -> x0, waiting for transfers between devices: 14 us -> none  [the longest x12 6.16 us: over_z(): lax.ppermute(self.give[k - 1], 'dp', dp_pairs(4 * k))]
    dot_general x11 -> x7, matrix products: 48.1 us -> 59.5 us  [dot_dims(): lax.dot_general(a, b, (((ca,), (cb,)), ((), ())), precision=precision, pr...]
    squeeze x14 -> x3, local copies, waits for them, and re-layouts: 16.9 us -> 5.6 us  [pick(): return lax.dynamic_index_in_dim(parts, at, axis, keepdims=False)]
  transfers between devices with their start and end apart: 42 -> 2, of which waited for: 10 -> 0; matrix products, arithmetic and copies ran while one was open for 20% -> 3% of each run, Pallas kernels for 43% -> 25%
where the time goes in v4:
time: 528 us; the launch traced here: 521 us
  Pallas kernels  393 us (74%)
  matrix products  59.5 us (11%)
  local copies, waits for them, and re-layouts  32.1 us (6%)
  other arithmetic  30 us (6%)
    pallas_call x1, Pallas kernels, reduce_all(): pl.pallas_call(functools.partial(reduce_kernel, planes, cuts, len(gives))...  108 us
    pallas_call x1, Pallas kernels, gather_weights(): pl.pallas_call(functools.partial(gather_kernel, halved, count, kinds), in...  80.2 us
    pallas_call x1, Pallas kernels, middle(): pl.pallas_call(middle_kernel, grid_spec=pltpu.PrefetchScalarGridSpec(num_...  64 us
    pallas_call x2, Pallas kernels, attn_bwd(): pl.pallas_call(attn_bwd_kernel, grid=(count + 1, 3), in_specs=[spec(0), s...  61.3 us
    dot_general x7, matrix products, dot_dims(): lax.dot_general(a, b, (((ca,), (cb,)), ((), ())), precision=precision, pr...  59.5 us
    pallas_call x2, Pallas kernels, attn_fwd(): pl.pallas_call(attn_fwd_kernel if held is None else attn_fwd_after_kernel...  27.1 us
    pallas_call x2, Pallas kernels, mem_call(): pl.pallas_call(kernel, in_specs=[vmem] * len(given) + [pl.BlockSpec(memor...  25.4 us
    pallas_call x1, Pallas kernels, enter(): pl.pallas_call(enter_kernel, grid_spec=pltpu.PrefetchScalarGridSpec(num_s...  14.7 us
  transfers between devices with their start and end apart: 2, of which 0 were waited for; matrix products, arithmetic and copies ran while one was open for 3% of the time, Pallas kernels for 25%

profile of v4, /device:TPU:0, one launch (start us, length us, event | category | flops | bytes accessed | tf_op | source)
XLA Modules:
  0.0 521.5 jit_solution(17620634621423779378)
XLA Ops:
  0.8 2.9 dynamic-slice_bitcast_fusion.1
  3.7 3.0 collective-permute-start
  6.8 0.6 fusion.38
  9.4 0.6 broadcast_in_dim.45.shift
  12.5 80.2 %gather_weights.1 = (bf16[768,3072]{1,0:T(8,128)(2,1)S(1)}, bf16[768,3072]{1,0:T(8,128)(2,1)S(1)}, bf16[768,3072]{1,0:T(8,128)(2,1)S(1)}, bf16[768,1536]{1,0:T(8,128)(2,1)S(1)}) custom-call(bf16[48,3072]{1,0:T(8,128)(2,1)S(1)} %pad_maximum_fusion.2.refs_0_, bf16[48,3072]{1,0:T(8,128)(2,1)S(1)} %copy-done.1, bf16[48,3072]{1,0:T(8,128)(2,1)S(1)} %copy-done.2, ...), custom_call_target="tpu_custom_call" | custom-call | flops 80000000000 | bytes 33030144 | tf_op jit(solution)/shard_map/gather_weights/pallas_call | solution.py:850
  92.7 2.2 copy-done.3
  94.9 2.1 copy-done.4
  97.1 2.2 copy-done.5
  99.3 1.2 slice.153.out_w
  100.4 0.6 copy-done
  101.0 10.7 %mem_fwd.1 = (bf16[16,2304]{1,0:T(8,128)(2,1)}, bf16[16,768]{1,0:T(8,128)(2,1)}, f32[16,768]{1,0:T(8,128)}, f32[16,3072]{1,0:T(8,128)}, f32[16,768]{1,0:T(8,128)...) custom-call(f32[16,768]{1,0:T(8,128)} %mt_ref.3, ...), custom_call_target="tpu_custom_call" | custom-call | flops 15000000512 | bytes 17000000 | tf_op jit(solution)/shard_map/mem_fwd/pallas_call | solution.py:540
  111.8 0.8 slice.151.km_ref.vm_ref
  113.2 1.3 fusion.33
  115.1 0.8 fusion.31.chosen
  115.9 0.9 broadcast_select_fusion.km_ref.vm_ref
  116.8 0.6 copy-done.24
  117.4 0.6 slice_bitcast_fusion.km_ref.vm_ref
  118.1 2.7 dynamic-slice_bitcast_fusion
  120.7 1.5 collective-permute-start.1
  122.2 14.7 %enter.1 = (bf16[2048,768]{1,0:T(8,128)(2,1)}, bf16[2048,768]{1,0:T(8,128)(2,1)}, bf16[2048,2304]{1,0:T(8,128)(2,1)}) custom-call(s32[2]{0:T(128)} %pad_add_fusion.told, bf16[2,2,512,768]{3,2,1,0:T(8,128)(2,1)} %kept.2, bf16[2,512,768]{2,1,0:T(8,128)(2,1)} %collective-permute-done.got, f32[1,768]{1,0:T(1,128)} %broadcast_in_dim.42.gain.one_gain, ...), custom_call_target="tpu_custom_call" | custom-call | flops 14495514624 | bytes 22020096 | tf_op jit(solution)/shard_map/enter/pallas_call | solution.py:316
  137.0 13.5 %attn_fwd.2 = (bf16[2048,768]{1,0:T(8,128)(2,1)}, f32[6,2,1024]{2,1,0:T(2,128)}) custom-call(bf16[2048,2304]{1,0:T(8,128)(2,1)} %get-tuple-element.90.q_ref.k_ref.v_ref, bf16[2048,2304]{1,0:T(8,128)(2,1)} %get-tuple-element.90.q_ref.k_ref.v_ref, bf16[2048,2304]{1,0:T(8,128)(2,1)} %get-tuple-element.90.q_ref.k_ref.v_ref, bf16[16,1536]{1,0:T(8,128)(2,1)} %copy-done.25, ...), custom_call_target="tpu_custom_call" | custom-call | flops 25165824000 | bytes 6291456 | tf_op jit(solution)/shard_map/attn_fwd/pallas_call | solution.py:111
  150.4 0.8 constant_dynamic-update-slice_fusion.1
  151.3 13.6 %attn_fwd.3 = (bf16[2048,768]{1,0:T(8,128)(2,1)}, f32[6,2,1024]{2,1,0:T(2,128)}) custom-call(bf16[2048,2304]{1,0:T(8,128)(2,1)} %get-tuple-element.90.q_ref.k_ref.v_ref, bf16[2048,2304]{1,0:T(8,128)(2,1)} %get-tuple-element.90.q_ref.k_ref.v_ref, bf16[2048,2304]{1,0:T(8,128)(2,1)} %get-tuple-element.90.q_ref.k_ref.v_ref, ...), custom_call_target="tpu_custom_call", output_to_operand_aliasing={{0}: (5, {})} | custom-call | flops 25165824000 | bytes 6291456 | tf_op jit(solution)/shard_map/attn_fwd/pallas_call | solution.py:111
  164.9 0.8 constant_dynamic-update-slice_fusion.lse_ref
  166.2 1.4 fusion.16
  167.6 0.6 add_rsqrt_fusion.1
  168.2 0.6 add_rsqrt_fusion
  168.8 64.0 %middle.1 = (bf16[2048,768]{1,0:T(8,128)(2,1)}, bf16[2048,768]{1,0:T(8,128)(2,1)}, bf16[2048,768]{1,0:T(8,128)(2,1)}, bf16[2048,3072]{1,0:T(8,128)(2,1)}, bf16[2...) custom-call(s32[2]{0:T(128)} %pad_add_fusion.told, ...), custom_call_target="tpu_custom_call" | custom-call | flops 86973087744 | bytes 47185920 | tf_op jit(solution)/shard_map/middle/pallas_call | solution.py:392
  232.8 11.8 %attn_mem.1 = (f32[2,16,768]{2,1,0:T(8,128)}, f32[2,16,768]{2,1,0:T(8,128)}, f32[12,2,1024]{2,1,0:T(2,128)}) custom-call(bf16[2048,2304]{1,0:T(8,128)(2,1)} %get-tuple-element.90.q_ref.k_ref.v_ref, bf16[2,16,1536]{2,1,0:T(8,128)(2,1)} %copy-done.24, bf16[2,16,1536]{2,1,0:T(8,128)(2,1)} %copy-done.24, bf16[2048,768]{1,0:T(8,128)(2,1)} %get-tuple-element.95.attended.o_ref, ...), custom_call_target="tpu_custom_call" | custom-call | flops 6291456000 | bytes 9437184 | tf_op jit(solution)/shard_map/attn_mem/pallas_call | solution.py:164
  244.7 30.7 %attn_bwd.3 = bf16[1024,2304]{1,0:T(8,128)(2,1)} custom-call(bf16[2048,2304]{1,0:T(8,128)(2,1)} %get-tuple-element.90.q_ref.k_ref.v_ref, bf16[2048,2304]{1,0:T(8,128)(2,1)} %get-tuple-element.90.q_ref.k_ref.v_ref, bf16[2048,2304]{1,0:T(8,128)(2,1)} %get-tuple-element.90.q_ref.k_ref.v_ref, bf16[16,1536]{1,0:T(8,128)(2,1)} %slice_bitcast_fusion.km_ref.vm_ref, ...), custom_call_target="tpu_custom_call" | custom-call | flops 40894464000 | bytes 14155776 | tf_op jit(solution)/shard_map/attn_bwd/pallas_call | solution.py:254
  275.4 30.6 %attn_bwd.2 = bf16[1024,2304]{1,0:T(8,128)(2,1)} custom-call(bf16[2048,2304]{1,0:T(8,128)(2,1)} %get-tuple-element.90.q_ref.k_ref.v_ref, bf16[2048,2304]{1,0:T(8,128)(2,1)} %get-tuple-element.90.q_ref.k_ref.v_ref, bf16[2048,2304]{1,0:T(8,128)(2,1)} %get-tuple-element.90.q_ref.k_ref.v_ref, bf16[16,1536]{1,0:T(8,128)(2,1)} %copy-done.25, ...), custom_call_target="tpu_custom_call" | custom-call | flops 40894464000 | bytes 14155776 | tf_op jit(solution)/shard_map/attn_bwd/pallas_call | solution.py:254
  306.0 7.1 %fusion.24 = f32[1024,768]{1,0:T(8,128)S(1)} fusion(bf16[1024,2304]{1,0:T(8,128)(2,1)} %attn_bwd.3, bf16[768,3072]{1,0:T(8,128)(2,1)} %copy-done.3), kind=kOutput, calls=%fused_computation.35 | convolution fusion | flops 3623878656 | bytes 11403264 | tf_op jit(solution)/shard_map/dot_general | solution.py:44
  313.2 0.7 convert_reduce_fusion
  313.9 4.0 fusion.28
  317.9 0.7 convert_reduce_fusion.1
  318.6 5.8 %add_convert_fusion = bf16[768,2304]{1,0:T(8,128)(2,1)} fusion(f32[768,2304]{1,0:T(8,128)S(1)} %fusion.28, bf16[1024,2304]{1,0:T(8,128)(2,1)S(1)} %bitcast.109, bf16[2048,768]{1,0:T(8,128)(2,1)S(1)} %copy-done.56), kind=kOutput, calls=%fused_computation.2 | convolution fusion | flops 3627417600 | bytes 16908288 | tf_op jit(solution)/shard_map/dot_general | solution.py:44
  324.5 5.8 %convolution_convert_fusion.2 = bf16[768,768]{1,0:T(8,128)(2,1)} fusion(bf16[2048,768]{1,0:T(8,128)(2,1)} %get-tuple-element.95.attended.o_ref, bf16[2048,768]{1,0:T(8,128)(2,1)S(1)} %copy-done.12), kind=kOutput, calls=%fused_computation.50 | convolution fusion | flops 2416508928 | bytes 7471104 | tf_op jit(solution)/shard_map/dot_general | solution.py:44
  330.3 1.9 fusion.35
  332.1 1.1 copy-done.7
  333.3 6.3 %fusion.22 = (f32[768]{0:T(1024)S(1)}, f32[1024]{0:T(1024)S(1)}, f32[1024]{0:T(1024)S(1)}, f32[768]{0:T(1024)S(1)}, f32[1024]{0:T(1024)S(1)}, /*index=5*/f32[102...) fusion(f32[1024]{0:T(1024)S(1)} %copy-done.42, f32[1024]{0:T(1024)S(1)} %copy-done.35, ...), kind=kOutput, calls=%fused_computation.31 | convolution fusion | flops 3639600128 | bytes 17743872 | tf_op jit(solution)/shard_map/dot_general | solution.py:44
  339.9 0.7 reshape.152.refs_8_
  340.9 0.7 reshape.154.refs_9_
  341.5 15.8 %convolution_convert_fusion.1 = bf16[768,3072]{1,0:T(8,128)(2,1)} fusion(bf16[2048,768]{1,0:T(8,128)(2,1)} %get-tuple-element.97, bf16[2048,3072]{1,0:T(8,128)(2,1)} %get-tuple-element.98), kind=kOutput, calls=%fused_computation.4 | convolution fusion | flops 9666035712 | bytes 20447232 | tf_op jit(solution)/shard_map/dot_general | solution.py:44
  357.4 14.7 %convolution_convert_fusion = bf16[768,3072]{1,0:T(8,128)(2,1)} fusion(bf16[2048,768]{1,0:T(8,128)(2,1)S(1)} %copy-done.57, bf16[2048,3072]{1,0:T(8,128)(2,1)} %get-tuple-element.100), kind=kOutput, calls=%fused_computation.3 | convolution fusion | flops 9666035712 | bytes 20447232 | tf_op jit(solution)/shard_map/dot_general | solution.py:44
  372.0 3.9 fusion.14
  375.9 108.1 %reduce_all.1 = (f32[48,3072]{1,0:T(8,128)}, f32[48,3072]{1,0:T(8,128)}, f32[48,2304]{1,0:T(8,128)}, f32[48,768]{1,0:T(8,128)}, bf16[512,768]{1,0:T(8,128)(2,1)}...) custom-call(bf16[4,2,2,48,3072]{4,3,2,1,0:T(8,128)(2,1)} %bitcast.12, ...), custom_call_target="tpu_custom_call" | custom-call | flops 80000000000 | bytes 50000000 | tf_op jit(solution)/shard_map/reduce_all/pallas_call | solution.py:1050
  484.0 0.7 fusion.36
  484.7 0.7 slice.178
  485.4 0.7 slice.189
  486.2 1.7 reshape.155.pooled
  487.8 14.6 %mem_bwd.1 = (f32[16,768]{1,0:T(8,128)}, f32[48,2304]{1,0:T(8,128)}, f32[48,768]{1,0:T(8,128)}, f32[48,3072]{1,0:T(8,128)}, f32[48,3072]{1,0:T(8,128)}, /*index=...) custom-call(f32[16,768]{1,0:T(8,128)} %mt_ref.3, ...), custom_call_target="tpu_custom_call" | custom-call | flops 24999999488 | bytes 17000000 | tf_op jit(solution)/shard_map/mem_bwd/pallas_call | solution.py:540
  502.5 1.0 slice_reduce_fusion
  503.5 1.3 slice_add_fusion
  504.9 4.1 select_bitcast_fusion.3
  509.3 1.9 pad_maximum_fusion
  511.6 1.9 pad_maximum_fusion.1
  513.5 0.6 add.105
  514.1 0.6 add.106
  514.7 0.8 add.107
  515.6 0.7 add.109
  516.2 0.6 add.110
  518.0 0.9 add.113
  518.9 0.6 add.114
  519.5 0.9 add.115
  (183 shorter events, 8.5 us)
Async XLA Ops:
  0.7 6.0 %copy-start.53 = (s32[2,32]{1,0:T(2,128)S(1)}, s32[2,32]{1,0:T(2,128)}, u32[]{:S(2)}) copy-start(s32[2,32]{1,0:T(2,128)} %param.22) | copy-start | bytes 772
  0.7 7.4 %copy-start.40 = (f32[768]{0:T(1024)S(1)}, f32[768]{0:T(1024)}, u32[]{:S(2)}) copy-start(f32[768]{0:T(1024)} %param.24) | copy-start | bytes 9220
  0.7 8.0 %copy-start.48 = (f32[768]{0:T(1024)S(1)}, f32[768]{0:T(1024)}, u32[]{:S(2)}) copy-start(f32[768]{0:T(1024)} %param.25) | copy-start | bytes 9220
  0.7 8.5 %copy-start.30 = (bf16[48,768]{1,0:T(8,128)(2,1)S(1)}, bf16[48,768]{1,0:T(8,128)(2,1)}, u32[]{:S(2)}) copy-start(bf16[48,768]{1,0:T(8,128)(2,1)} %param.38) | copy-start | bytes 221188
  0.7 8.5 %copy-start.31 = (bf16[48,768]{1,0:T(8,128)(2,1)S(1)}, bf16[48,768]{1,0:T(8,128)(2,1)}, u32[]{:S(2)}) copy-start(bf16[48,768]{1,0:T(8,128)(2,1)} %param.28) | copy-start | bytes 221188
  0.7 8.5 %copy-start.36 = (bf16[48,384]{1,0:T(8,128)(2,1)S(1)}, bf16[48,384]{1,0:T(8,128)(2,1)}, u32[]{:S(2)}) copy-start(bf16[48,384]{1,0:T(8,128)(2,1)} %param.37) | copy-start | bytes 110596
  0.7 8.5 %copy-start.37 = (bf16[48,384]{1,0:T(8,128)(2,1)S(1)}, bf16[48,384]{1,0:T(8,128)(2,1)}, u32[]{:S(2)}) copy-start(bf16[48,384]{1,0:T(8,128)(2,1)} %param.36) | copy-start | bytes 110596
  0.7 8.5 %copy-start.23 = (bf16[48,2304]{1,0:T(8,128)(2,1)S(1)}, bf16[48,2304]{1,0:T(8,128)(2,1)}, u32[]{:S(2)}) copy-start(bf16[48,2304]{1,0:T(8,128)(2,1)} %param.26) | copy-start | bytes 663556
  0.7 11.8 %copy-start.1 = (bf16[48,3072]{1,0:T(8,128)(2,1)S(1)}, bf16[48,3072]{1,0:T(8,128)(2,1)}, u32[]{:S(2)}) copy-start(bf16[48,3072]{1,0:T(8,128)(2,1)} %refs_1_) | copy-start | bytes 884740
  0.8 11.7 %copy-start.2 = (bf16[48,3072]{1,0:T(8,128)(2,1)S(1)}, bf16[48,3072]{1,0:T(8,128)(2,1)}, u32[]{:S(2)}) copy-start(bf16[48,3072]{1,0:T(8,128)(2,1)} %refs_2_) | copy-start | bytes 884740
  0.8 8.5 %copy-start.47 = (f32[2,768]{1,0:T(2,128)S(1)}, f32[2,768]{1,0:T(2,128)}, u32[]{:S(2)}) copy-start(f32[2,768]{1,0:T(2,128)} %param.27) | copy-start | bytes 18436
  0.8 9.4 %copy-start.49 = (f32[768]{0:T(1024)S(1)}, f32[768]{0:T(1024)}, u32[]{:S(2)}) copy-start(f32[768]{0:T(1024)} %param.30) | copy-start | bytes 9220
  0.8 10.0 %copy-start.50 = (f32[768]{0:T(1024)S(1)}, f32[768]{0:T(1024)}, u32[]{:S(2)}) copy-start(f32[768]{0:T(1024)} %param.31) | copy-start | bytes 9220
  0.8 10.5 %copy-start.51 = (f32[768]{0:T(1024)S(1)}, f32[768]{0:T(1024)}, u32[]{:S(2)}) copy-start(f32[768]{0:T(1024)} %param.29) | copy-start | bytes 9220
  0.8 11.1 %copy-start.52 = (f32[768]{0:T(1024)S(1)}, f32[768]{0:T(1024)}, u32[]{:S(2)}) copy-start(f32[768]{0:T(1024)} %param.35) | copy-start | bytes 9220
  3.7 114.4 %collective-permute-start = (bf16[2,512,768]{2,1,0:T(8,128)(2,1)}, bf16[2,512,768]{2,1,0:T(8,128)(2,1)}, u32[]{:S(2)}, u32[]{:S(2)}) collective-permute-start(bf16[2,512,768]{2,1,0:T(8,128)(2,1)} %dynamic-slice_bitcast_fusion.1), channel_id=1, source_target_pairs={{0,1},{1,0},{2,3},{3,2},{4,5},{5,4},{6,7},{7,6},{8,9},{9,8},{10,11... | collective-permute-start | bytes 4718600 | tf_op jit(solution)/shard_map/ppermute | solution.py:1287
  92.7 2.2 copy-start.3
  94.9 2.1 copy-start.4
  97.0 2.2 copy-start.5
  99.3 1.8 copy-start
  112.6 24.4 %copy-start.25 = (bf16[16,1536]{1,0:T(8,128)(2,1)}, bf16[16,1536]{1,0:T(8,128)(2,1)S(1)}, u32[]{:S(2)}) copy-start(bf16[16,1536]{1,0:T(8,128)(2,1)S(1)} %slice.151.km_ref.vm_ref) | copy-start | bytes 147460
  116.8 0.6 copy-start.24
  120.7 48.1 %collective-permute-start.1 = (bf16[2,512,768]{2,1,0:T(8,128)(2,1)}, bf16[2,512,768]{2,1,0:T(8,128)(2,1)}, u32[]{:S(2)}, u32[]{:S(2)}) collective-permute-start(bf16[2,512,768]{2,1,0:T(8,128)(2,1)} %dynamic-slice_bitcast_fusion), channel_id=1, source_target_pairs={{0,1},{1,0},{2,3},{3,2},{4,5},{5,4},{6,7},{7,6},{8,9},{9,8},{10,11... | collective-permute-start | bytes 4718600 | tf_op jit(solution)/shard_map/ppermute | solution.py:1287
  151.2 14.4 %copy-start.6 = (bf16[2048,768]{1,0:T(8,128)(2,1)S(1)}, bf16[2048,768]{1,0:T(8,128)(2,1)}, u32[]{:S(2)}) copy-start(bf16[2048,768]{1,0:T(8,128)(2,1)} %get-tuple-element.94.rows_ref) | copy-start | bytes 9437188
  165.7 1.9 copy-start.39
  166.2 1.4 copy-start.32
  166.2 1.4 copy-start.34
  306.0 7.1 %copy-start.8 = (bf16[1024,2304]{1,0:T(8,128)(2,1)S(1)}, bf16[1024,2304]{1,0:T(8,128)(2,1)}, u32[]{:S(2)}) copy-start(bf16[1024,2304]{1,0:T(8,128)(2,1)} %attn_bwd.3) | copy-start | bytes 14155780
  306.0 7.9 %copy-start.56 = (bf16[2048,768]{1,0:T(8,128)(2,1)S(1)}, bf16[2048,768]{1,0:T(8,128)(2,1)}, u32[]{:S(2)}) copy-start(bf16[2048,768]{1,0:T(8,128)(2,1)} %get-tuple-element.101) | copy-start | bytes 9437188
  313.1 19.0 %copy-start.14 = (f32[1024,768]{1,0:T(8,128)}, f32[1024,768]{1,0:T(8,128)S(1)}, u32[]{:S(2)}) copy-start(f32[1024,768]{1,0:T(8,128)S(1)} %fusion.24) | copy-start | bytes 9437188
  313.1 4.7 slice-start.2
  313.9 4.0 slice-start.3
  317.9 14.2 %slice-start = ((s8[4718592]{0:T(1024)(128)(4,1)}), s8[4194304]{0:T(1024)(128)(4,1)S(1)}, s32[]{:S(2)}) async-start(s8[4718592]{0:T(1024)(128)(4,1)} %bitcast.106), calls=%async_computation | async-start | bytes 8388608
  318.6 5.8 %copy-start.12 = (bf16[2048,768]{1,0:T(8,128)(2,1)S(1)}, bf16[2048,768]{1,0:T(8,128)(2,1)}, u32[]{:S(2)}) copy-start(bf16[2048,768]{1,0:T(8,128)(2,1)} %get-tuple-element.106) | copy-start | bytes 9437188
  318.6 13.5 %slice-start.1 = ((s8[4718592]{0:T(1024)(128)(4,1)}), s8[524288]{0:T(1024)(128)(4,1)S(1)}, s32[]{:S(2)}) async-start(s8[4718592]{0:T(1024)(128)(4,1)} %bitcast.106), calls=%async_computation.1 | async-start | bytes 1048576
  324.4 5.8 %copy-start.11 = (bf16[2048,768]{1,0:T(8,128)(2,1)S(1)}, bf16[2048,768]{1,0:T(8,128)(2,1)}, u32[]{:S(2)}) copy-start(bf16[2048,768]{1,0:T(8,128)(2,1)} %get-tuple-element.96) | copy-start | bytes 9437188
  330.2 3.0 copy-start.7
  330.2 3.0 copy-start.33
  330.2 3.0 copy-start.35
  330.2 3.0 copy-start.41
  330.2 3.0 copy-start.42
  330.2 3.0 copy-start.43
  333.3 6.4 %copy-start.29 = (f32[2,16,768]{2,1,0:T(8,128)S(1)}, f32[2,16,768]{2,1,0:T(8,128)}, u32[]{:S(2)}) copy-start(f32[2,16,768]{2,1,0:T(8,128)} %get-tuple-element.107) | copy-start | bytes 294916
  333.3 6.4 %copy-start.28 = (f32[2,16,768]{2,1,0:T(8,128)S(1)}, f32[2,16,768]{2,1,0:T(8,128)}, u32[]{:S(2)}) copy-start(f32[2,16,768]{2,1,0:T(8,128)} %get-tuple-element.108) | copy-start | bytes 294916
  333.3 6.4 %copy-start.54 = (f32[2]{0:T(128)S(1)}, f32[2]{0:T(128)}, u32[]{:S(2)}) copy-start(f32[2]{0:T(128)} %get-tuple-element.166) | copy-start | bytes 28
  333.3 6.4 %copy-start.55 = (f32[2]{0:T(128)S(1)}, f32[2]{0:T(128)}, u32[]{:S(2)}) copy-start(f32[2]{0:T(128)} %broadcast_subtract_fusion) | copy-start | bytes 28
  333.3 7.4 %copy-start.46 = (f32[8,768]{1,0:T(8,128)S(1)}, f32[8,768]{1,0:T(8,128)}, u32[]{:S(2)}) copy-start(f32[8,768]{1,0:T(8,128)} %get-tuple-element.109) | copy-start | bytes 73732
  333.3 7.4 %copy-start.38 = (f32[9216]{0:T(1024)S(1)}, f32[9216]{0:T(1024)}, u32[]{:S(2)}) copy-start(f32[9216]{0:T(1024)} %custom-call) | copy-start | bytes 110596
  333.3 7.5 %copy-start.44 = (f32[1,3072]{1,0:T(1,128)S(1)}, f32[1,3072]{1,0:T(1,128)}, u32[]{:S(2)}) copy-start(f32[1,3072]{1,0:T(1,128)} %get-tuple-element.110) | copy-start | bytes 36868
  341.5 15.8 %copy-start.57 = (bf16[2048,768]{1,0:T(8,128)(2,1)S(1)}, bf16[2048,768]{1,0:T(8,128)(2,1)}, u32[]{:S(2)}) copy-start(bf16[2048,768]{1,0:T(8,128)(2,1)} %get-tuple-element.99) | copy-start | bytes 9437188
  357.3 14.7 %copy-start.13 = (bf16[2048,768]{1,0:T(8,128)(2,1)S(1)}, bf16[2048,768]{1,0:T(8,128)(2,1)}, u32[]{:S(2)}) copy-start(bf16[2048,768]{1,0:T(8,128)(2,1)} %get-tuple-element.106) | copy-start | bytes 9437188
  357.3 14.7 %copy-start.15 = (f32[1024,768]{1,0:T(8,128)S(1)}, f32[1024,768]{1,0:T(8,128)}, u32[]{:S(2)}) copy-start(f32[1024,768]{1,0:T(8,128)} %copy-done.14) | copy-start | bytes 9437188
  357.4 14.7 %copy-start.16 = (f32[1024,768]{1,0:T(8,128)S(1)}, f32[1024,768]{1,0:T(8,128)}, u32[]{:S(2)}) copy-start(f32[1024,768]{1,0:T(8,128)} %get-tuple-element.191) | copy-start | bytes 9437188
  487.8 17.1 %copy-start.9 = (bf16[1024,768]{1,0:T(8,128)(2,1)S(1)}, bf16[1024,768]{1,0:T(8,128)(2,1)}, u32[]{:S(2)}) copy-start(bf16[1024,768]{1,0:T(8,128)(2,1)} %get-tuple-element.168) | copy-start | bytes 4718596
  487.8 17.1 %copy-start.10 = (bf16[1024,768]{1,0:T(8,128)(2,1)S(1)}, bf16[1024,768]{1,0:T(8,128)(2,1)}, u32[]{:S(2)}) copy-start(bf16[1024,768]{1,0:T(8,128)(2,1)} %get-tuple-element.169) | copy-start | bytes 4718596
  511.5 3.2 copy-start.21
  511.6 3.2 copy-start.22
  511.6 4.0 copy-start.26
  511.6 4.0 copy-start.27
  511.6 6.4 %copy-start.18 = (f32[48,3072]{1,0:T(8,128)S(1)}, f32[48,3072]{1,0:T(8,128)}, u32[]{:S(2)}) copy-start(f32[48,3072]{1,0:T(8,128)} %get-tuple-element.130) | copy-start | bytes 1769476
  511.6 6.4 %copy-start.20 = (f32[48,3072]{1,0:T(8,128)S(1)}, f32[48,3072]{1,0:T(8,128)}, u32[]{:S(2)}) copy-start(f32[48,3072]{1,0:T(8,128)} %get-tuple-element.131) | copy-start | bytes 1769476
  513.5 5.4 %copy-start.45 = (f32[1,3072]{1,0:T(1,128)S(1)}, f32[1,3072]{1,0:T(1,128)}, u32[]{:S(2)}) copy-start(f32[1,3072]{1,0:T(1,128)} %get-tuple-element.132) | copy-start | bytes 36868
  513.5 6.0 %copy-start.17 = (f32[48,3072]{1,0:T(8,128)S(1)}, f32[48,3072]{1,0:T(8,128)}, u32[]{:S(2)}) copy-start(f32[48,3072]{1,0:T(8,128)} %get-tuple-element.133) | copy-start | bytes 1769476
  513.5 6.0 %copy-start.19 = (f32[48,3072]{1,0:T(8,128)S(1)}, f32[48,3072]{1,0:T(8,128)}, u32[]{:S(2)}) copy-start(f32[48,3072]{1,0:T(8,128)} %get-tuple-element.134) | copy-start | bytes 1769476

commit v5 on v4

--- a/solution.py
+++ b/solution.py
@@ -185,17 +185,17 @@
     keys, vals, keys_t, kmem_t, dq, dk, dv,
 ):
     phase = pl.program_id(1)
-    mem = km_ref.shape[0]
+    mem = km_ref.shape[1]
     rows = q_ref.shape[0]
 
     @pl.when((phase == 2) & (pl.program_id(0) < pl.num_programs(0) - 1))
     def _():
-        keys[0:mem, :] = km_ref[...]
+        keys[0:mem, :] = km_ref[0]
         keys[mem:, :] = k_ref[...]
-        vals[0:mem, :] = vm_ref[...]
+        vals[0:mem, :] = vm_ref[0]
         vals[mem:, :] = v_ref[...]
         keys_t[...] = k_ref[...].T
-        kmem_t[...] = km_ref[...].T
+        kmem_t[...] = km_ref[0].T
         dk[...] = jnp.zeros_like(dk)
         dv[...] = jnp.zeros_like(dv)
         scaled_picks = head_rows(HD**-0.5)
@@ -234,48 +234,6 @@
     @pl.when((phase == 1) & (pl.program_id(0) > 0))
     def _():
         out_ref[...] = dv[mem:, :].astype(BF16)
-
-
-def attn_bwd(qkv, kv_mem, grad, lse, middle, seg, first, count):
-    pairs = H // 2
-    rows, width = lse.shape[2], qkv.shape[1] // 3
-    mem = kv_mem.shape[0]
-    wide = 2 * HD
-    at = lambda p: first + jnp.minimum(p, count - 1)
-    spec = lambda off: pl.BlockSpec((rows, wide), lambda p, f, off=off: (seg, off * pairs + at(p)))
-    mspec = lambda off: pl.BlockSpec((mem, wide), lambda p, f, off=off: (0, off * pairs + at(p)))
-    lspec = pl.BlockSpec((1, 2, rows), lambda p, f: (seg * pairs + at(p), 0, 0))
-
-    def place(p, f):
-        late = jnp.where(f == 0, count, 2 * count) + p - 1
-        now = jnp.where(p == count, 3 * count - 1, p)
-        return (0, jnp.where((f == 2) | (p == 0), now, late))
-
-    return pl.pallas_call(
-        attn_bwd_kernel,
-        grid=(count + 1, 3),
-        in_specs=[
-            spec(0), spec(1), spec(2), mspec(0), mspec(1), spec(0), lspec, lspec,
-        ],
-        out_specs=pl.BlockSpec((rows, wide), place),
-        out_shape=jax.ShapeDtypeStruct((rows, 3 * count * wide), BF16),
-        scratch_shapes=[
-            pltpu.VMEM((mem + rows, wide), BF16),
-            pltpu.VMEM((mem + rows, wide), BF16),
-            pltpu.VMEM((wide, rows), BF16),
-            pltpu.VMEM((wide, mem), BF16),
-            pltpu.VMEM((rows, wide), BF16),
-            pltpu.VMEM((mem + rows, wide), F32),
-            pltpu.VMEM((mem + rows, wide), F32),
-        ],
-        compiler_params=pltpu.CompilerParams(vmem_limit_bytes=60 * 2**20),
-        cost_estimate=pl.CostEstimate(
-            flops=count * rows * rows * 6500,
-            bytes_accessed=rows * count * wide * 18,
-            transcendentals=0,
-        ),
-        name="attn_bwd",
-    )(qkv, qkv, qkv, kv_mem, kv_mem, grad, lse, middle)
 
 
 def choose(told, kept, got, out):
@@ -669,22 +627,42 @@
     value_grad[...] = exact(my_result, grad_value, 0, 0)
 
 
-def mem_backward(mt, norms, pooled, shard, group, kept, weights):
+def mem_reduce(mt, norms, pooled, shard, group, kept, weights, terms, gives, small, planes):
     mem, width = mt.shape
     wide, feat = weights[2].shape[1], (weights[0].shape[1] - 3 * width) // 2
     at = lax.broadcasted_iota(jnp.int32, (width, shard), 0) - group * shard
     chosen = (at == lax.broadcasted_iota(jnp.int32, (width, shard), 1)).astype(BF16)
     sizes = (3 * width, width, wide, wide, feat, feat, width)
     shape = jax.ShapeDtypeStruct
-    outs = [
+    mem_outs = [
         shape((mem, width), F32), *[shape((shard, c), F32) for c in sizes], shape((8, width), F32), shape((1, wide), F32),
     ]
-    grad_mt, *rest = mem_call(
-        mem_bwd_kernel, "mem_bwd", (mt, *norms, pooled, chosen, *kept), weights, outs, 25
-    )
+    given = (mt, *norms, pooled, chosen, *kept)
+    cuts, inputs, in_specs, outs, out_specs, scratch = reducer_call(terms, gives, small)
+    vmem = pl.BlockSpec(memory_space=pltpu.VMEM)
+    out = pl.pallas_call(
+        functools.partial(
+            mem_reduce_kernel, planes, cuts, (len(terms), len(gives), len(given) + len(weights), len(mem_outs))
+        ),
+        in_specs=[*in_specs, *[vmem] * len(given), *[pl.BlockSpec(memory_space=pl.ANY)] * len(weights)],
+        out_specs=[*out_specs, *[vmem] * len(mem_outs)],
+        out_shape=[*outs, *mem_outs],
+        scratch_shapes=[
+            *[pltpu.VMEM(w.shape, w.dtype) for w in weights],
+            pltpu.SemaphoreType.DMA((len(weights),)),
+            *scratch,
+        ],
+        compiler_params=pltpu.CompilerParams(
+            collective_id=2, has_side_effects=True, vmem_limit_bytes=60 * 2**20
+        ),
+        cost_estimate=pl.CostEstimate(flops=5 * 10**10, bytes_accessed=30 * 10**6, transcendentals=0),
+        name="mem_reduce",
+    )(*inputs, *given, *weights)
+    n, g = len(terms), len(gives)
+    grad_mt, *rest = out[n + g + 1 :]
     sums, expand_sums = rest[7:]
     vectors = (sums[0], sums[1], sums[2:4], sums[4], sums[5], sums[6], expand_sums[0], sums[7])
-    return grad_mt, tuple(rest[:7]), vectors
+    return out[:n], out[n : n + g], out[n + g], grad_mt, tuple(rest[:7]), vectors
 
 
 def gather_kernel(halved, count, kinds, *refs):
@@ -883,190 +861,286 @@
     return (a.astype(F32) + b.astype(F32)).astype(BF16)
 
 
-def reduce_kernel(planes, cuts, swaps, *refs):
-    count = 1 + max(k for k, _, _ in cuts)
-    grads, gives = refs[:count], refs[count : count + swaps]
-    long_ref, short_ref = refs[count + swaps : count + swaps + 2]
-    outs = refs[count + swaps + 2 : 2 * count + swaps + 2]
-    gots = refs[2 * count + swaps + 2 : 2 * count + 2 * swaps + 2]
-    long_out, short_out = refs[2 * count + 2 * swaps + 2 : 2 * count + 2 * swaps + 4]
-    (
-        mine, got_core, got_x, line, got_z, low, got_y, parts, held, total,
-        load_sem, core_sem, x_sem, z_sem, y_sem, swap_sem, sum_sem,
-    ) = refs[2 * count + 2 * swaps + 4 :]
-    index, plane = lax.axis_index("dp"), lax.axis_index("ctx")
-    deep, cross, core = index // 4, (index // 2) % 2, index % 2
-    place = lambda z, x, c: (z * 2 + x) * 2 + c
-    deeps = (deep + 1 - 2 * lax.rem(deep, 2), lax.rem(deep + 2, 4), 3 - deep)
-    beside, sibling = {"dp": place(deep, 1 - cross, core)}, {"dp": place(deep, cross, 1 - core)}
-    other = {"ctx": 1 - plane}
-    chunks = len(cuts)
-    peers = long_ref.shape[0]
-    rows = long_ref.shape[1]
-    me = index * planes + plane
-
-    def remote(source, landing, sems, at, device):
+class Reducer:
+    def __init__(self, planes, cuts, grads, gives, small_ref, outs, gots, small_out, scratch):
+        self.planes, self.cuts, self.grads, self.gives, self.small_ref = planes, cuts, grads, gives, small_ref
+        self.outs, self.gots, self.small_out = outs, gots, small_out
+        (
+            self.mine, self.got_core, self.got_x, self.line, self.got_z, self.low, self.got_y, self.held, self.total,
+            self.load_sem, self.core_sem, self.x_sem, self.z_sem, self.y_sem, self.swap_sem, self.sum_sem,
+        ) = scratch
+        self.index, self.plane = lax.axis_index("dp"), lax.axis_index("ctx")
+        deep, cross, core = self.index // 4, lax.rem(self.index // 2, 2), lax.rem(self.index, 2)
+        self.deep, self.cross, self.core = deep, cross, core
+        self.place = lambda z, x, c: (z * 2 + x) * 2 + c
+        self.deeps = (deep + 1 - 2 * lax.rem(deep, 2), lax.rem(deep + 2, 4), 3 - deep)
+        self.chunks, self.peers = len(cuts), small_ref.shape[0]
+        self.me = self.index * planes + self.plane
+
+    def remote(self, source, landing, sems, at, device):
         return pltpu.make_async_remote_copy(
             source, landing, sems.at[(0, *at)], sems.at[(1, *at)], device_id=device, device_id_type=pl.DeviceIdType.MESH
         )
 
-    def device(j):
-        return (j // planes, lax.rem(j, planes))
-
-    def small(phase, j, sender):
-        source, landing = (parts.at[j], held.at[sender]) if phase == 0 else (total.at[sender], total.at[sender])
+    def peer(self, j):
+        return (j // self.planes, lax.rem(j, self.planes))
+
+    def small(self, phase, j, sender):
+        source, landing = (
+            (self.small_ref.at[j], self.held.at[sender]) if phase == 0 else (self.total.at[sender], self.total.at[sender])
+        )
         return pltpu.make_async_remote_copy(
-            source, landing, sum_sem.at[0, phase, j], sum_sem.at[1, phase, sender],
-            device_id=device(j), device_id_type=pl.DeviceIdType.MESH,
-        )
-
-    def every(work):
+            source, landing, self.sum_sem.at[0, phase, j], self.sum_sem.at[1, phase, sender],
+            device_id=self.peer(j), device_id_type=pl.DeviceIdType.MESH,
+        )
+
+    def every(self, work):
         def body(step, carry):
-            work(lax.rem(me + step, peers))
+            work(lax.rem(self.me + step, self.peers))
             return carry
 
-        lax.fori_loop(1, peers, body, 0)
-
-    def loop(first, last, work):
+        lax.fori_loop(1, self.peers, body, 0)
+
+    def loop(self, first, last, work):
         def body(c, carry):
             work(c)
             return carry
 
         lax.fori_loop(first, last, body, 0)
 
-    def load(c, x):
-        k, start, wide = cuts[c]
-        return pltpu.make_async_copy(
-            grads[k].at[:, x, core, :, pl.ds(start, wide)], mine.at[c, x], load_sem.at[c, x]
-        )
-
-    def to_core(c, x):
-        k, start, wide = cuts[c]
-        return remote(
-            grads[k].at[:, x, 1 - core, :, pl.ds(start, wide)], got_core.at[c, x], core_sem, (c, x), sibling
-        )
-
-    def swap(k):
-        return remote(gives[k].at[1 - plane], gots[k], swap_sem, (k,), other)
-
-    def arrived(landing, sems, at):
-        remote(landing, landing, sems, at, sibling).wait_recv()
-
-    def to_x(c):
-        return remote(mine.at[c, 1 - cross], got_x.at[c], x_sem, (c,), beside)
-
-    def to_z(c, k):
-        return remote(line.at[c, deeps[k]], got_z.at[c, k], z_sem, (c, k), {"dp": place(deeps[k], cross, core)})
-
-    def to_y(c):
-        return remote(low.at[c], got_y.at[c], y_sem, (c,), other)
-
-    for c in range(chunks):
+    def to_core(self, c, x):
+        k, start, wide = self.cuts[c]
+        source = self.grads[k].at[:, x, 1 - self.core, :, pl.ds(start, wide)]
+        sibling = {"dp": self.place(self.deep, self.cross, 1 - self.core)}
+        return self.remote(source, self.got_core.at[c, x], self.core_sem, (c, x), sibling)
+
+    def to_x(self, c):
+        beside = {"dp": self.place(self.deep, 1 - self.cross, self.core)}
+        return self.remote(self.mine.at[c, 1 - self.cross], self.got_x.at[c], self.x_sem, (c,), beside)
+
+    def to_z(self, c, k):
+        far = {"dp": self.place(self.deeps[k], self.cross, self.core)}
+        return self.remote(self.line.at[c, self.deeps[k]], self.got_z.at[c, k], self.z_sem, (c, k), far)
+
+    def to_y(self, c):
+        return self.remote(self.low.at[c], self.got_y.at[c], self.y_sem, (c,), {"ctx": 1 - self.plane})
+
+    def swap(self, k):
+        return self.remote(
+            self.gives[k].at[1 - self.plane], self.gots[k], self.swap_sem, (k,), {"ctx": 1 - self.plane}
+        )
+
+    def arrived(self, landing, sems, at):
+        self.remote(landing, landing, sems, at, {"ctx": 1 - self.plane}).wait_recv()
+
+    def begin(self):
+        for c, (k, start, wide) in enumerate(self.cuts):
+            for x in range(2):
+                source = self.grads[k].at[:, x, self.core, :, pl.ds(start, wide)]
+                pltpu.make_async_copy(source, self.mine.at[c, x], self.load_sem.at[c, x]).start()
+        barrier = pltpu.get_barrier_semaphore()
+        self.every(
+            lambda j: pl.semaphore_signal(
+                barrier, inc=1, device_id=self.peer(j), device_id_type=pl.DeviceIdType.MESH
+            )
+        )
+        pl.semaphore_wait(barrier, self.peers - 1)
+        for c in range(self.chunks):
+            for x in range(2):
+                self.to_core(c, x).start()
+        self.every(lambda j: self.small(0, j, self.me).start())
+        for k in range(len(self.gives)):
+            self.swap(k).start()
+        self.held[self.me] = self.small_ref[self.me]
+
+    def over_core(self, c):
+        mine, got = self.mine, self.got_core
         for x in range(2):
-            load(c, x).start()
-    parts[:, :rows, :] = long_ref[...]
-    parts[:, rows:, :] = short_ref[...]
-    barrier = pltpu.get_barrier_semaphore()
-    every(lambda j: pl.semaphore_signal(barrier, inc=1, device_id=device(j), device_id_type=pl.DeviceIdType.MESH))
-    pl.semaphore_wait(barrier, peers - 1)
-    for c in range(chunks):
-        for x in range(2):
-            to_core(c, x).start()
-    every(lambda j: small(0, j, me).start())
-    for k in range(swaps):
-        swap(k).start()
-    held[me] = parts[me]
-
-    def over_core(c):
-        for x in range(2):
-            pltpu.make_async_copy(mine.at[c, x], mine.at[c, x], load_sem.at[c, x]).wait()
-            arrived(got_core.at[c, x], core_sem, (c, x))
+            pltpu.make_async_copy(mine.at[c, x], mine.at[c, x], self.load_sem.at[c, x]).wait()
+            self.arrived(got.at[c, x], self.core_sem, (c, x))
             for z in range(4):
-                mine[c, x, z] = add_low(mine[c, x, z], got_core[c, x, z])
-        to_x(c).start()
-
-    loop(0, chunks, over_core)
-    every(lambda j: small(0, j, j).wait_recv())
-    total[me] = jnp.sum(held[...], axis=0)
-    every(lambda j: small(1, j, me).start())
-
-    def over_x(c):
-        arrived(got_x.at[c], x_sem, (c,))
+                mine[c, x, z] = add_low(mine[c, x, z], got[c, x, z])
+        self.to_x(c).start()
+
+    def add_small(self):
+        self.every(lambda j: self.small(0, j, j).wait_recv())
+        self.total[self.me] = jnp.sum(self.held[...], axis=0)
+        self.every(lambda j: self.small(1, j, self.me).start())
+
+    def over_x(self, c):
+        self.arrived(self.got_x.at[c], self.x_sem, (c,))
         for z in range(4):
-            line[c, z] = add_low(mine[c, cross, z], got_x[c, z])
+            self.line[c, z] = add_low(self.mine[c, self.cross, z], self.got_x[c, z])
         for k in range(3):
-            to_z(c, k).start()
-
-    def over_z(c):
-        value = line[c, deep].astype(F32)
+            self.to_z(c, k).start()
+
+    def over_z(self, c):
+        value = self.line[c, self.deep].astype(F32)
         for k in range(3):
-            arrived(got_z.at[c, k], z_sem, (c, k))
-            value = value + got_z[c, k].astype(F32)
-        low[c] = value.astype(BF16)
-        to_y(c).start()
-
-    def both(c):
-        over_x(c)
-        over_z(c - 1)
-
-    over_x(0)
-    loop(1, chunks, both)
-    over_z(chunks - 1)
-    for c, (k, start, wide) in enumerate(cuts):
-        arrived(got_y.at[c], y_sem, (c,))
-        outs[k][:, start : start + wide] = low[c].astype(F32) + got_y[c].astype(F32)
-    every(lambda j: small(1, j, j).wait_recv())
-    long_out[...] = total[:, :rows, :]
-    short_out[...] = total[:, rows:, :]
-    for k in range(swaps):
-        swap(k).wait_recv()
-    every(lambda j: small(0, j, me).wait_send())
-    every(lambda j: small(1, j, me).wait_send())
-    for k in range(swaps):
-        swap(k).wait_send()
-    for c in range(chunks):
-        for x in range(2):
-            to_core(c, x).wait_send()
-
-    def finish(c):
-        to_x(c).wait_send()
-        for k in range(3):
-            to_z(c, k).wait_send()
-        to_y(c).wait_send()
-
-    loop(0, chunks, finish)
-
-
-def reduce_all(grads, gives, long, short, planes):
+            self.arrived(self.got_z.at[c, k], self.z_sem, (c, k))
+            value = value + self.got_z[c, k].astype(F32)
+        self.low[c] = value.astype(BF16)
+        self.to_y(c).start()
+
+    def end(self):
+        for c, (k, start, wide) in enumerate(self.cuts):
+            self.arrived(self.got_y.at[c], self.y_sem, (c,))
+            self.outs[k][:, start : start + wide] = self.low[c].astype(F32) + self.got_y[c].astype(F32)
+        self.every(lambda j: self.small(1, j, j).wait_recv())
+        self.small_out[...] = self.total[...]
+        for k in range(len(self.gives)):
+            self.swap(k).wait_recv()
+        self.every(lambda j: self.small(0, j, self.me).wait_send())
+        self.every(lambda j: self.small(1, j, self.me).wait_send())
+        for k in range(len(self.gives)):
+            self.swap(k).wait_send()
+        for c in range(self.chunks):
+            for x in range(2):
+                self.to_core(c, x).wait_send()
+
+        def finish(c):
+            self.to_x(c).wait_send()
+            for k in range(3):
+                self.to_z(c, k).wait_send()
+            self.to_y(c).wait_send()
+
+        self.loop(0, self.chunks, finish)
+
+
+REDUCER_SCRATCH = 16
+
+
+def reducer_call(grads, gives, small):
     wide = 768
     shard = grads[0].shape[0] // 16
     cuts = [(k, at, wide) for k, g in enumerate(grads) for at in range(0, g.shape[1], wide)]
-    chunks, peers = len(cuts), long.shape[0]
-    small = (peers, long.shape[1] + short.shape[1], long.shape[2])
+    chunks, peers = len(cuts), small.shape[0]
     vmem, hbm = pl.BlockSpec(memory_space=pltpu.VMEM), pl.BlockSpec(memory_space=pl.ANY)
-    shape = jax.ShapeDtypeStruct
-    dma = pltpu.SemaphoreType.DMA
+    shape, dma = jax.ShapeDtypeStruct, pltpu.SemaphoreType.DMA
     low = lambda *dims: pltpu.VMEM((chunks, *dims, shard, wide), BF16)
+    inputs = (*[g.reshape(4, 2, 2, shard, g.shape[1]) for g in grads], *gives, small)
+    in_specs = [hbm] * (len(grads) + len(gives)) + [vmem]
+    outs = [shape((shard, g.shape[1]), F32) for g in grads]
+    outs += [shape(g.shape[1:], BF16) for g in gives] + [shape(small.shape, F32)]
+    out_specs = [vmem] * len(grads) + [hbm] * len(gives) + [vmem]
+    scratch = [
+        low(2, 4), low(2, 4), low(4), low(4), low(3), low(), low(), pltpu.VMEM(small.shape, F32), pltpu.VMEM(small.shape, F32),
+        dma((chunks, 2)), dma((2, chunks, 2)), dma((2, chunks)), dma((2, chunks, 3)), dma((2, chunks)),
+        dma((2, len(gives))), dma((2, 2, peers)),
+    ]
+    return cuts, inputs, in_specs, outs, out_specs, scratch
+
+
+def back_reduce_kernel(planes, cuts, counts, *refs):
+    grads, gives = counts
+    given, rest = refs[:8], refs[8:]
+    ins, rest = rest[: grads + gives + 1], rest[grads + gives + 1 :]
+    out_ref, rest = rest[0], rest[1:]
+    outs, rest = rest[: grads + gives + 1], rest[grads + gives + 1 :]
+    own_scratch, scratch = rest[: len(rest) - REDUCER_SCRATCH], rest[len(rest) - REDUCER_SCRATCH :]
+    reducer = Reducer(
+        planes, cuts, ins[:grads], ins[grads:-1], ins[-1], outs[:grads], outs[grads:-1], outs[-1], scratch
+    )
+    turn, phase = pl.program_id(0), pl.program_id(1)
+    chunks = len(cuts)
+
+    @pl.when((turn == 0) & (phase == 0))
+    def _():
+        reducer.begin()
+
+    at_core = lambda t: jnp.clip(3 * t, 0, chunks)
+    at_x = lambda t: jnp.clip(jnp.maximum(7 * t - 12, 0) // 8, 0, chunks)
+    at_z = lambda t: at_x(t - 2)
+
+    @pl.when((turn > 0) & (phase == 0))
+    def _():
+        reducer.loop(at_core(turn - 1), at_core(turn), reducer.over_core)
+        reducer.loop(at_x(turn - 1), at_x(turn), reducer.over_x)
+        reducer.loop(at_z(turn - 1), at_z(turn), reducer.over_z)
+
+    @pl.when((turn == 4) & (phase == 1))
+    def _():
+        reducer.add_small()
+
+    attn_bwd_kernel(*given, out_ref, *own_scratch)
+
+    @pl.when((turn == pl.num_programs(0) - 1) & (phase == 2))
+    def _():
+        reducer.loop(at_x(turn), chunks, reducer.over_x)
+        reducer.loop(at_z(turn), chunks, reducer.over_z)
+        reducer.end()
+
+
+def back_reduce(qkv, kv_mem, grad, lse, middle, terms, gives, small, planes):
+    pairs = H // 2
+    segs, rows, width = kv_mem.shape[0], lse.shape[2], qkv.shape[1] // 3
+    mem = kv_mem.shape[1]
+    wide = 2 * HD
+    count = segs * pairs
+    cuts, inputs, in_specs, outs, out_specs, scratch = reducer_call(terms, gives, small)
+    at = lambda p: jnp.minimum(p, count - 1)
+    spec = lambda off: pl.BlockSpec((rows, wide), lambda p, f, off=off: (at(p) // pairs, off * pairs + lax.rem(at(p), pairs)))
+    mspec = lambda off: pl.BlockSpec(
+        (1, mem, wide), lambda p, f, off=off: (at(p) // pairs, 0, off * pairs + lax.rem(at(p), pairs))
+    )
+    lspec = pl.BlockSpec((1, 2, rows), lambda p, f: (at(p), 0, 0))
+
+    def place(p, f):
+        which = jnp.where((f == 2) & (p < count), p, jnp.maximum(p - 1, 0))
+        block = jnp.where(p == count, jnp.minimum(f, 1) + 1, jnp.where((f == 2) | (p == 0), 0, f + 1))
+        return (which // pairs, block * pairs + lax.rem(which, pairs))
+
     out = pl.pallas_call(
-        functools.partial(reduce_kernel, planes, cuts, len(gives)),
-        in_specs=[hbm] * (len(grads) + len(gives)) + [vmem] * 2,
-        out_specs=[vmem] * len(grads) + [hbm] * len(gives) + [vmem] * 2,
-        out_shape=[shape((shard, g.shape[1]), F32) for g in grads]
-        + [shape(g.shape[1:], BF16) for g in gives]
-        + [shape(v.shape, F32) for v in (long, short)],
+        functools.partial(back_reduce_kernel, planes, cuts, (len(terms), len(gives))),
+        grid=(count + 1, 3),
+        in_specs=[spec(0), spec(1), spec(2), mspec(0), mspec(1), spec(0), lspec, lspec, *in_specs],
+        out_specs=[pl.BlockSpec((rows, wide), place), *out_specs],
+        out_shape=[jax.ShapeDtypeStruct(qkv.shape, BF16), *outs],
         scratch_shapes=[
-            low(2, 4), low(2, 4), low(4), low(4), low(3), low(), low(),
-            *[pltpu.VMEM(small, F32)] * 3,
-            dma((chunks, 2)), dma((2, chunks, 2)), dma((2, chunks)), dma((2, chunks, 3)), dma((2, chunks)),
-            dma((2, len(gives))), dma((2, 2, peers)),
+            pltpu.VMEM((mem + rows, wide), BF16),
+            pltpu.VMEM((mem + rows, wide), BF16),
+            pltpu.VMEM((wide, rows), BF16),
+            pltpu.VMEM((wide, mem), BF16),
+            pltpu.VMEM((rows, wide), BF16),
+            pltpu.VMEM((mem + rows, wide), F32),
+            pltpu.VMEM((mem + rows, wide), F32),
+            *scratch,
         ],
         compiler_params=pltpu.CompilerParams(
             collective_id=1, has_side_effects=True, vmem_limit_bytes=60 * 2**20
         ),
-        cost_estimate=pl.CostEstimate(flops=8 * 10**10, bytes_accessed=50 * 10**6, transcendentals=0),
-        name="reduce_all",
-    )(*[g.reshape(4, 2, 2, shard, g.shape[1]) for g in grads], *gives, long, short)
-    return out[: len(grads)], out[len(grads) : len(grads) + len(gives)], out[-2], out[-1]
+        cost_estimate=pl.CostEstimate(
+            flops=count * rows * rows * 6500, bytes_accessed=rows * count * wide * 18, transcendentals=0
+        ),
+        name="back_reduce",
+    )(qkv, qkv, qkv, kv_mem, kv_mem, grad, lse, middle, *inputs)
+    return out[0], out[1 : 1 + len(terms)], out[1 + len(terms) : -1], out[-1]
+
+
+def mem_reduce_kernel(planes, cuts, counts, *refs):
+    grads, gives, given, made = counts
+    ins, rest = refs[: grads + gives + 1], refs[grads + gives + 1 :]
+    mem_ins, rest = rest[:given], rest[given:]
+    outs, rest = rest[: grads + gives + 1], rest[grads + gives + 1 :]
+    mem_outs, rest = rest[:made], rest[made:]
+    mem_scratch, scratch = rest[: len(rest) - REDUCER_SCRATCH], rest[len(rest) - REDUCER_SCRATCH :]
+    reducer = Reducer(
+        planes, cuts, ins[:grads], ins[grads:-1], ins[-1], outs[:grads], outs[grads:-1], outs[-1], scratch
+    )
+    chunks = len(cuts)
+    reducer.begin()
+    reducer.loop(0, chunks, reducer.over_core)
+    mem_bwd_kernel(*mem_ins, *mem_outs, *mem_scratch)
+    reducer.add_small()
+    reducer.over_x(0)
+
+    def both(c):
+        reducer.over_x(c)
+        reducer.over_z(c - 1)
+
+    reducer.loop(1, chunks, both)
+    reducer.over_z(chunks - 1)
+    reducer.end()
 
 
 def split_heads(rows):
@@ -1371,20 +1445,25 @@
 
     if quick:
         lse = jnp.concatenate([lse_first, lse_second], axis=0)
-        mems = (kv_first, kv_mem[1])
         spans = [slice(0, seg_rows), slice(seg_rows, 2 * seg_rows)]
+        by_rank = lambda r: r.reshape(ranks, tok_rows, width)
+        peers = groups * ranks
         dk_mem, dv_mem, middle_sums = attn_mem(qkv, kv_mem, attended, grad_attended, lse)
         pooled = pool(jnp.concatenate([dk_mem, dv_mem], axis=2))
-        grads = [
-            attn_bwd(qkv, mems[seg], grad_attended, lse, middle_sums, seg, 0, H // 2) for seg in range(2)
-        ]
-        ends = [input_back(spans[k], [grads[k]], [p["qkv"]]) for k in range(2)]
-        one_gain, one_bias = ends[0][1] + ends[1][1], ends[0][2] + ends[1][2]
-        qkv_sums = sum(jnp.sum(g.astype(F32), axis=0) for g in grads).reshape(3, width)
-        terms = (
+        wide_terms = (
             dot_dims(rows_grad, activ, 0, 0).astype(BF16),
             dot_dims(normed_b, grad_expanded, 0, 0).astype(BF16),
-            sum(dot_dims(normed_a[spans[k]], grads[k], 0, 0) for k in range(2)).astype(BF16),
+        )
+        result_halves = [by_rank(result[a]) for a in spans]
+        grad_qkv, wide_sums, got_result, pooled = back_reduce(
+            qkv, kv_mem, grad_attended, lse, middle_sums, wide_terms, result_halves, pooled.reshape(peers, -1, 128), ranks
+        )
+        pooled = pooled.reshape(2, mem, 2 * width)
+        ends = [input_back(a, [grad_qkv[a]], [p["qkv"]]) for a in spans]
+        one_gain, one_bias = ends[0][1] + ends[1][1], ends[0][2] + ends[1][2]
+        qkv_sums = jnp.sum(grad_qkv.astype(F32), axis=0).reshape(3, width)
+        late_terms = (
+            dot_dims(normed_a, grad_qkv, 0, 0).astype(BF16),
             dot_dims(attended, grad_attn_out, 0, 0).astype(BF16),
         )
     else:
@@ -1430,20 +1509,15 @@
         pooled, vectors = lax.psum((pooled, vectors), ("dp", "ctx"))
 
     if quick:
-        peers = groups * ranks
         flat = jnp.concatenate([v.reshape(-1) for v in vectors])
         lines = pl.cdiv(flat.size, peers * 128)
         flat = jnp.pad(flat, (0, peers * lines * 128 - flat.size)).reshape(peers, lines, 128)
-        halves = [r.reshape(ranks, tok_rows, width) for r in (result[spans[0]], result[spans[1]], ends[0][0], ends[1][0])]
-        summed, gots, pooled, flat = reduce_all(
-            terms, halves, pooled.reshape(peers, -1, 128), flat, ranks
-        )
-        summed = (summed[2], summed[3], summed[1], summed[0])
+        grad_halves = [by_rank(ends[k][0]) for k in range(2)]
+        late_sums, got_grad_rows, flat, grad_mt, mem_matrices, mem_vectors = mem_reduce(
+            memory_tokens, norms, pooled, shard, group, kept, mem_weights_in, late_terms, grad_halves, flat, ranks
+        )
         flat = flat.reshape(-1)
-        pooled = pooled.reshape(2, mem, 2 * width)
-        grad_mt, mem_matrices, mem_vectors = mem_backward(
-            memory_tokens, norms, pooled, shard, group, kept, mem_weights_in
-        )
+        summed = (late_sums[0], late_sums[1], wide_sums[1], wide_sums[0])
     else:
         mine = lambda a: lax.dynamic_slice_in_dim(a, group * shard, shard, 1)
         grad_mt, mem_matrices, mem_vectors = memory_backward(
@@ -1458,9 +1532,9 @@
     matrices = tuple(a + b for a, b in zip(summed, mem_matrices)) + mem_matrices[4:]
     vectors = tuple(a + b for a, b in zip(vectors, mem_vectors))
     if quick:
-        own = [pick(h, rank, 0) for h in halves]
-        block_out = settle(list(zip(own[:2], gots[:2])), flips)
-        token_grad = settle(list(zip(own[2:], gots[2:])), flips)
+        own = lambda halves: [pick(h, rank, 0) for h in halves]
+        block_out = settle(list(zip(own(result_halves), got_result)), flips)
+        token_grad = settle(list(zip(own(grad_halves), got_grad_rows)), flips)
     else:
         block_out, token_grad = result.reshape(tokens.shape), grad_rows.reshape(tokens.shape)
     return (

time: 528 us -> 508 us (0.962)
  Pallas kernels: 393 us -> 353 us
  other arithmetic: 30 us -> 40.4 us
  local copies, waits for them, and re-layouts: 32.1 us -> 38.1 us
    pallas_call x3 -> x2, Pallas kernels: 169 us -> 144 us  [the longest x1 86.1 us: back_reduce(): pl.pallas_call(functools.partial(back_reduce_kernel, planes, cuts, (len(t...]
    pallas_call x2 -> x1, Pallas kernels: 25.4 us -> 10.7 us  [mem_call(): pl.pallas_call(kernel, in_specs=[vmem] * len(given) + [pl.BlockSpec(memor...]
    unnamed x131 -> x123, local copies, waits for them, and re-layouts: 9.98 us -> 14 us
    dot_general x7 -> x6, matrix products: 59.5 us -> 62.3 us  [dot_dims(): lax.dot_general(a, b, (((ca,), (cb,)), ((), ())), precision=precision, pr...]
  transfers between devices with their start and end apart: 2 -> 2, of which waited for: 0 -> 0; matrix products, arithmetic and copies ran while one was open for 3% -> 3% of each run, Pallas kernels for 25% -> 27%
where the time goes in v5:
time: 508 us; the launch traced here: 501 us
  Pallas kernels  353 us (69%)
  matrix products  62.3 us (12%)
  other arithmetic  40.4 us (8%)
  local copies, waits for them, and re-layouts  38.1 us (8%)
    pallas_call x1, Pallas kernels, back_reduce(): pl.pallas_call(functools.partial(back_reduce_kernel, planes, cuts, (len(t...  86.1 us
    pallas_call x1, Pallas kernels, gather_weights(): pl.pallas_call(functools.partial(gather_kernel, halved, count, kinds), in...  80.3 us
    pallas_call x1, Pallas kernels, middle(): pl.pallas_call(middle_kernel, grid_spec=pltpu.PrefetchScalarGridSpec(num_...  64 us
    dot_general x6, matrix products, dot_dims(): lax.dot_general(a, b, (((ca,), (cb,)), ((), ())), precision=precision, pr...  62.3 us
    pallas_call x1, Pallas kernels, mem_reduce(): pl.pallas_call(functools.partial(mem_reduce_kernel, planes, cuts, (len(te...  58.3 us
    pallas_call x2, Pallas kernels, attn_fwd(): pl.pallas_call(attn_fwd_kernel if held is None else attn_fwd_after_kernel...  27.1 us
    pallas_call x1, Pallas kernels, enter(): pl.pallas_call(enter_kernel, grid_spec=pltpu.PrefetchScalarGridSpec(num_s...  14.8 us
    unnamed x123, local copies, waits for them, and re-layouts  14 us
  transfers between devices with their start and end apart: 2, of which 0 were waited for; matrix products, arithmetic and copies ran while one was open for 3% of the time, Pallas kernels for 27%

profile of v5, /device:TPU:0, one launch (start us, length us, event | category | flops | bytes accessed | tf_op | source)
XLA Modules:
  0.0 501.0 jit_solution(7152526432694089173)
XLA Ops:
  0.8 2.8 dynamic-slice_bitcast_fusion.1
  3.6 3.0 collective-permute-start
  11.8 0.6 broadcast_in_dim.45.shift
  12.5 80.3 %gather_weights.1 = (bf16[768,3072]{1,0:T(8,128)(2,1)S(1)}, bf16[768,3072]{1,0:T(8,128)(2,1)S(1)}, bf16[768,3072]{1,0:T(8,128)(2,1)S(1)}, bf16[768,1536]{1,0:T(8,128)(2,1)S(1)}) custom-call(bf16[48,3072]{1,0:T(8,128)(2,1)S(1)} %pad_maximum_fusion.2.refs_0_, bf16[48,3072]{1,0:T(8,128)(2,1)S(1)} %copy-done.1, bf16[48,3072]{1,0:T(8,128)(2,1)S(1)} %copy-done.2, ...), custom_call_target="tpu_custom_call" | custom-call | flops 80000000000 | bytes 33030144 | tf_op jit(solution)/shard_map/gather_weights/pallas_call | solution.py:828
  92.8 2.2 copy-done.3
  95.0 2.1 copy-done.4
  97.1 2.2 copy-done.5
  99.4 1.2 slice.152.out_w
  100.6 0.6 copy-done
  101.2 10.7 %mem_fwd.1 = (bf16[16,2304]{1,0:T(8,128)(2,1)}, bf16[16,768]{1,0:T(8,128)(2,1)}, f32[16,768]{1,0:T(8,128)}, f32[16,3072]{1,0:T(8,128)}, f32[16,768]{1,0:T(8,128)...) custom-call(f32[16,768]{1,0:T(8,128)} %refs_5_.1, ...), custom_call_target="tpu_custom_call" | custom-call | flops 15000000512 | bytes 17000000 | tf_op jit(solution)/shard_map/mem_fwd/pallas_call | solution.py:498
  111.9 0.8 slice.150.km_ref.vm_ref
  113.3 1.3 fusion.32
  115.1 0.8 fusion.30.refs_11_
  116.0 0.9 broadcast_select_fusion.km_ref.vm_ref.refs_3_.refs_4_
  116.9 0.6 copy-done.17
  117.5 0.6 slice_bitcast_fusion.km_ref.vm_ref
  118.1 2.7 dynamic-slice_bitcast_fusion
  120.8 1.5 collective-permute-start.1
  122.3 14.8 %enter.1 = (bf16[2048,768]{1,0:T(8,128)(2,1)}, bf16[2048,768]{1,0:T(8,128)(2,1)}, bf16[2048,2304]{1,0:T(8,128)(2,1)}) custom-call(s32[2]{0:T(128)} %pad_add_fusion.told, bf16[2,2,512,768]{3,2,1,0:T(8,128)(2,1)} %kept.2, bf16[2,512,768]{2,1,0:T(8,128)(2,1)} %collective-permute-done.got, f32[1,768]{1,0:T(1,128)} %broadcast_in_dim.42.gain.one_gain.refs_6_, ...), custom_call_target="tpu_custom_call" | custom-call | flops 14495514624 | bytes 22020096 | tf_op jit(solution)/shard_map/enter/pallas_call | solution.py:274
  137.2 13.5 %attn_fwd.2 = (bf16[2048,768]{1,0:T(8,128)(2,1)}, f32[6,2,1024]{2,1,0:T(2,128)}) custom-call(bf16[2048,2304]{1,0:T(8,128)(2,1)} %get-tuple-element.91.q_ref.k_ref.v_ref.refs_0_.refs_1_.refs_2_, bf16[2048,2304]{1,0:T(8,128)(2,1)} %get-tuple-element.91.q_ref.k_ref.v_ref.refs_0_.refs_1_.refs_2_, ...), custom_call_target="tpu_custom_call" | custom-call | flops 25165824000 | bytes 6291456 | tf_op jit(solution)/shard_map/attn_fwd/pallas_call | solution.py:111
  150.6 0.8 constant_dynamic-update-slice_fusion.1
  151.4 13.6 %attn_fwd.3 = (bf16[2048,768]{1,0:T(8,128)(2,1)}, f32[6,2,1024]{2,1,0:T(2,128)}) custom-call(bf16[2048,2304]{1,0:T(8,128)(2,1)} %get-tuple-element.91.q_ref.k_ref.v_ref.refs_0_.refs_1_.refs_2_, bf16[2048,2304]{1,0:T(8,128)(2,1)} %get-tuple-element.91.q_ref.k_ref.v_ref.refs_0_.refs_1_.refs_2_, ...), custom_call_target="tpu_custom_call", output_to_operand_aliasing={{0}: (5, {})} | custom-call | flops 25165824000 | bytes 6291456 | tf_op jit(solution)/shard_map/attn_fwd/pallas_call | solution.py:111
  165.0 0.8 constant_dynamic-update-slice_fusion.lse_ref.refs_6_
  166.4 1.4 fusion.27
  167.8 0.6 add_rsqrt_fusion.1
  168.4 0.6 add_rsqrt_fusion
  169.0 64.0 %middle.1 = (bf16[2048,768]{1,0:T(8,128)(2,1)}, bf16[2048,768]{1,0:T(8,128)(2,1)}, bf16[2048,768]{1,0:T(8,128)(2,1)}, bf16[2048,3072]{1,0:T(8,128)(2,1)}, bf16[2...) custom-call(s32[2]{0:T(128)} %pad_add_fusion.told, ...), custom_call_target="tpu_custom_call" | custom-call | flops 86973087744 | bytes 47185920 | tf_op jit(solution)/shard_map/middle/pallas_call | solution.py:350
  232.9 3.7 fusion.34
  236.7 12.0 %attn_mem.1 = (f32[2,16,768]{2,1,0:T(8,128)}, f32[2,16,768]{2,1,0:T(8,128)}, f32[12,2,1024]{2,1,0:T(2,128)}) custom-call(bf16[2048,2304]{1,0:T(8,128)(2,1)} %get-tuple-element.91.q_ref.k_ref.v_ref.refs_0_.refs_1_.refs_2_, bf16[2,16,1536]{2,1,0:T(8,128)(2,1)} %copy-done.17, bf16[2,16,1536]{2,1,0:T(8,128)(2,1)} %copy-done.17, ...), custom_call_target="tpu_custom_call" | custom-call | flops 6291456000 | bytes 9437184 | tf_op jit(solution)/shard_map/attn_mem/pallas_call | solution.py:164
  248.7 0.9 constant_dynamic-update-slice_fusion.3
  249.6 0.9 constant_dynamic-update-slice_fusion.2
  250.6 0.7 reshape.148.refs_12_
  251.4 14.8 %convolution_convert_fusion.1 = bf16[768,3072]{1,0:T(8,128)(2,1)} fusion(bf16[2048,768]{1,0:T(8,128)(2,1)S(1)} %copy-done.53, bf16[2048,3072]{1,0:T(8,128)(2,1)} %get-tuple-element.103), kind=kOutput, calls=%fused_computation.2 | convolution fusion | flops 9666035712 | bytes 20447232 | tf_op jit(solution)/shard_map/dot_general | solution.py:44
  266.1 14.5 %convolution_convert_fusion = bf16[768,3072]{1,0:T(8,128)(2,1)} fusion(bf16[2048,768]{1,0:T(8,128)(2,1)S(1)} %copy-done.52, bf16[2048,3072]{1,0:T(8,128)(2,1)} %get-tuple-element.105), kind=kOutput, calls=%fused_computation.1 | convolution fusion | flops 9666035712 | bytes 20447232 | tf_op jit(solution)/shard_map/dot_general | solution.py:44
  280.6 86.1 %back_reduce.1 = (bf16[2048,2304]{1,0:T(8,128)(2,1)}, f32[48,3072]{1,0:T(8,128)}, f32[48,3072]{1,0:T(8,128)}, bf16[512,768]{1,0:T(8,128)(2,1)}, bf16[512,768]{1,0:T(8,128)(2,1)}, /*index=5*/f32[32,12,128]{2,1,0:T(8,128)}) custom-call(bf16[2048,2304]{1,0:T(8,128)(2,1)} %get-tuple-element.91.q_ref.k_ref.v_ref.refs_0_.refs_1_.refs_2_, ...), custom_call_target="tpu_custom_call" | custom-call | flops 81788928000 | bytes 28311552 | tf_op jit(solution)/shard_map/back_reduce/pallas_call | solution.py:1093
  366.8 5.2 %convert_reduce_fusion = f32[2304]{0:T(1024)S(1)} fusion(bf16[2048,2304]{1,0:T(8,128)(2,1)} %get-tuple-element.110), kind=kLoop, calls=%fused_computation | loop fusion | flops 9434880 | bytes 9446400 | tf_op jit(solution)/shard_map/reduce_sum | solution.py:1464
  372.0 1.2 copy-done.8
  373.1 7.6 %fusion.2 = f32[1024,768]{1,0:T(8,128)} fusion(bf16[2048,2304]{1,0:T(8,128)(2,1)S(1)} %copy-done.8, bf16[768,3072]{1,0:T(8,128)(2,1)} %copy-done.3), kind=kOutput, calls=%fused_computation.6 | convolution fusion | flops 3623878656 | bytes 11403264 | tf_op jit(solution)/shard_map/dot_general | solution.py:44
  380.8 3.8 convolution_convert_fusion.3
  384.7 0.7 reshape.155.refs_10_
  385.5 13.8 %convolution_convert_fusion.2 = bf16[768,2304]{1,0:T(8,128)(2,1)} fusion(bf16[2048,768]{1,0:T(8,128)(2,1)} %get-tuple-element.112, bf16[2048,2304]{1,0:T(8,128)(2,1)} %get-tuple-element.110), kind=kOutput, calls=%fused_computation.3 | convolution fusion | flops 7249526784 | bytes 16121856 | tf_op jit(solution)/shard_map/dot_general | solution.py:44
  399.4 7.8 %fusion.19 = (f32[768]{0:T(1024)S(1)}, f32[1024]{0:T(1024)S(1)}, f32[1024]{0:T(1024)S(1)}, f32[768]{0:T(1024)S(1)}, f32[1024]{0:T(1024)S(1)}, /*index=5*/f32[102...) fusion(f32[1024]{0:T(1024)S(1)} %copy-done.38, f32[1024]{0:T(1024)S(1)} %copy-done.30, ...), kind=kOutput, calls=%fused_computation.27 | convolution fusion | flops 3639600128 | bytes 17743872 | tf_op jit(solution)/shard_map/dot_general | solution.py:44
  407.3 0.7 reshape.154.refs_4_
  408.0 8.0 %fusion.25 = (bf16[1024,768]{1,0:T(8,128)(2,1)}, bf16[1024,768]{1,0:T(8,128)(2,1)}) fusion(f32[1024,768]{1,0:T(8,128)} %fusion.2, bf16[2048,768]{1,0:T(8,128)(2,1)} %get-tuple-element.111, f32[1024]{0:T(1024)S(1)} %broadcast_multiply_fusion.3, f32[1024]{0:T(1024)S(1)} %broadcast_multiply_fusion.4, f32[768]{0:T(1024)S(1)} %copy-done.36, ...), kind=kLoop, calls=%fused_computation.33 | loop fusion | flops 17301504 | bytes 15764480 | tf_op jit(solution)/shard_map/convert_element_type | solution.py:1439
  415.9 58.3 %mem_reduce.1 = (f32[48,2304]{1,0:T(8,128)}, f32[48,768]{1,0:T(8,128)}, bf16[512,768]{1,0:T(8,128)(2,1)}, bf16[512,768]{1,0:T(8,128)(2,1)}, f32[32,3,128]{2,1,0:...) custom-call(bf16[4,2,2,48,2304]{4,3,2,1,0:T(8,128)(2,1)} %bitcast.12, ...), custom_call_target="tpu_custom_call" | custom-call | flops 49999998976 | bytes 30000000 | tf_op jit(solution)/shard_map/mem_reduce/pallas_call | solution.py:643
  474.3 0.9 slice.177
  475.1 0.8 slice.188
  475.9 0.7 fusion.35
  476.7 1.0 slice_reduce_fusion
  477.7 1.3 slice_add_fusion
  479.1 2.1 add.107
  481.2 2.1 add.105
  483.3 4.1 select_bitcast_fusion.3
  488.2 0.6 add.106
  488.8 0.6 add.108
  490.0 0.6 add.103
  492.4 0.7 add.101
  493.0 0.8 add.99
  494.0 1.9 pad_maximum_fusion.1
  496.3 1.9 pad_maximum_fusion
  498.2 0.6 copy.53
  498.8 0.6 copy.54
  499.5 0.6 copy.55
  500.1 0.7 copy.56
  (169 shorter events, 10.1 us)
Async XLA Ops:
  0.7 5.9 %copy-start.48 = (s32[2,32]{1,0:T(2,128)S(1)}, s32[2,32]{1,0:T(2,128)}, u32[]{:S(2)}) copy-start(s32[2,32]{1,0:T(2,128)} %param.22) | copy-start | bytes 772
  0.7 7.5 %copy-start.43 = (f32[768]{0:T(1024)S(1)}, f32[768]{0:T(1024)}, u32[]{:S(2)}) copy-start(f32[768]{0:T(1024)} %param.25) | copy-start | bytes 9220
  0.7 8.1 %copy-start.44 = (f32[768]{0:T(1024)S(1)}, f32[768]{0:T(1024)}, u32[]{:S(2)}) copy-start(f32[768]{0:T(1024)} %param.30) | copy-start | bytes 9220
  0.7 8.7 %copy-start.45 = (f32[768]{0:T(1024)S(1)}, f32[768]{0:T(1024)}, u32[]{:S(2)}) copy-start(f32[768]{0:T(1024)} %param.31) | copy-start | bytes 9220
  0.7 9.2 %copy-start.35 = (f32[768]{0:T(1024)S(1)}, f32[768]{0:T(1024)}, u32[]{:S(2)}) copy-start(f32[768]{0:T(1024)} %param.24) | copy-start | bytes 9220
  0.7 9.8 %copy-start.46 = (f32[768]{0:T(1024)S(1)}, f32[768]{0:T(1024)}, u32[]{:S(2)}) copy-start(f32[768]{0:T(1024)} %param.29) | copy-start | bytes 9220
  0.7 10.4 %copy-start.47 = (f32[768]{0:T(1024)S(1)}, f32[768]{0:T(1024)}, u32[]{:S(2)}) copy-start(f32[768]{0:T(1024)} %param.35) | copy-start | bytes 9220
  0.7 11.0 %copy-start.42 = (f32[2,768]{1,0:T(2,128)S(1)}, f32[2,768]{1,0:T(2,128)}, u32[]{:S(2)}) copy-start(f32[2,768]{1,0:T(2,128)} %param.27) | copy-start | bytes 18436
  0.7 11.6 %copy-start.24 = (bf16[48,768]{1,0:T(8,128)(2,1)S(1)}, bf16[48,768]{1,0:T(8,128)(2,1)}, u32[]{:S(2)}) copy-start(bf16[48,768]{1,0:T(8,128)(2,1)} %param.38) | copy-start | bytes 221188
  0.8 11.6 %copy-start.25 = (bf16[48,768]{1,0:T(8,128)(2,1)S(1)}, bf16[48,768]{1,0:T(8,128)(2,1)}, u32[]{:S(2)}) copy-start(bf16[48,768]{1,0:T(8,128)(2,1)} %param.28) | copy-start | bytes 221188
  0.8 11.6 %copy-start.31 = (bf16[48,384]{1,0:T(8,128)(2,1)S(1)}, bf16[48,384]{1,0:T(8,128)(2,1)}, u32[]{:S(2)}) copy-start(bf16[48,384]{1,0:T(8,128)(2,1)} %param.37) | copy-start | bytes 110596
  0.8 11.6 %copy-start.32 = (bf16[48,384]{1,0:T(8,128)(2,1)S(1)}, bf16[48,384]{1,0:T(8,128)(2,1)}, u32[]{:S(2)}) copy-start(bf16[48,384]{1,0:T(8,128)(2,1)} %param.36) | copy-start | bytes 110596
  0.8 11.6 %copy-start.16 = (bf16[48,2304]{1,0:T(8,128)(2,1)S(1)}, bf16[48,2304]{1,0:T(8,128)(2,1)}, u32[]{:S(2)}) copy-start(bf16[48,2304]{1,0:T(8,128)(2,1)} %param.26) | copy-start | bytes 663556
  0.8 11.7 %copy-start.2 = (bf16[48,3072]{1,0:T(8,128)(2,1)S(1)}, bf16[48,3072]{1,0:T(8,128)(2,1)}, u32[]{:S(2)}) copy-start(bf16[48,3072]{1,0:T(8,128)(2,1)} %refs_2_) | copy-start | bytes 884740
  0.8 11.7 %copy-start.1 = (bf16[48,3072]{1,0:T(8,128)(2,1)S(1)}, bf16[48,3072]{1,0:T(8,128)(2,1)}, u32[]{:S(2)}) copy-start(bf16[48,3072]{1,0:T(8,128)(2,1)} %refs_1_) | copy-start | bytes 884740
  3.6 114.5 %collective-permute-start = (bf16[2,512,768]{2,1,0:T(8,128)(2,1)}, bf16[2,512,768]{2,1,0:T(8,128)(2,1)}, u32[]{:S(2)}, u32[]{:S(2)}) collective-permute-start(bf16[2,512,768]{2,1,0:T(8,128)(2,1)} %dynamic-slice_bitcast_fusion.1), channel_id=1, source_target_pairs={{0,1},{1,0},{2,3},{3,2},{4,5},{5,4},{6,7},{7,6},{8,9},{9,8},{10,11... | collective-permute-start | bytes 4718600 | tf_op jit(solution)/shard_map/ppermute | solution.py:1361
  92.8 2.2 copy-start.3
  95.0 2.1 copy-start.4
  97.1 2.2 copy-start.5
  99.4 1.8 copy-start
  112.7 24.4 %copy-start.18 = (bf16[16,1536]{1,0:T(8,128)(2,1)}, bf16[16,1536]{1,0:T(8,128)(2,1)S(1)}, u32[]{:S(2)}) copy-start(bf16[16,1536]{1,0:T(8,128)(2,1)S(1)} %slice.150.km_ref.vm_ref) | copy-start | bytes 147460
  116.9 0.6 copy-start.17
  120.8 48.2 %collective-permute-start.1 = (bf16[2,512,768]{2,1,0:T(8,128)(2,1)}, bf16[2,512,768]{2,1,0:T(8,128)(2,1)}, u32[]{:S(2)}, u32[]{:S(2)}) collective-permute-start(bf16[2,512,768]{2,1,0:T(8,128)(2,1)} %dynamic-slice_bitcast_fusion), channel_id=1, source_target_pairs={{0,1},{1,0},{2,3},{3,2},{4,5},{5,4},{6,7},{7,6},{8,9},{9,8},{10,11... | collective-permute-start | bytes 4718600 | tf_op jit(solution)/shard_map/ppermute | solution.py:1361
  151.4 14.4 %copy-start.6 = (bf16[2048,768]{1,0:T(8,128)(2,1)S(1)}, bf16[2048,768]{1,0:T(8,128)(2,1)}, u32[]{:S(2)}) copy-start(bf16[2048,768]{1,0:T(8,128)(2,1)} %get-tuple-element.95.rows_ref) | copy-start | bytes 9437188
  165.8 1.9 copy-start.34
  166.3 1.4 copy-start.27
  166.4 1.4 copy-start.29
  236.7 13.8 %copy-start.49 = (f32[2]{0:T(128)S(1)}, f32[2]{0:T(128)}, u32[]{:S(2)}) copy-start(f32[2]{0:T(128)} %get-tuple-element.168) | copy-start | bytes 28
  236.7 13.8 %copy-start.50 = (f32[2]{0:T(128)S(1)}, f32[2]{0:T(128)}, u32[]{:S(2)}) copy-start(f32[2]{0:T(128)} %broadcast_subtract_fusion) | copy-start | bytes 28
  236.7 14.7 %copy-start.53 = (bf16[2048,768]{1,0:T(8,128)(2,1)S(1)}, bf16[2048,768]{1,0:T(8,128)(2,1)}, u32[]{:S(2)}) copy-start(bf16[2048,768]{1,0:T(8,128)(2,1)} %get-tuple-element.102) | copy-start | bytes 9437188
  251.3 14.8 %copy-start.52 = (bf16[2048,768]{1,0:T(8,128)(2,1)S(1)}, bf16[2048,768]{1,0:T(8,128)(2,1)}, u32[]{:S(2)}) copy-start(bf16[2048,768]{1,0:T(8,128)(2,1)} %get-tuple-element.104) | copy-start | bytes 9437188
  366.8 6.4 %copy-start.8 = (bf16[2048,2304]{1,0:T(8,128)(2,1)S(1)}, bf16[2048,2304]{1,0:T(8,128)(2,1)}, u32[]{:S(2)}) copy-start(bf16[2048,2304]{1,0:T(8,128)(2,1)} %get-tuple-element.110) | copy-start | bytes 28311556
  373.1 7.6 %copy-start.41 = (f32[8,768]{1,0:T(8,128)S(1)}, f32[8,768]{1,0:T(8,128)}, u32[]{:S(2)}) copy-start(f32[8,768]{1,0:T(8,128)} %get-tuple-element.113) | copy-start | bytes 73732
  373.1 7.7 %copy-start.11 = (bf16[2048,768]{1,0:T(8,128)(2,1)S(1)}, bf16[2048,768]{1,0:T(8,128)(2,1)}, u32[]{:S(2)}) copy-start(bf16[2048,768]{1,0:T(8,128)(2,1)} %get-tuple-element.111) | copy-start | bytes 9437188
  373.1 7.7 %copy-start.51 = (bf16[2048,768]{1,0:T(8,128)(2,1)S(1)}, bf16[2048,768]{1,0:T(8,128)(2,1)}, u32[]{:S(2)}) copy-start(bf16[2048,768]{1,0:T(8,128)(2,1)} %get-tuple-element.96.attended.o_ref) | copy-start | bytes 9437188
  380.8 3.9 copy-start.15
  380.8 18.5 %slice-start = ((s8[4718592]{0:T(1024)(128)(4,1)}), s8[524288]{0:T(1024)(128)(4,1)S(1)}, s32[]{:S(2)}) async-start(s8[4718592]{0:T(1024)(128)(4,1)} %bitcast.104), calls=%async_computation | async-start | bytes 1048576
  385.4 13.9 %slice-start.1 = ((s8[4718592]{0:T(1024)(128)(4,1)}), s8[4194304]{0:T(1024)(128)(4,1)S(1)}, s32[]{:S(2)}) async-start(s8[4718592]{0:T(1024)(128)(4,1)} %bitcast.104), calls=%async_computation.1 | async-start | bytes 8388608
  385.4 13.9 %copy-start.7 = (bf16[2048,768]{1,0:T(8,128)(2,1)S(1)}, bf16[2048,768]{1,0:T(8,128)(2,1)}, u32[]{:S(2)}) copy-start(bf16[2048,768]{1,0:T(8,128)(2,1)} %get-tuple-element.95.rows_ref) | copy-start | bytes 9437188
  385.4 13.9 %copy-start.12 = (f32[1024,768]{1,0:T(8,128)S(1)}, f32[1024,768]{1,0:T(8,128)}, u32[]{:S(2)}) copy-start(f32[1024,768]{1,0:T(8,128)} %fusion.2) | copy-start | bytes 9437188
  385.4 13.9 %copy-start.28 = (f32[1024]{0:T(1024)S(1)}, f32[1024]{0:T(1024)}, u32[]{:S(2)}) copy-start(f32[1024]{0:T(1024)} %copy-done.27) | copy-start | bytes 12292
  385.4 13.9 %copy-start.30 = (f32[1024]{0:T(1024)S(1)}, f32[1024]{0:T(1024)}, u32[]{:S(2)}) copy-start(f32[1024]{0:T(1024)} %copy-done.29) | copy-start | bytes 12292
  385.4 13.9 %copy-start.36 = (f32[768]{0:T(1024)S(1)}, f32[768]{0:T(1024)}, u32[]{:S(2)}) copy-start(f32[768]{0:T(1024)} %param.24) | copy-start | bytes 9220
  385.5 13.9 %copy-start.37 = (f32[1024]{0:T(1024)S(1)}, f32[1024]{0:T(1024)}, u32[]{:S(2)}) copy-start(f32[1024]{0:T(1024)} %add_rsqrt_fusion.1) | copy-start | bytes 12292
  385.5 13.9 %copy-start.38 = (f32[1024]{0:T(1024)S(1)}, f32[1024]{0:T(1024)}, u32[]{:S(2)}) copy-start(f32[1024]{0:T(1024)} %add_rsqrt_fusion) | copy-start | bytes 12292
  399.4 7.8 %copy-start.33 = (f32[9216]{0:T(1024)S(1)}, f32[9216]{0:T(1024)}, u32[]{:S(2)}) copy-start(f32[9216]{0:T(1024)} %custom-call) | copy-start | bytes 110596
  399.4 7.9 %copy-start.39 = (f32[1,3072]{1,0:T(1,128)S(1)}, f32[1,3072]{1,0:T(1,128)}, u32[]{:S(2)}) copy-start(f32[1,3072]{1,0:T(1,128)} %get-tuple-element.114) | copy-start | bytes 36868
  474.2 9.1 %copy-start.9 = (bf16[1024,768]{1,0:T(8,128)(2,1)S(1)}, bf16[1024,768]{1,0:T(8,128)(2,1)}, u32[]{:S(2)}) copy-start(bf16[1024,768]{1,0:T(8,128)(2,1)} %get-tuple-element.170) | copy-start | bytes 4718596
  474.3 9.1 %copy-start.10 = (bf16[1024,768]{1,0:T(8,128)(2,1)S(1)}, bf16[1024,768]{1,0:T(8,128)(2,1)}, u32[]{:S(2)}) copy-start(bf16[1024,768]{1,0:T(8,128)(2,1)} %get-tuple-element.171) | copy-start | bytes 4718596
  487.5 0.7 copy-start.40
  487.5 4.9 copy-start.19
  487.5 4.9 copy-start.20
  487.5 5.5 %copy-start.13 = (f32[48,2304]{1,0:T(8,128)S(1)}, f32[48,2304]{1,0:T(8,128)}, u32[]{:S(2)}) copy-start(f32[48,2304]{1,0:T(8,128)} %get-tuple-element.128) | copy-start | bytes 1327108
  487.5 5.5 %copy-start.14 = (f32[48,2304]{1,0:T(8,128)S(1)}, f32[48,2304]{1,0:T(8,128)}, u32[]{:S(2)}) copy-start(f32[48,2304]{1,0:T(8,128)} %get-tuple-element.129) | copy-start | bytes 1327108
  496.2 2.0 copy-start.26
  496.3 2.6 copy-start.23
  496.3 3.2 copy-start.22
  496.3 3.8 copy-start.21
